TPU v7x, 128 devices: a whole 4x4x4 slice. The times are simulated.
128 devices in a mesh: leaf: 128 (over y, x, z, core).
Axes of the slice: x: 4, y: 4, z: 4, core: 2. Of those that a mesh axis runs over, the one named last changes fastest.
Arguments:
- rhs_solved: float32 [64, 524288], P(None, 'leaf'), may hold values from -6 to 6
- basis: float32 [4, 128, 524288], P(None, None, 'leaf'), may hold values from -0.03125 to 0.03125
- solved_gen: float32 [4, 128, 524288], P(None, None, 'leaf'), may hold values from -0.5 to 0.5
- capacitance: float32 [15, 256, 256], replicated, may hold values from -0.375 to 0.375
Outputs:
- solution: float32 [64, 524288], P(None, 'leaf')
All inputs are finite; a program needn't handle non-finite values.
Results may differ from a plain program's by a relative error of at most 0.00021.
Values sent between devices are 32-bit elements; how exact they have to be, the bound alone decides.
No kernel may reach another device: no remote copies, remote signals or barrier semaphores. Data moves between devices by JAX's collectives and lax.ppermute only.
A program may use at most 128 MiB of HBM per device.

v0:
```python
import jax
import jax.numpy as jnp
from jax import lax
from jax.sharding import PartitionSpec as P


def group_sums(local, child_bit, device, count):
    group = device >> child_bit
    groups_count = count >> child_bit
    marker = (jnp.arange(groups_count, dtype=jnp.int32) == group).astype(jnp.float32)
    slots = marker[:, None, None] * local[None]
    summed = lax.psum(slots, "leaf")
    own = lax.dynamic_index_in_dim(summed, group, 0, keepdims=False)
    other = lax.dynamic_index_in_dim(summed, group ^ 1, 0, keepdims=False)
    return (own, other)


def coefficients(local, level, bits, device, count, capacitance):
    rank = local.shape[1]
    child_bit = bits - level - 1
    own, other = group_sums(local, child_bit, device, count)
    in_second = device >> child_bit & 1 == 1
    joined = jnp.where(
        in_second, jnp.concatenate([own, other], axis=1), jnp.concatenate([other, own], axis=1)
    )
    node = (1 << level) - 1 + (device >> child_bit + 1)
    cap = lax.dynamic_index_in_dim(capacitance, node, 0, keepdims=False)
    coeff = jnp.dot(joined, cap, precision=lax.Precision.HIGHEST)
    return jnp.where(in_second, coeff[:, rank:], coeff[:, :rank])


def body(rhs_solved, basis, solved_gen, capacitance):
    highest = lax.Precision.HIGHEST
    count = lax.axis_size("leaf")
    device = lax.axis_index("leaf")
    bits = count.bit_length() - 1
    levels = basis.shape[0]
    current = rhs_solved
    for level in range(levels - 1, -1, -1):
        local = jnp.einsum("hp,rp->hr", current, basis[level], precision=highest)
        part = coefficients(local, level, bits, device, count, capacitance)
        current = current - jnp.dot(part, solved_gen[level], precision=highest)
    return current


def solution(mesh):
    in_specs = (P(None, "leaf"), P(None, None, "leaf"), P(None, None, "leaf"), P())
    out_specs = P(None, "leaf")
    return jax.shard_map(body, mesh=mesh, in_specs=in_specs, out_specs=out_specs, check_vma=False)
```

profile of v0, /device:TPU:1, one launch (start us, length us, event | category | flops | bytes accessed | tf_op | source)
XLA Modules:
  0.0 614.7 jit_solution(13309382848839735667)
XLA Ops:
  6.5 0.0 all-reduce.5.cloned.1.call-start
  6.5 4.3 fusion.10
  10.8 0.9 broadcast_multiply_fusion
  11.7 0.0 all-reduce.5.cloned.1.call-update
  11.7 0.0 all-reduce.7.cloned.1.call-start
  11.8 148.8 %all-reduce.5.cloned.1.call-done = f32[16,64,128]{2,1,0:T(8,128)} async-done(((f32[16,64,128]{2,1,0:T(8,128)}), f32[16,64,128]{2,1,0:T(8,128)}) %all-reduce.5.cloned.1.call-update) | async-done | bytes 524304 | tf_op jit(solution)/shard_map/psum | solution.py:12
  160.7 0.8 dynamic-slice_bitcast_fusion.7
  161.4 1.2 fusion.26
  162.7 2.8 convolution_subtract_fusion.3
  165.5 3.9 fusion.7
  169.4 0.8 broadcast_multiply_fusion.1
  170.1 0.0 all-reduce.7.cloned.1.call-update
  170.2 0.0 all-reduce.9.cloned.1.call-start
  170.2 140.2 %all-reduce.7.cloned.1.call-done = f32[8,64,128]{2,1,0:T(8,128)} async-done(((f32[8,64,128]{2,1,0:T(8,128)}), f32[8,64,128]{2,1,0:T(8,128)}) %all-reduce.7.cloned.1.call-update) | async-done | bytes 262160 | tf_op jit(solution)/shard_map/psum | solution.py:12
  310.5 0.8 dynamic-slice_bitcast_fusion.5
  311.3 1.2 fusion.24
  312.5 2.8 convolution_subtract_fusion.2
  315.3 3.9 fusion.4
  319.2 0.7 broadcast_multiply_fusion.2
  319.9 0.0 all-reduce.9.cloned.1.call-update
  319.9 0.2 all-reduce.11.cloned.1.call-start
  320.2 137.4 %all-reduce.9.cloned.1.call-done = f32[4,64,128]{2,1,0:T(8,128)} async-done(((f32[4,64,128]{2,1,0:T(8,128)}), f32[4,64,128]{2,1,0:T(8,128)}) %all-reduce.9.cloned.1.call-update) | async-done | bytes 131088 | tf_op jit(solution)/shard_map/psum | solution.py:12
  457.6 0.8 dynamic-slice_bitcast_fusion.3
  458.4 1.2 fusion.22
  459.6 2.8 convolution_subtract_fusion.1
  462.4 3.9 fusion.1
  466.3 0.7 broadcast_multiply_fusion.3
  467.0 0.0 all-reduce.11.cloned.1.call-update
  467.0 135.4 %all-reduce.11.cloned.1.call-done = f32[2,64,128]{2,1,0:T(8,128)} async-done(((f32[2,64,128]{2,1,0:T(8,128)}), f32[2,64,128]{2,1,0:T(8,128)}) %all-reduce.11.cloned.1.call-update) | async-done | bytes 65552 | tf_op jit(solution)/shard_map/psum | solution.py:12
  602.4 0.8 dynamic-slice_bitcast_fusion.1
  603.1 1.2 fusion.20
  604.3 3.8 convolution_subtract_fusion
  (6 shorter events, 0.0 us)
Async XLA Ops:
  6.5 156.1 %copy-start = (f32[64,4096]{1,0:T(8,128)S(1)}, f32[64,4096]{1,0:T(8,128)}, u32[]{:S(2)}) copy-start(f32[64,4096]{1,0:T(8,128)} %param.4) | copy-start | bytes 3145732
  6.5 154.1 %all-reduce.5.cloned.1.call-start = ((), (), s32[]{:S(2)}) async-start(), calls=%async_computation | async-start | bytes 1048576 | tf_op jit(solution)/shard_map/psum | solution.py:12
  11.7 298.7 %all-reduce.7.cloned.1.call-start = ((), (), s32[]{:S(2)}) async-start(), calls=%async_computation.1 | async-start | bytes 524288 | tf_op jit(solution)/shard_map/psum | solution.py:12
  170.2 287.4 %all-reduce.9.cloned.1.call-start = ((), (), s32[]{:S(2)}) async-start(), calls=%async_computation.2 | async-start | bytes 262144 | tf_op jit(solution)/shard_map/psum | solution.py:12
  319.9 282.4 %all-reduce.11.cloned.1.call-start = ((), (), s32[]{:S(2)}) async-start(), calls=%async_computation.3 | async-start | bytes 131072 | tf_op jit(solution)/shard_map/psum | solution.py:12
Sparse Core Ops, SparseCore 0:
  12.1 148.5 all-reduce.4
  170.3 140.1 all-reduce.6
  320.0 137.4 all-reduce.8
  467.1 135.2 all-reduce.10
where the time goes:
time: 615 us
  waiting for transfers between devices  562 us (91%)
  matrix products  32.9 us (5%)
  between operations  13.3 us (2%)
    psum x4, waiting for transfers between devices, group_sums(): summed = lax.psum(slots, 'leaf')  562 us
    dot_general x4, matrix products, body(): local = jnp.einsum('hp,rp->hr', current, basis[level], precision=highest)  15.9 us
  transfers between devices with their start and end apart: 4, of which 4 were waited for; matrix products, arithmetic and copies ran while one was open for 0% of the time, Pallas kernels for 0%

commit v1 on v0

v1 whole, which is shorter than its diff:
```python
import functools

import jax
import jax.numpy as jnp
from jax import lax
from jax.experimental import pallas as pl
from jax.experimental.pallas import tpu as pltpu
from jax.sharding import PartitionSpec as P

F32 = jnp.float32
BF16 = jnp.bfloat16
RANK = 128
RHS = 64
DEVICES = 128
CHUNK = 1024
ANY = pl.BlockSpec(memory_space=pl.ANY)
VMEM = pl.BlockSpec(memory_space=pltpu.VMEM)
SMEM = pl.BlockSpec(memory_space=pltpu.SMEM)

CORE = 1
Z_MASKS = (2, 6, 4)
X_MASKS = (8, 24, 16)
Y_MASKS = (32, 96, 64)


def split(value):
    high = value.astype(BF16)
    return high, (value - high.astype(F32)).astype(BF16)


def stacked(values):
    parts = [split(v) for v in values]
    return jnp.concatenate([h for h, _ in parts] + [l for _, l in parts], axis=0)


def product(left, right):
    lh, ll = split(left)
    rh, rl = split(right)
    rows = left.shape[0]
    both = jnp.dot(jnp.concatenate([lh, ll], axis=0), rh, preferred_element_type=F32)
    return both[:rows] + both[rows:] + jnp.dot(lh, rl, preferred_element_type=F32)


def contract(left, right):
    return lax.dot_general(left, right, (((1,), (1,)), ((), ())), preferred_element_type=F32)


def fold(total, rows):
    half = total.shape[1] // 2
    wide = total[:rows] + total[rows:]
    return wide[:, :half] + wide[:, half:]


def params(limit):
    return pltpu.CompilerParams(vmem_limit_bytes=limit)


def chunk_copies(sources, buffers, sems, points):
    copies = []
    for i in range(points // CHUNK):
        cols = pl.ds(i * CHUNK, CHUNK)
        row = []
        for j, (ref, level) in enumerate(sources):
            src = ref.at[:, cols] if level is None else ref.at[level, :, cols]
            row.append(pltpu.make_async_copy(src, buffers[j].at[:, cols], sems.at[i, j]))
        copies.append(row)
    return copies


def first_kernel(points, core_ref, rhs_ref, basis_ref, gen_ref, keep_ref, send_ref,
                 rhs_buf, v3_buf, v2_buf, u3_buf, acc2, acc3, sems):
    buffers = (rhs_buf, v3_buf, v2_buf, u3_buf)
    sources = ((rhs_ref, None), (basis_ref, 3), (basis_ref, 2), (gen_ref, 3))
    copies = chunk_copies(sources, buffers, sems, points)
    for row in copies:
        for copy in row:
            copy.start()
    for i, row in enumerate(copies):
        for copy in row:
            copy.wait()
        cols = pl.ds(i * CHUNK, CHUNK)
        rhs = stacked([rhs_buf[:, cols]])
        u3 = stacked([u3_buf[:, cols]])
        v3 = stacked([v3_buf[:, cols]])
        v2 = stacked([v2_buf[:, cols]])
        left = jnp.concatenate([rhs, u3], axis=0)
        two, three = contract(left, v2), contract(rhs, v3)
        if i == 0:
            acc2[...] = two
            acc3[...] = three
        else:
            acc2[...] += two
            acc3[...] += three
    p3 = fold(acc3[...], RHS)
    p2 = fold(acc2[: 2 * RHS], RHS)
    g32 = fold(acc2[2 * RHS :], RANK)
    first = core_ref[0] == 0

    @pl.when(first)
    def _():
        keep_ref[:RHS] = p3
        keep_ref[RHS:] = p2
        send_ref[...] = g32

    @pl.when(jnp.logical_not(first))
    def _():
        send_ref[:RHS] = p3
        send_ref[RHS:] = p2
        keep_ref[...] = g32


def first_step(core, rhs, basis, gen):
    points = rhs.shape[1]
    half = jax.ShapeDtypeStruct((RANK, RANK), F32)
    return pl.pallas_call(
        functools.partial(first_kernel, points),
        out_shape=(half, half),
        in_specs=[SMEM, ANY, ANY, ANY],
        out_specs=(VMEM, VMEM),
        scratch_shapes=[
            pltpu.VMEM((RHS, points), F32),
            pltpu.VMEM((RANK, points), F32),
            pltpu.VMEM((RANK, points), F32),
            pltpu.VMEM((RANK, points), F32),
            pltpu.VMEM((2 * (RHS + RANK), 2 * RANK), F32),
            pltpu.VMEM((2 * RHS, 2 * RANK), F32),
            pltpu.SemaphoreType.DMA((points // CHUNK, 4)),
        ],
        compiler_params=params(24 << 20),
        cost_estimate=pl.CostEstimate(flops=800_000_000, bytes_accessed=7_340_032, transcendentals=0),
        name="project_low",
    )(core, rhs, basis, gen)


def related(cap_ref, out_ref, sems, node, s, base, columns):
    copies = []
    for r, row in enumerate((1 - s, s)):
        for c, col in enumerate((s, 1 - s)[:columns]):
            copies.append(
                pltpu.make_async_copy(
                    cap_ref.at[node, pl.ds(pl.multiple_of(row * RANK, RANK), RANK), pl.ds(pl.multiple_of(col * RANK, RANK), RANK)],
                    out_ref.at[r * RANK : (r + 1) * RANK, c * RANK : (c + 1) * RANK],
                    sems.at[base + 2 * r + c],
                )
            )
    for copy in copies:
        copy.start()
    return copies


def grams_kernel(points, place_ref, rhs_ref, basis_ref, gen_ref, cap_ref,
                 p_ref, g_ref, g10_ref, c3a_ref, c3b_ref, c2_ref, c1a_ref, c1b_ref, c0_ref,
                 rhs_buf, v1_buf, v0_buf, u3_buf, u2_buf, u1_buf, acc1, acc0, sems, cap_sems):
    buffers = (rhs_buf, v1_buf, v0_buf, u3_buf, u2_buf, u1_buf)
    sources = ((rhs_ref, None), (basis_ref, 1), (basis_ref, 0), (gen_ref, 3), (gen_ref, 2), (gen_ref, 1))
    copies = chunk_copies(sources, buffers, sems, points)
    for row in copies:
        for copy in row:
            copy.start()
    s3, s2, s1, s0 = place_ref[0], place_ref[1], place_ref[2], place_ref[3]
    n3, n2, n1 = place_ref[4], place_ref[5], place_ref[6]
    caps = related(cap_ref, c3a_ref, cap_sems, 7 + n3, s3, 0, 2)
    caps += related(cap_ref, c3b_ref, cap_sems, 7 + (n3 ^ 1), s3, 4, 2)
    caps += related(cap_ref, c2_ref, cap_sems, 3 + n2, s2, 8, 1)
    caps += related(cap_ref, c1a_ref, cap_sems, 1 + n1, s1, 12, 2)
    caps += related(cap_ref, c1b_ref, cap_sems, 1 + (n1 ^ 1), s1, 16, 2)
    caps += related(cap_ref, c0_ref, cap_sems, 0, s0, 20, 1)
    for i, row in enumerate(copies):
        for copy in row:
            copy.wait()
        cols = pl.ds(i * CHUNK, CHUNK)
        rhs = stacked([rhs_buf[:, cols]])
        u3 = stacked([u3_buf[:, cols]])
        u2 = stacked([u2_buf[:, cols]])
        u1 = stacked([u1_buf[:, cols]])
        v1 = stacked([v1_buf[:, cols]])
        v0 = stacked([v0_buf[:, cols]])
        left1 = jnp.concatenate([rhs, u3, u2], axis=0)
        left0 = jnp.concatenate([rhs, u3, u2, u1], axis=0)
        one, zero = contract(left1, v1), contract(left0, v0)
        if i == 0:
            acc1[...] = one
            acc0[...] = zero
        else:
            acc1[...] += one
            acc0[...] += zero
    at3, at2, at1 = 2 * RHS, 2 * RHS + 2 * RANK, 2 * RHS + 4 * RANK
    p_ref[:, :RANK] = fold(acc1[:at3], RHS)
    p_ref[:, RANK:] = fold(acc0[:at3], RHS)
    g_ref[:RANK, :RANK] = fold(acc1[at3:at2], RANK)
    g_ref[:RANK, RANK:] = fold(acc0[at3:at2], RANK)
    g_ref[RANK:, :RANK] = fold(acc1[at2:at1], RANK)
    g_ref[RANK:, RANK:] = fold(acc0[at2:at1], RANK)
    g10_ref[...] = fold(acc0[at1:], RANK)
    for copy in caps:
        copy.wait()


def grams_step(place, rhs, basis, gen, cap):
    points = rhs.shape[1]

    def out(rows, cols):
        return jax.ShapeDtypeStruct((rows, cols), F32)

    wide = pltpu.VMEM((RANK, points), F32)
    rows1 = 2 * RHS + 4 * RANK
    return pl.pallas_call(
        functools.partial(grams_kernel, points),
        out_shape=(
            out(RHS, 2 * RANK), out(2 * RANK, 2 * RANK), out(RANK, RANK),
            out(2 * RANK, 2 * RANK), out(2 * RANK, 2 * RANK), out(2 * RANK, RANK),
            out(2 * RANK, 2 * RANK), out(2 * RANK, 2 * RANK), out(2 * RANK, RANK),
        ),
        in_specs=[SMEM, ANY, ANY, ANY, ANY],
        out_specs=(VMEM,) * 9,
        scratch_shapes=[
            pltpu.VMEM((RHS, points), F32), wide, wide, wide, wide, wide,
            pltpu.VMEM((rows1, 2 * RANK), F32),
            pltpu.VMEM((rows1 + 2 * RANK, 2 * RANK), F32),
            pltpu.SemaphoreType.DMA((points // CHUNK, 6)),
            pltpu.SemaphoreType.DMA((24,)),
        ],
        compiler_params=params(32 << 20),
        cost_estimate=pl.CostEstimate(flops=3_000_000_000, bytes_accessed=11_534_336, transcendentals=0),
        name="grams_high",
    )(place, rhs, basis, gen, cap)


def middle_kernel(core_ref, mine_ref, other_ref, c3a_ref, c3b_ref, c2_ref, p_ref, g_ref, g10_ref,
                  t_ref, keep_ref, send_ref):
    first = core_ref[0] == 0
    p, g = [], []
    for m in range(4):
        mine, other = mine_ref[m], other_ref[m]
        p.append(jnp.where(first, mine, other))
        g.append(jnp.where(first, other, mine))
    t = []
    for pair, cap in ((0, c3a_ref), (2, c3b_ref)):
        joined = jnp.concatenate([p[pair][:RHS], p[pair + 1][:RHS]], axis=1)
        both = product(joined, cap[...])
        t += [both[:, :RANK], both[:, RANK:]]
    q2 = [p[m][RHS:] - product(t[m], g[m]) for m in range(4)]
    joined = jnp.concatenate([q2[0] + q2[1], q2[2] + q2[3]], axis=1)
    coeff = jnp.concatenate([t[0], product(joined, c2_ref[...])], axis=1)
    t_ref[...] = coeff
    q = p_ref[...] - product(coeff, g_ref[...])
    half = RHS // 2

    def put(ref, c):
        rows = slice(c * half, (c + 1) * half)
        ref[:half] = q[rows, :RANK]
        ref[half : 2 * half] = q[rows, RANK:]
        ref[2 * half :] = g10_ref[c * RHS : (c + 1) * RHS]

    @pl.when(first)
    def _():
        put(keep_ref, 0)
        put(send_ref, 1)

    @pl.when(jnp.logical_not(first))
    def _():
        put(keep_ref, 1)
        put(send_ref, 0)


def middle_step(core, mine, other, c3a, c3b, c2, p, g, g10):
    half = jax.ShapeDtypeStruct((RANK, RANK), F32)
    return pl.pallas_call(
        middle_kernel,
        out_shape=(jax.ShapeDtypeStruct((RHS, 2 * RANK), F32), half, half),
        in_specs=[SMEM] + [VMEM] * 8,
        out_specs=(VMEM,) * 3,
        compiler_params=params(16 << 20),
        cost_estimate=pl.CostEstimate(flops=120_000_000, bytes_accessed=1_500_000, transcendentals=0),
        name="coefficients_low",
    )(core, mine, other, c3a, c3b, c2, p, g, g10)


def apply_chunks(points, levels, coeff, cur_ref, gen_ref, out_ref, cur_buf, hi_buf, lo_buf, sems, out_sems, compute):
    sources = ((cur_ref, None), (gen_ref, levels[0]), (gen_ref, levels[1]))
    copies = chunk_copies(sources, (cur_buf, hi_buf, lo_buf), sems, points)
    for row in copies:
        for copy in row:
            copy.start()
    th, tl = split(compute() if coeff is None else coeff)
    left = jnp.concatenate([th, tl], axis=0)
    outs = []
    for i, row in enumerate(copies):
        for copy in row:
            copy.wait()
        cols = pl.ds(i * CHUNK, CHUNK)
        gens = jnp.concatenate([hi_buf[:, cols], lo_buf[:, cols]], axis=0)
        gh, gl = split(gens)
        both = jnp.dot(left, gh, preferred_element_type=F32)
        update = both[:RHS] + both[RHS:] + jnp.dot(th, gl, preferred_element_type=F32)
        cur_buf[:, cols] = cur_buf[:, cols] - update
        copy = pltpu.make_async_copy(cur_buf.at[:, cols], out_ref.at[:, cols], out_sems.at[i])
        copy.start()
        outs.append(copy)
    for copy in outs:
        copy.wait()


def apply_scratch(points):
    wide = pltpu.VMEM((RANK, points), F32)
    return [
        pltpu.VMEM((RHS, points), F32), wide, wide,
        pltpu.SemaphoreType.DMA((points // CHUNK, 3)),
        pltpu.SemaphoreType.DMA((points // CHUNK,)),
    ]


def low_update_kernel(points, t_ref, cur_ref, gen_ref, out_ref, *scratch):
    apply_chunks(points, (3, 2), t_ref[...], cur_ref, gen_ref, out_ref, *scratch, None)


def low_update(t, rhs, gen):
    points = rhs.shape[1]
    return pl.pallas_call(
        functools.partial(low_update_kernel, points),
        out_shape=jax.ShapeDtypeStruct(rhs.shape, F32),
        in_specs=[VMEM, ANY, ANY],
        out_specs=ANY,
        scratch_shapes=apply_scratch(points),
        compiler_params=params(16 << 20),
        cost_estimate=pl.CostEstimate(flops=402_653_184, bytes_accessed=6_291_456, transcendentals=0),
        name="update_low",
    )(t, rhs, gen)


def last_kernel(points, core_ref, mine_ref, other_ref, c1a_ref, c1b_ref, c0_ref, cur_ref, gen_ref, out_ref, *scratch):
    def compute():
        first = core_ref[0] == 0
        half = RHS // 2
        q1, q0, g = [], [], []
        for m in range(4):
            mine, other = mine_ref[m], other_ref[m]
            low = jnp.where(first, mine, other)
            high = jnp.where(first, other, mine)
            q1.append(jnp.concatenate([low[:half], high[:half]], axis=0))
            q0.append(jnp.concatenate([low[half:RHS], high[half:RHS]], axis=0))
            g.append(jnp.concatenate([low[RHS:], high[RHS:]], axis=0))
        t = []
        for pair, cap in ((0, c1a_ref), (2, c1b_ref)):
            both = product(jnp.concatenate([q1[pair], q1[pair + 1]], axis=1), cap[...])
            t += [both[:, :RANK], both[:, RANK:]]
        r = [q0[m] - product(t[m], g[m]) for m in range(4)]
        joined = jnp.concatenate([r[0] + r[1], r[2] + r[3]], axis=1)
        return jnp.concatenate([t[0], product(joined, c0_ref[...])], axis=1)

    apply_chunks(points, (1, 0), None, cur_ref, gen_ref, out_ref, *scratch, compute)


def last_step(core, mine, other, c1a, c1b, c0, cur, gen):
    points = cur.shape[1]
    return pl.pallas_call(
        functools.partial(last_kernel, points),
        out_shape=jax.ShapeDtypeStruct(cur.shape, F32),
        in_specs=[SMEM] + [VMEM] * 5 + [ANY, ANY],
        out_specs=ANY,
        scratch_shapes=apply_scratch(points),
        compiler_params=params(16 << 20),
        cost_estimate=pl.CostEstimate(flops=500_000_000, bytes_accessed=7_000_000, transcendentals=0),
        name="update_high",
    )(core, mine, other, c1a, c1b, c0, cur, gen)


def swap(value, even, odd):
    pairs = [(i, i ^ (odd if i & CORE else even)) for i in range(DEVICES)]
    return lax.ppermute(value, "leaf", pairs)


def gathered(value, even, odd):
    one, three, two = (swap(value, e, o) for e, o in zip(even, odd))
    return value, one, two, three


def body(rhs, basis, gen, cap):
    device = lax.axis_index("leaf").astype(jnp.int32)
    core = (device & 1).reshape(1)
    place = jnp.stack([
        device >> 3 & 1, device >> 4 & 1, device >> 5 & 1, device >> 6 & 1,
        device >> 4, device >> 5, device >> 6,
    ])
    keep, send = first_step(core, rhs, basis, gen)
    p, g, g10, c3a, c3b, c2, c1a, c1b, c0 = grams_step(place, rhs, basis, gen, cap)
    chip = keep + swap(send, CORE, CORE)
    a, b, c, d = gathered(chip, Z_MASKS, Z_MASKS)
    line = a + b + c + d
    lines = jnp.stack(gathered(line, X_MASKS, X_MASKS))
    other = swap(lines, CORE, CORE)
    t, keep, send = middle_step(core, lines, other, c3a, c3b, c2, p, g, g10)
    current = low_update(t, rhs, gen)
    chip = keep + swap(send, CORE, CORE)
    a, b, c, d = gathered(chip, X_MASKS, Z_MASKS)
    part = a + b + c + d
    a, b, c, d = gathered(part, Z_MASKS, X_MASKS)
    plane = a + b + c + d
    planes = jnp.stack(gathered(plane, Y_MASKS, Y_MASKS))
    other = swap(planes, CORE, CORE)
    return last_step(core, planes, other, c1a, c1b, c0, current, gen)


def solution(mesh):
    in_specs = (P(None, "leaf"), P(None, None, "leaf"), P(None, None, "leaf"), P())
    return jax.shard_map(body, mesh=mesh, in_specs=in_specs, out_specs=P(None, "leaf"), check_vma=False)
```

time: 615 us -> 76.9 us (0.13)
  waiting for transfers between devices: 562 us -> 18.4 us
  matrix products: 32.9 us -> 0 us
  starting transfers between devices: 0.31 us -> 29 us
  Pallas kernels: 0 us -> 15.3 us
  between operations: 13.3 us -> 0.27 us
  local copies, waits for them, and re-layouts: 3.12 us -> 13.6 us
    psum x4 -> x0, waiting for transfers between devices: 562 us -> none  [group_sums(): summed = lax.psum(slots, 'leaf')]
    dot_general x12 -> x0, matrix products: 32.9 us -> none  [the longest x4 15.9 us: body(): local = jnp.einsum('hp,rp->hr', current, basis[level], precision=highest)]
    ppermute x0 -> x19, starting transfers between devices: none -> 29 us  [swap(): return lax.ppermute(value, 'leaf', pairs)]
    ppermute x0 -> x19, waiting for transfers between devices: none -> 18.4 us  [swap(): return lax.ppermute(value, 'leaf', pairs)]
    pallas_call x0 -> x5, Pallas kernels: none -> 15.3 us  [the longest x1 7.06 us: grams_step(): pl.pallas_call(functools.partial(grams_kernel, points), out_shape=(out(RH...]
    unnamed x2 -> x16, local copies, waits for them, and re-layouts: 0.01 us -> 13.5 us
  transfers between devices with their start and end apart: 4 -> 19, of which waited for: 4 -> 12; matrix products, arithmetic and copies ran while one was open for 0% -> 0% of each run, Pallas kernels for 0% -> 12%
where the time goes in v1:
time: 76.9 us; the launch traced here: 76.6 us
  starting transfers between devices  29 us (38%)
  waiting for transfers between devices  18.4 us (24%)
  Pallas kernels  15.3 us (20%)
  local copies, waits for them, and re-layouts  13.6 us (18%)
    ppermute x19, starting transfers between devices, swap(): return lax.ppermute(value, 'leaf', pairs)  29 us
    ppermute x19, waiting for transfers between devices, swap(): return lax.ppermute(value, 'leaf', pairs)  18.4 us
    unnamed x16, local copies, waits for them, and re-layouts  13.5 us
    pallas_call x1, Pallas kernels, grams_step(): pl.pallas_call(functools.partial(grams_kernel, points), out_shape=(out(RH...  7.06 us
    pallas_call x1, Pallas kernels, last_step(): pl.pallas_call(functools.partial(last_kernel, points), out_shape=jax.Shap...  3.01 us
    pallas_call x1, Pallas kernels, first_step(): pl.pallas_call(functools.partial(first_kernel, points), out_shape=(half,...  2.7 us
    pallas_call x1, Pallas kernels, low_update(): pl.pallas_call(functools.partial(low_update_kernel, points), out_shape=ja...  1.81 us
  transfers between devices with their start and end apart: 19, of which 12 were waited for; matrix products, arithmetic and copies ran while one was open for 0% of the time, Pallas kernels for 12%

profile of v1, /device:TPU:1, one launch (start us, length us, event | category | flops | bytes accessed | tf_op | source)
XLA Modules:
  0.0 76.6 jit_solution(416499902511880750)
XLA Ops:
  0.0 3.4 %copy-done = f32[4,128,4096]{2,1,0:T(8,128)S(1)} copy-done((f32[4,128,4096]{2,1,0:T(8,128)S(1)}, f32[4,128,4096]{2,1,0:T(8,128)}, u32[]{:S(2)}) %copy-start) | copy-done | bytes 8388632
  3.4 3.4 %copy-done.1 = f32[4,128,4096]{2,1,0:T(8,128)S(1)} copy-done((f32[4,128,4096]{2,1,0:T(8,128)S(1)}, f32[4,128,4096]{2,1,0:T(8,128)}, u32[]{:S(2)}) %copy-start.1) | copy-done | bytes 8388632
  6.8 1.2 %copy-done.3 = f32[64,4096]{1,0:T(8,128)S(1)} copy-done((f32[64,4096]{1,0:T(8,128)S(1)}, f32[64,4096]{1,0:T(8,128)}, u32[]{:S(2)}) %copy-start.3) | copy-done | bytes 1048600
  8.0 2.7 %project_low.1 = (f32[128,128]{1,0:T(8,128)S(1)}, f32[128,128]{1,0:T(8,128)S(1)}) custom-call(s32[1]{0:T(128)} %bitcast.core_ref, f32[64,4096]{1,0:T(8,128)S(1)} %copy-done.3, f32[4,128,4096]{2,1,0:T(8,128)S(1)} %copy-done.1, f32[4,128,4096]{2,1,0:T(8,128)S(1)} %copy-done), custom_call_target="tpu_custom_call" | custom-call | flops 800000000 | bytes 7340032 | tf_op jit(solution)/shard_map/project_low/pallas_call | solution.py:115
  10.7 1.5 %collective-permute-start = (f32[128,128]{1,0:T(8,128)S(1)}, f32[128,128]{1,0:T(8,128)S(1)}, u32[]{:S(2)}, u32[]{:S(2)}) collective-permute-start(f32[128,128]{1,0:T(8,128)S(1)} %get-tuple-element.20), channel_id=1, source_target_pairs={{0,1},{1,0},{2,3},{3,2},{4,5},{5,4},{6,7},{7,6},{8,9},{9,8},{10,11... | collective-permute-start | bytes 196616 | tf_op jit(solution)/shard_map/ppermute | solution.py:370
  12.2 0.9 %collective-permute-done = f32[128,128]{1,0:T(8,128)S(1)} collective-permute-done((f32[128,128]{1,0:T(8,128)S(1)}, f32[128,128]{1,0:T(8,128)S(1)}, u32[]{:S(2)}, u32[]{:S(2)}) %collective-permute-start) | collective-permute-done | bytes 65568 | tf_op jit(solution)/shard_map/ppermute | solution.py:370
  13.1 3.9 %collective-permute-start.3 = (f32[128,128]{1,0:T(8,128)S(1)}, f32[128,128]{1,0:T(8,128)S(1)}, u32[]{:S(2)}, u32[]{:S(2)}) collective-permute-start(f32[128,128]{1,0:T(8,128)S(1)} %add.33), channel_id=1, source_target_pairs={{0,6},{1,7},{2,4},{3,5},{4,2},{5,3},{6,0},{7,1},{8,14},{9,15},{10,... | collective-permute-start | bytes 196616 | tf_op jit(solution)/shard_map/ppermute | solution.py:370
  17.7 1.5 %collective-permute-done.3 = f32[128,128]{1,0:T(8,128)S(1)} collective-permute-done((f32[128,128]{1,0:T(8,128)S(1)}, f32[128,128]{1,0:T(8,128)S(1)}, u32[]{:S(2)}, u32[]{:S(2)}) %collective-permute-start.3) | collective-permute-done | bytes 65568 | tf_op jit(solution)/shard_map/ppermute | solution.py:370
  19.2 2.4 %collective-permute-done.2 = f32[128,128]{1,0:T(8,128)S(1)} collective-permute-done((f32[128,128]{1,0:T(8,128)S(1)}, f32[128,128]{1,0:T(8,128)S(1)}, u32[]{:S(2)}, u32[]{:S(2)}) %collective-permute-start.2) | collective-permute-done | bytes 65568 | tf_op jit(solution)/shard_map/ppermute | solution.py:370
  21.7 2.6 %collective-permute-start.6 = (f32[128,128]{1,0:T(8,128)S(1)}, f32[128,128]{1,0:T(8,128)S(1)}, u32[]{:S(2)}, u32[]{:S(2)}) collective-permute-start(f32[128,128]{1,0:T(8,128)S(1)} %add_add_fusion.2), channel_id=1, source_target_pairs={{0,24},{1,25},{2,26},{3,27},{4,28},{5,29},{6,30},{7,31},{8,16},{9,... | collective-permute-start | bytes 196616 | tf_op jit(solution)/shard_map/ppermute | solution.py:370
  25.1 1.0 %collective-permute-done.6 = f32[128,128]{1,0:T(8,128)S(1)} collective-permute-done((f32[128,128]{1,0:T(8,128)S(1)}, f32[128,128]{1,0:T(8,128)S(1)}, u32[]{:S(2)}, u32[]{:S(2)}) %collective-permute-start.6) | collective-permute-done | bytes 65568 | tf_op jit(solution)/shard_map/ppermute | solution.py:370
  26.1 2.9 %collective-permute-done.5 = f32[128,128]{1,0:T(8,128)S(1)} collective-permute-done((f32[128,128]{1,0:T(8,128)S(1)}, f32[128,128]{1,0:T(8,128)S(1)}, u32[]{:S(2)}, u32[]{:S(2)}) %collective-permute-start.5) | collective-permute-done | bytes 65568 | tf_op jit(solution)/shard_map/ppermute | solution.py:370
  29.0 3.5 %collective-permute-start.7 = (f32[4,128,128]{2,1,0:T(8,128)S(1)}, f32[4,128,128]{2,1,0:T(8,128)S(1)}, u32[]{:S(2)}, u32[]{:S(2)}) collective-permute-start(f32[4,128,128]{2,1,0:T(8,128)S(1)} %pad_maximum_fusion.mine_ref), channel_id=1, source_target_pairs={{0,1},{1,0},{2,3},{3,2},{4,5},{5,4},{6,7},{7,6},{8,9},{9,8},{10,11... | collective-permute-start | bytes 786440 | tf_op jit(solution)/shard_map/ppermute | solution.py:370
  32.5 3.4 %copy-done.2 = f32[4,128,4096]{2,1,0:T(8,128)S(1)} copy-done((f32[4,128,4096]{2,1,0:T(8,128)S(1)}, f32[4,128,4096]{2,1,0:T(8,128)}, u32[]{:S(2)}) %copy-start.2) | copy-done | bytes 8388632
  35.9 2.1 %copy-done.5 = f32[15,256,256]{2,1,0:T(8,128)S(1)} copy-done((f32[15,256,256]{2,1,0:T(8,128)S(1)}, f32[15,256,256]{2,1,0:T(8,128)}, u32[]{:S(2)}) %copy-start.5) | copy-done | bytes 3932184
  38.0 7.1 %grams_high.1 = (f32[64,256]{1,0:T(8,128)S(1)}, f32[256,256]{1,0:T(8,128)S(1)}, f32[128,128]{1,0:T(8,128)S(1)}, f32[256,256]{1,0:T(8,128)S(1)}, f32[256,256]{1,0...) custom-call(s32[7]{0:T(128)S(1)} %stack.66.place_ref, ...), custom_call_target="tpu_custom_call" | custom-call | flops 3000000000 | bytes 11534336 | tf_op jit(solution)/shard_map/grams_high/pallas_call | solution.py:207
  45.8 1.0 %collective-permute-start.8 = (f32[128,128]{1,0:T(8,128)S(1)}, f32[128,128]{1,0:T(8,128)S(1)}, u32[]{:S(2)}, u32[]{:S(2)}) collective-permute-start(f32[128,128]{1,0:T(8,128)S(1)} %get-tuple-element.28), channel_id=1, source_target_pairs={{0,1},{1,0},{2,3},{3,2},{4,5},{5,4},{6,7},{7,6},{8,9},{9,8},{10,11... | collective-permute-start | bytes 196616 | tf_op jit(solution)/shard_map/ppermute | solution.py:370
  47.7 1.1 %collective-permute-start.11 = (f32[128,128]{1,0:T(8,128)S(1)}, f32[128,128]{1,0:T(8,128)S(1)}, u32[]{:S(2)}, u32[]{:S(2)}) collective-permute-start(f32[128,128]{1,0:T(8,128)S(1)} %add.37), channel_id=1, source_target_pairs={{0,24},{1,7},{2,26},{3,5},{4,28},{5,3},{6,30},{7,1},{8,16},{9,15},... | collective-permute-start | bytes 196616 | tf_op jit(solution)/shard_map/ppermute | solution.py:370
  49.3 1.7 %collective-permute-start.9 = (f32[128,128]{1,0:T(8,128)S(1)}, f32[128,128]{1,0:T(8,128)S(1)}, u32[]{:S(2)}, u32[]{:S(2)}) collective-permute-start(f32[128,128]{1,0:T(8,128)S(1)} %add.37), channel_id=1, source_target_pairs={{0,8},{1,3},{2,10},{3,1},{4,12},{5,7},{6,14},{7,5},{8,0},{9,11},{1... | collective-permute-start | bytes 196616 | tf_op jit(solution)/shard_map/ppermute | solution.py:370
  51.0 1.1 %collective-permute-done.11 = f32[128,128]{1,0:T(8,128)S(1)} collective-permute-done((f32[128,128]{1,0:T(8,128)S(1)}, f32[128,128]{1,0:T(8,128)S(1)}, u32[]{:S(2)}, u32[]{:S(2)}) %collective-permute-start.11) | collective-permute-done | bytes 65568 | tf_op jit(solution)/shard_map/ppermute | solution.py:370
  52.1 1.3 %collective-permute-done.10 = f32[128,128]{1,0:T(8,128)S(1)} collective-permute-done((f32[128,128]{1,0:T(8,128)S(1)}, f32[128,128]{1,0:T(8,128)S(1)}, u32[]{:S(2)}, u32[]{:S(2)}) %collective-permute-start.10) | collective-permute-done | bytes 65568 | tf_op jit(solution)/shard_map/ppermute | solution.py:370
  53.4 1.2 %collective-permute-start.14 = (f32[128,128]{1,0:T(8,128)S(1)}, f32[128,128]{1,0:T(8,128)S(1)}, u32[]{:S(2)}, u32[]{:S(2)}) collective-permute-start(f32[128,128]{1,0:T(8,128)S(1)} %add_add_fusion.1), channel_id=1, source_target_pairs={{0,6},{1,25},{2,4},{3,27},{4,2},{5,29},{6,0},{7,31},{8,14},{9,17},... | collective-permute-start | bytes 196616 | tf_op jit(solution)/shard_map/ppermute | solution.py:370
  54.6 1.0 %collective-permute-start.13 = (f32[128,128]{1,0:T(8,128)S(1)}, f32[128,128]{1,0:T(8,128)S(1)}, u32[]{:S(2)}, u32[]{:S(2)}) collective-permute-start(f32[128,128]{1,0:T(8,128)S(1)} %add_add_fusion.1), channel_id=1, source_target_pairs={{0,4},{1,17},{2,6},{3,19},{4,0},{5,21},{6,2},{7,23},{8,12},{9,25},... | collective-permute-start | bytes 196616 | tf_op jit(solution)/shard_map/ppermute | solution.py:370
  55.6 1.1 %collective-permute-start.12 = (f32[128,128]{1,0:T(8,128)S(1)}, f32[128,128]{1,0:T(8,128)S(1)}, u32[]{:S(2)}, u32[]{:S(2)}) collective-permute-start(f32[128,128]{1,0:T(8,128)S(1)} %add_add_fusion.1), channel_id=1, source_target_pairs={{0,2},{1,9},{2,0},{3,11},{4,6},{5,13},{6,4},{7,15},{8,10},{9,1},{1... | collective-permute-start | bytes 196616 | tf_op jit(solution)/shard_map/ppermute | solution.py:370
  56.8 1.1 %collective-permute-done.14 = f32[128,128]{1,0:T(8,128)S(1)} collective-permute-done((f32[128,128]{1,0:T(8,128)S(1)}, f32[128,128]{1,0:T(8,128)S(1)}, u32[]{:S(2)}, u32[]{:S(2)}) %collective-permute-start.14) | collective-permute-done | bytes 65568 | tf_op jit(solution)/shard_map/ppermute | solution.py:370
  57.8 1.4 %collective-permute-done.13 = f32[128,128]{1,0:T(8,128)S(1)} collective-permute-done((f32[128,128]{1,0:T(8,128)S(1)}, f32[128,128]{1,0:T(8,128)S(1)}, u32[]{:S(2)}, u32[]{:S(2)}) %collective-permute-start.13) | collective-permute-done | bytes 65568 | tf_op jit(solution)/shard_map/ppermute | solution.py:370
  59.3 2.8 %collective-permute-start.17 = (f32[128,128]{1,0:T(8,128)S(1)}, f32[128,128]{1,0:T(8,128)S(1)}, u32[]{:S(2)}, u32[]{:S(2)}) collective-permute-start(f32[128,128]{1,0:T(8,128)S(1)} %add_add_fusion), channel_id=1, source_target_pairs={{0,96},{1,97},{2,98},{3,99},{4,100},{5,101},{6,102},{7,103},{8,104... | collective-permute-start | bytes 196616 | tf_op jit(solution)/shard_map/ppermute | solution.py:370
  62.7 1.2 %collective-permute-done.17 = f32[128,128]{1,0:T(8,128)S(1)} collective-permute-done((f32[128,128]{1,0:T(8,128)S(1)}, f32[128,128]{1,0:T(8,128)S(1)}, u32[]{:S(2)}, u32[]{:S(2)}) %collective-permute-start.17) | collective-permute-done | bytes 65568 | tf_op jit(solution)/shard_map/ppermute | solution.py:370
  64.0 2.7 %collective-permute-done.16 = f32[128,128]{1,0:T(8,128)S(1)} collective-permute-done((f32[128,128]{1,0:T(8,128)S(1)}, f32[128,128]{1,0:T(8,128)S(1)}, u32[]{:S(2)}, u32[]{:S(2)}) %collective-permute-start.16) | collective-permute-done | bytes 65568 | tf_op jit(solution)/shard_map/ppermute | solution.py:370
  66.7 4.9 %collective-permute-start.18 = (f32[4,128,128]{2,1,0:T(8,128)S(1)}, f32[4,128,128]{2,1,0:T(8,128)S(1)}, u32[]{:S(2)}, u32[]{:S(2)}) collective-permute-start(f32[4,128,128]{2,1,0:T(8,128)S(1)} %pad_maximum_fusion.1.mine_ref), channel_id=1, source_target_pairs={{0,1},{1,0},{2,3},{3,2},{4,5},{5,4},{6,7},{7,6},{8,9},{9,8},{10,11... | collective-permute-start | bytes 786440 | tf_op jit(solution)/shard_map/ppermute | solution.py:370
  71.6 1.8 %update_low.1.cur_ref = f32[64,4096]{1,0:T(8,128)S(1)} custom-call(f32[64,256]{1,0:T(8,128)S(1)} %get-tuple-element.32.t_ref, f32[64,4096]{1,0:T(8,128)S(1)} %copy-done.4, f32[4,128,4096]{2,1,0:T(8,128)S(1)} %bitcast.17), custom_call_target="tpu_custom_call" | custom-call | flops 402653184 | bytes 6291456 | tf_op jit(solution)/shard_map/update_low/pallas_call | solution.py:319
  73.5 3.0 %update_high.1 = f32[64,4096]{1,0:T(8,128)} custom-call(s32[1]{0:T(128)} %bitcast.core_ref, f32[4,128,128]{2,1,0:T(8,128)S(1)} %pad_maximum_fusion.1.mine_ref, f32[4,128,128]{2,1,0:T(8,128)S(1)} %collective-permute-done.18.other_ref, f32[256,256]{1,0:T(8,128)S(1)} %get-tuple-element.29.c1a_ref, f32[256,256]{1,0:T(8,128)S(1)} %get-tuple-element.30.c1b_ref, ...), custom_call_target="tpu_custom_call" | custom-call | flops 500000000 | bytes 7000000 | tf_op jit(solution)/shard_map/update_high/pallas_call | solution.py:356
  (36 shorter events, 4.5 us)
Async XLA Ops:
  0.0 3.4 %copy-start = (f32[4,128,4096]{2,1,0:T(8,128)S(1)}, f32[4,128,4096]{2,1,0:T(8,128)}, u32[]{:S(2)}) copy-start(f32[4,128,4096]{2,1,0:T(8,128)} %gen_ref.7) | copy-start | bytes 25165828
  3.4 3.4 %copy-start.1 = (f32[4,128,4096]{2,1,0:T(8,128)S(1)}, f32[4,128,4096]{2,1,0:T(8,128)}, u32[]{:S(2)}) copy-start(f32[4,128,4096]{2,1,0:T(8,128)} %basis_ref.3) | copy-start | bytes 25165828
  6.8 1.2 %copy-start.3 = (f32[64,4096]{1,0:T(8,128)S(1)}, f32[64,4096]{1,0:T(8,128)}, u32[]{:S(2)}) copy-start(f32[64,4096]{1,0:T(8,128)} %cur_ref.1) | copy-start | bytes 3145732
  8.0 24.5 %copy-start.4 = (f32[64,4096]{1,0:T(8,128)S(1)}, f32[64,4096]{1,0:T(8,128)}, u32[]{:S(2)}) copy-start(f32[64,4096]{1,0:T(8,128)} %cur_ref.1) | copy-start | bytes 3145732
  10.7 2.4 %collective-permute-start = (f32[128,128]{1,0:T(8,128)S(1)}, f32[128,128]{1,0:T(8,128)S(1)}, u32[]{:S(2)}, u32[]{:S(2)}) collective-permute-start(f32[128,128]{1,0:T(8,128)S(1)} %get-tuple-element.20), channel_id=1, source_target_pairs={{0,1},{1,0},{2,3},{3,2},{4,5},{5,4},{6,7},{7,6},{8,9},{9,8},{10,11... | collective-permute-start | bytes 196616 | tf_op jit(solution)/shard_map/ppermute | solution.py:370
  13.1 6.1 %collective-permute-start.3 = (f32[128,128]{1,0:T(8,128)S(1)}, f32[128,128]{1,0:T(8,128)S(1)}, u32[]{:S(2)}, u32[]{:S(2)}) collective-permute-start(f32[128,128]{1,0:T(8,128)S(1)} %add.33), channel_id=1, source_target_pairs={{0,6},{1,7},{2,4},{3,5},{4,2},{5,3},{6,0},{7,1},{8,14},{9,15},{10,... | collective-permute-start | bytes 196616 | tf_op jit(solution)/shard_map/ppermute | solution.py:370
  17.0 4.6 %collective-permute-start.2 = (f32[128,128]{1,0:T(8,128)S(1)}, f32[128,128]{1,0:T(8,128)S(1)}, u32[]{:S(2)}, u32[]{:S(2)}) collective-permute-start(f32[128,128]{1,0:T(8,128)S(1)} %add.33), channel_id=1, source_target_pairs={{0,4},{1,5},{2,6},{3,7},{4,0},{5,1},{6,2},{7,3},{8,12},{9,13},{10,... | collective-permute-start | bytes 196616 | tf_op jit(solution)/shard_map/ppermute | solution.py:370
  17.0 4.6 %collective-permute-start.1 = (f32[128,128]{1,0:T(8,128)S(1)}, f32[128,128]{1,0:T(8,128)S(1)}, u32[]{:S(2)}, u32[]{:S(2)}) collective-permute-start(f32[128,128]{1,0:T(8,128)S(1)} %add.33), channel_id=1, source_target_pairs={{0,2},{1,3},{2,0},{3,1},{4,6},{5,7},{6,4},{7,5},{8,10},{9,11},{10,... | collective-permute-start | bytes 196616 | tf_op jit(solution)/shard_map/ppermute | solution.py:370
  21.7 4.4 %collective-permute-start.6 = (f32[128,128]{1,0:T(8,128)S(1)}, f32[128,128]{1,0:T(8,128)S(1)}, u32[]{:S(2)}, u32[]{:S(2)}) collective-permute-start(f32[128,128]{1,0:T(8,128)S(1)} %add_add_fusion.2), channel_id=1, source_target_pairs={{0,24},{1,25},{2,26},{3,27},{4,28},{5,29},{6,30},{7,31},{8,16},{9,... | collective-permute-start | bytes 196616 | tf_op jit(solution)/shard_map/ppermute | solution.py:370
  24.2 4.7 %collective-permute-start.5 = (f32[128,128]{1,0:T(8,128)S(1)}, f32[128,128]{1,0:T(8,128)S(1)}, u32[]{:S(2)}, u32[]{:S(2)}) collective-permute-start(f32[128,128]{1,0:T(8,128)S(1)} %add_add_fusion.2), channel_id=1, source_target_pairs={{0,16},{1,17},{2,18},{3,19},{4,20},{5,21},{6,22},{7,23},{8,24},{9,... | collective-permute-start | bytes 196616 | tf_op jit(solution)/shard_map/ppermute | solution.py:370
  24.8 4.2 %collective-permute-start.4 = (f32[128,128]{1,0:T(8,128)S(1)}, f32[128,128]{1,0:T(8,128)S(1)}, u32[]{:S(2)}, u32[]{:S(2)}) collective-permute-start(f32[128,128]{1,0:T(8,128)S(1)} %add_add_fusion.2), channel_id=1, source_target_pairs={{0,8},{1,9},{2,10},{3,11},{4,12},{5,13},{6,14},{7,15},{8,0},{9,1},... | collective-permute-start | bytes 196616 | tf_op jit(solution)/shard_map/ppermute | solution.py:370
  29.0 42.7 %slice-start = ((s8[8388608]{0:T(1024)(128)(4,1)}), s8[4194304]{0:T(1024)(128)(4,1)S(1)}, s32[]{:S(2)}) async-start(s8[8388608]{0:T(1024)(128)(4,1)} %bitcast.16), calls=%async_computation | async-start | bytes 8388608
  29.0 42.6 %slice-start.1 = ((s8[8388608]{0:T(1024)(128)(4,1)}), s8[4194304]{0:T(1024)(128)(4,1)S(1)}, s32[]{:S(2)}) async-start(s8[8388608]{0:T(1024)(128)(4,1)} %bitcast.16), calls=%async_computation.1 | async-start | bytes 8388608
  29.0 16.1 %collective-permute-start.7 = (f32[4,128,128]{2,1,0:T(8,128)S(1)}, f32[4,128,128]{2,1,0:T(8,128)S(1)}, u32[]{:S(2)}, u32[]{:S(2)}) collective-permute-start(f32[4,128,128]{2,1,0:T(8,128)S(1)} %pad_maximum_fusion.mine_ref), channel_id=1, source_target_pairs={{0,1},{1,0},{2,3},{3,2},{4,5},{5,4},{6,7},{7,6},{8,9},{9,8},{10,11... | collective-permute-start | bytes 786440 | tf_op jit(solution)/shard_map/ppermute | solution.py:370
  32.5 3.4 %copy-start.2 = (f32[4,128,4096]{2,1,0:T(8,128)S(1)}, f32[4,128,4096]{2,1,0:T(8,128)}, u32[]{:S(2)}) copy-start(f32[4,128,4096]{2,1,0:T(8,128)} %basis_ref.3) | copy-start | bytes 25165828
  35.9 2.1 %copy-start.5 = (f32[15,256,256]{2,1,0:T(8,128)S(1)}, f32[15,256,256]{2,1,0:T(8,128)}, u32[]{:S(2)}) copy-start(f32[15,256,256]{2,1,0:T(8,128)} %cap_ref.1) | copy-start | bytes 11796484
  45.8 1.9 %collective-permute-start.8 = (f32[128,128]{1,0:T(8,128)S(1)}, f32[128,128]{1,0:T(8,128)S(1)}, u32[]{:S(2)}, u32[]{:S(2)}) collective-permute-start(f32[128,128]{1,0:T(8,128)S(1)} %get-tuple-element.28), channel_id=1, source_target_pairs={{0,1},{1,0},{2,3},{3,2},{4,5},{5,4},{6,7},{7,6},{8,9},{9,8},{10,11... | collective-permute-start | bytes 196616 | tf_op jit(solution)/shard_map/ppermute | solution.py:370
  47.7 4.4 %collective-permute-start.11 = (f32[128,128]{1,0:T(8,128)S(1)}, f32[128,128]{1,0:T(8,128)S(1)}, u32[]{:S(2)}, u32[]{:S(2)}) collective-permute-start(f32[128,128]{1,0:T(8,128)S(1)} %add.37), channel_id=1, source_target_pairs={{0,24},{1,7},{2,26},{3,5},{4,28},{5,3},{6,30},{7,1},{8,16},{9,15},... | collective-permute-start | bytes 196616 | tf_op jit(solution)/shard_map/ppermute | solution.py:370
  48.8 4.6 %collective-permute-start.10 = (f32[128,128]{1,0:T(8,128)S(1)}, f32[128,128]{1,0:T(8,128)S(1)}, u32[]{:S(2)}, u32[]{:S(2)}) collective-permute-start(f32[128,128]{1,0:T(8,128)S(1)} %add.37), channel_id=1, source_target_pairs={{0,16},{1,5},{2,18},{3,7},{4,20},{5,1},{6,22},{7,3},{8,24},{9,13},... | collective-permute-start | bytes 196616 | tf_op jit(solution)/shard_map/ppermute | solution.py:370
  49.3 4.1 %collective-permute-start.9 = (f32[128,128]{1,0:T(8,128)S(1)}, f32[128,128]{1,0:T(8,128)S(1)}, u32[]{:S(2)}, u32[]{:S(2)}) collective-permute-start(f32[128,128]{1,0:T(8,128)S(1)} %add.37), channel_id=1, source_target_pairs={{0,8},{1,3},{2,10},{3,1},{4,12},{5,7},{6,14},{7,5},{8,0},{9,11},{1... | collective-permute-start | bytes 196616 | tf_op jit(solution)/shard_map/ppermute | solution.py:370
  53.4 4.4 %collective-permute-start.14 = (f32[128,128]{1,0:T(8,128)S(1)}, f32[128,128]{1,0:T(8,128)S(1)}, u32[]{:S(2)}, u32[]{:S(2)}) collective-permute-start(f32[128,128]{1,0:T(8,128)S(1)} %add_add_fusion.1), channel_id=1, source_target_pairs={{0,6},{1,25},{2,4},{3,27},{4,2},{5,29},{6,0},{7,31},{8,14},{9,17},... | collective-permute-start | bytes 196616 | tf_op jit(solution)/shard_map/ppermute | solution.py:370
  54.6 4.6 %collective-permute-start.13 = (f32[128,128]{1,0:T(8,128)S(1)}, f32[128,128]{1,0:T(8,128)S(1)}, u32[]{:S(2)}, u32[]{:S(2)}) collective-permute-start(f32[128,128]{1,0:T(8,128)S(1)} %add_add_fusion.1), channel_id=1, source_target_pairs={{0,4},{1,17},{2,6},{3,19},{4,0},{5,21},{6,2},{7,23},{8,12},{9,25},... | collective-permute-start | bytes 196616 | tf_op jit(solution)/shard_map/ppermute | solution.py:370
  55.6 3.6 %collective-permute-start.12 = (f32[128,128]{1,0:T(8,128)S(1)}, f32[128,128]{1,0:T(8,128)S(1)}, u32[]{:S(2)}, u32[]{:S(2)}) collective-permute-start(f32[128,128]{1,0:T(8,128)S(1)} %add_add_fusion.1), channel_id=1, source_target_pairs={{0,2},{1,9},{2,0},{3,11},{4,6},{5,13},{6,4},{7,15},{8,10},{9,1},{1... | collective-permute-start | bytes 196616 | tf_op jit(solution)/shard_map/ppermute | solution.py:370
  59.3 4.7 %collective-permute-start.17 = (f32[128,128]{1,0:T(8,128)S(1)}, f32[128,128]{1,0:T(8,128)S(1)}, u32[]{:S(2)}, u32[]{:S(2)}) collective-permute-start(f32[128,128]{1,0:T(8,128)S(1)} %add_add_fusion), channel_id=1, source_target_pairs={{0,96},{1,97},{2,98},{3,99},{4,100},{5,101},{6,102},{7,103},{8,104... | collective-permute-start | bytes 196616 | tf_op jit(solution)/shard_map/ppermute | solution.py:370
  62.1 4.6 %collective-permute-start.16 = (f32[128,128]{1,0:T(8,128)S(1)}, f32[128,128]{1,0:T(8,128)S(1)}, u32[]{:S(2)}, u32[]{:S(2)}) collective-permute-start(f32[128,128]{1,0:T(8,128)S(1)} %add_add_fusion), channel_id=1, source_target_pairs={{0,64},{1,65},{2,66},{3,67},{4,68},{5,69},{6,70},{7,71},{8,72},{9,... | collective-permute-start | bytes 196616 | tf_op jit(solution)/shard_map/ppermute | solution.py:370
  62.4 4.3 %collective-permute-start.15 = (f32[128,128]{1,0:T(8,128)S(1)}, f32[128,128]{1,0:T(8,128)S(1)}, u32[]{:S(2)}, u32[]{:S(2)}) collective-permute-start(f32[128,128]{1,0:T(8,128)S(1)} %add_add_fusion), channel_id=1, source_target_pairs={{0,32},{1,33},{2,34},{3,35},{4,36},{5,37},{6,38},{7,39},{8,40},{9,... | collective-permute-start | bytes 196616 | tf_op jit(solution)/shard_map/ppermute | solution.py:370
  66.7 6.7 %collective-permute-start.18 = (f32[4,128,128]{2,1,0:T(8,128)S(1)}, f32[4,128,128]{2,1,0:T(8,128)S(1)}, u32[]{:S(2)}, u32[]{:S(2)}) collective-permute-start(f32[4,128,128]{2,1,0:T(8,128)S(1)} %pad_maximum_fusion.1.mine_ref), channel_id=1, source_target_pairs={{0,1},{1,0},{2,3},{3,2},{4,5},{5,4},{6,7},{7,6},{8,9},{9,8},{10,11... | collective-permute-start | bytes 786440 | tf_op jit(solution)/shard_map/ppermute | solution.py:370

commit v2 on v1

--- a/solution.py
+++ b/solution.py
@@ -13,7 +13,11 @@
 RHS = 64
 DEVICES = 128
 CHUNK = 1024
+FULL = 53 << 20
+BIG = 51 << 20
+SMALL = 16 << 20
 ANY = pl.BlockSpec(memory_space=pl.ANY)
+HBM = pl.BlockSpec(memory_space=pltpu.HBM)
 VMEM = pl.BlockSpec(memory_space=pltpu.VMEM)
 SMEM = pl.BlockSpec(memory_space=pltpu.SMEM)
 
@@ -115,7 +119,7 @@
     return pl.pallas_call(
         functools.partial(first_kernel, points),
         out_shape=(half, half),
-        in_specs=[SMEM, ANY, ANY, ANY],
+        in_specs=[SMEM, HBM, HBM, HBM],
         out_specs=(VMEM, VMEM),
         scratch_shapes=[
             pltpu.VMEM((RHS, points), F32),
@@ -126,7 +130,7 @@
             pltpu.VMEM((2 * RHS, 2 * RANK), F32),
             pltpu.SemaphoreType.DMA((points // CHUNK, 4)),
         ],
-        compiler_params=params(24 << 20),
+        compiler_params=params(FULL),
         cost_estimate=pl.CostEstimate(flops=800_000_000, bytes_accessed=7_340_032, transcendentals=0),
         name="project_low",
     )(core, rhs, basis, gen)
@@ -148,15 +152,66 @@
     return copies
 
 
-def grams_kernel(points, place_ref, rhs_ref, basis_ref, gen_ref, cap_ref,
-                 p_ref, g_ref, g10_ref, c3a_ref, c3b_ref, c2_ref, c1a_ref, c1b_ref, c0_ref,
-                 rhs_buf, v1_buf, v0_buf, u3_buf, u2_buf, u1_buf, acc1, acc0, sems, cap_sems):
-    buffers = (rhs_buf, v1_buf, v0_buf, u3_buf, u2_buf, u1_buf)
-    sources = ((rhs_ref, None), (basis_ref, 1), (basis_ref, 0), (gen_ref, 3), (gen_ref, 2), (gen_ref, 1))
+def grams_kernel(points, rhs_ref, basis_ref, gen_ref, sent_ref, sent_out, p_ref, g_ref,
+                 rhs_buf, v1_buf, v0_buf, u3_buf, acc1, acc0, sems):
+    buffers = (rhs_buf, v1_buf, v0_buf, u3_buf)
+    sources = ((rhs_ref, None), (basis_ref, 1), (basis_ref, 0), (gen_ref, 3))
     copies = chunk_copies(sources, buffers, sems, points)
     for row in copies:
         for copy in row:
             copy.start()
+    sent_out[...] = sent_ref[...]
+    for i, row in enumerate(copies):
+        for copy in row:
+            copy.wait()
+        cols = pl.ds(i * CHUNK, CHUNK)
+        left = stacked([rhs_buf[:, cols], u3_buf[:, cols]])
+        one, zero = contract(left, stacked([v1_buf[:, cols]])), contract(left, stacked([v0_buf[:, cols]]))
+        if i == 0:
+            acc1[...] = one
+            acc0[...] = zero
+        else:
+            acc1[...] += one
+            acc0[...] += zero
+    for k, acc in enumerate((acc1, acc0)):
+        both = fold(acc[...], RHS + RANK)
+        p_ref[:, k * RANK : (k + 1) * RANK] = both[:RHS]
+        g_ref[:, k * RANK : (k + 1) * RANK] = both[RHS:]
+
+
+def grams_step(rhs, basis, gen, sent):
+    points = rhs.shape[1]
+    wide = pltpu.VMEM((RANK, points), F32)
+    total = pltpu.VMEM((2 * (RHS + RANK), 2 * RANK), F32)
+    return pl.pallas_call(
+        functools.partial(grams_kernel, points),
+        out_shape=(
+            jax.ShapeDtypeStruct(sent.shape, F32),
+            jax.ShapeDtypeStruct((RHS, 2 * RANK), F32),
+            jax.ShapeDtypeStruct((RANK, 2 * RANK), F32),
+        ),
+        in_specs=[HBM, HBM, HBM, VMEM],
+        out_specs=(VMEM,) * 3,
+        scratch_shapes=[
+            pltpu.VMEM((RHS, points), F32), wide, wide, wide, total, total,
+            pltpu.SemaphoreType.DMA((points // CHUNK, 4)),
+        ],
+        compiler_params=params(FULL),
+        cost_estimate=pl.CostEstimate(flops=1_500_000_000, bytes_accessed=7_340_032, transcendentals=0),
+        name="grams_three",
+    )(rhs, basis, gen, sent)
+
+
+def rest_kernel(points, place_ref, basis_ref, gen_ref, cap_ref, sent_ref, sent_out,
+                g_ref, g10_ref, c3a_ref, c3b_ref, c2_ref, c1a_ref, c1b_ref, c0_ref,
+                v1_buf, v0_buf, u2_buf, u1_buf, acc1, acc0, sems, cap_sems):
+    buffers = (v1_buf, v0_buf, u2_buf, u1_buf)
+    sources = ((basis_ref, 1), (basis_ref, 0), (gen_ref, 2), (gen_ref, 1))
+    copies = chunk_copies(sources, buffers, sems, points)
+    for row in copies:
+        for copy in row:
+            copy.start()
+    sent_out[...] = sent_ref[...]
     s3, s2, s1, s0 = place_ref[0], place_ref[1], place_ref[2], place_ref[3]
     n3, n2, n1 = place_ref[4], place_ref[5], place_ref[6]
     caps = related(cap_ref, c3a_ref, cap_sems, 7 + n3, s3, 0, 2)
@@ -169,64 +224,52 @@
         for copy in row:
             copy.wait()
         cols = pl.ds(i * CHUNK, CHUNK)
-        rhs = stacked([rhs_buf[:, cols]])
-        u3 = stacked([u3_buf[:, cols]])
         u2 = stacked([u2_buf[:, cols]])
-        u1 = stacked([u1_buf[:, cols]])
-        v1 = stacked([v1_buf[:, cols]])
-        v0 = stacked([v0_buf[:, cols]])
-        left1 = jnp.concatenate([rhs, u3, u2], axis=0)
-        left0 = jnp.concatenate([rhs, u3, u2, u1], axis=0)
-        one, zero = contract(left1, v1), contract(left0, v0)
+        left = jnp.concatenate([u2, stacked([u1_buf[:, cols]])], axis=0)
+        one, zero = contract(u2, stacked([v1_buf[:, cols]])), contract(left, stacked([v0_buf[:, cols]]))
         if i == 0:
             acc1[...] = one
             acc0[...] = zero
         else:
             acc1[...] += one
             acc0[...] += zero
-    at3, at2, at1 = 2 * RHS, 2 * RHS + 2 * RANK, 2 * RHS + 4 * RANK
-    p_ref[:, :RANK] = fold(acc1[:at3], RHS)
-    p_ref[:, RANK:] = fold(acc0[:at3], RHS)
-    g_ref[:RANK, :RANK] = fold(acc1[at3:at2], RANK)
-    g_ref[:RANK, RANK:] = fold(acc0[at3:at2], RANK)
-    g_ref[RANK:, :RANK] = fold(acc1[at2:at1], RANK)
-    g_ref[RANK:, RANK:] = fold(acc0[at2:at1], RANK)
-    g10_ref[...] = fold(acc0[at1:], RANK)
+    g_ref[:, :RANK] = fold(acc1[...], RANK)
+    g_ref[:, RANK:] = fold(acc0[: 2 * RANK], RANK)
+    g10_ref[...] = fold(acc0[2 * RANK :], RANK)
     for copy in caps:
         copy.wait()
 
 
-def grams_step(place, rhs, basis, gen, cap):
-    points = rhs.shape[1]
+def rest_step(place, basis, gen, cap, sent):
+    points = basis.shape[2]
 
     def out(rows, cols):
         return jax.ShapeDtypeStruct((rows, cols), F32)
 
     wide = pltpu.VMEM((RANK, points), F32)
-    rows1 = 2 * RHS + 4 * RANK
-    return pl.pallas_call(
-        functools.partial(grams_kernel, points),
+    return pl.pallas_call(
+        functools.partial(rest_kernel, points),
         out_shape=(
-            out(RHS, 2 * RANK), out(2 * RANK, 2 * RANK), out(RANK, RANK),
+            out(*sent.shape), out(RANK, 2 * RANK), out(RANK, RANK),
             out(2 * RANK, 2 * RANK), out(2 * RANK, 2 * RANK), out(2 * RANK, RANK),
             out(2 * RANK, 2 * RANK), out(2 * RANK, 2 * RANK), out(2 * RANK, RANK),
         ),
-        in_specs=[SMEM, ANY, ANY, ANY, ANY],
+        in_specs=[SMEM, HBM, HBM, HBM, VMEM],
         out_specs=(VMEM,) * 9,
         scratch_shapes=[
-            pltpu.VMEM((RHS, points), F32), wide, wide, wide, wide, wide,
-            pltpu.VMEM((rows1, 2 * RANK), F32),
-            pltpu.VMEM((rows1 + 2 * RANK, 2 * RANK), F32),
-            pltpu.SemaphoreType.DMA((points // CHUNK, 6)),
+            wide, wide, wide, wide,
+            pltpu.VMEM((2 * RANK, 2 * RANK), F32),
+            pltpu.VMEM((4 * RANK, 2 * RANK), F32),
+            pltpu.SemaphoreType.DMA((points // CHUNK, 4)),
             pltpu.SemaphoreType.DMA((24,)),
         ],
-        compiler_params=params(32 << 20),
-        cost_estimate=pl.CostEstimate(flops=3_000_000_000, bytes_accessed=11_534_336, transcendentals=0),
-        name="grams_high",
-    )(place, rhs, basis, gen, cap)
-
-
-def middle_kernel(core_ref, mine_ref, other_ref, c3a_ref, c3b_ref, c2_ref, p_ref, g_ref, g10_ref,
+        compiler_params=params(BIG),
+        cost_estimate=pl.CostEstimate(flops=1_500_000_000, bytes_accessed=9_437_184, transcendentals=0),
+        name="grams_rest",
+    )(place, basis, gen, cap, sent)
+
+
+def middle_kernel(core_ref, mine_ref, other_ref, c3a_ref, c3b_ref, c2_ref, p_ref, g3_ref, g2_ref, g10_ref,
                   t_ref, keep_ref, send_ref):
     first = core_ref[0] == 0
     p, g = [], []
@@ -243,7 +286,7 @@
     joined = jnp.concatenate([q2[0] + q2[1], q2[2] + q2[3]], axis=1)
     coeff = jnp.concatenate([t[0], product(joined, c2_ref[...])], axis=1)
     t_ref[...] = coeff
-    q = p_ref[...] - product(coeff, g_ref[...])
+    q = p_ref[...] - product(coeff, jnp.concatenate([g3_ref[...], g2_ref[...]], axis=0))
     half = RHS // 2
 
     def put(ref, c):
@@ -263,17 +306,17 @@
         put(send_ref, 0)
 
 
-def middle_step(core, mine, other, c3a, c3b, c2, p, g, g10):
+def middle_step(core, mine, other, c3a, c3b, c2, p, g3, g2, g10):
     half = jax.ShapeDtypeStruct((RANK, RANK), F32)
     return pl.pallas_call(
         middle_kernel,
         out_shape=(jax.ShapeDtypeStruct((RHS, 2 * RANK), F32), half, half),
-        in_specs=[SMEM] + [VMEM] * 8,
+        in_specs=[SMEM] + [VMEM] * 9,
         out_specs=(VMEM,) * 3,
-        compiler_params=params(16 << 20),
+        compiler_params=params(SMALL),
         cost_estimate=pl.CostEstimate(flops=120_000_000, bytes_accessed=1_500_000, transcendentals=0),
         name="coefficients_low",
-    )(core, mine, other, c3a, c3b, c2, p, g, g10)
+    )(core, mine, other, c3a, c3b, c2, p, g3, g2, g10)
 
 
 def apply_chunks(points, levels, coeff, cur_ref, gen_ref, out_ref, cur_buf, hi_buf, lo_buf, sems, out_sems, compute):
@@ -310,22 +353,23 @@
     ]
 
 
-def low_update_kernel(points, t_ref, cur_ref, gen_ref, out_ref, *scratch):
+def low_update_kernel(points, t_ref, cur_ref, gen_ref, sent_ref, out_ref, sent_out, *scratch):
+    sent_out[...] = sent_ref[...]
     apply_chunks(points, (3, 2), t_ref[...], cur_ref, gen_ref, out_ref, *scratch, None)
 
 
-def low_update(t, rhs, gen):
+def low_update(t, rhs, gen, sent):
     points = rhs.shape[1]
     return pl.pallas_call(
         functools.partial(low_update_kernel, points),
-        out_shape=jax.ShapeDtypeStruct(rhs.shape, F32),
-        in_specs=[VMEM, ANY, ANY],
-        out_specs=ANY,
+        out_shape=(jax.ShapeDtypeStruct(rhs.shape, F32), jax.ShapeDtypeStruct(sent.shape, F32)),
+        in_specs=[VMEM, HBM, HBM, VMEM],
+        out_specs=(HBM, VMEM),
         scratch_shapes=apply_scratch(points),
-        compiler_params=params(16 << 20),
+        compiler_params=params(BIG),
         cost_estimate=pl.CostEstimate(flops=402_653_184, bytes_accessed=6_291_456, transcendentals=0),
         name="update_low",
-    )(t, rhs, gen)
+    )(t, rhs, gen, sent)
 
 
 def last_kernel(points, core_ref, mine_ref, other_ref, c1a_ref, c1b_ref, c0_ref, cur_ref, gen_ref, out_ref, *scratch):
@@ -356,10 +400,10 @@
     return pl.pallas_call(
         functools.partial(last_kernel, points),
         out_shape=jax.ShapeDtypeStruct(cur.shape, F32),
-        in_specs=[SMEM] + [VMEM] * 5 + [ANY, ANY],
-        out_specs=ANY,
+        in_specs=[SMEM] + [VMEM] * 5 + [HBM, HBM],
+        out_specs=HBM,
         scratch_shapes=apply_scratch(points),
-        compiler_params=params(16 << 20),
+        compiler_params=params(BIG),
         cost_estimate=pl.CostEstimate(flops=500_000_000, bytes_accessed=7_000_000, transcendentals=0),
         name="update_high",
     )(core, mine, other, c1a, c1b, c0, cur, gen)
@@ -383,17 +427,19 @@
         device >> 4, device >> 5, device >> 6,
     ])
     keep, send = first_step(core, rhs, basis, gen)
-    p, g, g10, c3a, c3b, c2, c1a, c1b, c0 = grams_step(place, rhs, basis, gen, cap)
     chip = keep + swap(send, CORE, CORE)
-    a, b, c, d = gathered(chip, Z_MASKS, Z_MASKS)
-    line = a + b + c + d
-    lines = jnp.stack(gathered(line, X_MASKS, X_MASKS))
+    _, b, c, d = gathered(chip, Z_MASKS, Z_MASKS)
+    chip, p, g3 = grams_step(rhs, basis, gen, chip)
+    line = chip + b + c + d
+    _, b, c, d = gathered(line, X_MASKS, X_MASKS)
+    line, g2, g10, c3a, c3b, c2, c1a, c1b, c0 = rest_step(place, basis, gen, cap, line)
+    lines = jnp.stack([line, b, c, d])
     other = swap(lines, CORE, CORE)
-    t, keep, send = middle_step(core, lines, other, c3a, c3b, c2, p, g, g10)
-    current = low_update(t, rhs, gen)
+    t, keep, send = middle_step(core, lines, other, c3a, c3b, c2, p, g3, g2, g10)
     chip = keep + swap(send, CORE, CORE)
-    a, b, c, d = gathered(chip, X_MASKS, Z_MASKS)
-    part = a + b + c + d
+    _, b, c, d = gathered(chip, X_MASKS, Z_MASKS)
+    current, chip = low_update(t, rhs, gen, chip)
+    part = chip + b + c + d
     a, b, c, d = gathered(part, Z_MASKS, X_MASKS)
     plane = a + b + c + d
     planes = jnp.stack(gathered(plane, Y_MASKS, Y_MASKS))

time: 76.9 us -> 60.5 us (0.79)
  local copies, waits for them, and re-layouts: 13.6 us -> 0.09 us
  waiting for transfers between devices: 18.4 us -> 12.2 us
  Pallas kernels: 15.3 us -> 20 us
  starting transfers between devices: 29 us -> 27.7 us
    unnamed x16 -> x2, local copies, waits for them, and re-layouts: 13.5 us -> 0.01 us
    ppermute x19, waiting for transfers between devices: 18.4 us -> 12.2 us  [swap(): return lax.ppermute(value, 'leaf', pairs)]
    pallas_call x2 -> x3, Pallas kernels: 8.87 us -> 12.1 us  [the longest x1 5.63 us: rest_step(): pl.pallas_call(functools.partial(rest_kernel, points), out_shape=(out(*se...]
    ppermute x19, starting transfers between devices: 29 us -> 27.7 us  [swap(): return lax.ppermute(value, 'leaf', pairs)]
    pallas_call x1, Pallas kernels: 2.7 us -> 3.78 us  [first_step(): pl.pallas_call(functools.partial(first_kernel, points), out_shape=(half,...]
  transfers between devices with their start and end apart: 19 -> 19, of which waited for: 12 -> 10; matrix products, arithmetic and copies ran while one was open for 0% -> 0% of each run, Pallas kernels for 12% -> 20%
where the time goes in v2:
time: 60.5 us; the launch traced here: 60.4 us
  starting transfers between devices  27.7 us (46%)
  Pallas kernels  20 us (33%)
  waiting for transfers between devices  12.2 us (20%)
    ppermute x19, starting transfers between devices, swap(): return lax.ppermute(value, 'leaf', pairs)  27.7 us
    ppermute x19, waiting for transfers between devices, swap(): return lax.ppermute(value, 'leaf', pairs)  12.2 us
    pallas_call x1, Pallas kernels, rest_step(): pl.pallas_call(functools.partial(rest_kernel, points), out_shape=(out(*se...  5.63 us
    pallas_call x1, Pallas kernels, grams_step(): pl.pallas_call(functools.partial(grams_kernel, points), out_shape=(jax.Sh...  3.84 us
    pallas_call x1, Pallas kernels, first_step(): pl.pallas_call(functools.partial(first_kernel, points), out_shape=(half,...  3.78 us
    pallas_call x1, Pallas kernels, last_step(): pl.pallas_call(functools.partial(last_kernel, points), out_shape=jax.Shap...  3.42 us
    pallas_call x1, Pallas kernels, low_update(): pl.pallas_call(functools.partial(low_update_kernel, points), out_shape=(j...  2.66 us
  transfers between devices with their start and end apart: 19, of which 10 were waited for; matrix products, arithmetic and copies ran while one was open for 0% of the time, Pallas kernels for 20%

profile of v2, /device:TPU:1, one launch (start us, length us, event | category | flops | bytes accessed | tf_op | source)
XLA Modules:
  0.0 60.4 jit_solution(13052034487613653346)
XLA Ops:
  0.0 3.8 %project_low.1 = (f32[128,128]{1,0:T(8,128)S(1)}, f32[128,128]{1,0:T(8,128)S(1)}) custom-call(s32[1]{0:T(128)} %bitcast.core_ref, f32[64,4096]{1,0:T(8,128)} %cur_ref.1, f32[4,128,4096]{2,1,0:T(8,128)} %basis_ref.5, f32[4,128,4096]{2,1,0:T(8,128)} %gen_ref.9), custom_call_target="tpu_custom_call" | custom-call | flops 800000000 | bytes 7340032 | tf_op jit(solution)/shard_map/project_low/pallas_call | solution.py:119
  3.8 1.5 %collective-permute-start = (f32[128,128]{1,0:T(8,128)S(1)}, f32[128,128]{1,0:T(8,128)S(1)}, u32[]{:S(2)}, u32[]{:S(2)}) collective-permute-start(f32[128,128]{1,0:T(8,128)S(1)} %get-tuple-element.25), channel_id=1, source_target_pairs={{0,1},{1,0},{2,3},{3,2},{4,5},{5,4},{6,7},{7,6},{8,9},{9,8},{10,11... | collective-permute-start | bytes 196616 | tf_op jit(solution)/shard_map/ppermute | solution.py:414
  5.4 0.8 %collective-permute-done = f32[128,128]{1,0:T(8,128)S(1)} collective-permute-done((f32[128,128]{1,0:T(8,128)S(1)}, f32[128,128]{1,0:T(8,128)S(1)}, u32[]{:S(2)}, u32[]{:S(2)}) %collective-permute-start) | collective-permute-done | bytes 65568 | tf_op jit(solution)/shard_map/ppermute | solution.py:414
  6.2 3.9 %collective-permute-start.3 = (f32[128,128]{1,0:T(8,128)S(1)}, f32[128,128]{1,0:T(8,128)S(1)}, u32[]{:S(2)}, u32[]{:S(2)}) collective-permute-start(f32[128,128]{1,0:T(8,128)S(1)} %add.33.sent_ref), channel_id=1, source_target_pairs={{0,6},{1,7},{2,4},{3,5},{4,2},{5,3},{6,0},{7,1},{8,14},{9,15},{10,... | collective-permute-start | bytes 196616 | tf_op jit(solution)/shard_map/ppermute | solution.py:414
  10.1 0.7 %collective-permute-start.1 = (f32[128,128]{1,0:T(8,128)S(1)}, f32[128,128]{1,0:T(8,128)S(1)}, u32[]{:S(2)}, u32[]{:S(2)}) collective-permute-start(f32[128,128]{1,0:T(8,128)S(1)} %add.33.sent_ref), channel_id=1, source_target_pairs={{0,2},{1,3},{2,0},{3,1},{4,6},{5,7},{6,4},{7,5},{8,10},{9,11},{10,... | collective-permute-start | bytes 196616 | tf_op jit(solution)/shard_map/ppermute | solution.py:414
  10.8 3.8 %grams_three.1 = (f32[128,128]{1,0:T(8,128)S(1)}, f32[64,256]{1,0:T(8,128)S(1)}, f32[128,256]{1,0:T(8,128)S(1)}) custom-call(f32[64,4096]{1,0:T(8,128)} %cur_ref.1, f32[4,128,4096]{2,1,0:T(8,128)} %basis_ref.5, f32[4,128,4096]{2,1,0:T(8,128)} %gen_ref.9, f32[128,128]{1,0:T(8,128)S(1)} %add.33.sent_ref), custom_call_target="tpu_custom_call" | custom-call | flops 1500000000 | bytes 7340032 | tf_op jit(solution)/shard_map/grams_three/pallas_call | solution.py:186
  14.8 2.6 %collective-permute-start.6 = (f32[128,128]{1,0:T(8,128)S(1)}, f32[128,128]{1,0:T(8,128)S(1)}, u32[]{:S(2)}, u32[]{:S(2)}) collective-permute-start(f32[128,128]{1,0:T(8,128)S(1)} %add_add_fusion.2.sent_ref), channel_id=1, source_target_pairs={{0,24},{1,25},{2,26},{3,27},{4,28},{5,29},{6,30},{7,31},{8,16},{9,... | collective-permute-start | bytes 196616 | tf_op jit(solution)/shard_map/ppermute | solution.py:414
  17.3 0.5 collective-permute-start.5
  17.8 0.3 collective-permute-start.4
  18.1 5.6 %grams_rest.1 = (f32[128,128]{1,0:T(8,128)S(1)}, f32[128,256]{1,0:T(8,128)S(1)}, f32[128,128]{1,0:T(8,128)S(1)}, f32[256,256]{1,0:T(8,128)S(1)}, f32[256,256]{1,...) custom-call(s32[7]{0:T(128)S(1)} %stack.61.place_ref, ...), custom_call_target="tpu_custom_call" | custom-call | flops 1500000000 | bytes 9437184 | tf_op jit(solution)/shard_map/grams_rest/pallas_call | solution.py:250
  23.8 3.0 %collective-permute-start.7 = (f32[4,128,128]{2,1,0:T(8,128)S(1)}, f32[4,128,128]{2,1,0:T(8,128)S(1)}, u32[]{:S(2)}, u32[]{:S(2)}) collective-permute-start(f32[4,128,128]{2,1,0:T(8,128)S(1)} %pad_maximum_fusion.mine_ref), channel_id=1, source_target_pairs={{0,1},{1,0},{2,3},{3,2},{4,5},{5,4},{6,7},{7,6},{8,9},{9,8},{10,11... | collective-permute-start | bytes 786440 | tf_op jit(solution)/shard_map/ppermute | solution.py:414
  26.8 1.2 %collective-permute-done.7.other_ref = f32[4,128,128]{2,1,0:T(8,128)S(1)} collective-permute-done((f32[4,128,128]{2,1,0:T(8,128)S(1)}, f32[4,128,128]{2,1,0:T(8,128)S(1)}, u32[]{:S(2)}, u32[]{:S(2)}) %collective-permute-start.7) | collective-permute-done | bytes 262176 | tf_op jit(solution)/shard_map/ppermute | solution.py:414
  28.0 0.7 %coefficients_low.1 = (f32[64,256]{1,0:T(8,128)S(1)}, f32[128,128]{1,0:T(8,128)S(1)}, f32[128,128]{1,0:T(8,128)S(1)}) custom-call(s32[1]{0:T(128)} %bitcast.core_ref, f32[4,128,128]{2,1,0:T(8,128)S(1)} %pad_maximum_fusion.mine_ref, f32[4,128,128]{2,1,0:T(8,128)S(1)} %collective-permute-done.7.other_ref, f32[256,256]{1,0:T(8,128)S(1)} %get-tuple-element.28.c3a_ref, ...), custom_call_target="tpu_custom_call" | custom-call | flops 120000000 | bytes 1500000 | tf_op jit(solution)/shard_map/coefficients_low/pallas_call | solution.py:311
  28.7 0.4 collective-permute-start.8
  29.1 0.9 %collective-permute-done.8 = f32[128,128]{1,0:T(8,128)S(1)} collective-permute-done((f32[128,128]{1,0:T(8,128)S(1)}, f32[128,128]{1,0:T(8,128)S(1)}, u32[]{:S(2)}, u32[]{:S(2)}) %collective-permute-start.8) | collective-permute-done | bytes 65568 | tf_op jit(solution)/shard_map/ppermute | solution.py:414
  30.1 1.7 %collective-permute-start.11 = (f32[128,128]{1,0:T(8,128)S(1)}, f32[128,128]{1,0:T(8,128)S(1)}, u32[]{:S(2)}, u32[]{:S(2)}) collective-permute-start(f32[128,128]{1,0:T(8,128)S(1)} %add.37.sent_ref), channel_id=1, source_target_pairs={{0,24},{1,7},{2,26},{3,5},{4,28},{5,3},{6,30},{7,1},{8,16},{9,15},... | collective-permute-start | bytes 196616 | tf_op jit(solution)/shard_map/ppermute | solution.py:414
  31.8 1.6 %collective-permute-start.9 = (f32[128,128]{1,0:T(8,128)S(1)}, f32[128,128]{1,0:T(8,128)S(1)}, u32[]{:S(2)}, u32[]{:S(2)}) collective-permute-start(f32[128,128]{1,0:T(8,128)S(1)} %add.37.sent_ref), channel_id=1, source_target_pairs={{0,8},{1,3},{2,10},{3,1},{4,12},{5,7},{6,14},{7,5},{8,0},{9,11},{1... | collective-permute-start | bytes 196616 | tf_op jit(solution)/shard_map/ppermute | solution.py:414
  33.4 2.7 %update_low.1 = (f32[64,4096]{1,0:T(8,128)S(1)}, f32[128,128]{1,0:T(8,128)S(1)}) custom-call(f32[64,256]{1,0:T(8,128)S(1)} %get-tuple-element.35.t_ref, f32[64,4096]{1,0:T(8,128)S(1)} %copy-done, f32[4,128,4096]{2,1,0:T(8,128)} %gen_ref.9, f32[128,128]{1,0:T(8,128)S(1)} %add.37.sent_ref), custom_call_target="tpu_custom_call" | custom-call | flops 402653184 | bytes 6291456 | tf_op jit(solution)/shard_map/update_low/pallas_call | solution.py:363
  36.1 0.3 collective-permute-done.10
  36.4 2.6 %collective-permute-start.14 = (f32[128,128]{1,0:T(8,128)S(1)}, f32[128,128]{1,0:T(8,128)S(1)}, u32[]{:S(2)}, u32[]{:S(2)}) collective-permute-start(f32[128,128]{1,0:T(8,128)S(1)} %add_add_fusion.1), channel_id=1, source_target_pairs={{0,6},{1,25},{2,4},{3,27},{4,2},{5,29},{6,0},{7,31},{8,14},{9,17},... | collective-permute-start | bytes 196616 | tf_op jit(solution)/shard_map/ppermute | solution.py:414
  39.0 0.5 collective-permute-start.13
  39.5 0.3 collective-permute-start.12
  39.7 1.1 %collective-permute-done.14 = f32[128,128]{1,0:T(8,128)S(1)} collective-permute-done((f32[128,128]{1,0:T(8,128)S(1)}, f32[128,128]{1,0:T(8,128)S(1)}, u32[]{:S(2)}, u32[]{:S(2)}) %collective-permute-start.14) | collective-permute-done | bytes 65568 | tf_op jit(solution)/shard_map/ppermute | solution.py:414
  40.8 2.8 %collective-permute-done.13 = f32[128,128]{1,0:T(8,128)S(1)} collective-permute-done((f32[128,128]{1,0:T(8,128)S(1)}, f32[128,128]{1,0:T(8,128)S(1)}, u32[]{:S(2)}, u32[]{:S(2)}) %collective-permute-start.13) | collective-permute-done | bytes 65568 | tf_op jit(solution)/shard_map/ppermute | solution.py:414
  43.6 2.8 %collective-permute-start.17 = (f32[128,128]{1,0:T(8,128)S(1)}, f32[128,128]{1,0:T(8,128)S(1)}, u32[]{:S(2)}, u32[]{:S(2)}) collective-permute-start(f32[128,128]{1,0:T(8,128)S(1)} %add_add_fusion), channel_id=1, source_target_pairs={{0,96},{1,97},{2,98},{3,99},{4,100},{5,101},{6,102},{7,103},{8,104... | collective-permute-start | bytes 196616 | tf_op jit(solution)/shard_map/ppermute | solution.py:414
  46.4 0.3 collective-permute-start.16
  46.8 0.3 collective-permute-start.15
  47.1 1.2 %collective-permute-done.17 = f32[128,128]{1,0:T(8,128)S(1)} collective-permute-done((f32[128,128]{1,0:T(8,128)S(1)}, f32[128,128]{1,0:T(8,128)S(1)}, u32[]{:S(2)}, u32[]{:S(2)}) %collective-permute-start.17) | collective-permute-done | bytes 65568 | tf_op jit(solution)/shard_map/ppermute | solution.py:414
  48.3 2.7 %collective-permute-done.16 = f32[128,128]{1,0:T(8,128)S(1)} collective-permute-done((f32[128,128]{1,0:T(8,128)S(1)}, f32[128,128]{1,0:T(8,128)S(1)}, u32[]{:S(2)}, u32[]{:S(2)}) %collective-permute-start.16) | collective-permute-done | bytes 65568 | tf_op jit(solution)/shard_map/ppermute | solution.py:414
  51.1 4.7 %collective-permute-start.18 = (f32[4,128,128]{2,1,0:T(8,128)S(1)}, f32[4,128,128]{2,1,0:T(8,128)S(1)}, u32[]{:S(2)}, u32[]{:S(2)}) collective-permute-start(f32[4,128,128]{2,1,0:T(8,128)S(1)} %pad_maximum_fusion.1.mine_ref), channel_id=1, source_target_pairs={{0,1},{1,0},{2,3},{3,2},{4,5},{5,4},{6,7},{7,6},{8,9},{9,8},{10,11... | collective-permute-start | bytes 786440 | tf_op jit(solution)/shard_map/ppermute | solution.py:414
  55.8 1.2 %collective-permute-done.18.other_ref = f32[4,128,128]{2,1,0:T(8,128)S(1)} collective-permute-done((f32[4,128,128]{2,1,0:T(8,128)S(1)}, f32[4,128,128]{2,1,0:T(8,128)S(1)}, u32[]{:S(2)}, u32[]{:S(2)}) %collective-permute-start.18) | collective-permute-done | bytes 262176 | tf_op jit(solution)/shard_map/ppermute | solution.py:414
  56.9 3.4 %update_high.1 = f32[64,4096]{1,0:T(8,128)} custom-call(s32[1]{0:T(128)} %bitcast.core_ref, f32[4,128,128]{2,1,0:T(8,128)S(1)} %pad_maximum_fusion.1.mine_ref, f32[4,128,128]{2,1,0:T(8,128)S(1)} %collective-permute-done.18.other_ref, f32[256,256]{1,0:T(8,128)S(1)} %get-tuple-element.39.c1a_ref, f32[256,256]{1,0:T(8,128)S(1)} %get-tuple-element.40.c1b_ref, ...), custom_call_target="tpu_custom_call" | custom-call | flops 500000000 | bytes 7000000 | tf_op jit(solution)/shard_map/update_high/pallas_call | solution.py:400
  (22 shorter events, 0.3 us)
Async XLA Ops:
  3.8 2.4 %collective-permute-start = (f32[128,128]{1,0:T(8,128)S(1)}, f32[128,128]{1,0:T(8,128)S(1)}, u32[]{:S(2)}, u32[]{:S(2)}) collective-permute-start(f32[128,128]{1,0:T(8,128)S(1)} %get-tuple-element.25), channel_id=1, source_target_pairs={{0,1},{1,0},{2,3},{3,2},{4,5},{5,4},{6,7},{7,6},{8,9},{9,8},{10,11... | collective-permute-start | bytes 196616 | tf_op jit(solution)/shard_map/ppermute | solution.py:414
  6.2 8.4 %collective-permute-start.3 = (f32[128,128]{1,0:T(8,128)S(1)}, f32[128,128]{1,0:T(8,128)S(1)}, u32[]{:S(2)}, u32[]{:S(2)}) collective-permute-start(f32[128,128]{1,0:T(8,128)S(1)} %add.33.sent_ref), channel_id=1, source_target_pairs={{0,6},{1,7},{2,4},{3,5},{4,2},{5,3},{6,0},{7,1},{8,14},{9,15},{10,... | collective-permute-start | bytes 196616 | tf_op jit(solution)/shard_map/ppermute | solution.py:414
  10.1 4.6 %collective-permute-start.2 = (f32[128,128]{1,0:T(8,128)S(1)}, f32[128,128]{1,0:T(8,128)S(1)}, u32[]{:S(2)}, u32[]{:S(2)}) collective-permute-start(f32[128,128]{1,0:T(8,128)S(1)} %add.33.sent_ref), channel_id=1, source_target_pairs={{0,4},{1,5},{2,6},{3,7},{4,0},{5,1},{6,2},{7,3},{8,12},{9,13},{10,... | collective-permute-start | bytes 196616 | tf_op jit(solution)/shard_map/ppermute | solution.py:414
  10.1 4.6 %collective-permute-start.1 = (f32[128,128]{1,0:T(8,128)S(1)}, f32[128,128]{1,0:T(8,128)S(1)}, u32[]{:S(2)}, u32[]{:S(2)}) collective-permute-start(f32[128,128]{1,0:T(8,128)S(1)} %add.33.sent_ref), channel_id=1, source_target_pairs={{0,2},{1,3},{2,0},{3,1},{4,6},{5,7},{6,4},{7,5},{8,10},{9,11},{10,... | collective-permute-start | bytes 196616 | tf_op jit(solution)/shard_map/ppermute | solution.py:414
  14.8 18.6 %copy-start = (f32[64,4096]{1,0:T(8,128)S(1)}, f32[64,4096]{1,0:T(8,128)}, u32[]{:S(2)}) copy-start(f32[64,4096]{1,0:T(8,128)} %cur_ref.1) | copy-start | bytes 3145732
  14.8 9.0 %collective-permute-start.6 = (f32[128,128]{1,0:T(8,128)S(1)}, f32[128,128]{1,0:T(8,128)S(1)}, u32[]{:S(2)}, u32[]{:S(2)}) collective-permute-start(f32[128,128]{1,0:T(8,128)S(1)} %add_add_fusion.2.sent_ref), channel_id=1, source_target_pairs={{0,24},{1,25},{2,26},{3,27},{4,28},{5,29},{6,30},{7,31},{8,16},{9,... | collective-permute-start | bytes 196616 | tf_op jit(solution)/shard_map/ppermute | solution.py:414
  17.3 6.4 %collective-permute-start.5 = (f32[128,128]{1,0:T(8,128)S(1)}, f32[128,128]{1,0:T(8,128)S(1)}, u32[]{:S(2)}, u32[]{:S(2)}) collective-permute-start(f32[128,128]{1,0:T(8,128)S(1)} %add_add_fusion.2.sent_ref), channel_id=1, source_target_pairs={{0,16},{1,17},{2,18},{3,19},{4,20},{5,21},{6,22},{7,23},{8,24},{9,... | collective-permute-start | bytes 196616 | tf_op jit(solution)/shard_map/ppermute | solution.py:414
  17.8 5.9 %collective-permute-start.4 = (f32[128,128]{1,0:T(8,128)S(1)}, f32[128,128]{1,0:T(8,128)S(1)}, u32[]{:S(2)}, u32[]{:S(2)}) collective-permute-start(f32[128,128]{1,0:T(8,128)S(1)} %add_add_fusion.2.sent_ref), channel_id=1, source_target_pairs={{0,8},{1,9},{2,10},{3,11},{4,12},{5,13},{6,14},{7,15},{8,0},{9,1},... | collective-permute-start | bytes 196616 | tf_op jit(solution)/shard_map/ppermute | solution.py:414
  23.8 4.2 %collective-permute-start.7 = (f32[4,128,128]{2,1,0:T(8,128)S(1)}, f32[4,128,128]{2,1,0:T(8,128)S(1)}, u32[]{:S(2)}, u32[]{:S(2)}) collective-permute-start(f32[4,128,128]{2,1,0:T(8,128)S(1)} %pad_maximum_fusion.mine_ref), channel_id=1, source_target_pairs={{0,1},{1,0},{2,3},{3,2},{4,5},{5,4},{6,7},{7,6},{8,9},{9,8},{10,11... | collective-permute-start | bytes 786440 | tf_op jit(solution)/shard_map/ppermute | solution.py:414
  28.7 1.3 %collective-permute-start.8 = (f32[128,128]{1,0:T(8,128)S(1)}, f32[128,128]{1,0:T(8,128)S(1)}, u32[]{:S(2)}, u32[]{:S(2)}) collective-permute-start(f32[128,128]{1,0:T(8,128)S(1)} %get-tuple-element.37), channel_id=1, source_target_pairs={{0,1},{1,0},{2,3},{3,2},{4,5},{5,4},{6,7},{7,6},{8,9},{9,8},{10,11... | collective-permute-start | bytes 196616 | tf_op jit(solution)/shard_map/ppermute | solution.py:414
  30.1 6.0 %collective-permute-start.11 = (f32[128,128]{1,0:T(8,128)S(1)}, f32[128,128]{1,0:T(8,128)S(1)}, u32[]{:S(2)}, u32[]{:S(2)}) collective-permute-start(f32[128,128]{1,0:T(8,128)S(1)} %add.37.sent_ref), channel_id=1, source_target_pairs={{0,24},{1,7},{2,26},{3,5},{4,28},{5,3},{6,30},{7,1},{8,16},{9,15},... | collective-permute-start | bytes 196616 | tf_op jit(solution)/shard_map/ppermute | solution.py:414
  31.8 4.6 %collective-permute-start.10 = (f32[128,128]{1,0:T(8,128)S(1)}, f32[128,128]{1,0:T(8,128)S(1)}, u32[]{:S(2)}, u32[]{:S(2)}) collective-permute-start(f32[128,128]{1,0:T(8,128)S(1)} %add.37.sent_ref), channel_id=1, source_target_pairs={{0,16},{1,5},{2,18},{3,7},{4,20},{5,1},{6,22},{7,3},{8,24},{9,13},... | collective-permute-start | bytes 196616 | tf_op jit(solution)/shard_map/ppermute | solution.py:414
  31.8 4.6 %collective-permute-start.9 = (f32[128,128]{1,0:T(8,128)S(1)}, f32[128,128]{1,0:T(8,128)S(1)}, u32[]{:S(2)}, u32[]{:S(2)}) collective-permute-start(f32[128,128]{1,0:T(8,128)S(1)} %add.37.sent_ref), channel_id=1, source_target_pairs={{0,8},{1,3},{2,10},{3,1},{4,12},{5,7},{6,14},{7,5},{8,0},{9,11},{1... | collective-permute-start | bytes 196616 | tf_op jit(solution)/shard_map/ppermute | solution.py:414
  36.4 4.4 %collective-permute-start.14 = (f32[128,128]{1,0:T(8,128)S(1)}, f32[128,128]{1,0:T(8,128)S(1)}, u32[]{:S(2)}, u32[]{:S(2)}) collective-permute-start(f32[128,128]{1,0:T(8,128)S(1)} %add_add_fusion.1), channel_id=1, source_target_pairs={{0,6},{1,25},{2,4},{3,27},{4,2},{5,29},{6,0},{7,31},{8,14},{9,17},... | collective-permute-start | bytes 196616 | tf_op jit(solution)/shard_map/ppermute | solution.py:414
  39.0 4.6 %collective-permute-start.13 = (f32[128,128]{1,0:T(8,128)S(1)}, f32[128,128]{1,0:T(8,128)S(1)}, u32[]{:S(2)}, u32[]{:S(2)}) collective-permute-start(f32[128,128]{1,0:T(8,128)S(1)} %add_add_fusion.1), channel_id=1, source_target_pairs={{0,4},{1,17},{2,6},{3,19},{4,0},{5,21},{6,2},{7,23},{8,12},{9,25},... | collective-permute-start | bytes 196616 | tf_op jit(solution)/shard_map/ppermute | solution.py:414
  39.5 4.1 %collective-permute-start.12 = (f32[128,128]{1,0:T(8,128)S(1)}, f32[128,128]{1,0:T(8,128)S(1)}, u32[]{:S(2)}, u32[]{:S(2)}) collective-permute-start(f32[128,128]{1,0:T(8,128)S(1)} %add_add_fusion.1), channel_id=1, source_target_pairs={{0,2},{1,9},{2,0},{3,11},{4,6},{5,13},{6,4},{7,15},{8,10},{9,1},{1... | collective-permute-start | bytes 196616 | tf_op jit(solution)/shard_map/ppermute | solution.py:414
  43.6 4.7 %collective-permute-start.17 = (f32[128,128]{1,0:T(8,128)S(1)}, f32[128,128]{1,0:T(8,128)S(1)}, u32[]{:S(2)}, u32[]{:S(2)}) collective-permute-start(f32[128,128]{1,0:T(8,128)S(1)} %add_add_fusion), channel_id=1, source_target_pairs={{0,96},{1,97},{2,98},{3,99},{4,100},{5,101},{6,102},{7,103},{8,104... | collective-permute-start | bytes 196616 | tf_op jit(solution)/shard_map/ppermute | solution.py:414
  46.4 4.6 %collective-permute-start.16 = (f32[128,128]{1,0:T(8,128)S(1)}, f32[128,128]{1,0:T(8,128)S(1)}, u32[]{:S(2)}, u32[]{:S(2)}) collective-permute-start(f32[128,128]{1,0:T(8,128)S(1)} %add_add_fusion), channel_id=1, source_target_pairs={{0,64},{1,65},{2,66},{3,67},{4,68},{5,69},{6,70},{7,71},{8,72},{9,... | collective-permute-start | bytes 196616 | tf_op jit(solution)/shard_map/ppermute | solution.py:414
  46.8 4.3 %collective-permute-start.15 = (f32[128,128]{1,0:T(8,128)S(1)}, f32[128,128]{1,0:T(8,128)S(1)}, u32[]{:S(2)}, u32[]{:S(2)}) collective-permute-start(f32[128,128]{1,0:T(8,128)S(1)} %add_add_fusion), channel_id=1, source_target_pairs={{0,32},{1,33},{2,34},{3,35},{4,36},{5,37},{6,38},{7,39},{8,40},{9,... | collective-permute-start | bytes 196616 | tf_op jit(solution)/shard_map/ppermute | solution.py:414
  51.1 5.9 %collective-permute-start.18 = (f32[4,128,128]{2,1,0:T(8,128)S(1)}, f32[4,128,128]{2,1,0:T(8,128)S(1)}, u32[]{:S(2)}, u32[]{:S(2)}) collective-permute-start(f32[4,128,128]{2,1,0:T(8,128)S(1)} %pad_maximum_fusion.1.mine_ref), channel_id=1, source_target_pairs={{0,1},{1,0},{2,3},{3,2},{4,5},{5,4},{6,7},{7,6},{8,9},{9,8},{10,11... | collective-permute-start | bytes 786440 | tf_op jit(solution)/shard_map/ppermute | solution.py:414

commit v3 on v2

v3 whole, which is shorter than its diff:
```python
import functools

import jax
import jax.numpy as jnp
from jax import lax
from jax.experimental import pallas as pl
from jax.experimental.pallas import tpu as pltpu
from jax.sharding import PartitionSpec as P

F32 = jnp.float32
BF16 = jnp.bfloat16
RANK = 128
RHS = 64
DEVICES = 128
LIMITS = (47, 44, 40, 41, 41, 43, 46)
HBM = pl.BlockSpec(memory_space=pltpu.HBM)
VMEM = pl.BlockSpec(memory_space=pltpu.VMEM)
SMEM = pl.BlockSpec(memory_space=pltpu.SMEM)

CORE = 1
Z_MASKS = (2, 6, 4)
X_MASKS = (8, 24, 16)
Y_MASKS = (32, 96, 64)


def split(value):
    high = value.astype(BF16)
    return high, (value - high.astype(F32)).astype(BF16)


def stacked(values):
    parts = [split(v) for v in values]
    return jnp.concatenate([h for h, _ in parts] + [l for _, l in parts], axis=0)


def product(left, right):
    lh, ll = split(left)
    rh, rl = split(right)
    rows = left.shape[0]
    both = jnp.dot(jnp.concatenate([lh, ll], axis=0), rh, preferred_element_type=F32)
    return both[:rows] + both[rows:] + jnp.dot(lh, rl, preferred_element_type=F32)


def contract(left, right):
    return lax.dot_general(left, right, (((1,), (1,)), ((), ())), preferred_element_type=F32)


def fold(total, rows):
    half = total.shape[1] // 2
    wide = total[:rows] + total[rows:]
    return wide[:, :half] + wide[:, half:]


def params(limit):
    return pltpu.CompilerParams(vmem_limit_bytes=limit << 20)


def spans(sizes, points):
    at = 0
    for size in sizes:
        yield pl.ds(at * points // 8, size * points // 8)
        at += size


def fetch(sources, sems, sizes, points):
    parts = []
    for i, cols in enumerate(spans(sizes, points)):
        row = []
        for j, (ref, level, buffer) in enumerate(sources):
            src = ref.at[:, cols] if level is None else ref.at[level, :, cols]
            row.append(pltpu.make_async_copy(src, buffer.at[:, cols], sems.at[i, j]))
        parts.append((cols, row))
    for _, row in parts:
        for copy in row:
            copy.start()
    return parts


def add_to(acc, value, first):
    if first:
        acc[...] = value
    else:
        acc[...] += value


LATE = (4, 2, 1, 1)
EARLY = (1, 1, 2, 4)


def first_kernel(points, core_ref, rhs_ref, basis_ref, gen_ref, keep_ref, send_ref, held_ref,
                 v3_buf, v2_buf, acc2, acc3, sems):
    rhs_buf, u3_buf = held_ref.at[:RHS], held_ref.at[RHS:]
    sources = ((rhs_ref, None, rhs_buf), (basis_ref, 3, v3_buf), (basis_ref, 2, v2_buf), (gen_ref, 3, u3_buf))
    for i, (cols, row) in enumerate(fetch(sources, sems, LATE, points)):
        for copy in row:
            copy.wait()
        rhs = stacked([rhs_buf[:, cols]])
        left = jnp.concatenate([rhs, stacked([u3_buf[:, cols]])], axis=0)
        add_to(acc2, contract(left, stacked([v2_buf[:, cols]])), i == 0)
        add_to(acc3, contract(rhs, stacked([v3_buf[:, cols]])), i == 0)
    p3 = fold(acc3[...], RHS)
    p2 = fold(acc2[: 2 * RHS], RHS)
    g32 = fold(acc2[2 * RHS :], RANK)
    first = core_ref[0] == 0

    @pl.when(first)
    def _():
        keep_ref[:RHS] = p3
        keep_ref[RHS:] = p2
        send_ref[...] = g32

    @pl.when(jnp.logical_not(first))
    def _():
        send_ref[:RHS] = p3
        send_ref[RHS:] = p2
        keep_ref[...] = g32


def array(*shape):
    return jax.ShapeDtypeStruct(shape, F32)


def first_step(core, rhs, basis, gen):
    points = rhs.shape[1]
    wide = pltpu.VMEM((RANK, points), F32)
    return pl.pallas_call(
        functools.partial(first_kernel, points),
        out_shape=(array(RANK, RANK), array(RANK, RANK), array(RHS + RANK, points)),
        in_specs=[SMEM, HBM, HBM, HBM],
        out_specs=(VMEM,) * 3,
        scratch_shapes=[
            wide, wide,
            pltpu.VMEM((2 * (RHS + RANK), 2 * RANK), F32),
            pltpu.VMEM((2 * RHS, 2 * RANK), F32),
            pltpu.SemaphoreType.DMA((len(LATE), 4)),
        ],
        compiler_params=params(LIMITS[0]),
        cost_estimate=pl.CostEstimate(flops=800_000_000, bytes_accessed=7_340_032, transcendentals=0),
        name="project_low",
    )(core, rhs, basis, gen)


def related(cap_ref, out_ref, sems, node, s, base, columns):
    copies = []
    for r, row in enumerate((1 - s, s)):
        for c, col in enumerate((s, 1 - s)[:columns]):
            copies.append(
                pltpu.make_async_copy(
                    cap_ref.at[node, pl.ds(pl.multiple_of(row * RANK, RANK), RANK), pl.ds(pl.multiple_of(col * RANK, RANK), RANK)],
                    out_ref.at[r * RANK : (r + 1) * RANK, c * RANK : (c + 1) * RANK],
                    sems.at[base + 2 * r + c],
                )
            )
    for copy in copies:
        copy.start()
    return copies


def grams_kernel(points, held_ref, basis_ref, sent_ref, sent_out, p_ref, g_ref, v1_buf, v0_buf,
                 acc1, acc0, sems):
    parts = fetch(((basis_ref, 1, v1_buf), (basis_ref, 0, v0_buf)), sems, EARLY, points)
    sent_out[...] = sent_ref[...]
    for i, (cols, row) in enumerate(parts):
        left = stacked([held_ref[:, cols]])
        for copy, buffer, acc in zip(row, (v1_buf, v0_buf), (acc1, acc0)):
            copy.wait()
            add_to(acc, contract(left, stacked([buffer[:, cols]])), i == 0)
    for k, acc in enumerate((acc1, acc0)):
        both = fold(acc[...], RHS + RANK)
        p_ref[:, k * RANK : (k + 1) * RANK] = both[:RHS]
        g_ref[:, k * RANK : (k + 1) * RANK] = both[RHS:]


def grams_step(held, basis, sent):
    points = held.shape[1]
    total = pltpu.VMEM((2 * (RHS + RANK), 2 * RANK), F32)
    return pl.pallas_call(
        functools.partial(grams_kernel, points),
        out_shape=(
            array(*sent.shape), array(RHS, 2 * RANK), array(RANK, 2 * RANK),
            array(RANK, points), array(RANK, points),
        ),
        in_specs=[VMEM, HBM, VMEM],
        out_specs=(VMEM,) * 5,
        scratch_shapes=[total, total, pltpu.SemaphoreType.DMA((len(EARLY), 2))],
        compiler_params=params(LIMITS[1]),
        cost_estimate=pl.CostEstimate(flops=1_500_000_000, bytes_accessed=7_340_032, transcendentals=0),
        name="grams_three",
    )(held, basis, sent)


def rest_kernel(points, place_ref, v1_ref, v0_ref, gen_ref, cap_ref, sent_ref, sent_out,
                g_ref, g10_ref, c3a_ref, c3b_ref, c2_ref, c1a_ref, c1b_ref, c0_ref, u2_buf, u1_buf,
                acc1, acc0, acc, sems, cap_sems):
    parts = fetch(((gen_ref, 2, u2_buf), (gen_ref, 1, u1_buf)), sems, EARLY, points)
    sent_out[...] = sent_ref[...]
    s3, s2, s1, s0 = place_ref[0], place_ref[1], place_ref[2], place_ref[3]
    n3, n2, n1 = place_ref[4], place_ref[5], place_ref[6]
    caps = related(cap_ref, c3a_ref, cap_sems, 7 + n3, s3, 0, 2)
    caps += related(cap_ref, c3b_ref, cap_sems, 7 + (n3 ^ 1), s3, 4, 2)
    caps += related(cap_ref, c2_ref, cap_sems, 3 + n2, s2, 8, 1)
    caps += related(cap_ref, c1a_ref, cap_sems, 1 + n1, s1, 12, 2)
    caps += related(cap_ref, c1b_ref, cap_sems, 1 + (n1 ^ 1), s1, 16, 2)
    caps += related(cap_ref, c0_ref, cap_sems, 0, s0, 20, 1)
    for i, (cols, row) in enumerate(parts):
        v1, v0 = stacked([v1_ref[:, cols]]), stacked([v0_ref[:, cols]])
        row[0].wait()
        u2 = stacked([u2_buf[:, cols]])
        add_to(acc1, contract(u2, v1), i == 0)
        add_to(acc0, contract(u2, v0), i == 0)
        row[1].wait()
        add_to(acc, contract(stacked([u1_buf[:, cols]]), v0), i == 0)
    g_ref[:, :RANK] = fold(acc1[...], RANK)
    g_ref[:, RANK:] = fold(acc0[...], RANK)
    g10_ref[...] = fold(acc[...], RANK)
    for copy in caps:
        copy.wait()


def rest_step(place, v1, v0, gen, cap, sent):
    points = v1.shape[1]
    square, column = array(2 * RANK, 2 * RANK), array(2 * RANK, RANK)
    total = pltpu.VMEM((2 * RANK, 2 * RANK), F32)
    return pl.pallas_call(
        functools.partial(rest_kernel, points),
        out_shape=(
            array(*sent.shape), array(RANK, 2 * RANK), array(RANK, RANK),
            square, square, column, square, square, column, array(RANK, points), array(RANK, points),
        ),
        in_specs=[SMEM, VMEM, VMEM, HBM, HBM, VMEM],
        out_specs=(VMEM,) * 11,
        scratch_shapes=[
            total, total, total,
            pltpu.SemaphoreType.DMA((len(EARLY), 2)),
            pltpu.SemaphoreType.DMA((24,)),
        ],
        compiler_params=params(LIMITS[2]),
        cost_estimate=pl.CostEstimate(flops=1_500_000_000, bytes_accessed=9_437_184, transcendentals=0),
        name="grams_rest",
    )(place, v1, v0, gen, cap, sent)


def middle_kernel(core_ref, mine_ref, other_ref, c3a_ref, c3b_ref, c2_ref, p_ref, g3_ref, g2_ref, g10_ref,
                  t_ref, keep_ref, send_ref):
    first = core_ref[0] == 0
    p, g = [], []
    for m in range(4):
        mine, other = mine_ref[m], other_ref[m]
        p.append(jnp.where(first, mine, other))
        g.append(jnp.where(first, other, mine))
    t = []
    for pair, cap in ((0, c3a_ref), (2, c3b_ref)):
        joined = jnp.concatenate([p[pair][:RHS], p[pair + 1][:RHS]], axis=1)
        both = product(joined, cap[...])
        t += [both[:, :RANK], both[:, RANK:]]
    q2 = [p[m][RHS:] - product(t[m], g[m]) for m in range(4)]
    joined = jnp.concatenate([q2[0] + q2[1], q2[2] + q2[3]], axis=1)
    coeff = jnp.concatenate([t[0], product(joined, c2_ref[...])], axis=1)
    t_ref[...] = coeff
    q = p_ref[...] - product(coeff, jnp.concatenate([g3_ref[...], g2_ref[...]], axis=0))
    half = RHS // 2

    def put(ref, c):
        rows = slice(c * half, (c + 1) * half)
        ref[:half] = q[rows, :RANK]
        ref[half : 2 * half] = q[rows, RANK:]
        ref[2 * half :] = g10_ref[c * RHS : (c + 1) * RHS]

    @pl.when(first)
    def _():
        put(keep_ref, 0)
        put(send_ref, 1)

    @pl.when(jnp.logical_not(first))
    def _():
        put(keep_ref, 1)
        put(send_ref, 0)


def middle_step(core, mine, other, c3a, c3b, c2, p, g3, g2, g10):
    half = jax.ShapeDtypeStruct((RANK, RANK), F32)
    return pl.pallas_call(
        middle_kernel,
        out_shape=(jax.ShapeDtypeStruct((RHS, 2 * RANK), F32), half, half),
        in_specs=[SMEM] + [VMEM] * 9,
        out_specs=(VMEM,) * 3,
        compiler_params=params(LIMITS[3]),
        cost_estimate=pl.CostEstimate(flops=120_000_000, bytes_accessed=1_500_000, transcendentals=0),
        name="coefficients_low",
    )(core, mine, other, c3a, c3b, c2, p, g3, g2, g10)


def low_update_kernel(t_ref, held_ref, u2_ref, sent_ref, cur_ref, sent_out):
    sent_out[...] = sent_ref[...]
    th, tl = split(t_ref[...])
    left = jnp.concatenate([th, tl], axis=0)
    for cols in spans((2,) * 4, held_ref.shape[1]):
        gh, gl = split(jnp.concatenate([held_ref[RHS:, cols], u2_ref[:, cols]], axis=0))
        both = jnp.dot(left, gh, preferred_element_type=F32)
        update = both[:RHS] + both[RHS:] + jnp.dot(th, gl, preferred_element_type=F32)
        cur_ref[:, cols] = held_ref[:RHS, cols] - update


def low_update(t, held, u2, sent):
    return pl.pallas_call(
        low_update_kernel,
        out_shape=(array(RHS, held.shape[1]), array(*sent.shape)),
        in_specs=[VMEM] * 4,
        out_specs=(VMEM, VMEM),
        compiler_params=params(LIMITS[4]),
        cost_estimate=pl.CostEstimate(flops=402_653_184, bytes_accessed=6_291_456, transcendentals=0),
        name="update_low",
    )(t, held, u2, sent)


def pairs_kernel(points, u1_ref, gen_ref, sent_ref, sent_out, high_ref, low_ref, u0_buf, sems):
    parts = fetch(((gen_ref, 0, u0_buf),), sems, (4, 4), points)
    sent_out[...] = sent_ref[...]
    high_ref[:RANK], low_ref[:RANK] = split(u1_ref[...])
    for cols, row in parts:
        row[0].wait()
        high_ref[RANK:, cols], low_ref[RANK:, cols] = split(u0_buf[:, cols])


def pairs_step(u1, gen, sent):
    points = u1.shape[1]
    pair = jax.ShapeDtypeStruct((2 * RANK, points), BF16)
    return pl.pallas_call(
        functools.partial(pairs_kernel, points),
        out_shape=(array(*sent.shape), pair, pair),
        in_specs=[VMEM, HBM, VMEM],
        out_specs=(VMEM,) * 3,
        scratch_shapes=[pltpu.VMEM((RANK, points), F32), pltpu.SemaphoreType.DMA((2, 1))],
        compiler_params=params(LIMITS[5]),
        cost_estimate=pl.CostEstimate(flops=100_000_000, bytes_accessed=8_388_608, transcendentals=0),
        name="pairs_high",
    )(u1, gen, sent)


def last_kernel(core_ref, mine_ref, other_ref, c1a_ref, c1b_ref, c0_ref, cur_ref, high_ref, low_ref, out_ref,
                buf, sems):
    first = core_ref[0] == 0
    half = RHS // 2
    q1, q0, g = [], [], []
    for m in range(4):
        mine, other = mine_ref[m], other_ref[m]
        low = jnp.where(first, mine, other)
        high = jnp.where(first, other, mine)
        q1.append(jnp.concatenate([low[:half], high[:half]], axis=0))
        q0.append(jnp.concatenate([low[half:RHS], high[half:RHS]], axis=0))
        g.append(jnp.concatenate([low[RHS:], high[RHS:]], axis=0))
    t = []
    for pair, cap in ((0, c1a_ref), (2, c1b_ref)):
        both = product(jnp.concatenate([q1[pair], q1[pair + 1]], axis=1), cap[...])
        t += [both[:, :RANK], both[:, RANK:]]
    r = [q0[m] - product(t[m], g[m]) for m in range(4)]
    joined = jnp.concatenate([r[0] + r[1], r[2] + r[3]], axis=1)
    th, tl = split(jnp.concatenate([t[0], product(joined, c0_ref[...])], axis=1))
    left = jnp.concatenate([th, tl], axis=0)
    copies = []
    for i, cols in enumerate(spans((2,) * 4, cur_ref.shape[1])):
        both = jnp.dot(left, high_ref[:, cols], preferred_element_type=F32)
        update = both[:RHS] + both[RHS:] + jnp.dot(th, low_ref[:, cols], preferred_element_type=F32)
        buf[:, cols] = cur_ref[:, cols] - update
        copy = pltpu.make_async_copy(buf.at[:, cols], out_ref.at[:, cols], sems.at[i])
        copy.start()
        copies.append(copy)
    for copy in copies:
        copy.wait()


def last_step(core, mine, other, c1a, c1b, c0, cur, high, low):
    return pl.pallas_call(
        last_kernel,
        out_shape=array(*cur.shape),
        in_specs=[SMEM] + [VMEM] * 8,
        out_specs=HBM,
        scratch_shapes=[pltpu.VMEM(cur.shape, F32), pltpu.SemaphoreType.DMA((4,))],
        compiler_params=params(LIMITS[6]),
        cost_estimate=pl.CostEstimate(flops=500_000_000, bytes_accessed=7_000_000, transcendentals=0),
        name="update_high",
    )(core, mine, other, c1a, c1b, c0, cur, high, low)


def swap(value, even, odd):
    pairs = [(i, i ^ (odd if i & CORE else even)) for i in range(DEVICES)]
    return lax.ppermute(value, "leaf", pairs)


def gathered(value, even, odd):
    one, three, two = (swap(value, e, o) for e, o in zip(even, odd))
    return value, one, two, three


def body(rhs, basis, gen, cap):
    device = lax.axis_index("leaf").astype(jnp.int32)
    core = (device & 1).reshape(1)
    place = jnp.stack([
        device >> 3 & 1, device >> 4 & 1, device >> 5 & 1, device >> 6 & 1,
        device >> 4, device >> 5, device >> 6,
    ])
    keep, send, held = first_step(core, rhs, basis, gen)
    chip = keep + swap(send, CORE, CORE)
    _, b, c, d = gathered(chip, Z_MASKS, Z_MASKS)
    chip, p, g3, v1, v0 = grams_step(held, basis, chip)
    line = chip + b + c + d
    _, b, c, d = gathered(line, X_MASKS, X_MASKS)
    line, g2, g10, c3a, c3b, c2, c1a, c1b, c0, u2, u1 = rest_step(place, v1, v0, gen, cap, line)
    lines = jnp.stack([line, b, c, d])
    other = swap(lines, CORE, CORE)
    t, keep, send = middle_step(core, lines, other, c3a, c3b, c2, p, g3, g2, g10)
    chip = keep + swap(send, CORE, CORE)
    _, b, c, d = gathered(chip, X_MASKS, Z_MASKS)
    current, chip = low_update(t, held, u2, chip)
    part = chip + b + c + d
    _, b, c, d = gathered(part, Z_MASKS, X_MASKS)
    part, high, low = pairs_step(u1, gen, part)
    plane = part + b + c + d
    planes = jnp.stack(gathered(plane, Y_MASKS, Y_MASKS))
    other = swap(planes, CORE, CORE)
    return last_step(core, planes, other, c1a, c1b, c0, current, high, low)


def solution(mesh):
    in_specs = (P(None, "leaf"), P(None, None, "leaf"), P(None, None, "leaf"), P())
    return jax.shard_map(body, mesh=mesh, in_specs=in_specs, out_specs=P(None, "leaf"), check_vma=False)
```

time: 60.5 us -> 66.9 us (1.11)
  starting transfers between devices: 27.7 us -> 32.2 us
  local copies, waits for them, and re-layouts: 0.09 us -> 1.31 us
  Pallas kernels: 20 us -> 21.1 us
    ppermute x19, starting transfers between devices: 27.7 us -> 32.2 us  [swap(): return lax.ppermute(value, 'leaf', pairs)]
    unnamed x2 -> x4, local copies, waits for them, and re-layouts: 0.01 us -> 1.23 us
    pallas_call x5 -> x6, Pallas kernels: 19.3 us -> 20.4 us  [the longest x1 5.79 us: grams_step(): pl.pallas_call(functools.partial(grams_kernel, points), out_shape=(array(...]
  transfers between devices with their start and end apart: 19 -> 19, of which waited for: 10 -> 11; matrix products, arithmetic and copies ran while one was open for 0% -> 0% of each run, Pallas kernels for 20% -> 21%
where the time goes in v3:
time: 66.9 us; the launch traced here: 66.7 us
  starting transfers between devices  32.2 us (48%)
  Pallas kernels  21.1 us (32%)
  waiting for transfers between devices  11.7 us (17%)
  local copies, waits for them, and re-layouts  1.31 us (2%)
    ppermute x19, starting transfers between devices, swap(): return lax.ppermute(value, 'leaf', pairs)  32.2 us
    ppermute x19, waiting for transfers between devices, swap(): return lax.ppermute(value, 'leaf', pairs)  11.7 us
    pallas_call x1, Pallas kernels, grams_step(): pl.pallas_call(functools.partial(grams_kernel, points), out_shape=(array(...  5.79 us
    pallas_call x1, Pallas kernels, rest_step(): pl.pallas_call(functools.partial(rest_kernel, points), out_shape=(array(*...  5.73 us
    pallas_call x1, Pallas kernels, first_step(): pl.pallas_call(functools.partial(first_kernel, points), out_shape=(array(...  4.04 us
    pallas_call x1, Pallas kernels, last_step(): pl.pallas_call(last_kernel, out_shape=array(*cur.shape), in_specs=[SMEM]...  2.1 us
    pallas_call x1, Pallas kernels, pairs_step(): pl.pallas_call(functools.partial(pairs_kernel, points), out_shape=(array(...  1.7 us
  transfers between devices with their start and end apart: 19, of which 11 were waited for; matrix products, arithmetic and copies ran while one was open for 0% of the time, Pallas kernels for 21%

profile of v3, /device:TPU:1, one launch (start us, length us, event | category | flops | bytes accessed | tf_op | source)
XLA Modules:
  0.0 66.7 jit_solution(10364980673854333371)
XLA Ops:
  0.0 1.2 %copy-done.1 = f32[64,4096]{1,0:T(8,128)S(1)} copy-done((f32[64,4096]{1,0:T(8,128)S(1)}, f32[64,4096]{1,0:T(8,128)}, u32[]{:S(2)}) %copy-start.1) | copy-done | bytes 1048600
  1.2 4.0 %project_low.1 = (f32[128,128]{1,0:T(8,128)S(1)}, f32[128,128]{1,0:T(8,128)S(1)}, f32[192,4096]{1,0:T(8,128)S(1)}) custom-call(s32[1]{0:T(128)} %bitcast.core_ref, f32[64,4096]{1,0:T(8,128)S(1)} %copy-done.1, f32[4,128,4096]{2,1,0:T(8,128)} %basis_ref.3, f32[4,128,4096]{2,1,0:T(8,128)} %gen_ref.5), custom_call_target="tpu_custom_call" | custom-call | flops 800000000 | bytes 7340032 | tf_op jit(solution)/shard_map/project_low/pallas_call | solution.py:126
  5.3 1.5 %collective-permute-start = (f32[128,128]{1,0:T(8,128)S(1)}, f32[128,128]{1,0:T(8,128)S(1)}, u32[]{:S(2)}, u32[]{:S(2)}) collective-permute-start(f32[128,128]{1,0:T(8,128)S(1)} %get-tuple-element.34), channel_id=1, source_target_pairs={{0,1},{1,0},{2,3},{3,2},{4,5},{5,4},{6,7},{7,6},{8,9},{9,8},{10,11... | collective-permute-start | bytes 196616 | tf_op jit(solution)/shard_map/ppermute | solution.py:387
  6.9 0.8 %collective-permute-done = f32[128,128]{1,0:T(8,128)S(1)} collective-permute-done((f32[128,128]{1,0:T(8,128)S(1)}, f32[128,128]{1,0:T(8,128)S(1)}, u32[]{:S(2)}, u32[]{:S(2)}) %collective-permute-start) | collective-permute-done | bytes 65568 | tf_op jit(solution)/shard_map/ppermute | solution.py:387
  7.7 1.8 %collective-permute-start.1 = (f32[128,128]{1,0:T(8,128)S(1)}, f32[128,128]{1,0:T(8,128)S(1)}, u32[]{:S(2)}, u32[]{:S(2)}) collective-permute-start(f32[128,128]{1,0:T(8,128)S(1)} %add.33.sent_ref), channel_id=1, source_target_pairs={{0,2},{1,3},{2,0},{3,1},{4,6},{5,7},{6,4},{7,5},{8,10},{9,11},{10,... | collective-permute-start | bytes 196616 | tf_op jit(solution)/shard_map/ppermute | solution.py:387
  9.5 3.3 %collective-permute-start.2 = (f32[128,128]{1,0:T(8,128)S(1)}, f32[128,128]{1,0:T(8,128)S(1)}, u32[]{:S(2)}, u32[]{:S(2)}) collective-permute-start(f32[128,128]{1,0:T(8,128)S(1)} %add.33.sent_ref), channel_id=1, source_target_pairs={{0,4},{1,5},{2,6},{3,7},{4,0},{5,1},{6,2},{7,3},{8,12},{9,13},{10,... | collective-permute-start | bytes 196616 | tf_op jit(solution)/shard_map/ppermute | solution.py:387
  12.8 5.8 %grams_three.1 = (f32[128,128]{1,0:T(8,128)S(1)}, f32[64,256]{1,0:T(8,128)S(1)}, f32[128,256]{1,0:T(8,128)S(1)}, f32[128,4096]{1,0:T(8,128)S(1)}, f32[128,4096]{1,0:T(8,128)S(1)}) custom-call(f32[192,4096]{1,0:T(8,128)S(1)} %get-tuple-element.32.held_ref, f32[4,128,4096]{2,1,0:T(8,128)} %basis_ref.3, f32[128,128]{1,0:T(8,128)S(1)} %add.33.sent_ref), custom_call_target="tpu_custom_call" | custom-call | flops 1500000000 | bytes 7340032 | tf_op jit(solution)/shard_map/grams_three/pallas_call | solution.py:177
  18.6 2.8 %collective-permute-start.5 = (f32[128,128]{1,0:T(8,128)S(1)}, f32[128,128]{1,0:T(8,128)S(1)}, u32[]{:S(2)}, u32[]{:S(2)}) collective-permute-start(f32[128,128]{1,0:T(8,128)S(1)} %add_add_fusion.2.sent_ref), channel_id=1, source_target_pairs={{0,16},{1,17},{2,18},{3,19},{4,20},{5,21},{6,22},{7,23},{8,24},{9,... | collective-permute-start | bytes 196616 | tf_op jit(solution)/shard_map/ppermute | solution.py:387
  21.5 0.9 %collective-permute-start.6 = (f32[128,128]{1,0:T(8,128)S(1)}, f32[128,128]{1,0:T(8,128)S(1)}, u32[]{:S(2)}, u32[]{:S(2)}) collective-permute-start(f32[128,128]{1,0:T(8,128)S(1)} %add_add_fusion.2.sent_ref), channel_id=1, source_target_pairs={{0,24},{1,25},{2,26},{3,27},{4,28},{5,29},{6,30},{7,31},{8,16},{9,... | collective-permute-start | bytes 196616 | tf_op jit(solution)/shard_map/ppermute | solution.py:387
  22.3 5.7 %grams_rest.1 = (f32[128,128]{1,0:T(8,128)S(1)}, f32[128,256]{1,0:T(8,128)S(1)}, f32[128,128]{1,0:T(8,128)S(1)}, f32[256,256]{1,0:T(8,128)S(1)}, f32[256,256]{1,...) custom-call(s32[7]{0:T(128)S(1)} %stack.61.place_ref, ...), custom_call_target="tpu_custom_call" | custom-call | flops 1500000000 | bytes 9437184 | tf_op jit(solution)/shard_map/grams_rest/pallas_call | solution.py:224
  28.1 1.5 %collective-permute-start.7 = (f32[4,128,128]{2,1,0:T(8,128)S(1)}, f32[4,128,128]{2,1,0:T(8,128)S(1)}, u32[]{:S(2)}, u32[]{:S(2)}) collective-permute-start(f32[4,128,128]{2,1,0:T(8,128)S(1)} %pad_maximum_fusion.mine_ref), channel_id=1, source_target_pairs={{0,1},{1,0},{2,3},{3,2},{4,5},{5,4},{6,7},{7,6},{8,9},{9,8},{10,11... | collective-permute-start | bytes 786440 | tf_op jit(solution)/shard_map/ppermute | solution.py:387
  29.7 1.2 %collective-permute-done.7.other_ref = f32[4,128,128]{2,1,0:T(8,128)S(1)} collective-permute-done((f32[4,128,128]{2,1,0:T(8,128)S(1)}, f32[4,128,128]{2,1,0:T(8,128)S(1)}, u32[]{:S(2)}, u32[]{:S(2)}) %collective-permute-start.7) | collective-permute-done | bytes 262176 | tf_op jit(solution)/shard_map/ppermute | solution.py:387
  30.8 0.7 %coefficients_low.1 = (f32[64,256]{1,0:T(8,128)S(1)}, f32[128,128]{1,0:T(8,128)S(1)}, f32[128,128]{1,0:T(8,128)S(1)}) custom-call(s32[1]{0:T(128)} %bitcast.core_ref, f32[4,128,128]{2,1,0:T(8,128)S(1)} %pad_maximum_fusion.mine_ref, f32[4,128,128]{2,1,0:T(8,128)S(1)} %collective-permute-done.7.other_ref, f32[256,256]{1,0:T(8,128)S(1)} %get-tuple-element.40.c3a_ref, ...), custom_call_target="tpu_custom_call" | custom-call | flops 120000000 | bytes 1500000 | tf_op jit(solution)/shard_map/coefficients_low/pallas_call | solution.py:282
  31.5 0.4 collective-permute-start.8
  32.0 0.9 %collective-permute-done.8 = f32[128,128]{1,0:T(8,128)S(1)} collective-permute-done((f32[128,128]{1,0:T(8,128)S(1)}, f32[128,128]{1,0:T(8,128)S(1)}, u32[]{:S(2)}, u32[]{:S(2)}) %collective-permute-start.8) | collective-permute-done | bytes 65568 | tf_op jit(solution)/shard_map/ppermute | solution.py:387
  32.9 1.7 %collective-permute-start.10 = (f32[128,128]{1,0:T(8,128)S(1)}, f32[128,128]{1,0:T(8,128)S(1)}, u32[]{:S(2)}, u32[]{:S(2)}) collective-permute-start(f32[128,128]{1,0:T(8,128)S(1)} %add.37.sent_ref), channel_id=1, source_target_pairs={{0,16},{1,5},{2,18},{3,7},{4,20},{5,1},{6,22},{7,3},{8,24},{9,13},... | collective-permute-start | bytes 196616 | tf_op jit(solution)/shard_map/ppermute | solution.py:387
  34.6 1.4 %collective-permute-start.11 = (f32[128,128]{1,0:T(8,128)S(1)}, f32[128,128]{1,0:T(8,128)S(1)}, u32[]{:S(2)}, u32[]{:S(2)}) collective-permute-start(f32[128,128]{1,0:T(8,128)S(1)} %add.37.sent_ref), channel_id=1, source_target_pairs={{0,24},{1,7},{2,26},{3,5},{4,28},{5,3},{6,30},{7,1},{8,16},{9,15},... | collective-permute-start | bytes 196616 | tf_op jit(solution)/shard_map/ppermute | solution.py:387
  36.0 0.5 collective-permute-start.9
  36.5 1.0 %update_low.1 = (f32[64,4096]{1,0:T(8,128)S(1)}, f32[128,128]{1,0:T(8,128)S(1)}) custom-call(f32[64,256]{1,0:T(8,128)S(1)} %get-tuple-element.47.t_ref, f32[192,4096]{1,0:T(8,128)S(1)} %get-tuple-element.32.held_ref, f32[128,4096]{1,0:T(8,128)S(1)} %get-tuple-element.48.u2_ref, f32[128,128]{1,0:T(8,128)S(1)} %add.37.sent_ref), custom_call_target="tpu_custom_call" | custom-call | flops 402653184 | bytes 6291456 | tf_op jit(solution)/shard_map/update_low/pallas_call | solution.py:305
  37.6 1.3 %collective-permute-done.11 = f32[128,128]{1,0:T(8,128)S(1)} collective-permute-done((f32[128,128]{1,0:T(8,128)S(1)}, f32[128,128]{1,0:T(8,128)S(1)}, u32[]{:S(2)}, u32[]{:S(2)}) %collective-permute-start.11) | collective-permute-done | bytes 65568 | tf_op jit(solution)/shard_map/ppermute | solution.py:387
  39.2 2.1 %collective-permute-start.12 = (f32[128,128]{1,0:T(8,128)S(1)}, f32[128,128]{1,0:T(8,128)S(1)}, u32[]{:S(2)}, u32[]{:S(2)}) collective-permute-start(f32[128,128]{1,0:T(8,128)S(1)} %add_add_fusion.1.sent_ref), channel_id=1, source_target_pairs={{0,2},{1,9},{2,0},{3,11},{4,6},{5,13},{6,4},{7,15},{8,10},{9,1},{1... | collective-permute-start | bytes 196616 | tf_op jit(solution)/shard_map/ppermute | solution.py:387
  41.3 1.8 %collective-permute-start.13 = (f32[128,128]{1,0:T(8,128)S(1)}, f32[128,128]{1,0:T(8,128)S(1)}, u32[]{:S(2)}, u32[]{:S(2)}) collective-permute-start(f32[128,128]{1,0:T(8,128)S(1)} %add_add_fusion.1.sent_ref), channel_id=1, source_target_pairs={{0,4},{1,17},{2,6},{3,19},{4,0},{5,21},{6,2},{7,23},{8,12},{9,25},... | collective-permute-start | bytes 196616 | tf_op jit(solution)/shard_map/ppermute | solution.py:387
  43.1 0.9 %collective-permute-start.14 = (f32[128,128]{1,0:T(8,128)S(1)}, f32[128,128]{1,0:T(8,128)S(1)}, u32[]{:S(2)}, u32[]{:S(2)}) collective-permute-start(f32[128,128]{1,0:T(8,128)S(1)} %add_add_fusion.1.sent_ref), channel_id=1, source_target_pairs={{0,6},{1,25},{2,4},{3,27},{4,2},{5,29},{6,0},{7,31},{8,14},{9,17},... | collective-permute-start | bytes 196616 | tf_op jit(solution)/shard_map/ppermute | solution.py:387
  44.0 1.7 %pairs_high.1 = (f32[128,128]{1,0:T(8,128)S(1)}, bf16[256,4096]{1,0:T(8,128)(2,1)S(1)}, bf16[256,4096]{1,0:T(8,128)(2,1)S(1)}) custom-call(f32[128,4096]{1,0:T(8,128)S(1)} %get-tuple-element.38.u1_ref, f32[4,128,4096]{2,1,0:T(8,128)} %gen_ref.5, f32[128,128]{1,0:T(8,128)S(1)} %add_add_fusion.1.sent_ref), custom_call_target="tpu_custom_call" | custom-call | flops 100000000 | bytes 8388608 | tf_op jit(solution)/shard_map/pairs_high/pallas_call | solution.py:328
  45.9 1.5 %collective-permute-done.14 = f32[128,128]{1,0:T(8,128)S(1)} collective-permute-done((f32[128,128]{1,0:T(8,128)S(1)}, f32[128,128]{1,0:T(8,128)S(1)}, u32[]{:S(2)}, u32[]{:S(2)}) %collective-permute-start.14) | collective-permute-done | bytes 65568 | tf_op jit(solution)/shard_map/ppermute | solution.py:387
  47.4 1.4 %collective-permute-start.15 = (f32[128,128]{1,0:T(8,128)S(1)}, f32[128,128]{1,0:T(8,128)S(1)}, u32[]{:S(2)}, u32[]{:S(2)}) collective-permute-start(f32[128,128]{1,0:T(8,128)S(1)} %add_add_fusion), channel_id=1, source_target_pairs={{0,32},{1,33},{2,34},{3,35},{4,36},{5,37},{6,38},{7,39},{8,40},{9,... | collective-permute-start | bytes 196616 | tf_op jit(solution)/shard_map/ppermute | solution.py:387
  48.8 2.6 %collective-permute-start.16 = (f32[128,128]{1,0:T(8,128)S(1)}, f32[128,128]{1,0:T(8,128)S(1)}, u32[]{:S(2)}, u32[]{:S(2)}) collective-permute-start(f32[128,128]{1,0:T(8,128)S(1)} %add_add_fusion), channel_id=1, source_target_pairs={{0,64},{1,65},{2,66},{3,67},{4,68},{5,69},{6,70},{7,71},{8,72},{9,... | collective-permute-start | bytes 196616 | tf_op jit(solution)/shard_map/ppermute | solution.py:387
  51.5 2.3 %collective-permute-done.16 = f32[128,128]{1,0:T(8,128)S(1)} collective-permute-done((f32[128,128]{1,0:T(8,128)S(1)}, f32[128,128]{1,0:T(8,128)S(1)}, u32[]{:S(2)}, u32[]{:S(2)}) %collective-permute-start.16) | collective-permute-done | bytes 65568 | tf_op jit(solution)/shard_map/ppermute | solution.py:387
  53.8 2.0 %collective-permute-done.17 = f32[128,128]{1,0:T(8,128)S(1)} collective-permute-done((f32[128,128]{1,0:T(8,128)S(1)}, f32[128,128]{1,0:T(8,128)S(1)}, u32[]{:S(2)}, u32[]{:S(2)}) %collective-permute-start.17) | collective-permute-done | bytes 65568 | tf_op jit(solution)/shard_map/ppermute | solution.py:387
  55.8 7.5 %collective-permute-start.18 = (f32[4,128,128]{2,1,0:T(8,128)S(1)}, f32[4,128,128]{2,1,0:T(8,128)S(1)}, u32[]{:S(2)}, u32[]{:S(2)}) collective-permute-start(f32[4,128,128]{2,1,0:T(8,128)S(1)} %pad_maximum_fusion.1.mine_ref), channel_id=1, source_target_pairs={{0,1},{1,0},{2,3},{3,2},{4,5},{5,4},{6,7},{7,6},{8,9},{9,8},{10,11... | collective-permute-start | bytes 786440 | tf_op jit(solution)/shard_map/ppermute | solution.py:387
  63.3 1.2 %collective-permute-done.18.other_ref = f32[4,128,128]{2,1,0:T(8,128)S(1)} collective-permute-done((f32[4,128,128]{2,1,0:T(8,128)S(1)}, f32[4,128,128]{2,1,0:T(8,128)S(1)}, u32[]{:S(2)}, u32[]{:S(2)}) %collective-permute-start.18) | collective-permute-done | bytes 262176 | tf_op jit(solution)/shard_map/ppermute | solution.py:387
  64.5 2.1 %update_high.1 = f32[64,4096]{1,0:T(8,128)} custom-call(s32[1]{0:T(128)} %bitcast.core_ref, f32[4,128,128]{2,1,0:T(8,128)S(1)} %pad_maximum_fusion.1.mine_ref, f32[4,128,128]{2,1,0:T(8,128)S(1)} %collective-permute-done.18.other_ref, f32[256,256]{1,0:T(8,128)S(1)} %get-tuple-element.53.c1a_ref, f32[256,256]{1,0:T(8,128)S(1)} %get-tuple-element.54.c1b_ref, ...), custom_call_target="tpu_custom_call" | custom-call | flops 500000000 | bytes 7000000 | tf_op jit(solution)/shard_map/update_high/pallas_call | solution.py:373
  (25 shorter events, 0.8 us)
Async XLA Ops:
  0.0 1.2 %copy-start.1 = (f32[64,4096]{1,0:T(8,128)S(1)}, f32[64,4096]{1,0:T(8,128)}, u32[]{:S(2)}) copy-start(f32[64,4096]{1,0:T(8,128)} %rhs_ref.1) | copy-start | bytes 3145732
  5.3 2.4 %collective-permute-start = (f32[128,128]{1,0:T(8,128)S(1)}, f32[128,128]{1,0:T(8,128)S(1)}, u32[]{:S(2)}, u32[]{:S(2)}) collective-permute-start(f32[128,128]{1,0:T(8,128)S(1)} %get-tuple-element.34), channel_id=1, source_target_pairs={{0,1},{1,0},{2,3},{3,2},{4,5},{5,4},{6,7},{7,6},{8,9},{9,8},{10,11... | collective-permute-start | bytes 196616 | tf_op jit(solution)/shard_map/ppermute | solution.py:387
  7.7 10.9 %collective-permute-start.1 = (f32[128,128]{1,0:T(8,128)S(1)}, f32[128,128]{1,0:T(8,128)S(1)}, u32[]{:S(2)}, u32[]{:S(2)}) collective-permute-start(f32[128,128]{1,0:T(8,128)S(1)} %add.33.sent_ref), channel_id=1, source_target_pairs={{0,2},{1,3},{2,0},{3,1},{4,6},{5,7},{6,4},{7,5},{8,10},{9,11},{10,... | collective-permute-start | bytes 196616 | tf_op jit(solution)/shard_map/ppermute | solution.py:387
  9.5 9.1 %collective-permute-start.2 = (f32[128,128]{1,0:T(8,128)S(1)}, f32[128,128]{1,0:T(8,128)S(1)}, u32[]{:S(2)}, u32[]{:S(2)}) collective-permute-start(f32[128,128]{1,0:T(8,128)S(1)} %add.33.sent_ref), channel_id=1, source_target_pairs={{0,4},{1,5},{2,6},{3,7},{4,0},{5,1},{6,2},{7,3},{8,12},{9,13},{10,... | collective-permute-start | bytes 196616 | tf_op jit(solution)/shard_map/ppermute | solution.py:387
  12.8 5.8 %collective-permute-start.3 = (f32[128,128]{1,0:T(8,128)S(1)}, f32[128,128]{1,0:T(8,128)S(1)}, u32[]{:S(2)}, u32[]{:S(2)}) collective-permute-start(f32[128,128]{1,0:T(8,128)S(1)} %add.33.sent_ref), channel_id=1, source_target_pairs={{0,6},{1,7},{2,4},{3,5},{4,2},{5,3},{6,0},{7,1},{8,14},{9,15},{10,... | collective-permute-start | bytes 196616 | tf_op jit(solution)/shard_map/ppermute | solution.py:387
  12.8 9.5 %copy-start = (f32[15,256,256]{2,1,0:T(8,128)S(1)}, f32[15,256,256]{2,1,0:T(8,128)}, u32[]{:S(2)}) copy-start(f32[15,256,256]{2,1,0:T(8,128)} %cap_ref.1) | copy-start | bytes 11796484
  18.6 9.4 %collective-permute-start.5 = (f32[128,128]{1,0:T(8,128)S(1)}, f32[128,128]{1,0:T(8,128)S(1)}, u32[]{:S(2)}, u32[]{:S(2)}) collective-permute-start(f32[128,128]{1,0:T(8,128)S(1)} %add_add_fusion.2.sent_ref), channel_id=1, source_target_pairs={{0,16},{1,17},{2,18},{3,19},{4,20},{5,21},{6,22},{7,23},{8,24},{9,... | collective-permute-start | bytes 196616 | tf_op jit(solution)/shard_map/ppermute | solution.py:387
  21.5 6.6 %collective-permute-start.6 = (f32[128,128]{1,0:T(8,128)S(1)}, f32[128,128]{1,0:T(8,128)S(1)}, u32[]{:S(2)}, u32[]{:S(2)}) collective-permute-start(f32[128,128]{1,0:T(8,128)S(1)} %add_add_fusion.2.sent_ref), channel_id=1, source_target_pairs={{0,24},{1,25},{2,26},{3,27},{4,28},{5,29},{6,30},{7,31},{8,16},{9,... | collective-permute-start | bytes 196616 | tf_op jit(solution)/shard_map/ppermute | solution.py:387
  22.3 5.8 %collective-permute-start.4 = (f32[128,128]{1,0:T(8,128)S(1)}, f32[128,128]{1,0:T(8,128)S(1)}, u32[]{:S(2)}, u32[]{:S(2)}) collective-permute-start(f32[128,128]{1,0:T(8,128)S(1)} %add_add_fusion.2.sent_ref), channel_id=1, source_target_pairs={{0,8},{1,9},{2,10},{3,11},{4,12},{5,13},{6,14},{7,15},{8,0},{9,1},... | collective-permute-start | bytes 196616 | tf_op jit(solution)/shard_map/ppermute | solution.py:387
  28.1 2.7 %collective-permute-start.7 = (f32[4,128,128]{2,1,0:T(8,128)S(1)}, f32[4,128,128]{2,1,0:T(8,128)S(1)}, u32[]{:S(2)}, u32[]{:S(2)}) collective-permute-start(f32[4,128,128]{2,1,0:T(8,128)S(1)} %pad_maximum_fusion.mine_ref), channel_id=1, source_target_pairs={{0,1},{1,0},{2,3},{3,2},{4,5},{5,4},{6,7},{7,6},{8,9},{9,8},{10,11... | collective-permute-start | bytes 786440 | tf_op jit(solution)/shard_map/ppermute | solution.py:387
  31.5 1.4 %collective-permute-start.8 = (f32[128,128]{1,0:T(8,128)S(1)}, f32[128,128]{1,0:T(8,128)S(1)}, u32[]{:S(2)}, u32[]{:S(2)}) collective-permute-start(f32[128,128]{1,0:T(8,128)S(1)} %get-tuple-element.50), channel_id=1, source_target_pairs={{0,1},{1,0},{2,3},{3,2},{4,5},{5,4},{6,7},{7,6},{8,9},{9,8},{10,11... | collective-permute-start | bytes 196616 | tf_op jit(solution)/shard_map/ppermute | solution.py:387
  32.9 4.7 %collective-permute-start.10 = (f32[128,128]{1,0:T(8,128)S(1)}, f32[128,128]{1,0:T(8,128)S(1)}, u32[]{:S(2)}, u32[]{:S(2)}) collective-permute-start(f32[128,128]{1,0:T(8,128)S(1)} %add.37.sent_ref), channel_id=1, source_target_pairs={{0,16},{1,5},{2,18},{3,7},{4,20},{5,1},{6,22},{7,3},{8,24},{9,13},... | collective-permute-start | bytes 196616 | tf_op jit(solution)/shard_map/ppermute | solution.py:387
  34.6 4.3 %collective-permute-start.11 = (f32[128,128]{1,0:T(8,128)S(1)}, f32[128,128]{1,0:T(8,128)S(1)}, u32[]{:S(2)}, u32[]{:S(2)}) collective-permute-start(f32[128,128]{1,0:T(8,128)S(1)} %add.37.sent_ref), channel_id=1, source_target_pairs={{0,24},{1,7},{2,26},{3,5},{4,28},{5,3},{6,30},{7,1},{8,16},{9,15},... | collective-permute-start | bytes 196616 | tf_op jit(solution)/shard_map/ppermute | solution.py:387
  36.0 3.1 %collective-permute-start.9 = (f32[128,128]{1,0:T(8,128)S(1)}, f32[128,128]{1,0:T(8,128)S(1)}, u32[]{:S(2)}, u32[]{:S(2)}) collective-permute-start(f32[128,128]{1,0:T(8,128)S(1)} %add.37.sent_ref), channel_id=1, source_target_pairs={{0,8},{1,3},{2,10},{3,1},{4,12},{5,7},{6,14},{7,5},{8,0},{9,11},{1... | collective-permute-start | bytes 196616 | tf_op jit(solution)/shard_map/ppermute | solution.py:387
  39.2 6.5 %collective-permute-start.12 = (f32[128,128]{1,0:T(8,128)S(1)}, f32[128,128]{1,0:T(8,128)S(1)}, u32[]{:S(2)}, u32[]{:S(2)}) collective-permute-start(f32[128,128]{1,0:T(8,128)S(1)} %add_add_fusion.1.sent_ref), channel_id=1, source_target_pairs={{0,2},{1,9},{2,0},{3,11},{4,6},{5,13},{6,4},{7,15},{8,10},{9,1},{1... | collective-permute-start | bytes 196616 | tf_op jit(solution)/shard_map/ppermute | solution.py:387
  41.3 4.6 %collective-permute-start.13 = (f32[128,128]{1,0:T(8,128)S(1)}, f32[128,128]{1,0:T(8,128)S(1)}, u32[]{:S(2)}, u32[]{:S(2)}) collective-permute-start(f32[128,128]{1,0:T(8,128)S(1)} %add_add_fusion.1.sent_ref), channel_id=1, source_target_pairs={{0,4},{1,17},{2,6},{3,19},{4,0},{5,21},{6,2},{7,23},{8,12},{9,25},... | collective-permute-start | bytes 196616 | tf_op jit(solution)/shard_map/ppermute | solution.py:387
  43.1 4.3 %collective-permute-start.14 = (f32[128,128]{1,0:T(8,128)S(1)}, f32[128,128]{1,0:T(8,128)S(1)}, u32[]{:S(2)}, u32[]{:S(2)}) collective-permute-start(f32[128,128]{1,0:T(8,128)S(1)} %add_add_fusion.1.sent_ref), channel_id=1, source_target_pairs={{0,6},{1,25},{2,4},{3,27},{4,2},{5,29},{6,0},{7,31},{8,14},{9,17},... | collective-permute-start | bytes 196616 | tf_op jit(solution)/shard_map/ppermute | solution.py:387
  47.4 4.0 %collective-permute-start.15 = (f32[128,128]{1,0:T(8,128)S(1)}, f32[128,128]{1,0:T(8,128)S(1)}, u32[]{:S(2)}, u32[]{:S(2)}) collective-permute-start(f32[128,128]{1,0:T(8,128)S(1)} %add_add_fusion), channel_id=1, source_target_pairs={{0,32},{1,33},{2,34},{3,35},{4,36},{5,37},{6,38},{7,39},{8,40},{9,... | collective-permute-start | bytes 196616 | tf_op jit(solution)/shard_map/ppermute | solution.py:387
  48.8 5.0 %collective-permute-start.16 = (f32[128,128]{1,0:T(8,128)S(1)}, f32[128,128]{1,0:T(8,128)S(1)}, u32[]{:S(2)}, u32[]{:S(2)}) collective-permute-start(f32[128,128]{1,0:T(8,128)S(1)} %add_add_fusion), channel_id=1, source_target_pairs={{0,64},{1,65},{2,66},{3,67},{4,68},{5,69},{6,70},{7,71},{8,72},{9,... | collective-permute-start | bytes 196616 | tf_op jit(solution)/shard_map/ppermute | solution.py:387
  51.4 4.3 %collective-permute-start.17 = (f32[128,128]{1,0:T(8,128)S(1)}, f32[128,128]{1,0:T(8,128)S(1)}, u32[]{:S(2)}, u32[]{:S(2)}) collective-permute-start(f32[128,128]{1,0:T(8,128)S(1)} %add_add_fusion), channel_id=1, source_target_pairs={{0,96},{1,97},{2,98},{3,99},{4,100},{5,101},{6,102},{7,103},{8,104... | collective-permute-start | bytes 196616 | tf_op jit(solution)/shard_map/ppermute | solution.py:387
  55.8 8.7 %collective-permute-start.18 = (f32[4,128,128]{2,1,0:T(8,128)S(1)}, f32[4,128,128]{2,1,0:T(8,128)S(1)}, u32[]{:S(2)}, u32[]{:S(2)}) collective-permute-start(f32[4,128,128]{2,1,0:T(8,128)S(1)} %pad_maximum_fusion.1.mine_ref), channel_id=1, source_target_pairs={{0,1},{1,0},{2,3},{3,2},{4,5},{5,4},{6,7},{7,6},{8,9},{9,8},{10,11... | collective-permute-start | bytes 786440 | tf_op jit(solution)/shard_map/ppermute | solution.py:387

commit v4 on v3

--- a/solution.py
+++ b/solution.py
@@ -12,7 +12,7 @@
 RANK = 128
 RHS = 64
 DEVICES = 128
-LIMITS = (47, 44, 40, 41, 41, 43, 46)
+LIMITS = (53, 42, 38, 38, 40, 40, 44)
 HBM = pl.BlockSpec(memory_space=pltpu.HBM)
 VMEM = pl.BlockSpec(memory_space=pltpu.VMEM)
 SMEM = pl.BlockSpec(memory_space=pltpu.SMEM)
@@ -83,15 +83,13 @@
         acc[...] += value
 
 
-LATE = (4, 2, 1, 1)
-EARLY = (1, 1, 2, 4)
-
-
-def first_kernel(points, core_ref, rhs_ref, basis_ref, gen_ref, keep_ref, send_ref, held_ref,
-                 v3_buf, v2_buf, acc2, acc3, sems):
-    rhs_buf, u3_buf = held_ref.at[:RHS], held_ref.at[RHS:]
+PARTS = (2, 2, 2, 2)
+
+
+def first_kernel(points, core_ref, rhs_ref, basis_ref, gen_ref, keep_ref, send_ref,
+                 rhs_buf, v3_buf, v2_buf, u3_buf, acc2, acc3, sems):
     sources = ((rhs_ref, None, rhs_buf), (basis_ref, 3, v3_buf), (basis_ref, 2, v2_buf), (gen_ref, 3, u3_buf))
-    for i, (cols, row) in enumerate(fetch(sources, sems, LATE, points)):
+    for i, (cols, row) in enumerate(fetch(sources, sems, PARTS, points)):
         for copy in row:
             copy.wait()
         rhs = stacked([rhs_buf[:, cols]])
@@ -125,14 +123,14 @@
     wide = pltpu.VMEM((RANK, points), F32)
     return pl.pallas_call(
         functools.partial(first_kernel, points),
-        out_shape=(array(RANK, RANK), array(RANK, RANK), array(RHS + RANK, points)),
+        out_shape=(array(RANK, RANK), array(RANK, RANK)),
         in_specs=[SMEM, HBM, HBM, HBM],
-        out_specs=(VMEM,) * 3,
+        out_specs=(VMEM,) * 2,
         scratch_shapes=[
-            wide, wide,
+            pltpu.VMEM((RHS, points), F32), wide, wide, wide,
             pltpu.VMEM((2 * (RHS + RANK), 2 * RANK), F32),
             pltpu.VMEM((2 * RHS, 2 * RANK), F32),
-            pltpu.SemaphoreType.DMA((len(LATE), 4)),
+            pltpu.SemaphoreType.DMA((len(PARTS), 4)),
         ],
         compiler_params=params(LIMITS[0]),
         cost_estimate=pl.CostEstimate(flops=800_000_000, bytes_accessed=7_340_032, transcendentals=0),
@@ -156,43 +154,41 @@
     return copies
 
 
-def grams_kernel(points, held_ref, basis_ref, sent_ref, sent_out, p_ref, g_ref, v1_buf, v0_buf,
-                 acc1, acc0, sems):
-    parts = fetch(((basis_ref, 1, v1_buf), (basis_ref, 0, v0_buf)), sems, EARLY, points)
+def load_kernel(rhs_ref, basis_ref, gen_ref, sent_ref, sent_out, p_ref, v1_ref, v0_ref, u3_ref, u2_ref, sems):
+    sources = ((basis_ref, 1, v1_ref), (basis_ref, 0, v0_ref), (gen_ref, 3, u3_ref), (gen_ref, 2, u2_ref))
+    copies = [pltpu.make_async_copy(ref.at[k], out, sems.at[i]) for i, (ref, k, out) in enumerate(sources)]
+    for copy in copies:
+        copy.start()
     sent_out[...] = sent_ref[...]
-    for i, (cols, row) in enumerate(parts):
-        left = stacked([held_ref[:, cols]])
-        for copy, buffer, acc in zip(row, (v1_buf, v0_buf), (acc1, acc0)):
-            copy.wait()
-            add_to(acc, contract(left, stacked([buffer[:, cols]])), i == 0)
-    for k, acc in enumerate((acc1, acc0)):
-        both = fold(acc[...], RHS + RANK)
-        p_ref[:, k * RANK : (k + 1) * RANK] = both[:RHS]
-        g_ref[:, k * RANK : (k + 1) * RANK] = both[RHS:]
-
-
-def grams_step(held, basis, sent):
-    points = held.shape[1]
-    total = pltpu.VMEM((2 * (RHS + RANK), 2 * RANK), F32)
-    return pl.pallas_call(
-        functools.partial(grams_kernel, points),
-        out_shape=(
-            array(*sent.shape), array(RHS, 2 * RANK), array(RANK, 2 * RANK),
-            array(RANK, points), array(RANK, points),
-        ),
-        in_specs=[VMEM, HBM, VMEM],
-        out_specs=(VMEM,) * 5,
-        scratch_shapes=[total, total, pltpu.SemaphoreType.DMA((len(EARLY), 2))],
+    left = stacked([rhs_ref[...]])
+    copies[0].wait()
+    copies[1].wait()
+    p_ref[:, :RANK] = fold(contract(left, stacked([v1_ref[...]])), RHS)
+    p_ref[:, RANK:] = fold(contract(left, stacked([v0_ref[...]])), RHS)
+    copies[2].wait()
+    copies[3].wait()
+
+
+def load_step(rhs, basis, gen, sent):
+    wide = array(RANK, rhs.shape[1])
+    return pl.pallas_call(
+        load_kernel,
+        out_shape=(array(*sent.shape), array(RHS, 2 * RANK), wide, wide, wide, wide),
+        in_specs=[VMEM, HBM, HBM, VMEM],
+        out_specs=(VMEM,) * 6,
+        scratch_shapes=[pltpu.SemaphoreType.DMA((4,))],
         compiler_params=params(LIMITS[1]),
-        cost_estimate=pl.CostEstimate(flops=1_500_000_000, bytes_accessed=7_340_032, transcendentals=0),
-        name="grams_three",
-    )(held, basis, sent)
-
-
-def rest_kernel(points, place_ref, v1_ref, v0_ref, gen_ref, cap_ref, sent_ref, sent_out,
-                g_ref, g10_ref, c3a_ref, c3b_ref, c2_ref, c1a_ref, c1b_ref, c0_ref, u2_buf, u1_buf,
-                acc1, acc0, acc, sems, cap_sems):
-    parts = fetch(((gen_ref, 2, u2_buf), (gen_ref, 1, u1_buf)), sems, EARLY, points)
+        cost_estimate=pl.CostEstimate(flops=300_000_000, bytes_accessed=9_437_184, transcendentals=0),
+        name="load_project_high",
+    )(rhs, basis, gen, sent)
+
+
+def grams_kernel(place_ref, v1_ref, v0_ref, u3_ref, u2_ref, gen_ref, cap_ref, sent_ref, sent_out,
+                 g_ref, g10_ref, c3a_ref, c3b_ref, c2_ref, c1a_ref, c1b_ref, c0_ref, u1_ref, u0_ref,
+                 sems, cap_sems):
+    copies = [pltpu.make_async_copy(gen_ref.at[k], out, sems.at[k]) for k, out in ((1, u1_ref), (0, u0_ref))]
+    for copy in copies:
+        copy.start()
     sent_out[...] = sent_ref[...]
     s3, s2, s1, s0 = place_ref[0], place_ref[1], place_ref[2], place_ref[3]
     n3, n2, n1 = place_ref[4], place_ref[5], place_ref[6]
@@ -202,45 +198,37 @@
     caps += related(cap_ref, c1a_ref, cap_sems, 1 + n1, s1, 12, 2)
     caps += related(cap_ref, c1b_ref, cap_sems, 1 + (n1 ^ 1), s1, 16, 2)
     caps += related(cap_ref, c0_ref, cap_sems, 0, s0, 20, 1)
-    for i, (cols, row) in enumerate(parts):
-        v1, v0 = stacked([v1_ref[:, cols]]), stacked([v0_ref[:, cols]])
-        row[0].wait()
-        u2 = stacked([u2_buf[:, cols]])
-        add_to(acc1, contract(u2, v1), i == 0)
-        add_to(acc0, contract(u2, v0), i == 0)
-        row[1].wait()
-        add_to(acc, contract(stacked([u1_buf[:, cols]]), v0), i == 0)
-    g_ref[:, :RANK] = fold(acc1[...], RANK)
-    g_ref[:, RANK:] = fold(acc0[...], RANK)
-    g10_ref[...] = fold(acc[...], RANK)
+    v1, v0 = stacked([v1_ref[...]]), stacked([v0_ref[...]])
+    for k, ref in enumerate((u3_ref, u2_ref)):
+        left = stacked([ref[...]])
+        g_ref[k * RANK : (k + 1) * RANK, :RANK] = fold(contract(left, v1), RANK)
+        g_ref[k * RANK : (k + 1) * RANK, RANK:] = fold(contract(left, v0), RANK)
+    copies[0].wait()
+    g10_ref[...] = fold(contract(stacked([u1_ref[...]]), v0), RANK)
     for copy in caps:
         copy.wait()
-
-
-def rest_step(place, v1, v0, gen, cap, sent):
-    points = v1.shape[1]
+    copies[1].wait()
+
+
+def grams_step(place, v1, v0, u3, u2, gen, cap, sent):
+    wide = array(*v1.shape)
     square, column = array(2 * RANK, 2 * RANK), array(2 * RANK, RANK)
-    total = pltpu.VMEM((2 * RANK, 2 * RANK), F32)
-    return pl.pallas_call(
-        functools.partial(rest_kernel, points),
+    return pl.pallas_call(
+        grams_kernel,
         out_shape=(
-            array(*sent.shape), array(RANK, 2 * RANK), array(RANK, RANK),
-            square, square, column, square, square, column, array(RANK, points), array(RANK, points),
+            array(*sent.shape), square, array(RANK, RANK),
+            square, square, column, square, square, column, wide, wide,
         ),
-        in_specs=[SMEM, VMEM, VMEM, HBM, HBM, VMEM],
+        in_specs=[SMEM, VMEM, VMEM, VMEM, VMEM, HBM, HBM, VMEM],
         out_specs=(VMEM,) * 11,
-        scratch_shapes=[
-            total, total, total,
-            pltpu.SemaphoreType.DMA((len(EARLY), 2)),
-            pltpu.SemaphoreType.DMA((24,)),
-        ],
+        scratch_shapes=[pltpu.SemaphoreType.DMA((2,)), pltpu.SemaphoreType.DMA((24,))],
         compiler_params=params(LIMITS[2]),
-        cost_estimate=pl.CostEstimate(flops=1_500_000_000, bytes_accessed=9_437_184, transcendentals=0),
-        name="grams_rest",
-    )(place, v1, v0, gen, cap, sent)
-
-
-def middle_kernel(core_ref, mine_ref, other_ref, c3a_ref, c3b_ref, c2_ref, p_ref, g3_ref, g2_ref, g10_ref,
+        cost_estimate=pl.CostEstimate(flops=2_700_000_000, bytes_accessed=13_000_000, transcendentals=0),
+        name="grams_high",
+    )(place, v1, v0, u3, u2, gen, cap, sent)
+
+
+def middle_kernel(core_ref, mine_ref, other_ref, c3a_ref, c3b_ref, c2_ref, p_ref, g_ref, g10_ref,
                   t_ref, keep_ref, send_ref):
     first = core_ref[0] == 0
     p, g = [], []
@@ -257,7 +245,7 @@
     joined = jnp.concatenate([q2[0] + q2[1], q2[2] + q2[3]], axis=1)
     coeff = jnp.concatenate([t[0], product(joined, c2_ref[...])], axis=1)
     t_ref[...] = coeff
-    q = p_ref[...] - product(coeff, jnp.concatenate([g3_ref[...], g2_ref[...]], axis=0))
+    q = p_ref[...] - product(coeff, g_ref[...])
     half = RHS // 2
 
     def put(ref, c):
@@ -277,64 +265,59 @@
         put(send_ref, 0)
 
 
-def middle_step(core, mine, other, c3a, c3b, c2, p, g3, g2, g10):
+def middle_step(core, mine, other, c3a, c3b, c2, p, g, g10):
     half = jax.ShapeDtypeStruct((RANK, RANK), F32)
     return pl.pallas_call(
         middle_kernel,
         out_shape=(jax.ShapeDtypeStruct((RHS, 2 * RANK), F32), half, half),
-        in_specs=[SMEM] + [VMEM] * 9,
+        in_specs=[SMEM] + [VMEM] * 8,
         out_specs=(VMEM,) * 3,
         compiler_params=params(LIMITS[3]),
         cost_estimate=pl.CostEstimate(flops=120_000_000, bytes_accessed=1_500_000, transcendentals=0),
         name="coefficients_low",
-    )(core, mine, other, c3a, c3b, c2, p, g3, g2, g10)
-
-
-def low_update_kernel(t_ref, held_ref, u2_ref, sent_ref, cur_ref, sent_out):
+    )(core, mine, other, c3a, c3b, c2, p, g, g10)
+
+
+def low_update_kernel(t_ref, rhs_ref, u3_ref, u2_ref, sent_ref, cur_ref, sent_out):
     sent_out[...] = sent_ref[...]
     th, tl = split(t_ref[...])
     left = jnp.concatenate([th, tl], axis=0)
-    for cols in spans((2,) * 4, held_ref.shape[1]):
-        gh, gl = split(jnp.concatenate([held_ref[RHS:, cols], u2_ref[:, cols]], axis=0))
+    for cols in spans((2,) * 4, rhs_ref.shape[1]):
+        gh, gl = split(jnp.concatenate([u3_ref[:, cols], u2_ref[:, cols]], axis=0))
         both = jnp.dot(left, gh, preferred_element_type=F32)
         update = both[:RHS] + both[RHS:] + jnp.dot(th, gl, preferred_element_type=F32)
-        cur_ref[:, cols] = held_ref[:RHS, cols] - update
-
-
-def low_update(t, held, u2, sent):
+        cur_ref[:, cols] = rhs_ref[:, cols] - update
+
+
+def low_update(t, rhs, u3, u2, sent):
     return pl.pallas_call(
         low_update_kernel,
-        out_shape=(array(RHS, held.shape[1]), array(*sent.shape)),
-        in_specs=[VMEM] * 4,
+        out_shape=(array(*rhs.shape), array(*sent.shape)),
+        in_specs=[VMEM] * 5,
         out_specs=(VMEM, VMEM),
         compiler_params=params(LIMITS[4]),
         cost_estimate=pl.CostEstimate(flops=402_653_184, bytes_accessed=6_291_456, transcendentals=0),
         name="update_low",
-    )(t, held, u2, sent)
-
-
-def pairs_kernel(points, u1_ref, gen_ref, sent_ref, sent_out, high_ref, low_ref, u0_buf, sems):
-    parts = fetch(((gen_ref, 0, u0_buf),), sems, (4, 4), points)
+    )(t, rhs, u3, u2, sent)
+
+
+def pairs_kernel(u1_ref, u0_ref, sent_ref, sent_out, high_ref, low_ref):
     sent_out[...] = sent_ref[...]
     high_ref[:RANK], low_ref[:RANK] = split(u1_ref[...])
-    for cols, row in parts:
-        row[0].wait()
-        high_ref[RANK:, cols], low_ref[RANK:, cols] = split(u0_buf[:, cols])
-
-
-def pairs_step(u1, gen, sent):
-    points = u1.shape[1]
-    pair = jax.ShapeDtypeStruct((2 * RANK, points), BF16)
-    return pl.pallas_call(
-        functools.partial(pairs_kernel, points),
+    high_ref[RANK:], low_ref[RANK:] = split(u0_ref[...])
+
+
+def pairs_step(u1, u0, sent):
+    pair = jax.ShapeDtypeStruct((2 * RANK, u1.shape[1]), BF16)
+    return pl.pallas_call(
+        pairs_kernel,
         out_shape=(array(*sent.shape), pair, pair),
-        in_specs=[VMEM, HBM, VMEM],
+        in_specs=[VMEM] * 3,
         out_specs=(VMEM,) * 3,
-        scratch_shapes=[pltpu.VMEM((RANK, points), F32), pltpu.SemaphoreType.DMA((2, 1))],
         compiler_params=params(LIMITS[5]),
         cost_estimate=pl.CostEstimate(flops=100_000_000, bytes_accessed=8_388_608, transcendentals=0),
         name="pairs_high",
-    )(u1, gen, sent)
+    )(u1, u0, sent)
 
 
 def last_kernel(core_ref, mine_ref, other_ref, c1a_ref, c1b_ref, c0_ref, cur_ref, high_ref, low_ref, out_ref,
@@ -399,22 +382,22 @@
         device >> 3 & 1, device >> 4 & 1, device >> 5 & 1, device >> 6 & 1,
         device >> 4, device >> 5, device >> 6,
     ])
-    keep, send, held = first_step(core, rhs, basis, gen)
+    keep, send = first_step(core, rhs, basis, gen)
     chip = keep + swap(send, CORE, CORE)
     _, b, c, d = gathered(chip, Z_MASKS, Z_MASKS)
-    chip, p, g3, v1, v0 = grams_step(held, basis, chip)
+    chip, p, v1, v0, u3, u2 = load_step(rhs, basis, gen, chip)
     line = chip + b + c + d
     _, b, c, d = gathered(line, X_MASKS, X_MASKS)
-    line, g2, g10, c3a, c3b, c2, c1a, c1b, c0, u2, u1 = rest_step(place, v1, v0, gen, cap, line)
+    line, g, g10, c3a, c3b, c2, c1a, c1b, c0, u1, u0 = grams_step(place, v1, v0, u3, u2, gen, cap, line)
     lines = jnp.stack([line, b, c, d])
     other = swap(lines, CORE, CORE)
-    t, keep, send = middle_step(core, lines, other, c3a, c3b, c2, p, g3, g2, g10)
+    t, keep, send = middle_step(core, lines, other, c3a, c3b, c2, p, g, g10)
     chip = keep + swap(send, CORE, CORE)
     _, b, c, d = gathered(chip, X_MASKS, Z_MASKS)
-    current, chip = low_update(t, held, u2, chip)
+    current, chip = low_update(t, rhs, u3, u2, chip)
     part = chip + b + c + d
     _, b, c, d = gathered(part, Z_MASKS, X_MASKS)
-    part, high, low = pairs_step(u1, gen, part)
+    part, high, low = pairs_step(u1, u0, part)
     plane = part + b + c + d
     planes = jnp.stack(gathered(plane, Y_MASKS, Y_MASKS))
     other = swap(planes, CORE, CORE)

time: 66.9 us -> 65 us (0.972)
  Pallas kernels: 21.1 us -> 19.3 us
  waiting for transfers between devices: 11.7 us -> 13.5 us
  local copies, waits for them, and re-layouts: 1.31 us -> 0.09 us
  starting transfers between devices: 32.2 us -> 31.5 us
    ppermute x19, waiting for transfers between devices: 11.7 us -> 13.5 us  [swap(): return lax.ppermute(value, 'leaf', pairs)]
    pallas_call x4, Pallas kernels: 14.2 us -> 12.7 us  [the longest x1 7.13 us: grams_step(): pl.pallas_call(grams_kernel, out_shape=(array(*sent.shape), square, array...]
    unnamed x4 -> x2, local copies, waits for them, and re-layouts: 1.23 us -> 0.01 us
  transfers between devices with their start and end apart: 19 -> 19, of which waited for: 11 -> 11; matrix products, arithmetic and copies ran while one was open for 0% -> 0% of each run, Pallas kernels for 21% -> 20%
where the time goes in v4:
time: 65 us; the launch traced here: 64.9 us
  starting transfers between devices  31.5 us (48%)
  Pallas kernels  19.3 us (30%)
  waiting for transfers between devices  13.5 us (21%)
    ppermute x19, starting transfers between devices, swap(): return lax.ppermute(value, 'leaf', pairs)  31.5 us
    ppermute x19, waiting for transfers between devices, swap(): return lax.ppermute(value, 'leaf', pairs)  13.5 us
    pallas_call x1, Pallas kernels, grams_step(): pl.pallas_call(grams_kernel, out_shape=(array(*sent.shape), square, array...  7.13 us
    pallas_call x1, Pallas kernels, first_step(): pl.pallas_call(functools.partial(first_kernel, points), out_shape=(array(...  3.86 us
    pallas_call x1, Pallas kernels, load_step(): pl.pallas_call(load_kernel, out_shape=(array(*sent.shape), array(RHS, 2 *...  3.83 us
    pallas_call x1, Pallas kernels, last_step(): pl.pallas_call(last_kernel, out_shape=array(*cur.shape), in_specs=[SMEM]...  2.11 us
  transfers between devices with their start and end apart: 19, of which 11 were waited for; matrix products, arithmetic and copies ran while one was open for 0% of the time, Pallas kernels for 20%

profile of v4, /device:TPU:1, one launch (start us, length us, event | category | flops | bytes accessed | tf_op | source)
XLA Modules:
  0.0 64.9 jit_solution(6504108661444638746)
XLA Ops:
  0.0 3.9 %project_low.1 = (f32[128,128]{1,0:T(8,128)S(1)}, f32[128,128]{1,0:T(8,128)S(1)}) custom-call(s32[1]{0:T(128)} %bitcast.core_ref, f32[64,4096]{1,0:T(8,128)} %rhs_ref.5, f32[4,128,4096]{2,1,0:T(8,128)} %basis_ref.3, f32[4,128,4096]{2,1,0:T(8,128)} %gen_ref.5), custom_call_target="tpu_custom_call" | custom-call | flops 800000000 | bytes 7340032 | tf_op jit(solution)/shard_map/project_low/pallas_call | solution.py:124
  3.9 1.5 %collective-permute-start = (f32[128,128]{1,0:T(8,128)S(1)}, f32[128,128]{1,0:T(8,128)S(1)}, u32[]{:S(2)}, u32[]{:S(2)}) collective-permute-start(f32[128,128]{1,0:T(8,128)S(1)} %get-tuple-element.33), channel_id=1, source_target_pairs={{0,1},{1,0},{2,3},{3,2},{4,5},{5,4},{6,7},{7,6},{8,9},{9,8},{10,11... | collective-permute-start | bytes 196616 | tf_op jit(solution)/shard_map/ppermute | solution.py:370
  5.4 0.9 %collective-permute-done = f32[128,128]{1,0:T(8,128)S(1)} collective-permute-done((f32[128,128]{1,0:T(8,128)S(1)}, f32[128,128]{1,0:T(8,128)S(1)}, u32[]{:S(2)}, u32[]{:S(2)}) %collective-permute-start) | collective-permute-done | bytes 65568 | tf_op jit(solution)/shard_map/ppermute | solution.py:370
  6.3 1.8 %collective-permute-start.1 = (f32[128,128]{1,0:T(8,128)S(1)}, f32[128,128]{1,0:T(8,128)S(1)}, u32[]{:S(2)}, u32[]{:S(2)}) collective-permute-start(f32[128,128]{1,0:T(8,128)S(1)} %add.33.sent_ref), channel_id=1, source_target_pairs={{0,2},{1,3},{2,0},{3,1},{4,6},{5,7},{6,4},{7,5},{8,10},{9,11},{10,... | collective-permute-start | bytes 196616 | tf_op jit(solution)/shard_map/ppermute | solution.py:370
  8.1 3.3 %collective-permute-start.2 = (f32[128,128]{1,0:T(8,128)S(1)}, f32[128,128]{1,0:T(8,128)S(1)}, u32[]{:S(2)}, u32[]{:S(2)}) collective-permute-start(f32[128,128]{1,0:T(8,128)S(1)} %add.33.sent_ref), channel_id=1, source_target_pairs={{0,4},{1,5},{2,6},{3,7},{4,0},{5,1},{6,2},{7,3},{8,12},{9,13},{10,... | collective-permute-start | bytes 196616 | tf_op jit(solution)/shard_map/ppermute | solution.py:370
  11.5 3.8 %load_project_high.1 = (f32[128,128]{1,0:T(8,128)S(1)}, f32[64,256]{1,0:T(8,128)S(1)}, f32[128,4096]{1,0:T(8,128)S(1)}, f32[128,4096]{1,0:T(8,128)S(1)}, f32[128...) custom-call(f32[64,4096]{1,0:T(8,128)S(1)} %copy-done, f32[4,128,4096]{2,1,0:T(8,128)} %basis_ref.3, f32[4,128,4096]{2,1,0:T(8,128)} %gen_ref.5, ...), custom_call_target="tpu_custom_call" | custom-call | flops 300000000 | bytes 9437184 | tf_op jit(solution)/shard_map/load_project_high/pallas_call | solution.py:174
  15.3 0.5 collective-permute-done.3
  15.9 2.8 %collective-permute-start.5 = (f32[128,128]{1,0:T(8,128)S(1)}, f32[128,128]{1,0:T(8,128)S(1)}, u32[]{:S(2)}, u32[]{:S(2)}) collective-permute-start(f32[128,128]{1,0:T(8,128)S(1)} %add_add_fusion.2.sent_ref), channel_id=1, source_target_pairs={{0,16},{1,17},{2,18},{3,19},{4,20},{5,21},{6,22},{7,23},{8,24},{9,... | collective-permute-start | bytes 196616 | tf_op jit(solution)/shard_map/ppermute | solution.py:370
  18.7 0.9 %collective-permute-start.6 = (f32[128,128]{1,0:T(8,128)S(1)}, f32[128,128]{1,0:T(8,128)S(1)}, u32[]{:S(2)}, u32[]{:S(2)}) collective-permute-start(f32[128,128]{1,0:T(8,128)S(1)} %add_add_fusion.2.sent_ref), channel_id=1, source_target_pairs={{0,24},{1,25},{2,26},{3,27},{4,28},{5,29},{6,30},{7,31},{8,16},{9,... | collective-permute-start | bytes 196616 | tf_op jit(solution)/shard_map/ppermute | solution.py:370
  19.5 7.1 %grams_high.1 = (f32[128,128]{1,0:T(8,128)S(1)}, f32[256,256]{1,0:T(8,128)S(1)}, f32[128,128]{1,0:T(8,128)S(1)}, f32[256,256]{1,0:T(8,128)S(1)}, f32[256,256]{1,...) custom-call(s32[7]{0:T(128)S(1)} %stack.61.place_ref, ...), custom_call_target="tpu_custom_call" | custom-call | flops 2700000000 | bytes 13000000 | tf_op jit(solution)/shard_map/grams_high/pallas_call | solution.py:216
  26.7 2.6 %collective-permute-start.7 = (f32[4,128,128]{2,1,0:T(8,128)S(1)}, f32[4,128,128]{2,1,0:T(8,128)S(1)}, u32[]{:S(2)}, u32[]{:S(2)}) collective-permute-start(f32[4,128,128]{2,1,0:T(8,128)S(1)} %pad_maximum_fusion.mine_ref), channel_id=1, source_target_pairs={{0,1},{1,0},{2,3},{3,2},{4,5},{5,4},{6,7},{7,6},{8,9},{9,8},{10,11... | collective-permute-start | bytes 786440 | tf_op jit(solution)/shard_map/ppermute | solution.py:370
  29.3 1.2 %collective-permute-done.7.other_ref = f32[4,128,128]{2,1,0:T(8,128)S(1)} collective-permute-done((f32[4,128,128]{2,1,0:T(8,128)S(1)}, f32[4,128,128]{2,1,0:T(8,128)S(1)}, u32[]{:S(2)}, u32[]{:S(2)}) %collective-permute-start.7) | collective-permute-done | bytes 262176 | tf_op jit(solution)/shard_map/ppermute | solution.py:370
  30.5 0.7 %coefficients_low.1 = (f32[64,256]{1,0:T(8,128)S(1)}, f32[128,128]{1,0:T(8,128)S(1)}, f32[128,128]{1,0:T(8,128)S(1)}) custom-call(s32[1]{0:T(128)} %bitcast.core_ref, f32[4,128,128]{2,1,0:T(8,128)S(1)} %pad_maximum_fusion.mine_ref, f32[4,128,128]{2,1,0:T(8,128)S(1)} %collective-permute-done.7.other_ref, f32[256,256]{1,0:T(8,128)S(1)} %get-tuple-element.42.c3a_ref, ...), custom_call_target="tpu_custom_call" | custom-call | flops 120000000 | bytes 1500000 | tf_op jit(solution)/shard_map/coefficients_low/pallas_call | solution.py:270
  31.6 0.9 %collective-permute-done.8 = f32[128,128]{1,0:T(8,128)S(1)} collective-permute-done((f32[128,128]{1,0:T(8,128)S(1)}, f32[128,128]{1,0:T(8,128)S(1)}, u32[]{:S(2)}, u32[]{:S(2)}) %collective-permute-start.8) | collective-permute-done | bytes 65568 | tf_op jit(solution)/shard_map/ppermute | solution.py:370
  32.7 1.5 %collective-permute-start.11 = (f32[128,128]{1,0:T(8,128)S(1)}, f32[128,128]{1,0:T(8,128)S(1)}, u32[]{:S(2)}, u32[]{:S(2)}) collective-permute-start(f32[128,128]{1,0:T(8,128)S(1)} %add.37.sent_ref), channel_id=1, source_target_pairs={{0,24},{1,7},{2,26},{3,5},{4,28},{5,3},{6,30},{7,1},{8,16},{9,15},... | collective-permute-start | bytes 196616 | tf_op jit(solution)/shard_map/ppermute | solution.py:370
  34.2 1.1 %collective-permute-start.9 = (f32[128,128]{1,0:T(8,128)S(1)}, f32[128,128]{1,0:T(8,128)S(1)}, u32[]{:S(2)}, u32[]{:S(2)}) collective-permute-start(f32[128,128]{1,0:T(8,128)S(1)} %add.37.sent_ref), channel_id=1, source_target_pairs={{0,8},{1,3},{2,10},{3,1},{4,12},{5,7},{6,14},{7,5},{8,0},{9,11},{1... | collective-permute-start | bytes 196616 | tf_op jit(solution)/shard_map/ppermute | solution.py:370
  35.3 1.1 %update_low.1 = (f32[64,4096]{1,0:T(8,128)S(1)}, f32[128,128]{1,0:T(8,128)S(1)}) custom-call(f32[64,256]{1,0:T(8,128)S(1)} %get-tuple-element.48.t_ref, f32[64,4096]{1,0:T(8,128)S(1)} %copy-done, f32[128,4096]{1,0:T(8,128)S(1)} %get-tuple-element.36.u3_ref, f32[128,4096]{1,0:T(8,128)S(1)} %get-tuple-element.37.u2_ref, f32[128,128]{1,0:T(8,128)S(1)} %add.37.sent_ref), custom_call_target="tpu_custom_call" | custom-call | flops 402653184 | bytes 6291456 | tf_op jit(solution)/shard_map/update_low/pallas_call | solution.py:293
  36.4 1.0 %collective-permute-done.10 = f32[128,128]{1,0:T(8,128)S(1)} collective-permute-done((f32[128,128]{1,0:T(8,128)S(1)}, f32[128,128]{1,0:T(8,128)S(1)}, u32[]{:S(2)}, u32[]{:S(2)}) %collective-permute-start.10) | collective-permute-done | bytes 65568 | tf_op jit(solution)/shard_map/ppermute | solution.py:370
  37.4 0.7 %collective-permute-done.11 = f32[128,128]{1,0:T(8,128)S(1)} collective-permute-done((f32[128,128]{1,0:T(8,128)S(1)}, f32[128,128]{1,0:T(8,128)S(1)}, u32[]{:S(2)}, u32[]{:S(2)}) %collective-permute-start.11) | collective-permute-done | bytes 65568 | tf_op jit(solution)/shard_map/ppermute | solution.py:370
  38.1 1.7 %collective-permute-start.12 = (f32[128,128]{1,0:T(8,128)S(1)}, f32[128,128]{1,0:T(8,128)S(1)}, u32[]{:S(2)}, u32[]{:S(2)}) collective-permute-start(f32[128,128]{1,0:T(8,128)S(1)} %add_add_fusion.1.sent_ref), channel_id=1, source_target_pairs={{0,2},{1,9},{2,0},{3,11},{4,6},{5,13},{6,4},{7,15},{8,10},{9,1},{1... | collective-permute-start | bytes 196616 | tf_op jit(solution)/shard_map/ppermute | solution.py:370
  39.7 1.6 %collective-permute-start.13 = (f32[128,128]{1,0:T(8,128)S(1)}, f32[128,128]{1,0:T(8,128)S(1)}, u32[]{:S(2)}, u32[]{:S(2)}) collective-permute-start(f32[128,128]{1,0:T(8,128)S(1)} %add_add_fusion.1.sent_ref), channel_id=1, source_target_pairs={{0,4},{1,17},{2,6},{3,19},{4,0},{5,21},{6,2},{7,23},{8,12},{9,25},... | collective-permute-start | bytes 196616 | tf_op jit(solution)/shard_map/ppermute | solution.py:370
  41.4 0.9 %collective-permute-start.14 = (f32[128,128]{1,0:T(8,128)S(1)}, f32[128,128]{1,0:T(8,128)S(1)}, u32[]{:S(2)}, u32[]{:S(2)}) collective-permute-start(f32[128,128]{1,0:T(8,128)S(1)} %add_add_fusion.1.sent_ref), channel_id=1, source_target_pairs={{0,6},{1,25},{2,4},{3,27},{4,2},{5,29},{6,0},{7,31},{8,14},{9,17},... | collective-permute-start | bytes 196616 | tf_op jit(solution)/shard_map/ppermute | solution.py:370
  42.2 0.6 pairs_high.1
  42.9 1.5 %collective-permute-done.13 = f32[128,128]{1,0:T(8,128)S(1)} collective-permute-done((f32[128,128]{1,0:T(8,128)S(1)}, f32[128,128]{1,0:T(8,128)S(1)}, u32[]{:S(2)}, u32[]{:S(2)}) %collective-permute-start.13) | collective-permute-done | bytes 65568 | tf_op jit(solution)/shard_map/ppermute | solution.py:370
  44.4 1.3 %collective-permute-done.14 = f32[128,128]{1,0:T(8,128)S(1)} collective-permute-done((f32[128,128]{1,0:T(8,128)S(1)}, f32[128,128]{1,0:T(8,128)S(1)}, u32[]{:S(2)}, u32[]{:S(2)}) %collective-permute-start.14) | collective-permute-done | bytes 65568 | tf_op jit(solution)/shard_map/ppermute | solution.py:370
  45.7 1.4 %collective-permute-start.15 = (f32[128,128]{1,0:T(8,128)S(1)}, f32[128,128]{1,0:T(8,128)S(1)}, u32[]{:S(2)}, u32[]{:S(2)}) collective-permute-start(f32[128,128]{1,0:T(8,128)S(1)} %add_add_fusion), channel_id=1, source_target_pairs={{0,32},{1,33},{2,34},{3,35},{4,36},{5,37},{6,38},{7,39},{8,40},{9,... | collective-permute-start | bytes 196616 | tf_op jit(solution)/shard_map/ppermute | solution.py:370
  47.1 2.6 %collective-permute-start.16 = (f32[128,128]{1,0:T(8,128)S(1)}, f32[128,128]{1,0:T(8,128)S(1)}, u32[]{:S(2)}, u32[]{:S(2)}) collective-permute-start(f32[128,128]{1,0:T(8,128)S(1)} %add_add_fusion), channel_id=1, source_target_pairs={{0,64},{1,65},{2,66},{3,67},{4,68},{5,69},{6,70},{7,71},{8,72},{9,... | collective-permute-start | bytes 196616 | tf_op jit(solution)/shard_map/ppermute | solution.py:370
  49.7 2.3 %collective-permute-done.16 = f32[128,128]{1,0:T(8,128)S(1)} collective-permute-done((f32[128,128]{1,0:T(8,128)S(1)}, f32[128,128]{1,0:T(8,128)S(1)}, u32[]{:S(2)}, u32[]{:S(2)}) %collective-permute-start.16) | collective-permute-done | bytes 65568 | tf_op jit(solution)/shard_map/ppermute | solution.py:370
  52.1 2.0 %collective-permute-done.17 = f32[128,128]{1,0:T(8,128)S(1)} collective-permute-done((f32[128,128]{1,0:T(8,128)S(1)}, f32[128,128]{1,0:T(8,128)S(1)}, u32[]{:S(2)}, u32[]{:S(2)}) %collective-permute-start.17) | collective-permute-done | bytes 65568 | tf_op jit(solution)/shard_map/ppermute | solution.py:370
  54.1 7.4 %collective-permute-start.18 = (f32[4,128,128]{2,1,0:T(8,128)S(1)}, f32[4,128,128]{2,1,0:T(8,128)S(1)}, u32[]{:S(2)}, u32[]{:S(2)}) collective-permute-start(f32[4,128,128]{2,1,0:T(8,128)S(1)} %pad_maximum_fusion.1.mine_ref), channel_id=1, source_target_pairs={{0,1},{1,0},{2,3},{3,2},{4,5},{5,4},{6,7},{7,6},{8,9},{9,8},{10,11... | collective-permute-start | bytes 786440 | tf_op jit(solution)/shard_map/ppermute | solution.py:370
  61.4 1.2 %collective-permute-done.18.other_ref = f32[4,128,128]{2,1,0:T(8,128)S(1)} collective-permute-done((f32[4,128,128]{2,1,0:T(8,128)S(1)}, f32[4,128,128]{2,1,0:T(8,128)S(1)}, u32[]{:S(2)}, u32[]{:S(2)}) %collective-permute-start.18) | collective-permute-done | bytes 262176 | tf_op jit(solution)/shard_map/ppermute | solution.py:370
  62.6 2.1 %update_high.1 = f32[64,4096]{1,0:T(8,128)} custom-call(s32[1]{0:T(128)} %bitcast.core_ref, f32[4,128,128]{2,1,0:T(8,128)S(1)} %pad_maximum_fusion.1.mine_ref, f32[4,128,128]{2,1,0:T(8,128)S(1)} %collective-permute-done.18.other_ref, f32[256,256]{1,0:T(8,128)S(1)} %get-tuple-element.53.c1a_ref, f32[256,256]{1,0:T(8,128)S(1)} %get-tuple-element.54.c1b_ref, ...), custom_call_target="tpu_custom_call" | custom-call | flops 500000000 | bytes 7000000 | tf_op jit(solution)/shard_map/update_high/pallas_call | solution.py:356
  (23 shorter events, 0.8 us)
Async XLA Ops:
  0.0 11.5 %copy-start = (f32[64,4096]{1,0:T(8,128)S(1)}, f32[64,4096]{1,0:T(8,128)}, u32[]{:S(2)}) copy-start(f32[64,4096]{1,0:T(8,128)} %rhs_ref.5) | copy-start | bytes 3145732
  3.9 2.4 %collective-permute-start = (f32[128,128]{1,0:T(8,128)S(1)}, f32[128,128]{1,0:T(8,128)S(1)}, u32[]{:S(2)}, u32[]{:S(2)}) collective-permute-start(f32[128,128]{1,0:T(8,128)S(1)} %get-tuple-element.33), channel_id=1, source_target_pairs={{0,1},{1,0},{2,3},{3,2},{4,5},{5,4},{6,7},{7,6},{8,9},{9,8},{10,11... | collective-permute-start | bytes 196616 | tf_op jit(solution)/shard_map/ppermute | solution.py:370
  6.3 9.0 %collective-permute-start.1 = (f32[128,128]{1,0:T(8,128)S(1)}, f32[128,128]{1,0:T(8,128)S(1)}, u32[]{:S(2)}, u32[]{:S(2)}) collective-permute-start(f32[128,128]{1,0:T(8,128)S(1)} %add.33.sent_ref), channel_id=1, source_target_pairs={{0,2},{1,3},{2,0},{3,1},{4,6},{5,7},{6,4},{7,5},{8,10},{9,11},{10,... | collective-permute-start | bytes 196616 | tf_op jit(solution)/shard_map/ppermute | solution.py:370
  8.1 7.2 %collective-permute-start.2 = (f32[128,128]{1,0:T(8,128)S(1)}, f32[128,128]{1,0:T(8,128)S(1)}, u32[]{:S(2)}, u32[]{:S(2)}) collective-permute-start(f32[128,128]{1,0:T(8,128)S(1)} %add.33.sent_ref), channel_id=1, source_target_pairs={{0,4},{1,5},{2,6},{3,7},{4,0},{5,1},{6,2},{7,3},{8,12},{9,13},{10,... | collective-permute-start | bytes 196616 | tf_op jit(solution)/shard_map/ppermute | solution.py:370
  11.4 4.5 %collective-permute-start.3 = (f32[128,128]{1,0:T(8,128)S(1)}, f32[128,128]{1,0:T(8,128)S(1)}, u32[]{:S(2)}, u32[]{:S(2)}) collective-permute-start(f32[128,128]{1,0:T(8,128)S(1)} %add.33.sent_ref), channel_id=1, source_target_pairs={{0,6},{1,7},{2,4},{3,5},{4,2},{5,3},{6,0},{7,1},{8,14},{9,15},{10,... | collective-permute-start | bytes 196616 | tf_op jit(solution)/shard_map/ppermute | solution.py:370
  15.9 10.8 %collective-permute-start.5 = (f32[128,128]{1,0:T(8,128)S(1)}, f32[128,128]{1,0:T(8,128)S(1)}, u32[]{:S(2)}, u32[]{:S(2)}) collective-permute-start(f32[128,128]{1,0:T(8,128)S(1)} %add_add_fusion.2.sent_ref), channel_id=1, source_target_pairs={{0,16},{1,17},{2,18},{3,19},{4,20},{5,21},{6,22},{7,23},{8,24},{9,... | collective-permute-start | bytes 196616 | tf_op jit(solution)/shard_map/ppermute | solution.py:370
  18.7 8.0 %collective-permute-start.6 = (f32[128,128]{1,0:T(8,128)S(1)}, f32[128,128]{1,0:T(8,128)S(1)}, u32[]{:S(2)}, u32[]{:S(2)}) collective-permute-start(f32[128,128]{1,0:T(8,128)S(1)} %add_add_fusion.2.sent_ref), channel_id=1, source_target_pairs={{0,24},{1,25},{2,26},{3,27},{4,28},{5,29},{6,30},{7,31},{8,16},{9,... | collective-permute-start | bytes 196616 | tf_op jit(solution)/shard_map/ppermute | solution.py:370
  19.5 7.2 %collective-permute-start.4 = (f32[128,128]{1,0:T(8,128)S(1)}, f32[128,128]{1,0:T(8,128)S(1)}, u32[]{:S(2)}, u32[]{:S(2)}) collective-permute-start(f32[128,128]{1,0:T(8,128)S(1)} %add_add_fusion.2.sent_ref), channel_id=1, source_target_pairs={{0,8},{1,9},{2,10},{3,11},{4,12},{5,13},{6,14},{7,15},{8,0},{9,1},... | collective-permute-start | bytes 196616 | tf_op jit(solution)/shard_map/ppermute | solution.py:370
  26.7 3.7 %collective-permute-start.7 = (f32[4,128,128]{2,1,0:T(8,128)S(1)}, f32[4,128,128]{2,1,0:T(8,128)S(1)}, u32[]{:S(2)}, u32[]{:S(2)}) collective-permute-start(f32[4,128,128]{2,1,0:T(8,128)S(1)} %pad_maximum_fusion.mine_ref), channel_id=1, source_target_pairs={{0,1},{1,0},{2,3},{3,2},{4,5},{5,4},{6,7},{7,6},{8,9},{9,8},{10,11... | collective-permute-start | bytes 786440 | tf_op jit(solution)/shard_map/ppermute | solution.py:370
  31.2 1.3 %collective-permute-start.8 = (f32[128,128]{1,0:T(8,128)S(1)}, f32[128,128]{1,0:T(8,128)S(1)}, u32[]{:S(2)}, u32[]{:S(2)}) collective-permute-start(f32[128,128]{1,0:T(8,128)S(1)} %get-tuple-element.50), channel_id=1, source_target_pairs={{0,1},{1,0},{2,3},{3,2},{4,5},{5,4},{6,7},{7,6},{8,9},{9,8},{10,11... | collective-permute-start | bytes 196616 | tf_op jit(solution)/shard_map/ppermute | solution.py:370
  32.6 4.8 %collective-permute-start.10 = (f32[128,128]{1,0:T(8,128)S(1)}, f32[128,128]{1,0:T(8,128)S(1)}, u32[]{:S(2)}, u32[]{:S(2)}) collective-permute-start(f32[128,128]{1,0:T(8,128)S(1)} %add.37.sent_ref), channel_id=1, source_target_pairs={{0,16},{1,5},{2,18},{3,7},{4,20},{5,1},{6,22},{7,3},{8,24},{9,13},... | collective-permute-start | bytes 196616 | tf_op jit(solution)/shard_map/ppermute | solution.py:370
  32.7 5.3 %collective-permute-start.11 = (f32[128,128]{1,0:T(8,128)S(1)}, f32[128,128]{1,0:T(8,128)S(1)}, u32[]{:S(2)}, u32[]{:S(2)}) collective-permute-start(f32[128,128]{1,0:T(8,128)S(1)} %add.37.sent_ref), channel_id=1, source_target_pairs={{0,24},{1,7},{2,26},{3,5},{4,28},{5,3},{6,30},{7,1},{8,16},{9,15},... | collective-permute-start | bytes 196616 | tf_op jit(solution)/shard_map/ppermute | solution.py:370
  34.2 3.9 %collective-permute-start.9 = (f32[128,128]{1,0:T(8,128)S(1)}, f32[128,128]{1,0:T(8,128)S(1)}, u32[]{:S(2)}, u32[]{:S(2)}) collective-permute-start(f32[128,128]{1,0:T(8,128)S(1)} %add.37.sent_ref), channel_id=1, source_target_pairs={{0,8},{1,3},{2,10},{3,1},{4,12},{5,7},{6,14},{7,5},{8,0},{9,11},{1... | collective-permute-start | bytes 196616 | tf_op jit(solution)/shard_map/ppermute | solution.py:370
  38.1 4.8 %collective-permute-start.12 = (f32[128,128]{1,0:T(8,128)S(1)}, f32[128,128]{1,0:T(8,128)S(1)}, u32[]{:S(2)}, u32[]{:S(2)}) collective-permute-start(f32[128,128]{1,0:T(8,128)S(1)} %add_add_fusion.1.sent_ref), channel_id=1, source_target_pairs={{0,2},{1,9},{2,0},{3,11},{4,6},{5,13},{6,4},{7,15},{8,10},{9,1},{1... | collective-permute-start | bytes 196616 | tf_op jit(solution)/shard_map/ppermute | solution.py:370
  39.7 4.6 %collective-permute-start.13 = (f32[128,128]{1,0:T(8,128)S(1)}, f32[128,128]{1,0:T(8,128)S(1)}, u32[]{:S(2)}, u32[]{:S(2)}) collective-permute-start(f32[128,128]{1,0:T(8,128)S(1)} %add_add_fusion.1.sent_ref), channel_id=1, source_target_pairs={{0,4},{1,17},{2,6},{3,19},{4,0},{5,21},{6,2},{7,23},{8,12},{9,25},... | collective-permute-start | bytes 196616 | tf_op jit(solution)/shard_map/ppermute | solution.py:370
  41.4 4.3 %collective-permute-start.14 = (f32[128,128]{1,0:T(8,128)S(1)}, f32[128,128]{1,0:T(8,128)S(1)}, u32[]{:S(2)}, u32[]{:S(2)}) collective-permute-start(f32[128,128]{1,0:T(8,128)S(1)} %add_add_fusion.1.sent_ref), channel_id=1, source_target_pairs={{0,6},{1,25},{2,4},{3,27},{4,2},{5,29},{6,0},{7,31},{8,14},{9,17},... | collective-permute-start | bytes 196616 | tf_op jit(solution)/shard_map/ppermute | solution.py:370
  45.7 4.0 %collective-permute-start.15 = (f32[128,128]{1,0:T(8,128)S(1)}, f32[128,128]{1,0:T(8,128)S(1)}, u32[]{:S(2)}, u32[]{:S(2)}) collective-permute-start(f32[128,128]{1,0:T(8,128)S(1)} %add_add_fusion), channel_id=1, source_target_pairs={{0,32},{1,33},{2,34},{3,35},{4,36},{5,37},{6,38},{7,39},{8,40},{9,... | collective-permute-start | bytes 196616 | tf_op jit(solution)/shard_map/ppermute | solution.py:370
  47.1 5.0 %collective-permute-start.16 = (f32[128,128]{1,0:T(8,128)S(1)}, f32[128,128]{1,0:T(8,128)S(1)}, u32[]{:S(2)}, u32[]{:S(2)}) collective-permute-start(f32[128,128]{1,0:T(8,128)S(1)} %add_add_fusion), channel_id=1, source_target_pairs={{0,64},{1,65},{2,66},{3,67},{4,68},{5,69},{6,70},{7,71},{8,72},{9,... | collective-permute-start | bytes 196616 | tf_op jit(solution)/shard_map/ppermute | solution.py:370
  49.7 4.3 %collective-permute-start.17 = (f32[128,128]{1,0:T(8,128)S(1)}, f32[128,128]{1,0:T(8,128)S(1)}, u32[]{:S(2)}, u32[]{:S(2)}) collective-permute-start(f32[128,128]{1,0:T(8,128)S(1)} %add_add_fusion), channel_id=1, source_target_pairs={{0,96},{1,97},{2,98},{3,99},{4,100},{5,101},{6,102},{7,103},{8,104... | collective-permute-start | bytes 196616 | tf_op jit(solution)/shard_map/ppermute | solution.py:370
  54.1 8.5 %collective-permute-start.18 = (f32[4,128,128]{2,1,0:T(8,128)S(1)}, f32[4,128,128]{2,1,0:T(8,128)S(1)}, u32[]{:S(2)}, u32[]{:S(2)}) collective-permute-start(f32[4,128,128]{2,1,0:T(8,128)S(1)} %pad_maximum_fusion.1.mine_ref), channel_id=1, source_target_pairs={{0,1},{1,0},{2,3},{3,2},{4,5},{5,4},{6,7},{7,6},{8,9},{9,8},{10,11... | collective-permute-start | bytes 786440 | tf_op jit(solution)/shard_map/ppermute | solution.py:370

commit v5 on v4

v5 whole, which is shorter than its diff:
```python
import functools

import jax
import jax.numpy as jnp
from jax import lax
from jax.experimental import pallas as pl
from jax.experimental.pallas import tpu as pltpu
from jax.sharding import PartitionSpec as P

F32 = jnp.float32
BF16 = jnp.bfloat16
RANK = 128
RHS = 64
DEVICES = 128
LIMITS = (53, 40, 38, 38, 40, 40, 44, 50)
HBM = pl.BlockSpec(memory_space=pltpu.HBM)
VMEM = pl.BlockSpec(memory_space=pltpu.VMEM)
SMEM = pl.BlockSpec(memory_space=pltpu.SMEM)

CORE = 1
Z_MASKS = (6, 4, 2)
X_MASKS = (24, 16, 8)
Y_MASKS = (96, 64, 32)


def split(value):
    high = value.astype(BF16)
    return high, (value - high.astype(F32)).astype(BF16)


def stacked(values):
    parts = [split(v) for v in values]
    return jnp.concatenate([h for h, _ in parts] + [l for _, l in parts], axis=0)


def product(left, right):
    lh, ll = split(left)
    rh, rl = split(right)
    rows = left.shape[0]
    both = jnp.dot(jnp.concatenate([lh, ll], axis=0), rh, preferred_element_type=F32)
    return both[:rows] + both[rows:] + jnp.dot(lh, rl, preferred_element_type=F32)


def contract(left, right):
    return lax.dot_general(left, right, (((1,), (1,)), ((), ())), preferred_element_type=F32)


def fold(total, rows):
    half = total.shape[1] // 2
    wide = total[:rows] + total[rows:]
    return wide[:, :half] + wide[:, half:]


def params(limit):
    return pltpu.CompilerParams(vmem_limit_bytes=limit << 20)


def spans(sizes, points):
    at = 0
    for size in sizes:
        yield pl.ds(at * points // 8, size * points // 8)
        at += size


def fetch(sources, sems, sizes, points):
    parts = []
    for i, cols in enumerate(spans(sizes, points)):
        row = []
        for j, (ref, level, buffer) in enumerate(sources):
            src = ref.at[:, cols] if level is None else ref.at[level, :, cols]
            row.append(pltpu.make_async_copy(src, buffer.at[:, cols], sems.at[i, j]))
        parts.append((cols, row))
    for _, row in parts:
        for copy in row:
            copy.start()
    return parts


def add_to(acc, value, first):
    if first:
        acc[...] = value
    else:
        acc[...] += value


PARTS = (2, 2, 2, 2)


def first_kernel(points, core_ref, rhs_ref, basis_ref, gen_ref, keep_ref, send_ref,
                 rhs_buf, v3_buf, v2_buf, u3_buf, acc2, acc3, sems):
    sources = ((rhs_ref, None, rhs_buf), (basis_ref, 3, v3_buf), (basis_ref, 2, v2_buf), (gen_ref, 3, u3_buf))
    for i, (cols, row) in enumerate(fetch(sources, sems, PARTS, points)):
        for copy in row:
            copy.wait()
        rhs = stacked([rhs_buf[:, cols]])
        left = jnp.concatenate([rhs, stacked([u3_buf[:, cols]])], axis=0)
        add_to(acc2, contract(left, stacked([v2_buf[:, cols]])), i == 0)
        add_to(acc3, contract(rhs, stacked([v3_buf[:, cols]])), i == 0)
    p3 = fold(acc3[...], RHS)
    p2 = fold(acc2[: 2 * RHS], RHS)
    g32 = fold(acc2[2 * RHS :], RANK)
    first = core_ref[0] == 0

    @pl.when(first)
    def _():
        keep_ref[:RHS] = p3
        keep_ref[RHS:] = p2
        send_ref[...] = g32

    @pl.when(jnp.logical_not(first))
    def _():
        send_ref[:RHS] = p3
        send_ref[RHS:] = p2
        keep_ref[...] = g32


def array(*shape):
    return jax.ShapeDtypeStruct(shape, F32)


def first_step(core, rhs, basis, gen):
    points = rhs.shape[1]
    wide = pltpu.VMEM((RANK, points), F32)
    return pl.pallas_call(
        functools.partial(first_kernel, points),
        out_shape=(array(RANK, RANK), array(RANK, RANK)),
        in_specs=[SMEM, HBM, HBM, HBM],
        out_specs=(VMEM,) * 2,
        scratch_shapes=[
            pltpu.VMEM((RHS, points), F32), wide, wide, wide,
            pltpu.VMEM((2 * (RHS + RANK), 2 * RANK), F32),
            pltpu.VMEM((2 * RHS, 2 * RANK), F32),
            pltpu.SemaphoreType.DMA((len(PARTS), 4)),
        ],
        compiler_params=params(LIMITS[0]),
        cost_estimate=pl.CostEstimate(flops=800_000_000, bytes_accessed=7_340_032, transcendentals=0),
        name="project_low",
    )(core, rhs, basis, gen)


def load_kernel(basis_ref, gen_ref, sent_ref, sent_out, v1_ref, v0_ref, u3_ref, u2_ref, u1_ref, sems):
    sources = (
        (basis_ref, 1, v1_ref), (basis_ref, 0, v0_ref),
        (gen_ref, 3, u3_ref), (gen_ref, 2, u2_ref), (gen_ref, 1, u1_ref),
    )
    copies = [pltpu.make_async_copy(ref.at[k], out, sems.at[i]) for i, (ref, k, out) in enumerate(sources)]
    for copy in copies:
        copy.start()
    sent_out[...] = sent_ref[...]
    for copy in copies:
        copy.wait()


def load_step(basis, gen, sent):
    wide = array(*basis.shape[1:])
    return pl.pallas_call(
        load_kernel,
        out_shape=(array(*sent.shape), wide, wide, wide, wide, wide),
        in_specs=[HBM, HBM, VMEM],
        out_specs=(VMEM,) * 6,
        scratch_shapes=[pltpu.SemaphoreType.DMA((5,))],
        compiler_params=params(LIMITS[1]),
        cost_estimate=pl.CostEstimate(flops=1_000, bytes_accessed=10_485_760, transcendentals=0),
        name="load_high",
    )(basis, gen, sent)


def grams_kernel(rhs_ref, v1_ref, v0_ref, u3_ref, u2_ref, u1_ref, sent_ref, sent_out, p_ref, g_ref, g10_ref):
    sent_out[...] = sent_ref[...]
    left = stacked([rhs_ref[...], u3_ref[...]])
    u2 = stacked([u2_ref[...]])
    for k, ref in enumerate((v1_ref, v0_ref)):
        right = stacked([ref[...]])
        cols = slice(k * RANK, (k + 1) * RANK)
        both = fold(contract(left, right), RHS + RANK)
        p_ref[:, cols] = both[:RHS]
        g_ref[:RANK, cols] = both[RHS:]
        g_ref[RANK:, cols] = fold(contract(u2, right), RANK)
    g10_ref[...] = fold(contract(stacked([u1_ref[...]]), right), RANK)


def grams_step(rhs, v1, v0, u3, u2, u1, sent):
    return pl.pallas_call(
        grams_kernel,
        out_shape=(array(*sent.shape), array(RHS, 2 * RANK), array(2 * RANK, 2 * RANK), array(RANK, RANK)),
        in_specs=[VMEM] * 7,
        out_specs=(VMEM,) * 4,
        compiler_params=params(LIMITS[2]),
        cost_estimate=pl.CostEstimate(flops=3_200_000_000, bytes_accessed=11_534_336, transcendentals=0),
        name="grams_high",
    )(rhs, v1, v0, u3, u2, u1, sent)


def nodes_kernel(nodes_ref, cap_ref, sent_ref, sent_out, out_ref, sems):
    copies = [pltpu.make_async_copy(cap_ref.at[nodes_ref[i]], out_ref.at[i], sems.at[i]) for i in range(3)]
    for copy in copies:
        copy.start()
    sent_out[...] = sent_ref[...]
    for copy in copies:
        copy.wait()


def nodes_step(nodes, cap, sent, name):
    return pl.pallas_call(
        nodes_kernel,
        out_shape=(array(*sent.shape), array(3, 2 * RANK, 2 * RANK)),
        in_specs=[SMEM, HBM, VMEM],
        out_specs=(VMEM, VMEM),
        scratch_shapes=[pltpu.SemaphoreType.DMA((3,))],
        compiler_params=params(LIMITS[7]),
        cost_estimate=pl.CostEstimate(flops=1_000, bytes_accessed=786_432, transcendentals=0),
        name=name,
    )(nodes, cap, sent)


def related(caps_ref, node, s, columns):
    blocks = []
    for row in (1 - s, s):
        rows = pl.ds(pl.multiple_of(row * RANK, RANK), RANK)
        blocks.append(
            jnp.concatenate(
                [
                    caps_ref[node, rows, pl.ds(pl.multiple_of(col * RANK, RANK), RANK)]
                    for col in (s, 1 - s)[:columns]
                ],
                axis=1,
            )
        )
    return jnp.concatenate(blocks, axis=0)


def middle_kernel(place_ref, mine_ref, other_ref, caps_ref, p_ref, g_ref, g10_ref,
                  t_ref, keep_ref, send_ref):
    first = place_ref[0] == 0
    p, g = [], []
    for m in range(4):
        mine, other = mine_ref[(3, 1, 0, 2)[m]], other_ref[(3, 1, 0, 2)[m]]
        p.append(jnp.where(first, mine, other))
        g.append(jnp.where(first, other, mine))
    t = []
    for pair in (0, 2):
        joined = jnp.concatenate([p[pair][:RHS], p[pair + 1][:RHS]], axis=1)
        both = product(joined, related(caps_ref, pair // 2, place_ref[1], 2))
        t += [both[:, :RANK], both[:, RANK:]]
    q2 = [p[m][RHS:] - product(t[m], g[m]) for m in range(4)]
    joined = jnp.concatenate([q2[0] + q2[1], q2[2] + q2[3]], axis=1)
    coeff = jnp.concatenate([t[0], product(joined, related(caps_ref, 2, place_ref[2], 1))], axis=1)
    t_ref[...] = coeff
    q = p_ref[...] - product(coeff, g_ref[...])
    half = RHS // 2

    def put(ref, c):
        rows = slice(c * half, (c + 1) * half)
        ref[:half] = q[rows, :RANK]
        ref[half : 2 * half] = q[rows, RANK:]
        ref[2 * half :] = g10_ref[c * RHS : (c + 1) * RHS]

    @pl.when(first)
    def _():
        put(keep_ref, 0)
        put(send_ref, 1)

    @pl.when(jnp.logical_not(first))
    def _():
        put(keep_ref, 1)
        put(send_ref, 0)


def middle_step(place, mine, other, caps, p, g, g10):
    half = jax.ShapeDtypeStruct((RANK, RANK), F32)
    return pl.pallas_call(
        middle_kernel,
        out_shape=(jax.ShapeDtypeStruct((RHS, 2 * RANK), F32), half, half),
        in_specs=[SMEM] + [VMEM] * 6,
        out_specs=(VMEM,) * 3,
        compiler_params=params(LIMITS[3]),
        cost_estimate=pl.CostEstimate(flops=120_000_000, bytes_accessed=1_500_000, transcendentals=0),
        name="coefficients_low",
    )(place, mine, other, caps, p, g, g10)


def low_update_kernel(t_ref, rhs_ref, u3_ref, u2_ref, sent_ref, cur_ref, sent_out):
    sent_out[...] = sent_ref[...]
    th, tl = split(t_ref[...])
    left = jnp.concatenate([th, tl], axis=0)
    for cols in spans((2,) * 4, rhs_ref.shape[1]):
        gh, gl = split(jnp.concatenate([u3_ref[:, cols], u2_ref[:, cols]], axis=0))
        both = jnp.dot(left, gh, preferred_element_type=F32)
        update = both[:RHS] + both[RHS:] + jnp.dot(th, gl, preferred_element_type=F32)
        cur_ref[:, cols] = rhs_ref[:, cols] - update


def low_update(t, rhs, u3, u2, sent):
    return pl.pallas_call(
        low_update_kernel,
        out_shape=(array(*rhs.shape), array(*sent.shape)),
        in_specs=[VMEM] * 5,
        out_specs=(VMEM, VMEM),
        compiler_params=params(LIMITS[4]),
        cost_estimate=pl.CostEstimate(flops=402_653_184, bytes_accessed=6_291_456, transcendentals=0),
        name="update_low",
    )(t, rhs, u3, u2, sent)


def pairs_kernel(u1_ref, gen_ref, sent_ref, sent_out, high_ref, low_ref, u0_ref, sem):
    copy = pltpu.make_async_copy(gen_ref.at[0], u0_ref, sem)
    copy.start()
    sent_out[...] = sent_ref[...]
    high_ref[:RANK], low_ref[:RANK] = split(u1_ref[...])
    copy.wait()
    high_ref[RANK:], low_ref[RANK:] = split(u0_ref[...])


def pairs_step(u1, gen, sent):
    pair = jax.ShapeDtypeStruct((2 * RANK, u1.shape[1]), BF16)
    return pl.pallas_call(
        pairs_kernel,
        out_shape=(array(*sent.shape), pair, pair),
        in_specs=[VMEM, HBM, VMEM],
        out_specs=(VMEM,) * 3,
        scratch_shapes=[pltpu.VMEM(u1.shape, F32), pltpu.SemaphoreType.DMA(())],
        compiler_params=params(LIMITS[5]),
        cost_estimate=pl.CostEstimate(flops=100_000_000, bytes_accessed=8_388_608, transcendentals=0),
        name="pairs_high",
    )(u1, gen, sent)


def last_kernel(place_ref, mine_ref, other_ref, caps_ref, cur_ref, high_ref, low_ref, out_ref,
                buf, sems):
    first = place_ref[0] == 0
    half = RHS // 2
    q1, q0, g = [], [], []
    for m in range(4):
        mine, other = mine_ref[3 - m], other_ref[3 - m]
        low = jnp.where(first, mine, other)
        high = jnp.where(first, other, mine)
        q1.append(jnp.concatenate([low[:half], high[:half]], axis=0))
        q0.append(jnp.concatenate([low[half:RHS], high[half:RHS]], axis=0))
        g.append(jnp.concatenate([low[RHS:], high[RHS:]], axis=0))
    t = []
    for pair in (0, 2):
        both = product(
            jnp.concatenate([q1[pair], q1[pair + 1]], axis=1), related(caps_ref, pair // 2, place_ref[3], 2)
        )
        t += [both[:, :RANK], both[:, RANK:]]
    r = [q0[m] - product(t[m], g[m]) for m in range(4)]
    joined = jnp.concatenate([r[0] + r[1], r[2] + r[3]], axis=1)
    th, tl = split(jnp.concatenate([t[0], product(joined, related(caps_ref, 2, place_ref[4], 1))], axis=1))
    left = jnp.concatenate([th, tl], axis=0)
    copies = []
    for i, cols in enumerate(spans((2,) * 4, cur_ref.shape[1])):
        both = jnp.dot(left, high_ref[:, cols], preferred_element_type=F32)
        update = both[:RHS] + both[RHS:] + jnp.dot(th, low_ref[:, cols], preferred_element_type=F32)
        buf[:, cols] = cur_ref[:, cols] - update
        copy = pltpu.make_async_copy(buf.at[:, cols], out_ref.at[:, cols], sems.at[i])
        copy.start()
        copies.append(copy)
    for copy in copies:
        copy.wait()


def last_step(place, mine, other, caps, cur, high, low):
    return pl.pallas_call(
        last_kernel,
        out_shape=array(*cur.shape),
        in_specs=[SMEM] + [VMEM] * 6,
        out_specs=HBM,
        scratch_shapes=[pltpu.VMEM(cur.shape, F32), pltpu.SemaphoreType.DMA((4,))],
        compiler_params=params(LIMITS[6]),
        cost_estimate=pl.CostEstimate(flops=500_000_000, bytes_accessed=7_000_000, transcendentals=0),
        name="update_high",
    )(place, mine, other, caps, cur, high, low)


def swap(value, even, odd):
    pairs = [(i, i ^ (odd if i & CORE else even)) for i in range(DEVICES)]
    return lax.ppermute(value, "leaf", pairs)


def neighbours(value, even, odd):
    three, two, one = (swap(value, e, o) for e, o in zip(even, odd))
    return one, two, three


def body(rhs, basis, gen, cap):
    device = lax.axis_index("leaf").astype(jnp.int32)
    core = (device & 1).reshape(1)
    place = jnp.stack([device & 1, device >> 3 & 1, device >> 4 & 1, device >> 5 & 1, device >> 6 & 1])
    n3, n2, n1 = device >> 4, device >> 5, device >> 6
    low_nodes = jnp.stack([7 + n3, 7 + (n3 ^ 1), 3 + n2])
    high_nodes = jnp.stack([1 + n1, 1 + (n1 ^ 1), jnp.zeros_like(n1)])
    keep, send = first_step(core, rhs, basis, gen)
    chip = keep + swap(send, CORE, CORE)
    b, c, d = neighbours(chip, Z_MASKS, Z_MASKS)
    chip, v1, v0, u3, u2, u1 = load_step(basis, gen, chip)
    line = chip + d + c + b
    b, c, d = neighbours(line, X_MASKS, X_MASKS)
    line, p, g, g10 = grams_step(rhs, v1, v0, u3, u2, u1, line)
    lines = jnp.stack([c, b, d, line])
    other = swap(lines, CORE, CORE)
    lines, caps = nodes_step(low_nodes, cap, lines, "nodes_low")
    t, keep, send = middle_step(place, lines, other, caps, p, g, g10)
    chip = keep + swap(send, CORE, CORE)
    b, c, d = neighbours(chip, X_MASKS, Z_MASKS)
    current, chip = low_update(t, rhs, u3, u2, chip)
    part = chip + b + d + c
    b, c, d = neighbours(part, Z_MASKS, X_MASKS)
    part, high, low = pairs_step(u1, gen, part)
    plane = part + d + c + b
    b, c, d = neighbours(plane, Y_MASKS, Y_MASKS)
    plane, caps = nodes_step(high_nodes, cap, plane, "nodes_high")
    planes = jnp.stack([d, c, b, plane])
    other = swap(planes, CORE, CORE)
    return last_step(place, planes, other, caps, current, high, low)


def solution(mesh):
    in_specs = (P(None, "leaf"), P(None, None, "leaf"), P(None, None, "leaf"), P())
    return jax.shard_map(body, mesh=mesh, in_specs=in_specs, out_specs=P(None, "leaf"), check_vma=False)
```

time: 65 us -> 61.3 us (0.943)
  waiting for transfers between devices: 13.5 us -> 8.44 us
  starting transfers between devices: 31.5 us -> 27.2 us
  Pallas kernels: 19.3 us -> 22.3 us
  local copies, waits for them, and re-layouts: 0.09 us -> 2.72 us
    ppermute x19, waiting for transfers between devices: 13.5 us -> 8.44 us  [swap(): return lax.ppermute(value, 'leaf', pairs)]
    ppermute x19, starting transfers between devices: 31.5 us -> 27.2 us  [swap(): return lax.ppermute(value, 'leaf', pairs)]
    unnamed x2 -> x18, local copies, waits for them, and re-layouts: 0.01 us -> 2.64 us
    pallas_call x1, Pallas kernels: 0.64 us -> 1.9 us  [pairs_step(): pl.pallas_call(pairs_kernel, out_shape=(array(*sent.shape), pair, pair),...]
    pallas_call x1, Pallas kernels: 0.71 us -> 1.67 us  [middle_step(): pl.pallas_call(middle_kernel, out_shape=(jax.ShapeDtypeStruct((RHS, 2 * R...]
    pallas_call x2 -> x4, Pallas kernels: 11 us -> 11.2 us  [the longest x1 4.11 us: load_step(): pl.pallas_call(load_kernel, out_shape=(array(*sent.shape), wide, wide, wi...]
  transfers between devices with their start and end apart: 19 -> 19, of which waited for: 11 -> 6; matrix products, arithmetic and copies ran while one was open for 0% -> 0% of each run, Pallas kernels for 20% -> 23%
where the time goes in v5:
time: 61.3 us; the launch traced here: 61.1 us
  starting transfers between devices  27.2 us (44%)
  Pallas kernels  22.3 us (36%)
  waiting for transfers between devices  8.44 us (14%)
  local copies, waits for them, and re-layouts  2.72 us (4%)
    ppermute x19, starting transfers between devices, swap(): return lax.ppermute(value, 'leaf', pairs)  27.2 us
    ppermute x19, waiting for transfers between devices, swap(): return lax.ppermute(value, 'leaf', pairs)  8.44 us
    pallas_call x1, Pallas kernels, load_step(): pl.pallas_call(load_kernel, out_shape=(array(*sent.shape), wide, wide, wi...  4.11 us
    pallas_call x1, Pallas kernels, first_step(): pl.pallas_call(functools.partial(first_kernel, points), out_shape=(array(...  3.78 us
    pallas_call x2, Pallas kernels, nodes_step(): pl.pallas_call(nodes_kernel, out_shape=(array(*sent.shape), array(3, 2 *...  3.62 us
    pallas_call x1, Pallas kernels, grams_step(): pl.pallas_call(grams_kernel, out_shape=(array(*sent.shape), array(RHS, 2...  3.47 us
    pallas_call x1, Pallas kernels, last_step(): pl.pallas_call(last_kernel, out_shape=array(*cur.shape), in_specs=[SMEM]...  2.65 us
    unnamed x18, local copies, waits for them, and re-layouts  2.64 us
  transfers between devices with their start and end apart: 19, of which 6 were waited for; matrix products, arithmetic and copies ran while one was open for 0% of the time, Pallas kernels for 23%

profile of v5, /device:TPU:1, one launch (start us, length us, event | category | flops | bytes accessed | tf_op | source)
XLA Modules:
  0.0 61.1 jit_solution(13879718591115195799)
XLA Ops:
  0.0 3.8 %project_low.1 = (f32[128,128]{1,0:T(8,128)S(1)}, f32[128,128]{1,0:T(8,128)S(1)}) custom-call(s32[1]{0:T(128)} %bitcast.core_ref, f32[64,4096]{1,0:T(8,128)} %rhs_ref.5, f32[4,128,4096]{2,1,0:T(8,128)} %basis_ref.3, f32[4,128,4096]{2,1,0:T(8,128)} %gen_ref.5), custom_call_target="tpu_custom_call" | custom-call | flops 800000000 | bytes 7340032 | tf_op jit(solution)/shard_map/project_low/pallas_call | solution.py:124
  3.8 1.5 %collective-permute-start = (f32[128,128]{1,0:T(8,128)S(1)}, f32[128,128]{1,0:T(8,128)S(1)}, u32[]{:S(2)}, u32[]{:S(2)}) collective-permute-start(f32[128,128]{1,0:T(8,128)S(1)} %get-tuple-element.30), channel_id=1, source_target_pairs={{0,1},{1,0},{2,3},{3,2},{4,5},{5,4},{6,7},{7,6},{8,9},{9,8},{10,11... | collective-permute-start | bytes 196616 | tf_op jit(solution)/shard_map/ppermute | solution.py:377
  5.3 0.9 %collective-permute-done = f32[128,128]{1,0:T(8,128)S(1)} collective-permute-done((f32[128,128]{1,0:T(8,128)S(1)}, f32[128,128]{1,0:T(8,128)S(1)}, u32[]{:S(2)}, u32[]{:S(2)}) %collective-permute-start) | collective-permute-done | bytes 65568 | tf_op jit(solution)/shard_map/ppermute | solution.py:377
  6.2 3.9 %collective-permute-start.1 = (f32[128,128]{1,0:T(8,128)S(1)}, f32[128,128]{1,0:T(8,128)S(1)}, u32[]{:S(2)}, u32[]{:S(2)}) collective-permute-start(f32[128,128]{1,0:T(8,128)S(1)} %add.48.sent_ref), channel_id=1, source_target_pairs={{0,6},{1,7},{2,4},{3,5},{4,2},{5,3},{6,0},{7,1},{8,14},{9,15},{10,... | collective-permute-start | bytes 196616 | tf_op jit(solution)/shard_map/ppermute | solution.py:377
  10.1 0.7 %collective-permute-start.3 = (f32[128,128]{1,0:T(8,128)S(1)}, f32[128,128]{1,0:T(8,128)S(1)}, u32[]{:S(2)}, u32[]{:S(2)}) collective-permute-start(f32[128,128]{1,0:T(8,128)S(1)} %add.48.sent_ref), channel_id=1, source_target_pairs={{0,2},{1,3},{2,0},{3,1},{4,6},{5,7},{6,4},{7,5},{8,10},{9,11},{10,... | collective-permute-start | bytes 196616 | tf_op jit(solution)/shard_map/ppermute | solution.py:377
  10.8 4.1 %load_high.1 = (f32[128,128]{1,0:T(8,128)S(1)}, f32[128,4096]{1,0:T(8,128)S(1)}, f32[128,4096]{1,0:T(8,128)S(1)}, f32[128,4096]{1,0:T(8,128)S(1)}, f32[128,4096]{1,0:T(8,128)S(1)}, /*index=5*/f32[128,4096]{1,0:T(8,128)S(1)}) custom-call(f32[4,128,4096]{2,1,0:T(8,128)} %basis_ref.3, f32[4,128,4096]{2,1,0:T(8,128)} %gen_ref.5, f32[128,128]{1,0:T(8,128)S(1)} %add.48.sent_ref), custom_call_target="tpu_custom_call" | custom-call | flops 1000 | bytes 10485760 | tf_op jit(solution)/shard_map/load_high/pallas_call | solution.py:156
  15.0 2.6 %collective-permute-start.6 = (f32[128,128]{1,0:T(8,128)S(1)}, f32[128,128]{1,0:T(8,128)S(1)}, u32[]{:S(2)}, u32[]{:S(2)}) collective-permute-start(f32[128,128]{1,0:T(8,128)S(1)} %add_add_fusion.2.sent_ref), channel_id=1, source_target_pairs={{0,24},{1,25},{2,26},{3,27},{4,28},{5,29},{6,30},{7,31},{8,16},{9,... | collective-permute-start | bytes 196616 | tf_op jit(solution)/shard_map/ppermute | solution.py:377
  17.5 0.5 collective-permute-start.4
  18.3 3.5 %grams_high.1 = (f32[128,128]{1,0:T(8,128)S(1)}, f32[64,256]{1,0:T(8,128)S(1)}, f32[256,256]{1,0:T(8,128)S(1)}, f32[128,128]{1,0:T(8,128)S(1)}) custom-call(f32[64,4096]{1,0:T(8,128)S(1)} %copy-done, f32[128,4096]{1,0:T(8,128)S(1)} %get-tuple-element.33.v1_ref, f32[128,4096]{1,0:T(8,128)S(1)} %get-tuple-element.34.v0_ref, ...), custom_call_target="tpu_custom_call" | custom-call | flops 3200000000 | bytes 11534336 | tf_op jit(solution)/shard_map/grams_high/pallas_call | solution.py:183
  21.8 0.7 %copy-done.7 = f32[256,256]{1,0:T(8,128)} copy-done((f32[256,256]{1,0:T(8,128)}, f32[256,256]{1,0:T(8,128)S(1)}, u32[]{:S(2)}) %copy-start.7) | copy-done | bytes 262168
  22.6 3.0 %collective-permute-start.7 = (f32[4,128,128]{2,1,0:T(8,128)S(1)}, f32[4,128,128]{2,1,0:T(8,128)}, u32[]{:S(2)}, u32[]{:S(2)}) collective-permute-start(f32[4,128,128]{2,1,0:T(8,128)S(1)} %pad_maximum_fusion.sent_ref), channel_id=1, source_target_pairs={{0,1},{1,0},{2,3},{3,2},{4,5},{5,4},{6,7},{7,6},{8,9},{9,8},{10,11... | collective-permute-start | bytes 786440 | tf_op jit(solution)/shard_map/ppermute | solution.py:377
  25.7 1.9 %nodes_low.1 = (f32[4,128,128]{2,1,0:T(8,128)S(1)}, f32[3,256,256]{2,1,0:T(8,128)S(1)}) custom-call(s32[3]{0:T(128)S(1)} %pad_add_fusion.nodes_ref, f32[15,256,256]{2,1,0:T(8,128)} %cap_ref.3, f32[4,128,128]{2,1,0:T(8,128)S(1)} %pad_maximum_fusion.sent_ref), custom_call_target="tpu_custom_call" | custom-call | flops 1000 | bytes 786432 | tf_op jit(solution)/shard_map/nodes_low/pallas_call | solution.py:204
  27.7 0.9 %copy-done.8 = f32[256,256]{1,0:T(8,128)S(1)} copy-done((f32[256,256]{1,0:T(8,128)S(1)}, f32[256,256]{1,0:T(8,128)}, u32[]{:S(2)}) %copy-start.8) | copy-done | bytes 262168
  28.7 1.7 %coefficients_low.1 = (f32[64,256]{1,0:T(8,128)S(1)}, f32[128,128]{1,0:T(8,128)S(1)}, f32[128,128]{1,0:T(8,128)S(1)}) custom-call(s32[5]{0:T(128)S(1)} %stack.74.place_ref, f32[4,128,128]{2,1,0:T(8,128)S(1)} %get-tuple-element.38.mine_ref, f32[4,128,128]{2,1,0:T(8,128)} %collective-permute-done.7.other_ref, f32[3,256,256]{2,1,0:T(8,128)S(1)} %get-tuple-element.39.caps_ref, ...), custom_call_target="tpu_custom_call" | custom-call | flops 120000000 | bytes 1500000 | tf_op jit(solution)/shard_map/coefficients_low/pallas_call | solution.py:271
  30.4 1.2 %collective-permute-done.8 = f32[128,128]{1,0:T(8,128)S(1)} collective-permute-done((f32[128,128]{1,0:T(8,128)S(1)}, f32[128,128]{1,0:T(8,128)S(1)}, u32[]{:S(2)}, u32[]{:S(2)}) %collective-permute-start.8) | collective-permute-done | bytes 65568 | tf_op jit(solution)/shard_map/ppermute | solution.py:377
  31.7 2.0 %collective-permute-start.10 = (f32[128,128]{1,0:T(8,128)S(1)}, f32[128,128]{1,0:T(8,128)S(1)}, u32[]{:S(2)}, u32[]{:S(2)}) collective-permute-start(f32[128,128]{1,0:T(8,128)S(1)} %add.55.sent_ref), channel_id=1, source_target_pairs={{0,24},{1,7},{2,26},{3,5},{4,28},{5,3},{6,30},{7,1},{8,16},{9,15},... | collective-permute-start | bytes 196616 | tf_op jit(solution)/shard_map/ppermute | solution.py:377
  33.7 1.3 %collective-permute-start.9 = (f32[128,128]{1,0:T(8,128)S(1)}, f32[128,128]{1,0:T(8,128)S(1)}, u32[]{:S(2)}, u32[]{:S(2)}) collective-permute-start(f32[128,128]{1,0:T(8,128)S(1)} %add.55.sent_ref), channel_id=1, source_target_pairs={{0,8},{1,3},{2,10},{3,1},{4,12},{5,7},{6,14},{7,5},{8,0},{9,11},{1... | collective-permute-start | bytes 196616 | tf_op jit(solution)/shard_map/ppermute | solution.py:377
  35.0 1.1 %update_low.1 = (f32[64,4096]{1,0:T(8,128)S(1)}, f32[128,128]{1,0:T(8,128)S(1)}) custom-call(f32[64,256]{1,0:T(8,128)S(1)} %get-tuple-element.43.t_ref, f32[64,4096]{1,0:T(8,128)S(1)} %copy-done, f32[128,4096]{1,0:T(8,128)S(1)} %copy-done.2, f32[128,4096]{1,0:T(8,128)S(1)} %copy-done.4, f32[128,128]{1,0:T(8,128)S(1)} %add.55.sent_ref), custom_call_target="tpu_custom_call" | custom-call | flops 402653184 | bytes 6291456 | tf_op jit(solution)/shard_map/update_low/pallas_call | solution.py:294
  36.1 1.0 %copy-done.5 = f32[64,4096]{1,0:T(8,128)} copy-done((f32[64,4096]{1,0:T(8,128)}, f32[64,4096]{1,0:T(8,128)S(1)}, u32[]{:S(2)}) %copy-start.5) | copy-done | bytes 1048600
  37.1 1.2 %collective-permute-done.11 = f32[128,128]{1,0:T(8,128)S(1)} collective-permute-done((f32[128,128]{1,0:T(8,128)S(1)}, f32[128,128]{1,0:T(8,128)S(1)}, u32[]{:S(2)}, u32[]{:S(2)}) %collective-permute-start.11) | collective-permute-done | bytes 65568 | tf_op jit(solution)/shard_map/ppermute | solution.py:377
  38.3 2.3 %collective-permute-start.12 = (f32[128,128]{1,0:T(8,128)S(1)}, f32[128,128]{1,0:T(8,128)S(1)}, u32[]{:S(2)}, u32[]{:S(2)}) collective-permute-start(f32[128,128]{1,0:T(8,128)S(1)} %add_add_fusion.1.sent_ref), channel_id=1, source_target_pairs={{0,6},{1,25},{2,4},{3,27},{4,2},{5,29},{6,0},{7,31},{8,14},{9,17},... | collective-permute-start | bytes 196616 | tf_op jit(solution)/shard_map/ppermute | solution.py:377
  40.7 0.5 collective-permute-start.13
  41.2 0.5 collective-permute-start.14
  41.7 1.9 %pairs_high.1 = (f32[128,128]{1,0:T(8,128)S(1)}, bf16[256,4096]{1,0:T(8,128)(2,1)S(1)}, bf16[256,4096]{1,0:T(8,128)(2,1)S(1)}) custom-call(f32[128,4096]{1,0:T(8,128)S(1)} %get-tuple-element.31.u1_ref, f32[4,128,4096]{2,1,0:T(8,128)} %gen_ref.5, f32[128,128]{1,0:T(8,128)S(1)} %add_add_fusion.1.sent_ref), custom_call_target="tpu_custom_call" | custom-call | flops 100000000 | bytes 8388608 | tf_op jit(solution)/shard_map/pairs_high/pallas_call | solution.py:316
  43.6 1.7 %collective-permute-done.13 = f32[128,128]{1,0:T(8,128)S(1)} collective-permute-done((f32[128,128]{1,0:T(8,128)S(1)}, f32[128,128]{1,0:T(8,128)S(1)}, u32[]{:S(2)}, u32[]{:S(2)}) %collective-permute-start.13) | collective-permute-done | bytes 65568 | tf_op jit(solution)/shard_map/ppermute | solution.py:377
  45.3 2.8 %collective-permute-start.15 = (f32[128,128]{1,0:T(8,128)S(1)}, f32[128,128]{1,0:T(8,128)S(1)}, u32[]{:S(2)}, u32[]{:S(2)}) collective-permute-start(f32[128,128]{1,0:T(8,128)S(1)} %add_add_fusion.sent_ref), channel_id=1, source_target_pairs={{0,96},{1,97},{2,98},{3,99},{4,100},{5,101},{6,102},{7,103},{8,104... | collective-permute-start | bytes 196616 | tf_op jit(solution)/shard_map/ppermute | solution.py:377
  48.1 0.3 collective-permute-start.16
  48.9 1.7 %nodes_high.1 = (f32[128,128]{1,0:T(8,128)S(1)}, f32[3,256,256]{2,1,0:T(8,128)S(1)}) custom-call(s32[3]{0:T(128)S(1)} %pad_add_fusion.1.nodes_ref, f32[15,256,256]{2,1,0:T(8,128)} %cap_ref.3, f32[128,128]{1,0:T(8,128)S(1)} %add_add_fusion.sent_ref), custom_call_target="tpu_custom_call" | custom-call | flops 1000 | bytes 786432 | tf_op jit(solution)/shard_map/nodes_high/pallas_call | solution.py:204
  50.6 2.2 %collective-permute-done.16 = f32[128,128]{1,0:T(8,128)S(1)} collective-permute-done((f32[128,128]{1,0:T(8,128)S(1)}, f32[128,128]{1,0:T(8,128)S(1)}, u32[]{:S(2)}, u32[]{:S(2)}) %collective-permute-start.16) | collective-permute-done | bytes 65568 | tf_op jit(solution)/shard_map/ppermute | solution.py:377
  52.8 4.5 %collective-permute-start.18 = (f32[4,128,128]{2,1,0:T(8,128)S(1)}, f32[4,128,128]{2,1,0:T(8,128)S(1)}, u32[]{:S(2)}, u32[]{:S(2)}) collective-permute-start(f32[4,128,128]{2,1,0:T(8,128)S(1)} %pad_maximum_fusion.1.mine_ref), channel_id=1, source_target_pairs={{0,1},{1,0},{2,3},{3,2},{4,5},{5,4},{6,7},{7,6},{8,9},{9,8},{10,11... | collective-permute-start | bytes 786440 | tf_op jit(solution)/shard_map/ppermute | solution.py:377
  57.3 1.2 %collective-permute-done.18.other_ref = f32[4,128,128]{2,1,0:T(8,128)S(1)} collective-permute-done((f32[4,128,128]{2,1,0:T(8,128)S(1)}, f32[4,128,128]{2,1,0:T(8,128)S(1)}, u32[]{:S(2)}, u32[]{:S(2)}) %collective-permute-start.18) | collective-permute-done | bytes 262176 | tf_op jit(solution)/shard_map/ppermute | solution.py:377
  58.5 2.7 %update_high.1 = f32[64,4096]{1,0:T(8,128)} custom-call(s32[5]{0:T(128)S(1)} %stack.74.place_ref, f32[4,128,128]{2,1,0:T(8,128)S(1)} %pad_maximum_fusion.1.mine_ref, f32[4,128,128]{2,1,0:T(8,128)S(1)} %collective-permute-done.18.other_ref, f32[3,256,256]{2,1,0:T(8,128)S(1)} %get-tuple-element.49.caps_ref, f32[64,4096]{1,0:T(8,128)S(1)} %copy-done.6, ...), custom_call_target="tpu_custom_call" | custom-call | flops 500000000 | bytes 7000000 | tf_op jit(solution)/shard_map/update_high/pallas_call | solution.py:363
  (43 shorter events, 1.1 us)
Async XLA Ops:
  3.8 2.4 %collective-permute-start = (f32[128,128]{1,0:T(8,128)S(1)}, f32[128,128]{1,0:T(8,128)S(1)}, u32[]{:S(2)}, u32[]{:S(2)}) collective-permute-start(f32[128,128]{1,0:T(8,128)S(1)} %get-tuple-element.30), channel_id=1, source_target_pairs={{0,1},{1,0},{2,3},{3,2},{4,5},{5,4},{6,7},{7,6},{8,9},{9,8},{10,11... | collective-permute-start | bytes 196616 | tf_op jit(solution)/shard_map/ppermute | solution.py:377
  6.2 12.1 %copy-start = (f32[64,4096]{1,0:T(8,128)S(1)}, f32[64,4096]{1,0:T(8,128)}, u32[]{:S(2)}) copy-start(f32[64,4096]{1,0:T(8,128)} %rhs_ref.5) | copy-start | bytes 3145732
  6.2 8.7 %collective-permute-start.1 = (f32[128,128]{1,0:T(8,128)S(1)}, f32[128,128]{1,0:T(8,128)S(1)}, u32[]{:S(2)}, u32[]{:S(2)}) collective-permute-start(f32[128,128]{1,0:T(8,128)S(1)} %add.48.sent_ref), channel_id=1, source_target_pairs={{0,6},{1,7},{2,4},{3,5},{4,2},{5,3},{6,0},{7,1},{8,14},{9,15},{10,... | collective-permute-start | bytes 196616 | tf_op jit(solution)/shard_map/ppermute | solution.py:377
  10.1 4.8 %collective-permute-start.2 = (f32[128,128]{1,0:T(8,128)S(1)}, f32[128,128]{1,0:T(8,128)S(1)}, u32[]{:S(2)}, u32[]{:S(2)}) collective-permute-start(f32[128,128]{1,0:T(8,128)S(1)} %add.48.sent_ref), channel_id=1, source_target_pairs={{0,4},{1,5},{2,6},{3,7},{4,0},{5,1},{6,2},{7,3},{8,12},{9,13},{10,... | collective-permute-start | bytes 196616 | tf_op jit(solution)/shard_map/ppermute | solution.py:377
  10.1 4.8 %collective-permute-start.3 = (f32[128,128]{1,0:T(8,128)S(1)}, f32[128,128]{1,0:T(8,128)S(1)}, u32[]{:S(2)}, u32[]{:S(2)}) collective-permute-start(f32[128,128]{1,0:T(8,128)S(1)} %add.48.sent_ref), channel_id=1, source_target_pairs={{0,2},{1,3},{2,0},{3,1},{4,6},{5,7},{6,4},{7,5},{8,10},{9,11},{10,... | collective-permute-start | bytes 196616 | tf_op jit(solution)/shard_map/ppermute | solution.py:377
  14.9 6.9 %copy-start.1 = (f32[128,4096]{1,0:T(8,128)}, f32[128,4096]{1,0:T(8,128)S(1)}, u32[]{:S(2)}) copy-start(f32[128,4096]{1,0:T(8,128)S(1)} %get-tuple-element.35.u3_ref) | copy-start | bytes 6291460
  14.9 6.9 %copy-start.3 = (f32[128,4096]{1,0:T(8,128)}, f32[128,4096]{1,0:T(8,128)S(1)}, u32[]{:S(2)}) copy-start(f32[128,4096]{1,0:T(8,128)S(1)} %get-tuple-element.36.u2_ref) | copy-start | bytes 6291460
  15.0 7.5 %collective-permute-start.6 = (f32[128,128]{1,0:T(8,128)S(1)}, f32[128,128]{1,0:T(8,128)S(1)}, u32[]{:S(2)}, u32[]{:S(2)}) collective-permute-start(f32[128,128]{1,0:T(8,128)S(1)} %add_add_fusion.2.sent_ref), channel_id=1, source_target_pairs={{0,24},{1,25},{2,26},{3,27},{4,28},{5,29},{6,30},{7,31},{8,16},{9,... | collective-permute-start | bytes 196616 | tf_op jit(solution)/shard_map/ppermute | solution.py:377
  17.5 5.0 %collective-permute-start.4 = (f32[128,128]{1,0:T(8,128)S(1)}, f32[128,128]{1,0:T(8,128)S(1)}, u32[]{:S(2)}, u32[]{:S(2)}) collective-permute-start(f32[128,128]{1,0:T(8,128)S(1)} %add_add_fusion.2.sent_ref), channel_id=1, source_target_pairs={{0,16},{1,17},{2,18},{3,19},{4,20},{5,21},{6,22},{7,23},{8,24},{9,... | collective-permute-start | bytes 196616 | tf_op jit(solution)/shard_map/ppermute | solution.py:377
  18.1 4.5 %collective-permute-start.5 = (f32[128,128]{1,0:T(8,128)S(1)}, f32[128,128]{1,0:T(8,128)S(1)}, u32[]{:S(2)}, u32[]{:S(2)}) collective-permute-start(f32[128,128]{1,0:T(8,128)S(1)} %add_add_fusion.2.sent_ref), channel_id=1, source_target_pairs={{0,8},{1,9},{2,10},{3,11},{4,12},{5,13},{6,14},{7,15},{8,0},{9,1},... | collective-permute-start | bytes 196616 | tf_op jit(solution)/shard_map/ppermute | solution.py:377
  21.8 0.7 %copy-start.7 = (f32[256,256]{1,0:T(8,128)}, f32[256,256]{1,0:T(8,128)S(1)}, u32[]{:S(2)}) copy-start(f32[256,256]{1,0:T(8,128)S(1)} %get-tuple-element.41.g_ref) | copy-start | bytes 786436
  22.6 5.1 %collective-permute-start.7 = (f32[4,128,128]{2,1,0:T(8,128)S(1)}, f32[4,128,128]{2,1,0:T(8,128)}, u32[]{:S(2)}, u32[]{:S(2)}) collective-permute-start(f32[4,128,128]{2,1,0:T(8,128)S(1)} %pad_maximum_fusion.sent_ref), channel_id=1, source_target_pairs={{0,1},{1,0},{2,3},{3,2},{4,5},{5,4},{6,7},{7,6},{8,9},{9,8},{10,11... | collective-permute-start | bytes 786440 | tf_op jit(solution)/shard_map/ppermute | solution.py:377
  25.7 9.3 %copy-start.2 = (f32[128,4096]{1,0:T(8,128)S(1)}, f32[128,4096]{1,0:T(8,128)}, u32[]{:S(2)}) copy-start(f32[128,4096]{1,0:T(8,128)} %copy-done.1) | copy-start | bytes 6291460
  25.7 9.3 %copy-start.4 = (f32[128,4096]{1,0:T(8,128)S(1)}, f32[128,4096]{1,0:T(8,128)}, u32[]{:S(2)}) copy-start(f32[128,4096]{1,0:T(8,128)} %copy-done.3) | copy-start | bytes 6291460
  27.7 1.0 %copy-start.8 = (f32[256,256]{1,0:T(8,128)S(1)}, f32[256,256]{1,0:T(8,128)}, u32[]{:S(2)}) copy-start(f32[256,256]{1,0:T(8,128)} %copy-done.7) | copy-start | bytes 786436
  30.3 1.3 %collective-permute-start.8 = (f32[128,128]{1,0:T(8,128)S(1)}, f32[128,128]{1,0:T(8,128)S(1)}, u32[]{:S(2)}, u32[]{:S(2)}) collective-permute-start(f32[128,128]{1,0:T(8,128)S(1)} %get-tuple-element.45), channel_id=1, source_target_pairs={{0,1},{1,0},{2,3},{3,2},{4,5},{5,4},{6,7},{7,6},{8,9},{9,8},{10,11... | collective-permute-start | bytes 196616 | tf_op jit(solution)/shard_map/ppermute | solution.py:377
  31.7 5.4 %collective-permute-start.10 = (f32[128,128]{1,0:T(8,128)S(1)}, f32[128,128]{1,0:T(8,128)S(1)}, u32[]{:S(2)}, u32[]{:S(2)}) collective-permute-start(f32[128,128]{1,0:T(8,128)S(1)} %add.55.sent_ref), channel_id=1, source_target_pairs={{0,24},{1,7},{2,26},{3,5},{4,28},{5,3},{6,30},{7,1},{8,16},{9,15},... | collective-permute-start | bytes 196616 | tf_op jit(solution)/shard_map/ppermute | solution.py:377
  33.7 4.6 %collective-permute-start.11 = (f32[128,128]{1,0:T(8,128)S(1)}, f32[128,128]{1,0:T(8,128)S(1)}, u32[]{:S(2)}, u32[]{:S(2)}) collective-permute-start(f32[128,128]{1,0:T(8,128)S(1)} %add.55.sent_ref), channel_id=1, source_target_pairs={{0,16},{1,5},{2,18},{3,7},{4,20},{5,1},{6,22},{7,3},{8,24},{9,13},... | collective-permute-start | bytes 196616 | tf_op jit(solution)/shard_map/ppermute | solution.py:377
  33.7 4.6 %collective-permute-start.9 = (f32[128,128]{1,0:T(8,128)S(1)}, f32[128,128]{1,0:T(8,128)S(1)}, u32[]{:S(2)}, u32[]{:S(2)}) collective-permute-start(f32[128,128]{1,0:T(8,128)S(1)} %add.55.sent_ref), channel_id=1, source_target_pairs={{0,8},{1,3},{2,10},{3,1},{4,12},{5,7},{6,14},{7,5},{8,0},{9,11},{1... | collective-permute-start | bytes 196616 | tf_op jit(solution)/shard_map/ppermute | solution.py:377
  36.1 1.0 %copy-start.5 = (f32[64,4096]{1,0:T(8,128)}, f32[64,4096]{1,0:T(8,128)S(1)}, u32[]{:S(2)}) copy-start(f32[64,4096]{1,0:T(8,128)S(1)} %get-tuple-element.50.cur_ref) | copy-start | bytes 3145732
  38.3 5.2 %collective-permute-start.12 = (f32[128,128]{1,0:T(8,128)S(1)}, f32[128,128]{1,0:T(8,128)S(1)}, u32[]{:S(2)}, u32[]{:S(2)}) collective-permute-start(f32[128,128]{1,0:T(8,128)S(1)} %add_add_fusion.1.sent_ref), channel_id=1, source_target_pairs={{0,6},{1,25},{2,4},{3,27},{4,2},{5,29},{6,0},{7,31},{8,14},{9,17},... | collective-permute-start | bytes 196616 | tf_op jit(solution)/shard_map/ppermute | solution.py:377
  40.7 4.6 %collective-permute-start.13 = (f32[128,128]{1,0:T(8,128)S(1)}, f32[128,128]{1,0:T(8,128)S(1)}, u32[]{:S(2)}, u32[]{:S(2)}) collective-permute-start(f32[128,128]{1,0:T(8,128)S(1)} %add_add_fusion.1.sent_ref), channel_id=1, source_target_pairs={{0,4},{1,17},{2,6},{3,19},{4,0},{5,21},{6,2},{7,23},{8,12},{9,25},... | collective-permute-start | bytes 196616 | tf_op jit(solution)/shard_map/ppermute | solution.py:377
  41.2 4.1 %collective-permute-start.14 = (f32[128,128]{1,0:T(8,128)S(1)}, f32[128,128]{1,0:T(8,128)S(1)}, u32[]{:S(2)}, u32[]{:S(2)}) collective-permute-start(f32[128,128]{1,0:T(8,128)S(1)} %add_add_fusion.1.sent_ref), channel_id=1, source_target_pairs={{0,2},{1,9},{2,0},{3,11},{4,6},{5,13},{6,4},{7,15},{8,10},{9,1},{1... | collective-permute-start | bytes 196616 | tf_op jit(solution)/shard_map/ppermute | solution.py:377
  45.3 5.2 %collective-permute-start.15 = (f32[128,128]{1,0:T(8,128)S(1)}, f32[128,128]{1,0:T(8,128)S(1)}, u32[]{:S(2)}, u32[]{:S(2)}) collective-permute-start(f32[128,128]{1,0:T(8,128)S(1)} %add_add_fusion.sent_ref), channel_id=1, source_target_pairs={{0,96},{1,97},{2,98},{3,99},{4,100},{5,101},{6,102},{7,103},{8,104... | collective-permute-start | bytes 196616 | tf_op jit(solution)/shard_map/ppermute | solution.py:377
  48.1 4.6 %collective-permute-start.16 = (f32[128,128]{1,0:T(8,128)S(1)}, f32[128,128]{1,0:T(8,128)S(1)}, u32[]{:S(2)}, u32[]{:S(2)}) collective-permute-start(f32[128,128]{1,0:T(8,128)S(1)} %add_add_fusion.sent_ref), channel_id=1, source_target_pairs={{0,64},{1,65},{2,66},{3,67},{4,68},{5,69},{6,70},{7,71},{8,72},{9,... | collective-permute-start | bytes 196616 | tf_op jit(solution)/shard_map/ppermute | solution.py:377
  48.5 4.3 %collective-permute-start.17 = (f32[128,128]{1,0:T(8,128)S(1)}, f32[128,128]{1,0:T(8,128)S(1)}, u32[]{:S(2)}, u32[]{:S(2)}) collective-permute-start(f32[128,128]{1,0:T(8,128)S(1)} %add_add_fusion.sent_ref), channel_id=1, source_target_pairs={{0,32},{1,33},{2,34},{3,35},{4,36},{5,37},{6,38},{7,39},{8,40},{9,... | collective-permute-start | bytes 196616 | tf_op jit(solution)/shard_map/ppermute | solution.py:377
  48.9 9.6 %copy-start.6 = (f32[64,4096]{1,0:T(8,128)S(1)}, f32[64,4096]{1,0:T(8,128)}, u32[]{:S(2)}) copy-start(f32[64,4096]{1,0:T(8,128)} %copy-done.5) | copy-start | bytes 3145732
  52.8 5.7 %collective-permute-start.18 = (f32[4,128,128]{2,1,0:T(8,128)S(1)}, f32[4,128,128]{2,1,0:T(8,128)S(1)}, u32[]{:S(2)}, u32[]{:S(2)}) collective-permute-start(f32[4,128,128]{2,1,0:T(8,128)S(1)} %pad_maximum_fusion.1.mine_ref), channel_id=1, source_target_pairs={{0,1},{1,0},{2,3},{3,2},{4,5},{5,4},{6,7},{7,6},{8,9},{9,8},{10,11... | collective-permute-start | bytes 786440 | tf_op jit(solution)/shard_map/ppermute | solution.py:377

commit v6 on v5

--- a/solution.py
+++ b/solution.py
@@ -12,7 +12,7 @@
 RANK = 128
 RHS = 64
 DEVICES = 128
-LIMITS = (53, 40, 38, 38, 40, 40, 44, 50)
+LIMITS = (53, 39, 38, 38, 40, 40, 44)
 HBM = pl.BlockSpec(memory_space=pltpu.HBM)
 VMEM = pl.BlockSpec(memory_space=pltpu.VMEM)
 SMEM = pl.BlockSpec(memory_space=pltpu.SMEM)
@@ -21,6 +21,8 @@
 Z_MASKS = (6, 4, 2)
 X_MASKS = (24, 16, 8)
 Y_MASKS = (96, 64, 32)
+X_PLACES = (3, 0, 1, 2)
+Y_PLACES = (3, 0, 1, 2)
 
 
 def split(value):
@@ -138,11 +140,13 @@
     )(core, rhs, basis, gen)
 
 
-def load_kernel(basis_ref, gen_ref, sent_ref, sent_out, v1_ref, v0_ref, u3_ref, u2_ref, u1_ref, sems):
-    sources = (
+def load_kernel(nodes_ref, basis_ref, gen_ref, cap_ref, sent_ref, sent_out,
+                v1_ref, v0_ref, u3_ref, u2_ref, u1_ref, caps_ref, sems):
+    sources = [
         (basis_ref, 1, v1_ref), (basis_ref, 0, v0_ref),
         (gen_ref, 3, u3_ref), (gen_ref, 2, u2_ref), (gen_ref, 1, u1_ref),
-    )
+    ]
+    sources += [(cap_ref, nodes_ref[i], caps_ref.at[i]) for i in range(6)]
     copies = [pltpu.make_async_copy(ref.at[k], out, sems.at[i]) for i, (ref, k, out) in enumerate(sources)]
     for copy in copies:
         copy.start()
@@ -151,18 +155,18 @@
         copy.wait()
 
 
-def load_step(basis, gen, sent):
+def load_step(nodes, basis, gen, cap, sent):
     wide = array(*basis.shape[1:])
     return pl.pallas_call(
         load_kernel,
-        out_shape=(array(*sent.shape), wide, wide, wide, wide, wide),
-        in_specs=[HBM, HBM, VMEM],
-        out_specs=(VMEM,) * 6,
-        scratch_shapes=[pltpu.SemaphoreType.DMA((5,))],
+        out_shape=(array(*sent.shape), wide, wide, wide, wide, wide, array(6, 2 * RANK, 2 * RANK)),
+        in_specs=[SMEM, HBM, HBM, HBM, VMEM],
+        out_specs=(VMEM,) * 7,
+        scratch_shapes=[pltpu.SemaphoreType.DMA((11,))],
         compiler_params=params(LIMITS[1]),
-        cost_estimate=pl.CostEstimate(flops=1_000, bytes_accessed=10_485_760, transcendentals=0),
+        cost_estimate=pl.CostEstimate(flops=1_000, bytes_accessed=12_058_624, transcendentals=0),
         name="load_high",
-    )(basis, gen, sent)
+    )(nodes, basis, gen, cap, sent)
 
 
 def grams_kernel(rhs_ref, v1_ref, v0_ref, u3_ref, u2_ref, u1_ref, sent_ref, sent_out, p_ref, g_ref, g10_ref):
@@ -189,28 +193,6 @@
         cost_estimate=pl.CostEstimate(flops=3_200_000_000, bytes_accessed=11_534_336, transcendentals=0),
         name="grams_high",
     )(rhs, v1, v0, u3, u2, u1, sent)
-
-
-def nodes_kernel(nodes_ref, cap_ref, sent_ref, sent_out, out_ref, sems):
-    copies = [pltpu.make_async_copy(cap_ref.at[nodes_ref[i]], out_ref.at[i], sems.at[i]) for i in range(3)]
-    for copy in copies:
-        copy.start()
-    sent_out[...] = sent_ref[...]
-    for copy in copies:
-        copy.wait()
-
-
-def nodes_step(nodes, cap, sent, name):
-    return pl.pallas_call(
-        nodes_kernel,
-        out_shape=(array(*sent.shape), array(3, 2 * RANK, 2 * RANK)),
-        in_specs=[SMEM, HBM, VMEM],
-        out_specs=(VMEM, VMEM),
-        scratch_shapes=[pltpu.SemaphoreType.DMA((3,))],
-        compiler_params=params(LIMITS[7]),
-        cost_estimate=pl.CostEstimate(flops=1_000, bytes_accessed=786_432, transcendentals=0),
-        name=name,
-    )(nodes, cap, sent)
 
 
 def related(caps_ref, node, s, columns):
@@ -234,7 +216,7 @@
     first = place_ref[0] == 0
     p, g = [], []
     for m in range(4):
-        mine, other = mine_ref[(3, 1, 0, 2)[m]], other_ref[(3, 1, 0, 2)[m]]
+        mine, other = mine_ref[X_PLACES[m]], other_ref[X_PLACES[m]]
         p.append(jnp.where(first, mine, other))
         g.append(jnp.where(first, other, mine))
     t = []
@@ -331,7 +313,7 @@
     half = RHS // 2
     q1, q0, g = [], [], []
     for m in range(4):
-        mine, other = mine_ref[3 - m], other_ref[3 - m]
+        mine, other = mine_ref[Y_PLACES[m]], other_ref[Y_PLACES[m]]
         low = jnp.where(first, mine, other)
         high = jnp.where(first, other, mine)
         q1.append(jnp.concatenate([low[:half], high[:half]], axis=0))
@@ -340,12 +322,12 @@
     t = []
     for pair in (0, 2):
         both = product(
-            jnp.concatenate([q1[pair], q1[pair + 1]], axis=1), related(caps_ref, pair // 2, place_ref[3], 2)
+            jnp.concatenate([q1[pair], q1[pair + 1]], axis=1), related(caps_ref, 3 + pair // 2, place_ref[3], 2)
         )
         t += [both[:, :RANK], both[:, RANK:]]
     r = [q0[m] - product(t[m], g[m]) for m in range(4)]
     joined = jnp.concatenate([r[0] + r[1], r[2] + r[3]], axis=1)
-    th, tl = split(jnp.concatenate([t[0], product(joined, related(caps_ref, 2, place_ref[4], 1))], axis=1))
+    th, tl = split(jnp.concatenate([t[0], product(joined, related(caps_ref, 5, place_ref[4], 1))], axis=1))
     left = jnp.concatenate([th, tl], axis=0)
     copies = []
     for i, cols in enumerate(spans((2,) * 4, cur_ref.shape[1])):
@@ -387,29 +369,26 @@
     core = (device & 1).reshape(1)
     place = jnp.stack([device & 1, device >> 3 & 1, device >> 4 & 1, device >> 5 & 1, device >> 6 & 1])
     n3, n2, n1 = device >> 4, device >> 5, device >> 6
-    low_nodes = jnp.stack([7 + n3, 7 + (n3 ^ 1), 3 + n2])
-    high_nodes = jnp.stack([1 + n1, 1 + (n1 ^ 1), jnp.zeros_like(n1)])
+    nodes = jnp.stack([7 + n3, 7 + (n3 ^ 1), 3 + n2, 1 + n1, 1 + (n1 ^ 1), jnp.zeros_like(n1)])
     keep, send = first_step(core, rhs, basis, gen)
     chip = keep + swap(send, CORE, CORE)
     b, c, d = neighbours(chip, Z_MASKS, Z_MASKS)
-    chip, v1, v0, u3, u2, u1 = load_step(basis, gen, chip)
-    line = chip + d + c + b
+    chip, v1, v0, u3, u2, u1, caps = load_step(nodes, basis, gen, cap, chip)
+    line = chip + b + c + d
     b, c, d = neighbours(line, X_MASKS, X_MASKS)
     line, p, g, g10 = grams_step(rhs, v1, v0, u3, u2, u1, line)
-    lines = jnp.stack([c, b, d, line])
+    lines = jnp.stack([b, c, d, line])
     other = swap(lines, CORE, CORE)
-    lines, caps = nodes_step(low_nodes, cap, lines, "nodes_low")
     t, keep, send = middle_step(place, lines, other, caps, p, g, g10)
     chip = keep + swap(send, CORE, CORE)
     b, c, d = neighbours(chip, X_MASKS, Z_MASKS)
     current, chip = low_update(t, rhs, u3, u2, chip)
-    part = chip + b + d + c
+    part = chip + b + c + d
     b, c, d = neighbours(part, Z_MASKS, X_MASKS)
     part, high, low = pairs_step(u1, gen, part)
-    plane = part + d + c + b
+    plane = part + b + c + d
     b, c, d = neighbours(plane, Y_MASKS, Y_MASKS)
-    plane, caps = nodes_step(high_nodes, cap, plane, "nodes_high")
-    planes = jnp.stack([d, c, b, plane])
+    planes = jnp.stack([b, c, d, plane])
     other = swap(planes, CORE, CORE)
     return last_step(place, planes, other, caps, current, high, low)
 

time: 61.3 us -> 59.6 us (0.972)
  Pallas kernels: 22.3 us -> 19.3 us
  waiting for transfers between devices: 8.44 us -> 10.6 us
  local copies, waits for them, and re-layouts: 2.72 us -> 1.78 us
    pallas_call x2 -> x0, Pallas kernels: 3.62 us -> none  [nodes_step(): pl.pallas_call(nodes_kernel, out_shape=(array(*sent.shape), array(3, 2 *...]
    ppermute x19, waiting for transfers between devices: 8.44 us -> 10.6 us  [swap(): return lax.ppermute(value, 'leaf', pairs)]
    unnamed x18 -> x14, local copies, waits for them, and re-layouts: 2.64 us -> 1.61 us
    pallas_call x1, Pallas kernels: 4.11 us -> 5.02 us  [load_step(): pl.pallas_call(load_kernel, out_shape=(array(*sent.shape), wide, wide, wi...]
  transfers between devices with their start and end apart: 19 -> 19, of which waited for: 6 -> 9; matrix products, arithmetic and copies ran while one was open for 0% -> 0% of each run, Pallas kernels for 23% -> 20%
where the time goes in v6:
time: 59.6 us; the launch traced here: 59.4 us
  starting transfers between devices  27.4 us (46%)
  Pallas kernels  19.3 us (32%)
  waiting for transfers between devices  10.6 us (18%)
  local copies, waits for them, and re-layouts  1.78 us (3%)
    ppermute x19, starting transfers between devices, swap(): return lax.ppermute(value, 'leaf', pairs)  27.4 us
    ppermute x19, waiting for transfers between devices, swap(): return lax.ppermute(value, 'leaf', pairs)  10.6 us
    pallas_call x1, Pallas kernels, load_step(): pl.pallas_call(load_kernel, out_shape=(array(*sent.shape), wide, wide, wi...  5.02 us
    pallas_call x1, Pallas kernels, first_step(): pl.pallas_call(functools.partial(first_kernel, points), out_shape=(array(...  3.78 us
    pallas_call x1, Pallas kernels, grams_step(): pl.pallas_call(grams_kernel, out_shape=(array(*sent.shape), array(RHS, 2...  3.59 us
    pallas_call x1, Pallas kernels, last_step(): pl.pallas_call(last_kernel, out_shape=array(*cur.shape), in_specs=[SMEM]...  2.66 us
    pallas_call x1, Pallas kernels, pairs_step(): pl.pallas_call(pairs_kernel, out_shape=(array(*sent.shape), pair, pair),...  1.9 us
    unnamed x14, local copies, waits for them, and re-layouts  1.61 us
  transfers between devices with their start and end apart: 19, of which 9 were waited for; matrix products, arithmetic and copies ran while one was open for 0% of the time, Pallas kernels for 20%

profile of v6, /device:TPU:1, one launch (start us, length us, event | category | flops | bytes accessed | tf_op | source)
XLA Modules:
  0.0 59.4 jit_solution(5519248529921589313)
XLA Ops:
  0.0 3.8 %project_low.1 = (f32[128,128]{1,0:T(8,128)S(1)}, f32[128,128]{1,0:T(8,128)S(1)}) custom-call(s32[1]{0:T(128)} %bitcast.core_ref, f32[64,4096]{1,0:T(8,128)} %rhs_ref.5, f32[4,128,4096]{2,1,0:T(8,128)} %basis_ref.3, f32[4,128,4096]{2,1,0:T(8,128)} %gen_ref.5), custom_call_target="tpu_custom_call" | custom-call | flops 800000000 | bytes 7340032 | tf_op jit(solution)/shard_map/project_low/pallas_call | solution.py:126
  3.8 1.5 %collective-permute-start = (f32[128,128]{1,0:T(8,128)S(1)}, f32[128,128]{1,0:T(8,128)S(1)}, u32[]{:S(2)}, u32[]{:S(2)}) collective-permute-start(f32[128,128]{1,0:T(8,128)S(1)} %get-tuple-element.27), channel_id=1, source_target_pairs={{0,1},{1,0},{2,3},{3,2},{4,5},{5,4},{6,7},{7,6},{8,9},{9,8},{10,11... | collective-permute-start | bytes 196616 | tf_op jit(solution)/shard_map/ppermute | solution.py:359
  5.3 0.9 %collective-permute-done = f32[128,128]{1,0:T(8,128)S(1)} collective-permute-done((f32[128,128]{1,0:T(8,128)S(1)}, f32[128,128]{1,0:T(8,128)S(1)}, u32[]{:S(2)}, u32[]{:S(2)}) %collective-permute-start) | collective-permute-done | bytes 65568 | tf_op jit(solution)/shard_map/ppermute | solution.py:359
  6.2 3.9 %collective-permute-start.3 = (f32[128,128]{1,0:T(8,128)S(1)}, f32[128,128]{1,0:T(8,128)S(1)}, u32[]{:S(2)}, u32[]{:S(2)}) collective-permute-start(f32[128,128]{1,0:T(8,128)S(1)} %add.53.sent_ref), channel_id=1, source_target_pairs={{0,6},{1,7},{2,4},{3,5},{4,2},{5,3},{6,0},{7,1},{8,14},{9,15},{10,... | collective-permute-start | bytes 196616 | tf_op jit(solution)/shard_map/ppermute | solution.py:359
  10.1 0.7 %collective-permute-start.1 = (f32[128,128]{1,0:T(8,128)S(1)}, f32[128,128]{1,0:T(8,128)S(1)}, u32[]{:S(2)}, u32[]{:S(2)}) collective-permute-start(f32[128,128]{1,0:T(8,128)S(1)} %add.53.sent_ref), channel_id=1, source_target_pairs={{0,2},{1,3},{2,0},{3,1},{4,6},{5,7},{6,4},{7,5},{8,10},{9,11},{10,... | collective-permute-start | bytes 196616 | tf_op jit(solution)/shard_map/ppermute | solution.py:359
  10.9 5.0 %load_high.1 = (f32[128,128]{1,0:T(8,128)S(1)}, f32[128,4096]{1,0:T(8,128)S(1)}, f32[128,4096]{1,0:T(8,128)S(1)}, f32[128,4096]{1,0:T(8,128)S(1)}, f32[128,4096]...) custom-call(s32[6]{0:T(128)S(1)} %stack.77.nodes_ref, f32[4,128,4096]{2,1,0:T(8,128)} %basis_ref.3, ...), custom_call_target="tpu_custom_call" | custom-call | flops 1000 | bytes 12058624 | tf_op jit(solution)/shard_map/load_high/pallas_call | solution.py:160
  16.0 2.6 %collective-permute-start.6 = (f32[128,128]{1,0:T(8,128)S(1)}, f32[128,128]{1,0:T(8,128)S(1)}, u32[]{:S(2)}, u32[]{:S(2)}) collective-permute-start(f32[128,128]{1,0:T(8,128)S(1)} %add_add_fusion.2.sent_ref), channel_id=1, source_target_pairs={{0,24},{1,25},{2,26},{3,27},{4,28},{5,29},{6,30},{7,31},{8,16},{9,... | collective-permute-start | bytes 196616 | tf_op jit(solution)/shard_map/ppermute | solution.py:359
  18.5 0.5 collective-permute-start.5
  19.3 3.6 %grams_high.1 = (f32[128,128]{1,0:T(8,128)S(1)}, f32[64,256]{1,0:T(8,128)S(1)}, f32[256,256]{1,0:T(8,128)S(1)}, f32[128,128]{1,0:T(8,128)S(1)}) custom-call(f32[64,4096]{1,0:T(8,128)S(1)} %copy-done, f32[128,4096]{1,0:T(8,128)S(1)} %get-tuple-element.30.v1_ref, f32[128,4096]{1,0:T(8,128)S(1)} %get-tuple-element.31.v0_ref, ...), custom_call_target="tpu_custom_call" | custom-call | flops 3200000000 | bytes 11534336 | tf_op jit(solution)/shard_map/grams_high/pallas_call | solution.py:187
  23.2 2.4 %collective-permute-start.7 = (f32[4,128,128]{2,1,0:T(8,128)S(1)}, f32[4,128,128]{2,1,0:T(8,128)S(1)}, u32[]{:S(2)}, u32[]{:S(2)}) collective-permute-start(f32[4,128,128]{2,1,0:T(8,128)S(1)} %pad_maximum_fusion.mine_ref), channel_id=1, source_target_pairs={{0,1},{1,0},{2,3},{3,2},{4,5},{5,4},{6,7},{7,6},{8,9},{9,8},{10,11... | collective-permute-start | bytes 786440 | tf_op jit(solution)/shard_map/ppermute | solution.py:359
  25.7 1.1 %collective-permute-done.7.other_ref = f32[4,128,128]{2,1,0:T(8,128)S(1)} collective-permute-done((f32[4,128,128]{2,1,0:T(8,128)S(1)}, f32[4,128,128]{2,1,0:T(8,128)S(1)}, u32[]{:S(2)}, u32[]{:S(2)}) %collective-permute-start.7) | collective-permute-done | bytes 262176 | tf_op jit(solution)/shard_map/ppermute | solution.py:359
  26.8 1.3 %coefficients_low.1 = (f32[64,256]{1,0:T(8,128)S(1)}, f32[128,128]{1,0:T(8,128)S(1)}, f32[128,128]{1,0:T(8,128)S(1)}) custom-call(s32[5]{0:T(128)S(1)} %stack.71.place_ref, f32[4,128,128]{2,1,0:T(8,128)S(1)} %pad_maximum_fusion.mine_ref, f32[4,128,128]{2,1,0:T(8,128)S(1)} %collective-permute-done.7.other_ref, f32[6,256,256]{2,1,0:T(8,128)S(1)} %get-tuple-element.35.caps_ref, ...), custom_call_target="tpu_custom_call" | custom-call | flops 120000000 | bytes 1500000 | tf_op jit(solution)/shard_map/coefficients_low/pallas_call | solution.py:253
  28.0 0.4 collective-permute-start.8
  28.5 0.9 %collective-permute-done.8 = f32[128,128]{1,0:T(8,128)S(1)} collective-permute-done((f32[128,128]{1,0:T(8,128)S(1)}, f32[128,128]{1,0:T(8,128)S(1)}, u32[]{:S(2)}, u32[]{:S(2)}) %collective-permute-start.8) | collective-permute-done | bytes 65568 | tf_op jit(solution)/shard_map/ppermute | solution.py:359
  29.4 2.9 %collective-permute-start.11 = (f32[128,128]{1,0:T(8,128)S(1)}, f32[128,128]{1,0:T(8,128)S(1)}, u32[]{:S(2)}, u32[]{:S(2)}) collective-permute-start(f32[128,128]{1,0:T(8,128)S(1)} %add.57.sent_ref), channel_id=1, source_target_pairs={{0,24},{1,7},{2,26},{3,5},{4,28},{5,3},{6,30},{7,1},{8,16},{9,15},... | collective-permute-start | bytes 196616 | tf_op jit(solution)/shard_map/ppermute | solution.py:359
  32.3 0.7 %collective-permute-start.9 = (f32[128,128]{1,0:T(8,128)S(1)}, f32[128,128]{1,0:T(8,128)S(1)}, u32[]{:S(2)}, u32[]{:S(2)}) collective-permute-start(f32[128,128]{1,0:T(8,128)S(1)} %add.57.sent_ref), channel_id=1, source_target_pairs={{0,8},{1,3},{2,10},{3,1},{4,12},{5,7},{6,14},{7,5},{8,0},{9,11},{1... | collective-permute-start | bytes 196616 | tf_op jit(solution)/shard_map/ppermute | solution.py:359
  33.0 1.6 %copy-done.6 = f32[128,4096]{1,0:T(8,128)S(1)} copy-done((f32[128,4096]{1,0:T(8,128)S(1)}, f32[128,4096]{1,0:T(8,128)}, u32[]{:S(2)}) %copy-start.6) | copy-done | bytes 2097176
  34.6 1.1 %update_low.1 = (f32[64,4096]{1,0:T(8,128)S(1)}, f32[128,128]{1,0:T(8,128)S(1)}) custom-call(f32[64,256]{1,0:T(8,128)S(1)} %get-tuple-element.39.t_ref, f32[64,4096]{1,0:T(8,128)S(1)} %copy-done, f32[128,4096]{1,0:T(8,128)S(1)} %copy-done.4, f32[128,4096]{1,0:T(8,128)S(1)} %copy-done.6, f32[128,128]{1,0:T(8,128)S(1)} %add.57.sent_ref), custom_call_target="tpu_custom_call" | custom-call | flops 402653184 | bytes 6291456 | tf_op jit(solution)/shard_map/update_low/pallas_call | solution.py:276
  35.7 1.5 %collective-permute-done.10 = f32[128,128]{1,0:T(8,128)S(1)} collective-permute-done((f32[128,128]{1,0:T(8,128)S(1)}, f32[128,128]{1,0:T(8,128)S(1)}, u32[]{:S(2)}, u32[]{:S(2)}) %collective-permute-start.10) | collective-permute-done | bytes 65568 | tf_op jit(solution)/shard_map/ppermute | solution.py:359
  37.2 1.6 %collective-permute-start.14 = (f32[128,128]{1,0:T(8,128)S(1)}, f32[128,128]{1,0:T(8,128)S(1)}, u32[]{:S(2)}, u32[]{:S(2)}) collective-permute-start(f32[128,128]{1,0:T(8,128)S(1)} %add_add_fusion.1.sent_ref), channel_id=1, source_target_pairs={{0,6},{1,25},{2,4},{3,27},{4,2},{5,29},{6,0},{7,31},{8,14},{9,17},... | collective-permute-start | bytes 196616 | tf_op jit(solution)/shard_map/ppermute | solution.py:359
  38.8 0.5 collective-permute-start.13
  39.3 1.3 %collective-permute-start.12 = (f32[128,128]{1,0:T(8,128)S(1)}, f32[128,128]{1,0:T(8,128)S(1)}, u32[]{:S(2)}, u32[]{:S(2)}) collective-permute-start(f32[128,128]{1,0:T(8,128)S(1)} %add_add_fusion.1.sent_ref), channel_id=1, source_target_pairs={{0,2},{1,9},{2,0},{3,11},{4,6},{5,13},{6,4},{7,15},{8,10},{9,1},{1... | collective-permute-start | bytes 196616 | tf_op jit(solution)/shard_map/ppermute | solution.py:359
  40.6 1.9 %pairs_high.1 = (f32[128,128]{1,0:T(8,128)S(1)}, bf16[256,4096]{1,0:T(8,128)(2,1)S(1)}, bf16[256,4096]{1,0:T(8,128)(2,1)S(1)}) custom-call(f32[128,4096]{1,0:T(8,128)S(1)} %copy-done.2, f32[4,128,4096]{2,1,0:T(8,128)} %gen_ref.5, f32[128,128]{1,0:T(8,128)S(1)} %add_add_fusion.1.sent_ref), custom_call_target="tpu_custom_call" | custom-call | flops 100000000 | bytes 8388608 | tf_op jit(solution)/shard_map/pairs_high/pallas_call | solution.py:298
  42.5 0.9 %collective-permute-done.13 = f32[128,128]{1,0:T(8,128)S(1)} collective-permute-done((f32[128,128]{1,0:T(8,128)S(1)}, f32[128,128]{1,0:T(8,128)S(1)}, u32[]{:S(2)}, u32[]{:S(2)}) %collective-permute-start.13) | collective-permute-done | bytes 65568 | tf_op jit(solution)/shard_map/ppermute | solution.py:359
  43.4 2.8 %collective-permute-start.17 = (f32[128,128]{1,0:T(8,128)S(1)}, f32[128,128]{1,0:T(8,128)S(1)}, u32[]{:S(2)}, u32[]{:S(2)}) collective-permute-start(f32[128,128]{1,0:T(8,128)S(1)} %add_add_fusion), channel_id=1, source_target_pairs={{0,96},{1,97},{2,98},{3,99},{4,100},{5,101},{6,102},{7,103},{8,104... | collective-permute-start | bytes 196616 | tf_op jit(solution)/shard_map/ppermute | solution.py:359
  46.2 0.3 collective-permute-start.16
  46.6 0.3 collective-permute-start.15
  46.9 1.2 %collective-permute-done.17 = f32[128,128]{1,0:T(8,128)S(1)} collective-permute-done((f32[128,128]{1,0:T(8,128)S(1)}, f32[128,128]{1,0:T(8,128)S(1)}, u32[]{:S(2)}, u32[]{:S(2)}) %collective-permute-start.17) | collective-permute-done | bytes 65568 | tf_op jit(solution)/shard_map/ppermute | solution.py:359
  48.2 2.7 %collective-permute-done.16 = f32[128,128]{1,0:T(8,128)S(1)} collective-permute-done((f32[128,128]{1,0:T(8,128)S(1)}, f32[128,128]{1,0:T(8,128)S(1)}, u32[]{:S(2)}, u32[]{:S(2)}) %collective-permute-start.16) | collective-permute-done | bytes 65568 | tf_op jit(solution)/shard_map/ppermute | solution.py:359
  50.9 4.7 %collective-permute-start.18 = (f32[4,128,128]{2,1,0:T(8,128)S(1)}, f32[4,128,128]{2,1,0:T(8,128)S(1)}, u32[]{:S(2)}, u32[]{:S(2)}) collective-permute-start(f32[4,128,128]{2,1,0:T(8,128)S(1)} %pad_maximum_fusion.1.mine_ref), channel_id=1, source_target_pairs={{0,1},{1,0},{2,3},{3,2},{4,5},{5,4},{6,7},{7,6},{8,9},{9,8},{10,11... | collective-permute-start | bytes 786440 | tf_op jit(solution)/shard_map/ppermute | solution.py:359
  55.6 1.2 %collective-permute-done.18.other_ref = f32[4,128,128]{2,1,0:T(8,128)S(1)} collective-permute-done((f32[4,128,128]{2,1,0:T(8,128)S(1)}, f32[4,128,128]{2,1,0:T(8,128)S(1)}, u32[]{:S(2)}, u32[]{:S(2)}) %collective-permute-start.18) | collective-permute-done | bytes 262176 | tf_op jit(solution)/shard_map/ppermute | solution.py:359
  56.8 2.7 %update_high.1 = f32[64,4096]{1,0:T(8,128)} custom-call(s32[5]{0:T(128)S(1)} %stack.71.place_ref, f32[4,128,128]{2,1,0:T(8,128)S(1)} %pad_maximum_fusion.1.mine_ref, f32[4,128,128]{2,1,0:T(8,128)S(1)} %collective-permute-done.18.other_ref, f32[6,256,256]{2,1,0:T(8,128)S(1)} %get-tuple-element.35.caps_ref, f32[64,4096]{1,0:T(8,128)S(1)} %get-tuple-element.44.cur_ref, ...), custom_call_target="tpu_custom_call" | custom-call | flops 500000000 | bytes 7000000 | tf_op jit(solution)/shard_map/update_high/pallas_call | solution.py:345
  (36 shorter events, 0.8 us)
Async XLA Ops:
  3.8 2.4 %collective-permute-start = (f32[128,128]{1,0:T(8,128)S(1)}, f32[128,128]{1,0:T(8,128)S(1)}, u32[]{:S(2)}, u32[]{:S(2)}) collective-permute-start(f32[128,128]{1,0:T(8,128)S(1)} %get-tuple-element.27), channel_id=1, source_target_pairs={{0,1},{1,0},{2,3},{3,2},{4,5},{5,4},{6,7},{7,6},{8,9},{9,8},{10,11... | collective-permute-start | bytes 196616 | tf_op jit(solution)/shard_map/ppermute | solution.py:359
  6.2 9.7 %collective-permute-start.3 = (f32[128,128]{1,0:T(8,128)S(1)}, f32[128,128]{1,0:T(8,128)S(1)}, u32[]{:S(2)}, u32[]{:S(2)}) collective-permute-start(f32[128,128]{1,0:T(8,128)S(1)} %add.53.sent_ref), channel_id=1, source_target_pairs={{0,6},{1,7},{2,4},{3,5},{4,2},{5,3},{6,0},{7,1},{8,14},{9,15},{10,... | collective-permute-start | bytes 196616 | tf_op jit(solution)/shard_map/ppermute | solution.py:359
  10.1 5.8 %collective-permute-start.2 = (f32[128,128]{1,0:T(8,128)S(1)}, f32[128,128]{1,0:T(8,128)S(1)}, u32[]{:S(2)}, u32[]{:S(2)}) collective-permute-start(f32[128,128]{1,0:T(8,128)S(1)} %add.53.sent_ref), channel_id=1, source_target_pairs={{0,4},{1,5},{2,6},{3,7},{4,0},{5,1},{6,2},{7,3},{8,12},{9,13},{10,... | collective-permute-start | bytes 196616 | tf_op jit(solution)/shard_map/ppermute | solution.py:359
  10.1 5.8 %collective-permute-start.1 = (f32[128,128]{1,0:T(8,128)S(1)}, f32[128,128]{1,0:T(8,128)S(1)}, u32[]{:S(2)}, u32[]{:S(2)}) collective-permute-start(f32[128,128]{1,0:T(8,128)S(1)} %add.53.sent_ref), channel_id=1, source_target_pairs={{0,2},{1,3},{2,0},{3,1},{4,6},{5,7},{6,4},{7,5},{8,10},{9,11},{10,... | collective-permute-start | bytes 196616 | tf_op jit(solution)/shard_map/ppermute | solution.py:359
  10.9 8.5 %copy-start = (f32[64,4096]{1,0:T(8,128)S(1)}, f32[64,4096]{1,0:T(8,128)}, u32[]{:S(2)}) copy-start(f32[64,4096]{1,0:T(8,128)} %rhs_ref.5) | copy-start | bytes 3145732
  15.9 7.0 %copy-start.1 = (f32[128,4096]{1,0:T(8,128)}, f32[128,4096]{1,0:T(8,128)S(1)}, u32[]{:S(2)}) copy-start(f32[128,4096]{1,0:T(8,128)S(1)} %get-tuple-element.28.u1_ref) | copy-start | bytes 6291460
  15.9 7.0 %copy-start.3 = (f32[128,4096]{1,0:T(8,128)}, f32[128,4096]{1,0:T(8,128)S(1)}, u32[]{:S(2)}) copy-start(f32[128,4096]{1,0:T(8,128)S(1)} %get-tuple-element.32.u3_ref) | copy-start | bytes 6291460
  15.9 7.0 %copy-start.5 = (f32[128,4096]{1,0:T(8,128)}, f32[128,4096]{1,0:T(8,128)S(1)}, u32[]{:S(2)}) copy-start(f32[128,4096]{1,0:T(8,128)S(1)} %get-tuple-element.33.u2_ref) | copy-start | bytes 6291460
  16.0 7.0 %collective-permute-start.6 = (f32[128,128]{1,0:T(8,128)S(1)}, f32[128,128]{1,0:T(8,128)S(1)}, u32[]{:S(2)}, u32[]{:S(2)}) collective-permute-start(f32[128,128]{1,0:T(8,128)S(1)} %add_add_fusion.2.sent_ref), channel_id=1, source_target_pairs={{0,24},{1,25},{2,26},{3,27},{4,28},{5,29},{6,30},{7,31},{8,16},{9,... | collective-permute-start | bytes 196616 | tf_op jit(solution)/shard_map/ppermute | solution.py:359
  18.5 4.6 %collective-permute-start.5 = (f32[128,128]{1,0:T(8,128)S(1)}, f32[128,128]{1,0:T(8,128)S(1)}, u32[]{:S(2)}, u32[]{:S(2)}) collective-permute-start(f32[128,128]{1,0:T(8,128)S(1)} %add_add_fusion.2.sent_ref), channel_id=1, source_target_pairs={{0,16},{1,17},{2,18},{3,19},{4,20},{5,21},{6,22},{7,23},{8,24},{9,... | collective-permute-start | bytes 196616 | tf_op jit(solution)/shard_map/ppermute | solution.py:359
  19.1 4.1 %collective-permute-start.4 = (f32[128,128]{1,0:T(8,128)S(1)}, f32[128,128]{1,0:T(8,128)S(1)}, u32[]{:S(2)}, u32[]{:S(2)}) collective-permute-start(f32[128,128]{1,0:T(8,128)S(1)} %add_add_fusion.2.sent_ref), channel_id=1, source_target_pairs={{0,8},{1,9},{2,10},{3,11},{4,12},{5,13},{6,14},{7,15},{8,0},{9,1},... | collective-permute-start | bytes 196616 | tf_op jit(solution)/shard_map/ppermute | solution.py:359
  23.2 3.6 %collective-permute-start.7 = (f32[4,128,128]{2,1,0:T(8,128)S(1)}, f32[4,128,128]{2,1,0:T(8,128)S(1)}, u32[]{:S(2)}, u32[]{:S(2)}) collective-permute-start(f32[4,128,128]{2,1,0:T(8,128)S(1)} %pad_maximum_fusion.mine_ref), channel_id=1, source_target_pairs={{0,1},{1,0},{2,3},{3,2},{4,5},{5,4},{6,7},{7,6},{8,9},{9,8},{10,11... | collective-permute-start | bytes 786440 | tf_op jit(solution)/shard_map/ppermute | solution.py:359
  25.7 7.3 %copy-start.4 = (f32[128,4096]{1,0:T(8,128)S(1)}, f32[128,4096]{1,0:T(8,128)}, u32[]{:S(2)}) copy-start(f32[128,4096]{1,0:T(8,128)} %copy-done.3) | copy-start | bytes 6291460
  28.0 1.3 %collective-permute-start.8 = (f32[128,128]{1,0:T(8,128)S(1)}, f32[128,128]{1,0:T(8,128)S(1)}, u32[]{:S(2)}, u32[]{:S(2)}) collective-permute-start(f32[128,128]{1,0:T(8,128)S(1)} %get-tuple-element.41), channel_id=1, source_target_pairs={{0,1},{1,0},{2,3},{3,2},{4,5},{5,4},{6,7},{7,6},{8,9},{9,8},{10,11... | collective-permute-start | bytes 196616 | tf_op jit(solution)/shard_map/ppermute | solution.py:359
  29.4 6.3 %collective-permute-start.11 = (f32[128,128]{1,0:T(8,128)S(1)}, f32[128,128]{1,0:T(8,128)S(1)}, u32[]{:S(2)}, u32[]{:S(2)}) collective-permute-start(f32[128,128]{1,0:T(8,128)S(1)} %add.57.sent_ref), channel_id=1, source_target_pairs={{0,24},{1,7},{2,26},{3,5},{4,28},{5,3},{6,30},{7,1},{8,16},{9,15},... | collective-permute-start | bytes 196616 | tf_op jit(solution)/shard_map/ppermute | solution.py:359
  32.3 4.9 %collective-permute-start.10 = (f32[128,128]{1,0:T(8,128)S(1)}, f32[128,128]{1,0:T(8,128)S(1)}, u32[]{:S(2)}, u32[]{:S(2)}) collective-permute-start(f32[128,128]{1,0:T(8,128)S(1)} %add.57.sent_ref), channel_id=1, source_target_pairs={{0,16},{1,5},{2,18},{3,7},{4,20},{5,1},{6,22},{7,3},{8,24},{9,13},... | collective-permute-start | bytes 196616 | tf_op jit(solution)/shard_map/ppermute | solution.py:359
  32.3 4.9 %collective-permute-start.9 = (f32[128,128]{1,0:T(8,128)S(1)}, f32[128,128]{1,0:T(8,128)S(1)}, u32[]{:S(2)}, u32[]{:S(2)}) collective-permute-start(f32[128,128]{1,0:T(8,128)S(1)} %add.57.sent_ref), channel_id=1, source_target_pairs={{0,8},{1,3},{2,10},{3,1},{4,12},{5,7},{6,14},{7,5},{8,0},{9,11},{1... | collective-permute-start | bytes 196616 | tf_op jit(solution)/shard_map/ppermute | solution.py:359
  33.0 1.6 %copy-start.6 = (f32[128,4096]{1,0:T(8,128)S(1)}, f32[128,4096]{1,0:T(8,128)}, u32[]{:S(2)}) copy-start(f32[128,4096]{1,0:T(8,128)} %copy-done.5) | copy-start | bytes 6291460
  34.6 5.9 %copy-start.2 = (f32[128,4096]{1,0:T(8,128)S(1)}, f32[128,4096]{1,0:T(8,128)}, u32[]{:S(2)}) copy-start(f32[128,4096]{1,0:T(8,128)} %copy-done.1) | copy-start | bytes 6291460
  37.2 5.2 %collective-permute-start.14 = (f32[128,128]{1,0:T(8,128)S(1)}, f32[128,128]{1,0:T(8,128)S(1)}, u32[]{:S(2)}, u32[]{:S(2)}) collective-permute-start(f32[128,128]{1,0:T(8,128)S(1)} %add_add_fusion.1.sent_ref), channel_id=1, source_target_pairs={{0,6},{1,25},{2,4},{3,27},{4,2},{5,29},{6,0},{7,31},{8,14},{9,17},... | collective-permute-start | bytes 196616 | tf_op jit(solution)/shard_map/ppermute | solution.py:359
  38.8 4.6 %collective-permute-start.13 = (f32[128,128]{1,0:T(8,128)S(1)}, f32[128,128]{1,0:T(8,128)S(1)}, u32[]{:S(2)}, u32[]{:S(2)}) collective-permute-start(f32[128,128]{1,0:T(8,128)S(1)} %add_add_fusion.1.sent_ref), channel_id=1, source_target_pairs={{0,4},{1,17},{2,6},{3,19},{4,0},{5,21},{6,2},{7,23},{8,12},{9,25},... | collective-permute-start | bytes 196616 | tf_op jit(solution)/shard_map/ppermute | solution.py:359
  39.3 4.1 %collective-permute-start.12 = (f32[128,128]{1,0:T(8,128)S(1)}, f32[128,128]{1,0:T(8,128)S(1)}, u32[]{:S(2)}, u32[]{:S(2)}) collective-permute-start(f32[128,128]{1,0:T(8,128)S(1)} %add_add_fusion.1.sent_ref), channel_id=1, source_target_pairs={{0,2},{1,9},{2,0},{3,11},{4,6},{5,13},{6,4},{7,15},{8,10},{9,1},{1... | collective-permute-start | bytes 196616 | tf_op jit(solution)/shard_map/ppermute | solution.py:359
  43.4 4.7 %collective-permute-start.17 = (f32[128,128]{1,0:T(8,128)S(1)}, f32[128,128]{1,0:T(8,128)S(1)}, u32[]{:S(2)}, u32[]{:S(2)}) collective-permute-start(f32[128,128]{1,0:T(8,128)S(1)} %add_add_fusion), channel_id=1, source_target_pairs={{0,96},{1,97},{2,98},{3,99},{4,100},{5,101},{6,102},{7,103},{8,104... | collective-permute-start | bytes 196616 | tf_op jit(solution)/shard_map/ppermute | solution.py:359
  46.2 4.6 %collective-permute-start.16 = (f32[128,128]{1,0:T(8,128)S(1)}, f32[128,128]{1,0:T(8,128)S(1)}, u32[]{:S(2)}, u32[]{:S(2)}) collective-permute-start(f32[128,128]{1,0:T(8,128)S(1)} %add_add_fusion), channel_id=1, source_target_pairs={{0,64},{1,65},{2,66},{3,67},{4,68},{5,69},{6,70},{7,71},{8,72},{9,... | collective-permute-start | bytes 196616 | tf_op jit(solution)/shard_map/ppermute | solution.py:359
  46.6 4.3 %collective-permute-start.15 = (f32[128,128]{1,0:T(8,128)S(1)}, f32[128,128]{1,0:T(8,128)S(1)}, u32[]{:S(2)}, u32[]{:S(2)}) collective-permute-start(f32[128,128]{1,0:T(8,128)S(1)} %add_add_fusion), channel_id=1, source_target_pairs={{0,32},{1,33},{2,34},{3,35},{4,36},{5,37},{6,38},{7,39},{8,40},{9,... | collective-permute-start | bytes 196616 | tf_op jit(solution)/shard_map/ppermute | solution.py:359
  50.9 5.9 %collective-permute-start.18 = (f32[4,128,128]{2,1,0:T(8,128)S(1)}, f32[4,128,128]{2,1,0:T(8,128)S(1)}, u32[]{:S(2)}, u32[]{:S(2)}) collective-permute-start(f32[4,128,128]{2,1,0:T(8,128)S(1)} %pad_maximum_fusion.1.mine_ref), channel_id=1, source_target_pairs={{0,1},{1,0},{2,3},{3,2},{4,5},{5,4},{6,7},{7,6},{8,9},{9,8},{10,11... | collective-permute-start | bytes 786440 | tf_op jit(solution)/shard_map/ppermute | solution.py:359

commit v7 on v6

--- a/solution.py
+++ b/solution.py
@@ -88,7 +88,7 @@
 PARTS = (2, 2, 2, 2)
 
 
-def first_kernel(points, core_ref, rhs_ref, basis_ref, gen_ref, keep_ref, send_ref,
+def first_kernel(points, info_ref, rhs_ref, basis_ref, gen_ref, keep_ref, send_ref,
                  rhs_buf, v3_buf, v2_buf, u3_buf, acc2, acc3, sems):
     sources = ((rhs_ref, None, rhs_buf), (basis_ref, 3, v3_buf), (basis_ref, 2, v2_buf), (gen_ref, 3, u3_buf))
     for i, (cols, row) in enumerate(fetch(sources, sems, PARTS, points)):
@@ -101,7 +101,7 @@
     p3 = fold(acc3[...], RHS)
     p2 = fold(acc2[: 2 * RHS], RHS)
     g32 = fold(acc2[2 * RHS :], RANK)
-    first = core_ref[0] == 0
+    first = info_ref[0] == 0
 
     @pl.when(first)
     def _():
@@ -120,7 +120,7 @@
     return jax.ShapeDtypeStruct(shape, F32)
 
 
-def first_step(core, rhs, basis, gen):
+def first_step(info, rhs, basis, gen):
     points = rhs.shape[1]
     wide = pltpu.VMEM((RANK, points), F32)
     return pl.pallas_call(
@@ -137,16 +137,16 @@
         compiler_params=params(LIMITS[0]),
         cost_estimate=pl.CostEstimate(flops=800_000_000, bytes_accessed=7_340_032, transcendentals=0),
         name="project_low",
-    )(core, rhs, basis, gen)
-
-
-def load_kernel(nodes_ref, basis_ref, gen_ref, cap_ref, sent_ref, sent_out,
+    )(info, rhs, basis, gen)
+
+
+def load_kernel(info_ref, basis_ref, gen_ref, cap_ref, sent_ref, sent_out,
                 v1_ref, v0_ref, u3_ref, u2_ref, u1_ref, caps_ref, sems):
     sources = [
         (basis_ref, 1, v1_ref), (basis_ref, 0, v0_ref),
         (gen_ref, 3, u3_ref), (gen_ref, 2, u2_ref), (gen_ref, 1, u1_ref),
     ]
-    sources += [(cap_ref, nodes_ref[i], caps_ref.at[i]) for i in range(6)]
+    sources += [(cap_ref, info_ref[6 + i], caps_ref.at[i]) for i in range(6)]
     copies = [pltpu.make_async_copy(ref.at[k], out, sems.at[i]) for i, (ref, k, out) in enumerate(sources)]
     for copy in copies:
         copy.start()
@@ -155,7 +155,7 @@
         copy.wait()
 
 
-def load_step(nodes, basis, gen, cap, sent):
+def load_step(info, basis, gen, cap, sent):
     wide = array(*basis.shape[1:])
     return pl.pallas_call(
         load_kernel,
@@ -166,7 +166,7 @@
         compiler_params=params(LIMITS[1]),
         cost_estimate=pl.CostEstimate(flops=1_000, bytes_accessed=12_058_624, transcendentals=0),
         name="load_high",
-    )(nodes, basis, gen, cap, sent)
+    )(info, basis, gen, cap, sent)
 
 
 def grams_kernel(rhs_ref, v1_ref, v0_ref, u3_ref, u2_ref, u1_ref, sent_ref, sent_out, p_ref, g_ref, g10_ref):
@@ -211,9 +211,9 @@
     return jnp.concatenate(blocks, axis=0)
 
 
-def middle_kernel(place_ref, mine_ref, other_ref, caps_ref, p_ref, g_ref, g10_ref,
+def middle_kernel(info_ref, mine_ref, other_ref, caps_ref, p_ref, g_ref, g10_ref,
                   t_ref, keep_ref, send_ref):
-    first = place_ref[0] == 0
+    first = info_ref[0] == 0
     p, g = [], []
     for m in range(4):
         mine, other = mine_ref[X_PLACES[m]], other_ref[X_PLACES[m]]
@@ -222,11 +222,11 @@
     t = []
     for pair in (0, 2):
         joined = jnp.concatenate([p[pair][:RHS], p[pair + 1][:RHS]], axis=1)
-        both = product(joined, related(caps_ref, pair // 2, place_ref[1], 2))
+        both = product(joined, related(caps_ref, pair // 2, info_ref[2], 2))
         t += [both[:, :RANK], both[:, RANK:]]
     q2 = [p[m][RHS:] - product(t[m], g[m]) for m in range(4)]
     joined = jnp.concatenate([q2[0] + q2[1], q2[2] + q2[3]], axis=1)
-    coeff = jnp.concatenate([t[0], product(joined, related(caps_ref, 2, place_ref[2], 1))], axis=1)
+    coeff = jnp.concatenate([t[0], product(joined, related(caps_ref, 2, info_ref[3], 1))], axis=1)
     t_ref[...] = coeff
     q = p_ref[...] - product(coeff, g_ref[...])
     half = RHS // 2
@@ -237,18 +237,20 @@
         ref[half : 2 * half] = q[rows, RANK:]
         ref[2 * half :] = g10_ref[c * RHS : (c + 1) * RHS]
 
-    @pl.when(first)
+    low_half = info_ref[1] == 0
+
+    @pl.when(low_half)
     def _():
         put(keep_ref, 0)
         put(send_ref, 1)
 
-    @pl.when(jnp.logical_not(first))
+    @pl.when(jnp.logical_not(low_half))
     def _():
         put(keep_ref, 1)
         put(send_ref, 0)
 
 
-def middle_step(place, mine, other, caps, p, g, g10):
+def middle_step(info, mine, other, caps, p, g, g10):
     half = jax.ShapeDtypeStruct((RANK, RANK), F32)
     return pl.pallas_call(
         middle_kernel,
@@ -258,7 +260,7 @@
         compiler_params=params(LIMITS[3]),
         cost_estimate=pl.CostEstimate(flops=120_000_000, bytes_accessed=1_500_000, transcendentals=0),
         name="coefficients_low",
-    )(place, mine, other, caps, p, g, g10)
+    )(info, mine, other, caps, p, g, g10)
 
 
 def low_update_kernel(t_ref, rhs_ref, u3_ref, u2_ref, sent_ref, cur_ref, sent_out):
@@ -307,9 +309,9 @@
     )(u1, gen, sent)
 
 
-def last_kernel(place_ref, mine_ref, other_ref, caps_ref, cur_ref, high_ref, low_ref, out_ref,
+def last_kernel(info_ref, mine_ref, other_ref, caps_ref, cur_ref, high_ref, low_ref, out_ref,
                 buf, sems):
-    first = place_ref[0] == 0
+    first = info_ref[1] == 0
     half = RHS // 2
     q1, q0, g = [], [], []
     for m in range(4):
@@ -322,12 +324,12 @@
     t = []
     for pair in (0, 2):
         both = product(
-            jnp.concatenate([q1[pair], q1[pair + 1]], axis=1), related(caps_ref, 3 + pair // 2, place_ref[3], 2)
+            jnp.concatenate([q1[pair], q1[pair + 1]], axis=1), related(caps_ref, 3 + pair // 2, info_ref[4], 2)
         )
         t += [both[:, :RANK], both[:, RANK:]]
     r = [q0[m] - product(t[m], g[m]) for m in range(4)]
     joined = jnp.concatenate([r[0] + r[1], r[2] + r[3]], axis=1)
-    th, tl = split(jnp.concatenate([t[0], product(joined, related(caps_ref, 5, place_ref[4], 1))], axis=1))
+    th, tl = split(jnp.concatenate([t[0], product(joined, related(caps_ref, 5, info_ref[5], 1))], axis=1))
     left = jnp.concatenate([th, tl], axis=0)
     copies = []
     for i, cols in enumerate(spans((2,) * 4, cur_ref.shape[1])):
@@ -341,7 +343,7 @@
         copy.wait()
 
 
-def last_step(place, mine, other, caps, cur, high, low):
+def last_step(info, mine, other, caps, cur, high, low):
     return pl.pallas_call(
         last_kernel,
         out_shape=array(*cur.shape),
@@ -351,46 +353,62 @@
         compiler_params=params(LIMITS[6]),
         cost_estimate=pl.CostEstimate(flops=500_000_000, bytes_accessed=7_000_000, transcendentals=0),
         name="update_high",
-    )(place, mine, other, caps, cur, high, low)
-
-
-def swap(value, even, odd):
-    pairs = [(i, i ^ (odd if i & CORE else even)) for i in range(DEVICES)]
-    return lax.ppermute(value, "leaf", pairs)
-
-
-def neighbours(value, even, odd):
-    three, two, one = (swap(value, e, o) for e, o in zip(even, odd))
+    )(info, mine, other, caps, cur, high, low)
+
+
+def swap(value, mask):
+    return lax.ppermute(value, "leaf", [(i, i ^ mask) for i in range(DEVICES)])
+
+
+def parity(index):
+    return bin(index).count("1") & 1
+
+
+def crossed(value, even, odd):
+    def partner(i):
+        mask = odd if parity(i & 31) else even
+        return i ^ mask ^ parity(mask)
+
+    return lax.ppermute(value, "leaf", [(i, partner(i)) for i in range(DEVICES)])
+
+
+def neighbours(value, masks):
+    three, two, one = (swap(value, m) for m in masks)
+    return one, two, three
+
+
+def crossed_neighbours(value, even, odd):
+    three, two, one = (crossed(value, e, o) for e, o in zip(even, odd))
     return one, two, three
 
 
 def body(rhs, basis, gen, cap):
     device = lax.axis_index("leaf").astype(jnp.int32)
-    core = (device & 1).reshape(1)
-    place = jnp.stack([device & 1, device >> 3 & 1, device >> 4 & 1, device >> 5 & 1, device >> 6 & 1])
+    bit = [device >> k & 1 for k in range(7)]
     n3, n2, n1 = device >> 4, device >> 5, device >> 6
-    nodes = jnp.stack([7 + n3, 7 + (n3 ^ 1), 3 + n2, 1 + n1, 1 + (n1 ^ 1), jnp.zeros_like(n1)])
-    keep, send = first_step(core, rhs, basis, gen)
-    chip = keep + swap(send, CORE, CORE)
-    b, c, d = neighbours(chip, Z_MASKS, Z_MASKS)
-    chip, v1, v0, u3, u2, u1, caps = load_step(nodes, basis, gen, cap, chip)
+    half = bit[0] ^ bit[1] ^ bit[2] ^ bit[3] ^ bit[4]
+    info = jnp.stack([bit[0], half, *bit[3:], 7 + n3, 7 + (n3 ^ 1), 3 + n2, 1 + n1, 1 + (n1 ^ 1), jnp.zeros_like(n1)])
+    keep, send = first_step(info, rhs, basis, gen)
+    chip = keep + swap(send, CORE)
+    b, c, d = neighbours(chip, Z_MASKS)
+    chip, v1, v0, u3, u2, u1, caps = load_step(info, basis, gen, cap, chip)
     line = chip + b + c + d
-    b, c, d = neighbours(line, X_MASKS, X_MASKS)
+    b, c, d = neighbours(line, X_MASKS)
     line, p, g, g10 = grams_step(rhs, v1, v0, u3, u2, u1, line)
     lines = jnp.stack([b, c, d, line])
-    other = swap(lines, CORE, CORE)
-    t, keep, send = middle_step(place, lines, other, caps, p, g, g10)
-    chip = keep + swap(send, CORE, CORE)
-    b, c, d = neighbours(chip, X_MASKS, Z_MASKS)
+    other = swap(lines, CORE)
+    t, keep, send = middle_step(info, lines, other, caps, p, g, g10)
+    chip = keep + swap(send, CORE)
+    b, c, d = crossed_neighbours(chip, X_MASKS, Z_MASKS)
     current, chip = low_update(t, rhs, u3, u2, chip)
     part = chip + b + c + d
-    b, c, d = neighbours(part, Z_MASKS, X_MASKS)
+    b, c, d = crossed_neighbours(part, Z_MASKS, X_MASKS)
     part, high, low = pairs_step(u1, gen, part)
     plane = part + b + c + d
-    b, c, d = neighbours(plane, Y_MASKS, Y_MASKS)
+    b, c, d = neighbours(plane, Y_MASKS)
     planes = jnp.stack([b, c, d, plane])
-    other = swap(planes, CORE, CORE)
-    return last_step(place, planes, other, caps, current, high, low)
+    other = swap(planes, CORE)
+    return last_step(info, planes, other, caps, current, high, low)
 
 
 def solution(mesh):

time: 59.6 us -> 58.9 us (0.988)
  waiting for transfers between devices: 10.6 us -> 13.3 us
  starting transfers between devices: 27.4 us -> 25.5 us
  local copies, waits for them, and re-layouts: 1.78 us -> 0.09 us
    ppermute x19, waiting for transfers between devices: 10.6 us -> 13.3 us  [the longest x13 8.36 us: swap(): return lax.ppermute(value, 'leaf', [(i, i ^ mask) for i in range(DEVICES)])]
    ppermute x19, starting transfers between devices: 27.4 us -> 25.5 us  [the longest x13 18 us: swap(): return lax.ppermute(value, 'leaf', [(i, i ^ mask) for i in range(DEVICES)])]
    unnamed x14 -> x2, local copies, waits for them, and re-layouts: 1.61 us -> 0.01 us
where the time goes in v7:
time: 58.9 us; the launch traced here: 58.8 us
  starting transfers between devices  25.5 us (43%)
  Pallas kernels  19.7 us (33%)
  waiting for transfers between devices  13.3 us (23%)
    ppermute x13, starting transfers between devices, swap(): return lax.ppermute(value, 'leaf', [(i, i ^ mask) for i in range(DEVICES)])  18 us
    ppermute x13, waiting for transfers between devices, swap(): return lax.ppermute(value, 'leaf', [(i, i ^ mask) for i in range(DEVICES)])  8.36 us
    ppermute x6, starting transfers between devices, crossed(): lax.ppermute(value, 'leaf', [(i, partner(i)) for i in range(DEVICES)])  7.43 us
    pallas_call x1, Pallas kernels, load_step(): pl.pallas_call(load_kernel, out_shape=(array(*sent.shape), wide, wide, wi...  5.02 us
    ppermute x6, waiting for transfers between devices, crossed(): lax.ppermute(value, 'leaf', [(i, partner(i)) for i in range(DEVICES)])  4.9 us
    pallas_call x1, Pallas kernels, first_step(): pl.pallas_call(functools.partial(first_kernel, points), out_shape=(array(...  4.32 us
    pallas_call x1, Pallas kernels, grams_step(): pl.pallas_call(grams_kernel, out_shape=(array(*sent.shape), array(RHS, 2...  3.56 us
    pallas_call x1, Pallas kernels, last_step(): pl.pallas_call(last_kernel, out_shape=array(*cur.shape), in_specs=[SMEM]...  2.66 us
  transfers between devices with their start and end apart: 19, of which 9 were waited for; matrix products, arithmetic and copies ran while one was open for 0% of the time, Pallas kernels for 20%

profile of v7, /device:TPU:1, one launch (start us, length us, event | category | flops | bytes accessed | tf_op | source)
XLA Modules:
  0.0 58.8 jit_solution(12752576904684855110)
XLA Ops:
  0.1 4.3 %project_low.1 = (f32[128,128]{1,0:T(8,128)S(1)}, f32[128,128]{1,0:T(8,128)S(1)}) custom-call(s32[12]{0:T(128)S(1)} %stack.77.info_ref, f32[64,4096]{1,0:T(8,128)} %rhs_ref.5, f32[4,128,4096]{2,1,0:T(8,128)} %basis_ref.3, f32[4,128,4096]{2,1,0:T(8,128)} %gen_ref.5), custom_call_target="tpu_custom_call" | custom-call | flops 800000000 | bytes 7340032 | tf_op jit(solution)/shard_map/project_low/pallas_call | solution.py:126
  4.4 1.5 %collective-permute-start = (f32[128,128]{1,0:T(8,128)S(1)}, f32[128,128]{1,0:T(8,128)S(1)}, u32[]{:S(2)}, u32[]{:S(2)}) collective-permute-start(f32[128,128]{1,0:T(8,128)S(1)} %get-tuple-element.27), channel_id=1, source_target_pairs={{0,1},{1,0},{2,3},{3,2},{4,5},{5,4},{6,7},{7,6},{8,9},{9,8},{10,11... | collective-permute-start | bytes 196616 | tf_op jit(solution)/shard_map/ppermute | solution.py:360
  5.9 0.9 %collective-permute-done = f32[128,128]{1,0:T(8,128)S(1)} collective-permute-done((f32[128,128]{1,0:T(8,128)S(1)}, f32[128,128]{1,0:T(8,128)S(1)}, u32[]{:S(2)}, u32[]{:S(2)}) %collective-permute-start) | collective-permute-done | bytes 65568 | tf_op jit(solution)/shard_map/ppermute | solution.py:360
  6.8 3.9 %collective-permute-start.3 = (f32[128,128]{1,0:T(8,128)S(1)}, f32[128,128]{1,0:T(8,128)S(1)}, u32[]{:S(2)}, u32[]{:S(2)}) collective-permute-start(f32[128,128]{1,0:T(8,128)S(1)} %add.53.sent_ref), channel_id=1, source_target_pairs={{0,6},{1,7},{2,4},{3,5},{4,2},{5,3},{6,0},{7,1},{8,14},{9,15},{10,... | collective-permute-start | bytes 196616 | tf_op jit(solution)/shard_map/ppermute | solution.py:360
  10.8 0.7 %collective-permute-start.1 = (f32[128,128]{1,0:T(8,128)S(1)}, f32[128,128]{1,0:T(8,128)S(1)}, u32[]{:S(2)}, u32[]{:S(2)}) collective-permute-start(f32[128,128]{1,0:T(8,128)S(1)} %add.53.sent_ref), channel_id=1, source_target_pairs={{0,2},{1,3},{2,0},{3,1},{4,6},{5,7},{6,4},{7,5},{8,10},{9,11},{10,... | collective-permute-start | bytes 196616 | tf_op jit(solution)/shard_map/ppermute | solution.py:360
  11.4 5.0 %load_high.1 = (f32[128,128]{1,0:T(8,128)S(1)}, f32[128,4096]{1,0:T(8,128)S(1)}, f32[128,4096]{1,0:T(8,128)S(1)}, f32[128,4096]{1,0:T(8,128)S(1)}, f32[128,4096]...) custom-call(s32[12]{0:T(128)S(1)} %stack.77.info_ref, f32[4,128,4096]{2,1,0:T(8,128)} %basis_ref.3, ...), custom_call_target="tpu_custom_call" | custom-call | flops 1000 | bytes 12058624 | tf_op jit(solution)/shard_map/load_high/pallas_call | solution.py:160
  16.5 2.6 %collective-permute-start.6 = (f32[128,128]{1,0:T(8,128)S(1)}, f32[128,128]{1,0:T(8,128)S(1)}, u32[]{:S(2)}, u32[]{:S(2)}) collective-permute-start(f32[128,128]{1,0:T(8,128)S(1)} %add_add_fusion.2.sent_ref), channel_id=1, source_target_pairs={{0,24},{1,25},{2,26},{3,27},{4,28},{5,29},{6,30},{7,31},{8,16},{9,... | collective-permute-start | bytes 196616 | tf_op jit(solution)/shard_map/ppermute | solution.py:360
  19.1 0.5 collective-permute-start.5
  19.9 3.6 %grams_high.1 = (f32[128,128]{1,0:T(8,128)S(1)}, f32[64,256]{1,0:T(8,128)S(1)}, f32[256,256]{1,0:T(8,128)S(1)}, f32[128,128]{1,0:T(8,128)S(1)}) custom-call(f32[64,4096]{1,0:T(8,128)S(1)} %copy-done, f32[128,4096]{1,0:T(8,128)S(1)} %get-tuple-element.30.v1_ref, f32[128,4096]{1,0:T(8,128)S(1)} %get-tuple-element.31.v0_ref, ...), custom_call_target="tpu_custom_call" | custom-call | flops 3200000000 | bytes 11534336 | tf_op jit(solution)/shard_map/grams_high/pallas_call | solution.py:187
  23.4 0.3 collective-permute-done.5
  23.7 2.5 %collective-permute-start.7 = (f32[4,128,128]{2,1,0:T(8,128)S(1)}, f32[4,128,128]{2,1,0:T(8,128)S(1)}, u32[]{:S(2)}, u32[]{:S(2)}) collective-permute-start(f32[4,128,128]{2,1,0:T(8,128)S(1)} %pad_maximum_fusion.mine_ref), channel_id=1, source_target_pairs={{0,1},{1,0},{2,3},{3,2},{4,5},{5,4},{6,7},{7,6},{8,9},{9,8},{10,11... | collective-permute-start | bytes 786440 | tf_op jit(solution)/shard_map/ppermute | solution.py:360
  26.2 1.2 %collective-permute-done.7.other_ref = f32[4,128,128]{2,1,0:T(8,128)S(1)} collective-permute-done((f32[4,128,128]{2,1,0:T(8,128)S(1)}, f32[4,128,128]{2,1,0:T(8,128)S(1)}, u32[]{:S(2)}, u32[]{:S(2)}) %collective-permute-start.7) | collective-permute-done | bytes 262176 | tf_op jit(solution)/shard_map/ppermute | solution.py:360
  27.4 1.3 %coefficients_low.1 = (f32[64,256]{1,0:T(8,128)S(1)}, f32[128,128]{1,0:T(8,128)S(1)}, f32[128,128]{1,0:T(8,128)S(1)}) custom-call(s32[12]{0:T(128)S(1)} %stack.77.info_ref, f32[4,128,128]{2,1,0:T(8,128)S(1)} %pad_maximum_fusion.mine_ref, f32[4,128,128]{2,1,0:T(8,128)S(1)} %collective-permute-done.7.other_ref, f32[6,256,256]{2,1,0:T(8,128)S(1)} %get-tuple-element.35.caps_ref, ...), custom_call_target="tpu_custom_call" | custom-call | flops 120000000 | bytes 1500000 | tf_op jit(solution)/shard_map/coefficients_low/pallas_call | solution.py:255
  28.6 0.5 collective-permute-start.8
  29.1 0.9 %collective-permute-done.8 = f32[128,128]{1,0:T(8,128)S(1)} collective-permute-done((f32[128,128]{1,0:T(8,128)S(1)}, f32[128,128]{1,0:T(8,128)S(1)}, u32[]{:S(2)}, u32[]{:S(2)}) %collective-permute-start.8) | collective-permute-done | bytes 65568 | tf_op jit(solution)/shard_map/ppermute | solution.py:360
  30.0 2.9 %collective-permute-start.11 = (f32[128,128]{1,0:T(8,128)S(1)}, f32[128,128]{1,0:T(8,128)S(1)}, u32[]{:S(2)}, u32[]{:S(2)}) collective-permute-start(f32[128,128]{1,0:T(8,128)S(1)} %add.57.sent_ref), channel_id=1, source_target_pairs={{0,24},{1,7},{2,4},{3,27},{4,2},{5,29},{6,30},{7,1},{8,14},{9,17},... | collective-permute-start | bytes 196616 | tf_op jit(solution)/shard_map/ppermute | solution.py:372
  33.1 0.7 %collective-permute-start.9 = (f32[128,128]{1,0:T(8,128)S(1)}, f32[128,128]{1,0:T(8,128)S(1)}, u32[]{:S(2)}, u32[]{:S(2)}) collective-permute-start(f32[128,128]{1,0:T(8,128)S(1)} %add.57.sent_ref), channel_id=1, source_target_pairs={{0,9},{1,2},{2,1},{3,10},{4,7},{5,12},{6,15},{7,4},{8,11},{9,0},{1... | collective-permute-start | bytes 196616 | tf_op jit(solution)/shard_map/ppermute | solution.py:372
  33.8 1.0 %update_low.1 = (f32[64,4096]{1,0:T(8,128)S(1)}, f32[128,128]{1,0:T(8,128)S(1)}) custom-call(f32[64,256]{1,0:T(8,128)S(1)} %get-tuple-element.39.t_ref, f32[64,4096]{1,0:T(8,128)S(1)} %copy-done, f32[128,4096]{1,0:T(8,128)S(1)} %get-tuple-element.32.u3_ref, f32[128,4096]{1,0:T(8,128)S(1)} %get-tuple-element.33.u2_ref, f32[128,128]{1,0:T(8,128)S(1)} %add.57.sent_ref), custom_call_target="tpu_custom_call" | custom-call | flops 402653184 | bytes 6291456 | tf_op jit(solution)/shard_map/update_low/pallas_call | solution.py:278
  34.9 3.2 %collective-permute-done.10 = f32[128,128]{1,0:T(8,128)S(1)} collective-permute-done((f32[128,128]{1,0:T(8,128)S(1)}, f32[128,128]{1,0:T(8,128)S(1)}, u32[]{:S(2)}, u32[]{:S(2)}) %collective-permute-start.10) | collective-permute-done | bytes 65568 | tf_op jit(solution)/shard_map/ppermute | solution.py:372
  38.1 1.7 %collective-permute-start.14 = (f32[128,128]{1,0:T(8,128)S(1)}, f32[128,128]{1,0:T(8,128)S(1)}, u32[]{:S(2)}, u32[]{:S(2)}) collective-permute-start(f32[128,128]{1,0:T(8,128)S(1)} %add_add_fusion.1.sent_ref), channel_id=1, source_target_pairs={{0,6},{1,25},{2,26},{3,5},{4,28},{5,3},{6,0},{7,31},{8,16},{9,15},... | collective-permute-start | bytes 196616 | tf_op jit(solution)/shard_map/ppermute | solution.py:372
  39.8 1.3 %collective-permute-start.13 = (f32[128,128]{1,0:T(8,128)S(1)}, f32[128,128]{1,0:T(8,128)S(1)}, u32[]{:S(2)}, u32[]{:S(2)}) collective-permute-start(f32[128,128]{1,0:T(8,128)S(1)} %add_add_fusion.1.sent_ref), channel_id=1, source_target_pairs={{0,5},{1,16},{2,19},{3,6},{4,21},{5,0},{6,3},{7,22},{8,25},{9,12},... | collective-permute-start | bytes 196616 | tf_op jit(solution)/shard_map/ppermute | solution.py:372
  41.1 0.6 collective-permute-start.12
  41.7 1.9 %pairs_high.1 = (f32[128,128]{1,0:T(8,128)S(1)}, bf16[256,4096]{1,0:T(8,128)(2,1)S(1)}, bf16[256,4096]{1,0:T(8,128)(2,1)S(1)}) custom-call(f32[128,4096]{1,0:T(8,128)S(1)} %get-tuple-element.28.u1_ref, f32[4,128,4096]{2,1,0:T(8,128)} %gen_ref.5, f32[128,128]{1,0:T(8,128)S(1)} %add_add_fusion.1.sent_ref), custom_call_target="tpu_custom_call" | custom-call | flops 100000000 | bytes 8388608 | tf_op jit(solution)/shard_map/pairs_high/pallas_call | solution.py:300
  43.6 1.7 %collective-permute-done.13 = f32[128,128]{1,0:T(8,128)S(1)} collective-permute-done((f32[128,128]{1,0:T(8,128)S(1)}, f32[128,128]{1,0:T(8,128)S(1)}, u32[]{:S(2)}, u32[]{:S(2)}) %collective-permute-start.13) | collective-permute-done | bytes 65568 | tf_op jit(solution)/shard_map/ppermute | solution.py:372
  45.3 2.8 %collective-permute-start.17 = (f32[128,128]{1,0:T(8,128)S(1)}, f32[128,128]{1,0:T(8,128)S(1)}, u32[]{:S(2)}, u32[]{:S(2)}) collective-permute-start(f32[128,128]{1,0:T(8,128)S(1)} %add_add_fusion), channel_id=1, source_target_pairs={{0,96},{1,97},{2,98},{3,99},{4,100},{5,101},{6,102},{7,103},{8,104... | collective-permute-start | bytes 196616 | tf_op jit(solution)/shard_map/ppermute | solution.py:360
  48.2 0.3 collective-permute-start.16
  48.5 0.3 collective-permute-start.15
  48.8 1.3 %collective-permute-done.17 = f32[128,128]{1,0:T(8,128)S(1)} collective-permute-done((f32[128,128]{1,0:T(8,128)S(1)}, f32[128,128]{1,0:T(8,128)S(1)}, u32[]{:S(2)}, u32[]{:S(2)}) %collective-permute-start.17) | collective-permute-done | bytes 65568 | tf_op jit(solution)/shard_map/ppermute | solution.py:360
  50.1 2.6 %collective-permute-done.16 = f32[128,128]{1,0:T(8,128)S(1)} collective-permute-done((f32[128,128]{1,0:T(8,128)S(1)}, f32[128,128]{1,0:T(8,128)S(1)}, u32[]{:S(2)}, u32[]{:S(2)}) %collective-permute-start.16) | collective-permute-done | bytes 65568 | tf_op jit(solution)/shard_map/ppermute | solution.py:360
  52.8 2.2 %collective-permute-start.18 = (f32[4,128,128]{2,1,0:T(8,128)S(1)}, f32[4,128,128]{2,1,0:T(8,128)S(1)}, u32[]{:S(2)}, u32[]{:S(2)}) collective-permute-start(f32[4,128,128]{2,1,0:T(8,128)S(1)} %pad_maximum_fusion.1.mine_ref), channel_id=1, source_target_pairs={{0,1},{1,0},{2,3},{3,2},{4,5},{5,4},{6,7},{7,6},{8,9},{9,8},{10,11... | collective-permute-start | bytes 786440 | tf_op jit(solution)/shard_map/ppermute | solution.py:360
  55.0 1.2 %collective-permute-done.18.other_ref = f32[4,128,128]{2,1,0:T(8,128)S(1)} collective-permute-done((f32[4,128,128]{2,1,0:T(8,128)S(1)}, f32[4,128,128]{2,1,0:T(8,128)S(1)}, u32[]{:S(2)}, u32[]{:S(2)}) %collective-permute-start.18) | collective-permute-done | bytes 262176 | tf_op jit(solution)/shard_map/ppermute | solution.py:360
  56.1 2.7 %update_high.1 = f32[64,4096]{1,0:T(8,128)} custom-call(s32[12]{0:T(128)S(1)} %stack.77.info_ref, f32[4,128,128]{2,1,0:T(8,128)S(1)} %pad_maximum_fusion.1.mine_ref, f32[4,128,128]{2,1,0:T(8,128)S(1)} %collective-permute-done.18.other_ref, f32[6,256,256]{2,1,0:T(8,128)S(1)} %get-tuple-element.35.caps_ref, f32[64,4096]{1,0:T(8,128)S(1)} %get-tuple-element.44.cur_ref, ...), custom_call_target="tpu_custom_call" | custom-call | flops 500000000 | bytes 7000000 | tf_op jit(solution)/shard_map/update_high/pallas_call | solution.py:347
  (23 shorter events, 0.7 us)
Async XLA Ops:
  4.4 2.4 %collective-permute-start = (f32[128,128]{1,0:T(8,128)S(1)}, f32[128,128]{1,0:T(8,128)S(1)}, u32[]{:S(2)}, u32[]{:S(2)}) collective-permute-start(f32[128,128]{1,0:T(8,128)S(1)} %get-tuple-element.27), channel_id=1, source_target_pairs={{0,1},{1,0},{2,3},{3,2},{4,5},{5,4},{6,7},{7,6},{8,9},{9,8},{10,11... | collective-permute-start | bytes 196616 | tf_op jit(solution)/shard_map/ppermute | solution.py:360
  6.8 13.0 %copy-start = (f32[64,4096]{1,0:T(8,128)S(1)}, f32[64,4096]{1,0:T(8,128)}, u32[]{:S(2)}) copy-start(f32[64,4096]{1,0:T(8,128)} %rhs_ref.5) | copy-start | bytes 3145732
  6.8 9.6 %collective-permute-start.3 = (f32[128,128]{1,0:T(8,128)S(1)}, f32[128,128]{1,0:T(8,128)S(1)}, u32[]{:S(2)}, u32[]{:S(2)}) collective-permute-start(f32[128,128]{1,0:T(8,128)S(1)} %add.53.sent_ref), channel_id=1, source_target_pairs={{0,6},{1,7},{2,4},{3,5},{4,2},{5,3},{6,0},{7,1},{8,14},{9,15},{10,... | collective-permute-start | bytes 196616 | tf_op jit(solution)/shard_map/ppermute | solution.py:360
  10.8 5.7 %collective-permute-start.2 = (f32[128,128]{1,0:T(8,128)S(1)}, f32[128,128]{1,0:T(8,128)S(1)}, u32[]{:S(2)}, u32[]{:S(2)}) collective-permute-start(f32[128,128]{1,0:T(8,128)S(1)} %add.53.sent_ref), channel_id=1, source_target_pairs={{0,4},{1,5},{2,6},{3,7},{4,0},{5,1},{6,2},{7,3},{8,12},{9,13},{10,... | collective-permute-start | bytes 196616 | tf_op jit(solution)/shard_map/ppermute | solution.py:360
  10.8 5.7 %collective-permute-start.1 = (f32[128,128]{1,0:T(8,128)S(1)}, f32[128,128]{1,0:T(8,128)S(1)}, u32[]{:S(2)}, u32[]{:S(2)}) collective-permute-start(f32[128,128]{1,0:T(8,128)S(1)} %add.53.sent_ref), channel_id=1, source_target_pairs={{0,2},{1,3},{2,0},{3,1},{4,6},{5,7},{6,4},{7,5},{8,10},{9,11},{10,... | collective-permute-start | bytes 196616 | tf_op jit(solution)/shard_map/ppermute | solution.py:360
  16.5 6.9 %collective-permute-start.6 = (f32[128,128]{1,0:T(8,128)S(1)}, f32[128,128]{1,0:T(8,128)S(1)}, u32[]{:S(2)}, u32[]{:S(2)}) collective-permute-start(f32[128,128]{1,0:T(8,128)S(1)} %add_add_fusion.2.sent_ref), channel_id=1, source_target_pairs={{0,24},{1,25},{2,26},{3,27},{4,28},{5,29},{6,30},{7,31},{8,16},{9,... | collective-permute-start | bytes 196616 | tf_op jit(solution)/shard_map/ppermute | solution.py:360
  19.1 4.6 %collective-permute-start.5 = (f32[128,128]{1,0:T(8,128)S(1)}, f32[128,128]{1,0:T(8,128)S(1)}, u32[]{:S(2)}, u32[]{:S(2)}) collective-permute-start(f32[128,128]{1,0:T(8,128)S(1)} %add_add_fusion.2.sent_ref), channel_id=1, source_target_pairs={{0,16},{1,17},{2,18},{3,19},{4,20},{5,21},{6,22},{7,23},{8,24},{9,... | collective-permute-start | bytes 196616 | tf_op jit(solution)/shard_map/ppermute | solution.py:360
  19.6 4.1 %collective-permute-start.4 = (f32[128,128]{1,0:T(8,128)S(1)}, f32[128,128]{1,0:T(8,128)S(1)}, u32[]{:S(2)}, u32[]{:S(2)}) collective-permute-start(f32[128,128]{1,0:T(8,128)S(1)} %add_add_fusion.2.sent_ref), channel_id=1, source_target_pairs={{0,8},{1,9},{2,10},{3,11},{4,12},{5,13},{6,14},{7,15},{8,0},{9,1},... | collective-permute-start | bytes 196616 | tf_op jit(solution)/shard_map/ppermute | solution.py:360
  23.7 3.7 %collective-permute-start.7 = (f32[4,128,128]{2,1,0:T(8,128)S(1)}, f32[4,128,128]{2,1,0:T(8,128)S(1)}, u32[]{:S(2)}, u32[]{:S(2)}) collective-permute-start(f32[4,128,128]{2,1,0:T(8,128)S(1)} %pad_maximum_fusion.mine_ref), channel_id=1, source_target_pairs={{0,1},{1,0},{2,3},{3,2},{4,5},{5,4},{6,7},{7,6},{8,9},{9,8},{10,11... | collective-permute-start | bytes 786440 | tf_op jit(solution)/shard_map/ppermute | solution.py:360
  28.6 1.4 %collective-permute-start.8 = (f32[128,128]{1,0:T(8,128)S(1)}, f32[128,128]{1,0:T(8,128)S(1)}, u32[]{:S(2)}, u32[]{:S(2)}) collective-permute-start(f32[128,128]{1,0:T(8,128)S(1)} %get-tuple-element.41), channel_id=1, source_target_pairs={{0,1},{1,0},{2,3},{3,2},{4,5},{5,4},{6,7},{7,6},{8,9},{9,8},{10,11... | collective-permute-start | bytes 196616 | tf_op jit(solution)/shard_map/ppermute | solution.py:360
  30.0 4.9 %collective-permute-start.11 = (f32[128,128]{1,0:T(8,128)S(1)}, f32[128,128]{1,0:T(8,128)S(1)}, u32[]{:S(2)}, u32[]{:S(2)}) collective-permute-start(f32[128,128]{1,0:T(8,128)S(1)} %add.57.sent_ref), channel_id=1, source_target_pairs={{0,24},{1,7},{2,4},{3,27},{4,2},{5,29},{6,30},{7,1},{8,14},{9,17},... | collective-permute-start | bytes 196616 | tf_op jit(solution)/shard_map/ppermute | solution.py:372
  32.9 5.2 %collective-permute-start.10 = (f32[128,128]{1,0:T(8,128)S(1)}, f32[128,128]{1,0:T(8,128)S(1)}, u32[]{:S(2)}, u32[]{:S(2)}) collective-permute-start(f32[128,128]{1,0:T(8,128)S(1)} %add.57.sent_ref), channel_id=1, source_target_pairs={{0,17},{1,4},{2,7},{3,18},{4,1},{5,20},{6,23},{7,2},{8,13},{9,24},... | collective-permute-start | bytes 196616 | tf_op jit(solution)/shard_map/ppermute | solution.py:372
  33.1 5.0 %collective-permute-start.9 = (f32[128,128]{1,0:T(8,128)S(1)}, f32[128,128]{1,0:T(8,128)S(1)}, u32[]{:S(2)}, u32[]{:S(2)}) collective-permute-start(f32[128,128]{1,0:T(8,128)S(1)} %add.57.sent_ref), channel_id=1, source_target_pairs={{0,9},{1,2},{2,1},{3,10},{4,7},{5,12},{6,15},{7,4},{8,11},{9,0},{1... | collective-permute-start | bytes 196616 | tf_op jit(solution)/shard_map/ppermute | solution.py:372
  38.1 5.5 %collective-permute-start.14 = (f32[128,128]{1,0:T(8,128)S(1)}, f32[128,128]{1,0:T(8,128)S(1)}, u32[]{:S(2)}, u32[]{:S(2)}) collective-permute-start(f32[128,128]{1,0:T(8,128)S(1)} %add_add_fusion.1.sent_ref), channel_id=1, source_target_pairs={{0,6},{1,25},{2,26},{3,5},{4,28},{5,3},{6,0},{7,31},{8,16},{9,15},... | collective-permute-start | bytes 196616 | tf_op jit(solution)/shard_map/ppermute | solution.py:372
  39.8 5.5 %collective-permute-start.13 = (f32[128,128]{1,0:T(8,128)S(1)}, f32[128,128]{1,0:T(8,128)S(1)}, u32[]{:S(2)}, u32[]{:S(2)}) collective-permute-start(f32[128,128]{1,0:T(8,128)S(1)} %add_add_fusion.1.sent_ref), channel_id=1, source_target_pairs={{0,5},{1,16},{2,19},{3,6},{4,21},{5,0},{6,3},{7,22},{8,25},{9,12},... | collective-permute-start | bytes 196616 | tf_op jit(solution)/shard_map/ppermute | solution.py:372
  41.1 4.2 %collective-permute-start.12 = (f32[128,128]{1,0:T(8,128)S(1)}, f32[128,128]{1,0:T(8,128)S(1)}, u32[]{:S(2)}, u32[]{:S(2)}) collective-permute-start(f32[128,128]{1,0:T(8,128)S(1)} %add_add_fusion.1.sent_ref), channel_id=1, source_target_pairs={{0,3},{1,8},{2,11},{3,0},{4,13},{5,6},{6,5},{7,14},{8,1},{9,10},{1... | collective-permute-start | bytes 196616 | tf_op jit(solution)/shard_map/ppermute | solution.py:372
  45.3 4.8 %collective-permute-start.17 = (f32[128,128]{1,0:T(8,128)S(1)}, f32[128,128]{1,0:T(8,128)S(1)}, u32[]{:S(2)}, u32[]{:S(2)}) collective-permute-start(f32[128,128]{1,0:T(8,128)S(1)} %add_add_fusion), channel_id=1, source_target_pairs={{0,96},{1,97},{2,98},{3,99},{4,100},{5,101},{6,102},{7,103},{8,104... | collective-permute-start | bytes 196616 | tf_op jit(solution)/shard_map/ppermute | solution.py:360
  48.2 4.6 %collective-permute-start.16 = (f32[128,128]{1,0:T(8,128)S(1)}, f32[128,128]{1,0:T(8,128)S(1)}, u32[]{:S(2)}, u32[]{:S(2)}) collective-permute-start(f32[128,128]{1,0:T(8,128)S(1)} %add_add_fusion), channel_id=1, source_target_pairs={{0,64},{1,65},{2,66},{3,67},{4,68},{5,69},{6,70},{7,71},{8,72},{9,... | collective-permute-start | bytes 196616 | tf_op jit(solution)/shard_map/ppermute | solution.py:360
  48.5 4.3 %collective-permute-start.15 = (f32[128,128]{1,0:T(8,128)S(1)}, f32[128,128]{1,0:T(8,128)S(1)}, u32[]{:S(2)}, u32[]{:S(2)}) collective-permute-start(f32[128,128]{1,0:T(8,128)S(1)} %add_add_fusion), channel_id=1, source_target_pairs={{0,32},{1,33},{2,34},{3,35},{4,36},{5,37},{6,38},{7,39},{8,40},{9,... | collective-permute-start | bytes 196616 | tf_op jit(solution)/shard_map/ppermute | solution.py:360
  52.8 3.3 %collective-permute-start.18 = (f32[4,128,128]{2,1,0:T(8,128)S(1)}, f32[4,128,128]{2,1,0:T(8,128)S(1)}, u32[]{:S(2)}, u32[]{:S(2)}) collective-permute-start(f32[4,128,128]{2,1,0:T(8,128)S(1)} %pad_maximum_fusion.1.mine_ref), channel_id=1, source_target_pairs={{0,1},{1,0},{2,3},{3,2},{4,5},{5,4},{6,7},{7,6},{8,9},{9,8},{10,11... | collective-permute-start | bytes 786440 | tf_op jit(solution)/shard_map/ppermute | solution.py:360

commit v8 on v7

--- a/solution.py
+++ b/solution.py
@@ -15,7 +15,6 @@
 LIMITS = (53, 39, 38, 38, 40, 40, 44)
 HBM = pl.BlockSpec(memory_space=pltpu.HBM)
 VMEM = pl.BlockSpec(memory_space=pltpu.VMEM)
-SMEM = pl.BlockSpec(memory_space=pltpu.SMEM)
 
 CORE = 1
 Z_MASKS = (6, 4, 2)
@@ -25,6 +24,15 @@
 Y_PLACES = (3, 0, 1, 2)
 
 
+def position():
+    device = lax.axis_index("leaf").astype(jnp.int32)
+    return device, [device >> k & 1 for k in range(7)]
+
+
+def half_of(bit):
+    return bit[0] ^ bit[1] ^ bit[2] ^ bit[3] ^ bit[4]
+
+
 def split(value):
     high = value.astype(BF16)
     return high, (value - high.astype(F32)).astype(BF16)
@@ -41,6 +49,13 @@
     rows = left.shape[0]
     both = jnp.dot(jnp.concatenate([lh, ll], axis=0), rh, preferred_element_type=F32)
     return both[:rows] + both[rows:] + jnp.dot(lh, rl, preferred_element_type=F32)
+
+
+def product_of(left, high, low):
+    lh, ll = split(left)
+    rows = left.shape[0]
+    both = jnp.dot(jnp.concatenate([lh, ll], axis=0), high, preferred_element_type=F32)
+    return both[:rows] + both[rows:] + jnp.dot(lh, low, preferred_element_type=F32)
 
 
 def contract(left, right):
@@ -88,7 +103,7 @@
 PARTS = (2, 2, 2, 2)
 
 
-def first_kernel(points, info_ref, rhs_ref, basis_ref, gen_ref, keep_ref, send_ref,
+def first_kernel(points, rhs_ref, basis_ref, gen_ref, keep_ref, send_ref,
                  rhs_buf, v3_buf, v2_buf, u3_buf, acc2, acc3, sems):
     sources = ((rhs_ref, None, rhs_buf), (basis_ref, 3, v3_buf), (basis_ref, 2, v2_buf), (gen_ref, 3, u3_buf))
     for i, (cols, row) in enumerate(fetch(sources, sems, PARTS, points)):
@@ -101,7 +116,7 @@
     p3 = fold(acc3[...], RHS)
     p2 = fold(acc2[: 2 * RHS], RHS)
     g32 = fold(acc2[2 * RHS :], RANK)
-    first = info_ref[0] == 0
+    first = position()[1][0] == 0
 
     @pl.when(first)
     def _():
@@ -120,13 +135,17 @@
     return jax.ShapeDtypeStruct(shape, F32)
 
 
-def first_step(info, rhs, basis, gen):
+def half_array(*shape):
+    return jax.ShapeDtypeStruct(shape, BF16)
+
+
+def first_step(rhs, basis, gen):
     points = rhs.shape[1]
     wide = pltpu.VMEM((RANK, points), F32)
     return pl.pallas_call(
         functools.partial(first_kernel, points),
         out_shape=(array(RANK, RANK), array(RANK, RANK)),
-        in_specs=[SMEM, HBM, HBM, HBM],
+        in_specs=[HBM, HBM, HBM],
         out_specs=(VMEM,) * 2,
         scratch_shapes=[
             pltpu.VMEM((RHS, points), F32), wide, wide, wide,
@@ -137,16 +156,19 @@
         compiler_params=params(LIMITS[0]),
         cost_estimate=pl.CostEstimate(flops=800_000_000, bytes_accessed=7_340_032, transcendentals=0),
         name="project_low",
-    )(info, rhs, basis, gen)
-
-
-def load_kernel(info_ref, basis_ref, gen_ref, cap_ref, sent_ref, sent_out,
+    )(rhs, basis, gen)
+
+
+def load_kernel(basis_ref, gen_ref, cap_ref, sent_ref, sent_out,
                 v1_ref, v0_ref, u3_ref, u2_ref, u1_ref, caps_ref, sems):
     sources = [
         (basis_ref, 1, v1_ref), (basis_ref, 0, v0_ref),
         (gen_ref, 3, u3_ref), (gen_ref, 2, u2_ref), (gen_ref, 1, u1_ref),
     ]
-    sources += [(cap_ref, info_ref[6 + i], caps_ref.at[i]) for i in range(6)]
+    device, _ = position()
+    n3, n2, n1 = device >> 4, device >> 5, device >> 6
+    nodes = (7 + n3, 7 + (n3 ^ 1), 3 + n2, 1 + n1, 1 + (n1 ^ 1), 0)
+    sources += [(cap_ref, node, caps_ref.at[i]) for i, node in enumerate(nodes)]
     copies = [pltpu.make_async_copy(ref.at[k], out, sems.at[i]) for i, (ref, k, out) in enumerate(sources)]
     for copy in copies:
         copy.start()
@@ -155,22 +177,40 @@
         copy.wait()
 
 
-def load_step(info, basis, gen, cap, sent):
+def load_step(basis, gen, cap, sent):
     wide = array(*basis.shape[1:])
     return pl.pallas_call(
         load_kernel,
         out_shape=(array(*sent.shape), wide, wide, wide, wide, wide, array(6, 2 * RANK, 2 * RANK)),
-        in_specs=[SMEM, HBM, HBM, HBM, VMEM],
+        in_specs=[HBM, HBM, HBM, VMEM],
         out_specs=(VMEM,) * 7,
         scratch_shapes=[pltpu.SemaphoreType.DMA((11,))],
         compiler_params=params(LIMITS[1]),
         cost_estimate=pl.CostEstimate(flops=1_000, bytes_accessed=12_058_624, transcendentals=0),
         name="load_high",
-    )(info, basis, gen, cap, sent)
-
-
-def grams_kernel(rhs_ref, v1_ref, v0_ref, u3_ref, u2_ref, u1_ref, sent_ref, sent_out, p_ref, g_ref, g10_ref):
+    )(basis, gen, cap, sent)
+
+
+def ordered(caps_ref, base, s_high, s_low, high_ref, low_ref):
+    for i, (s, columns) in enumerate(((s_high, 2), (s_high, 2), (s_low, 1))):
+        for r, row in enumerate((1 - s, s)):
+            for c, col in enumerate((s, 1 - s)[:columns]):
+                high, low = split(
+                    caps_ref[
+                        base + i,
+                        pl.ds(pl.multiple_of(row * RANK, RANK), RANK),
+                        pl.ds(pl.multiple_of(col * RANK, RANK), RANK),
+                    ]
+                )
+                high_ref[i, r * RANK : (r + 1) * RANK, c * RANK : (c + 1) * RANK] = high
+                low_ref[i, r * RANK : (r + 1) * RANK, c * RANK : (c + 1) * RANK] = low
+
+
+def grams_kernel(rhs_ref, v1_ref, v0_ref, u3_ref, u2_ref, u1_ref, caps_ref, sent_ref, sent_out,
+                 p_ref, gh_ref, gl_ref, g10_ref, ch_ref, cl_ref):
     sent_out[...] = sent_ref[...]
+    _, bit = position()
+    ordered(caps_ref, 0, bit[3], bit[4], ch_ref, cl_ref)
     left = stacked([rhs_ref[...], u3_ref[...]])
     u2 = stacked([u2_ref[...]])
     for k, ref in enumerate((v1_ref, v0_ref)):
@@ -178,42 +218,30 @@
         cols = slice(k * RANK, (k + 1) * RANK)
         both = fold(contract(left, right), RHS + RANK)
         p_ref[:, cols] = both[:RHS]
-        g_ref[:RANK, cols] = both[RHS:]
-        g_ref[RANK:, cols] = fold(contract(u2, right), RANK)
+        gh_ref[:RANK, cols], gl_ref[:RANK, cols] = split(both[RHS:])
+        gh_ref[RANK:, cols], gl_ref[RANK:, cols] = split(fold(contract(u2, right), RANK))
     g10_ref[...] = fold(contract(stacked([u1_ref[...]]), right), RANK)
 
 
-def grams_step(rhs, v1, v0, u3, u2, u1, sent):
+def grams_step(rhs, v1, v0, u3, u2, u1, caps, sent):
     return pl.pallas_call(
         grams_kernel,
-        out_shape=(array(*sent.shape), array(RHS, 2 * RANK), array(2 * RANK, 2 * RANK), array(RANK, RANK)),
-        in_specs=[VMEM] * 7,
-        out_specs=(VMEM,) * 4,
+        out_shape=(
+            array(*sent.shape), array(RHS, 2 * RANK), half_array(2 * RANK, 2 * RANK), half_array(2 * RANK, 2 * RANK),
+            array(RANK, RANK), half_array(3, 2 * RANK, 2 * RANK), half_array(3, 2 * RANK, 2 * RANK),
+        ),
+        in_specs=[VMEM] * 8,
+        out_specs=(VMEM,) * 7,
         compiler_params=params(LIMITS[2]),
         cost_estimate=pl.CostEstimate(flops=3_200_000_000, bytes_accessed=11_534_336, transcendentals=0),
         name="grams_high",
-    )(rhs, v1, v0, u3, u2, u1, sent)
-
-
-def related(caps_ref, node, s, columns):
-    blocks = []
-    for row in (1 - s, s):
-        rows = pl.ds(pl.multiple_of(row * RANK, RANK), RANK)
-        blocks.append(
-            jnp.concatenate(
-                [
-                    caps_ref[node, rows, pl.ds(pl.multiple_of(col * RANK, RANK), RANK)]
-                    for col in (s, 1 - s)[:columns]
-                ],
-                axis=1,
-            )
-        )
-    return jnp.concatenate(blocks, axis=0)
-
-
-def middle_kernel(info_ref, mine_ref, other_ref, caps_ref, p_ref, g_ref, g10_ref,
+    )(rhs, v1, v0, u3, u2, u1, caps, sent)
+
+
+def middle_kernel(mine_ref, other_ref, ch_ref, cl_ref, p_ref, gh_ref, gl_ref, g10_ref,
                   t_ref, keep_ref, send_ref):
-    first = info_ref[0] == 0
+    _, bit = position()
+    first = bit[0] == 0
     p, g = [], []
     for m in range(4):
         mine, other = mine_ref[X_PLACES[m]], other_ref[X_PLACES[m]]
@@ -222,13 +250,13 @@
     t = []
     for pair in (0, 2):
         joined = jnp.concatenate([p[pair][:RHS], p[pair + 1][:RHS]], axis=1)
-        both = product(joined, related(caps_ref, pair // 2, info_ref[2], 2))
+        both = product_of(joined, ch_ref[pair // 2], cl_ref[pair // 2])
         t += [both[:, :RANK], both[:, RANK:]]
     q2 = [p[m][RHS:] - product(t[m], g[m]) for m in range(4)]
     joined = jnp.concatenate([q2[0] + q2[1], q2[2] + q2[3]], axis=1)
-    coeff = jnp.concatenate([t[0], product(joined, related(caps_ref, 2, info_ref[3], 1))], axis=1)
+    coeff = jnp.concatenate([t[0], product_of(joined, ch_ref[2, :, :RANK], cl_ref[2, :, :RANK])], axis=1)
     t_ref[...] = coeff
-    q = p_ref[...] - product(coeff, g_ref[...])
+    q = p_ref[...] - product_of(coeff, gh_ref[...], gl_ref[...])
     half = RHS // 2
 
     def put(ref, c):
@@ -237,7 +265,7 @@
         ref[half : 2 * half] = q[rows, RANK:]
         ref[2 * half :] = g10_ref[c * RHS : (c + 1) * RHS]
 
-    low_half = info_ref[1] == 0
+    low_half = half_of(bit) == 0
 
     @pl.when(low_half)
     def _():
@@ -250,17 +278,17 @@
         put(send_ref, 0)
 
 
-def middle_step(info, mine, other, caps, p, g, g10):
+def middle_step(mine, other, ch, cl, p, gh, gl, g10):
     half = jax.ShapeDtypeStruct((RANK, RANK), F32)
     return pl.pallas_call(
         middle_kernel,
         out_shape=(jax.ShapeDtypeStruct((RHS, 2 * RANK), F32), half, half),
-        in_specs=[SMEM] + [VMEM] * 6,
+        in_specs=[VMEM] * 8,
         out_specs=(VMEM,) * 3,
         compiler_params=params(LIMITS[3]),
         cost_estimate=pl.CostEstimate(flops=120_000_000, bytes_accessed=1_500_000, transcendentals=0),
         name="coefficients_low",
-    )(info, mine, other, caps, p, g, g10)
+    )(mine, other, ch, cl, p, gh, gl, g10)
 
 
 def low_update_kernel(t_ref, rhs_ref, u3_ref, u2_ref, sent_ref, cur_ref, sent_out):
@@ -286,32 +314,34 @@
     )(t, rhs, u3, u2, sent)
 
 
-def pairs_kernel(u1_ref, gen_ref, sent_ref, sent_out, high_ref, low_ref, u0_ref, sem):
+def pairs_kernel(u1_ref, gen_ref, caps_ref, sent_ref, sent_out, high_ref, low_ref, ch_ref, cl_ref, u0_ref, sem):
     copy = pltpu.make_async_copy(gen_ref.at[0], u0_ref, sem)
     copy.start()
     sent_out[...] = sent_ref[...]
+    _, bit = position()
+    ordered(caps_ref, 3, bit[5], bit[6], ch_ref, cl_ref)
     high_ref[:RANK], low_ref[:RANK] = split(u1_ref[...])
     copy.wait()
     high_ref[RANK:], low_ref[RANK:] = split(u0_ref[...])
 
 
-def pairs_step(u1, gen, sent):
-    pair = jax.ShapeDtypeStruct((2 * RANK, u1.shape[1]), BF16)
+def pairs_step(u1, gen, caps, sent):
+    pair, nodes = half_array(2 * RANK, u1.shape[1]), half_array(3, 2 * RANK, 2 * RANK)
     return pl.pallas_call(
         pairs_kernel,
-        out_shape=(array(*sent.shape), pair, pair),
-        in_specs=[VMEM, HBM, VMEM],
-        out_specs=(VMEM,) * 3,
+        out_shape=(array(*sent.shape), pair, pair, nodes, nodes),
+        in_specs=[VMEM, HBM, VMEM, VMEM],
+        out_specs=(VMEM,) * 5,
         scratch_shapes=[pltpu.VMEM(u1.shape, F32), pltpu.SemaphoreType.DMA(())],
         compiler_params=params(LIMITS[5]),
         cost_estimate=pl.CostEstimate(flops=100_000_000, bytes_accessed=8_388_608, transcendentals=0),
         name="pairs_high",
-    )(u1, gen, sent)
-
-
-def last_kernel(info_ref, mine_ref, other_ref, caps_ref, cur_ref, high_ref, low_ref, out_ref,
+    )(u1, gen, caps, sent)
+
+
+def last_kernel(mine_ref, other_ref, ch_ref, cl_ref, cur_ref, high_ref, low_ref, out_ref,
                 buf, sems):
-    first = info_ref[1] == 0
+    first = half_of(position()[1]) == 0
     half = RHS // 2
     q1, q0, g = [], [], []
     for m in range(4):
@@ -323,13 +353,12 @@
         g.append(jnp.concatenate([low[RHS:], high[RHS:]], axis=0))
     t = []
     for pair in (0, 2):
-        both = product(
-            jnp.concatenate([q1[pair], q1[pair + 1]], axis=1), related(caps_ref, 3 + pair // 2, info_ref[4], 2)
-        )
+        joined = jnp.concatenate([q1[pair], q1[pair + 1]], axis=1)
+        both = product_of(joined, ch_ref[pair // 2], cl_ref[pair // 2])
         t += [both[:, :RANK], both[:, RANK:]]
     r = [q0[m] - product(t[m], g[m]) for m in range(4)]
     joined = jnp.concatenate([r[0] + r[1], r[2] + r[3]], axis=1)
-    th, tl = split(jnp.concatenate([t[0], product(joined, related(caps_ref, 5, info_ref[5], 1))], axis=1))
+    th, tl = split(jnp.concatenate([t[0], product_of(joined, ch_ref[2, :, :RANK], cl_ref[2, :, :RANK])], axis=1))
     left = jnp.concatenate([th, tl], axis=0)
     copies = []
     for i, cols in enumerate(spans((2,) * 4, cur_ref.shape[1])):
@@ -343,17 +372,17 @@
         copy.wait()
 
 
-def last_step(info, mine, other, caps, cur, high, low):
+def last_step(mine, other, ch, cl, cur, high, low):
     return pl.pallas_call(
         last_kernel,
         out_shape=array(*cur.shape),
-        in_specs=[SMEM] + [VMEM] * 6,
+        in_specs=[VMEM] * 7,
         out_specs=HBM,
         scratch_shapes=[pltpu.VMEM(cur.shape, F32), pltpu.SemaphoreType.DMA((4,))],
         compiler_params=params(LIMITS[6]),
         cost_estimate=pl.CostEstimate(flops=500_000_000, bytes_accessed=7_000_000, transcendentals=0),
         name="update_high",
-    )(info, mine, other, caps, cur, high, low)
+    )(mine, other, ch, cl, cur, high, low)
 
 
 def swap(value, mask):
@@ -383,32 +412,27 @@
 
 
 def body(rhs, basis, gen, cap):
-    device = lax.axis_index("leaf").astype(jnp.int32)
-    bit = [device >> k & 1 for k in range(7)]
-    n3, n2, n1 = device >> 4, device >> 5, device >> 6
-    half = bit[0] ^ bit[1] ^ bit[2] ^ bit[3] ^ bit[4]
-    info = jnp.stack([bit[0], half, *bit[3:], 7 + n3, 7 + (n3 ^ 1), 3 + n2, 1 + n1, 1 + (n1 ^ 1), jnp.zeros_like(n1)])
-    keep, send = first_step(info, rhs, basis, gen)
+    keep, send = first_step(rhs, basis, gen)
     chip = keep + swap(send, CORE)
     b, c, d = neighbours(chip, Z_MASKS)
-    chip, v1, v0, u3, u2, u1, caps = load_step(info, basis, gen, cap, chip)
+    chip, v1, v0, u3, u2, u1, caps = load_step(basis, gen, cap, chip)
     line = chip + b + c + d
     b, c, d = neighbours(line, X_MASKS)
-    line, p, g, g10 = grams_step(rhs, v1, v0, u3, u2, u1, line)
+    line, p, gh, gl, g10, ch, cl = grams_step(rhs, v1, v0, u3, u2, u1, caps, line)
     lines = jnp.stack([b, c, d, line])
     other = swap(lines, CORE)
-    t, keep, send = middle_step(info, lines, other, caps, p, g, g10)
+    t, keep, send = middle_step(lines, other, ch, cl, p, gh, gl, g10)
     chip = keep + swap(send, CORE)
     b, c, d = crossed_neighbours(chip, X_MASKS, Z_MASKS)
     current, chip = low_update(t, rhs, u3, u2, chip)
     part = chip + b + c + d
     b, c, d = crossed_neighbours(part, Z_MASKS, X_MASKS)
-    part, high, low = pairs_step(u1, gen, part)
+    part, high, low, ch, cl = pairs_step(u1, gen, caps, part)
     plane = part + b + c + d
     b, c, d = neighbours(plane, Y_MASKS)
     planes = jnp.stack([b, c, d, plane])
     other = swap(planes, CORE)
-    return last_step(info, planes, other, caps, current, high, low)
+    return last_step(planes, other, ch, cl, current, high, low)
 
 
 def solution(mesh):

time: 58.9 us -> 56.6 us (0.961)
  Pallas kernels: 19.7 us -> 17.4 us
  transfers between devices with their start and end apart: 19 -> 19, of which waited for: 9 -> 9; matrix products, arithmetic and copies ran while one was open for 0% -> 0% of each run, Pallas kernels for 20% -> 19%
where the time goes in v8:
time: 56.6 us; the launch traced here: 56.5 us
  starting transfers between devices  25.8 us (46%)
  Pallas kernels  17.4 us (31%)
  waiting for transfers between devices  13 us (23%)
    ppermute x13, starting transfers between devices, swap(): return lax.ppermute(value, 'leaf', [(i, i ^ mask) for i in range(DEVICES)])  18.6 us
    ppermute x13, waiting for transfers between devices, swap(): return lax.ppermute(value, 'leaf', [(i, i ^ mask) for i in range(DEVICES)])  8.35 us
    ppermute x6, starting transfers between devices, crossed(): lax.ppermute(value, 'leaf', [(i, partner(i)) for i in range(DEVICES)])  7.23 us
    ppermute x6, waiting for transfers between devices, crossed(): lax.ppermute(value, 'leaf', [(i, partner(i)) for i in range(DEVICES)])  4.67 us
    pallas_call x1, Pallas kernels, load_step(): pl.pallas_call(load_kernel, out_shape=(array(*sent.shape), wide, wide, wi...  4.48 us
    pallas_call x1, Pallas kernels, first_step(): pl.pallas_call(functools.partial(first_kernel, points), out_shape=(array(...  3.78 us
    pallas_call x1, Pallas kernels, grams_step(): pl.pallas_call(grams_kernel, out_shape=(array(*sent.shape), array(RHS, 2...  3.57 us
    pallas_call x1, Pallas kernels, last_step(): pl.pallas_call(last_kernel, out_shape=array(*cur.shape), in_specs=[VMEM]...  2.08 us
  transfers between devices with their start and end apart: 19, of which 9 were waited for; matrix products, arithmetic and copies ran while one was open for 0% of the time, Pallas kernels for 19%

profile of v8, /device:TPU:1, one launch (start us, length us, event | category | flops | bytes accessed | tf_op | source)
XLA Modules:
  0.0 56.5 jit_solution(6722299755344638049)
XLA Ops:
  0.0 3.8 %project_low.1 = (f32[128,128]{1,0:T(8,128)S(1)}, f32[128,128]{1,0:T(8,128)S(1)}) custom-call(f32[64,4096]{1,0:T(8,128)} %rhs_ref.5, f32[4,128,4096]{2,1,0:T(8,128)} %basis_ref.3, f32[4,128,4096]{2,1,0:T(8,128)} %gen_ref.5), custom_call_target="tpu_custom_call" | custom-call | flops 800000000 | bytes 7340032 | tf_op jit(solution)/shard_map/project_low/pallas_call | solution.py:145
  3.8 1.5 %collective-permute-start = (f32[128,128]{1,0:T(8,128)S(1)}, f32[128,128]{1,0:T(8,128)S(1)}, u32[]{:S(2)}, u32[]{:S(2)}) collective-permute-start(f32[128,128]{1,0:T(8,128)S(1)} %get-tuple-element.32), channel_id=1, source_target_pairs={{0,1},{1,0},{2,3},{3,2},{4,5},{5,4},{6,7},{7,6},{8,9},{9,8},{10,11... | collective-permute-start | bytes 196616 | tf_op jit(solution)/shard_map/ppermute | solution.py:389
  5.3 0.9 %collective-permute-done = f32[128,128]{1,0:T(8,128)S(1)} collective-permute-done((f32[128,128]{1,0:T(8,128)S(1)}, f32[128,128]{1,0:T(8,128)S(1)}, u32[]{:S(2)}, u32[]{:S(2)}) %collective-permute-start) | collective-permute-done | bytes 65568 | tf_op jit(solution)/shard_map/ppermute | solution.py:389
  6.2 3.9 %collective-permute-start.3 = (f32[128,128]{1,0:T(8,128)S(1)}, f32[128,128]{1,0:T(8,128)S(1)}, u32[]{:S(2)}, u32[]{:S(2)}) collective-permute-start(f32[128,128]{1,0:T(8,128)S(1)} %add.33.sent_ref), channel_id=1, source_target_pairs={{0,6},{1,7},{2,4},{3,5},{4,2},{5,3},{6,0},{7,1},{8,14},{9,15},{10,... | collective-permute-start | bytes 196616 | tf_op jit(solution)/shard_map/ppermute | solution.py:389
  10.1 0.7 %collective-permute-start.1 = (f32[128,128]{1,0:T(8,128)S(1)}, f32[128,128]{1,0:T(8,128)S(1)}, u32[]{:S(2)}, u32[]{:S(2)}) collective-permute-start(f32[128,128]{1,0:T(8,128)S(1)} %add.33.sent_ref), channel_id=1, source_target_pairs={{0,2},{1,3},{2,0},{3,1},{4,6},{5,7},{6,4},{7,5},{8,10},{9,11},{10,... | collective-permute-start | bytes 196616 | tf_op jit(solution)/shard_map/ppermute | solution.py:389
  10.8 4.5 %load_high.1 = (f32[128,128]{1,0:T(8,128)S(1)}, f32[128,4096]{1,0:T(8,128)S(1)}, f32[128,4096]{1,0:T(8,128)S(1)}, f32[128,4096]{1,0:T(8,128)S(1)}, f32[128,4096]...) custom-call(f32[4,128,4096]{2,1,0:T(8,128)} %basis_ref.3, f32[4,128,4096]{2,1,0:T(8,128)} %gen_ref.5, ...), custom_call_target="tpu_custom_call" | custom-call | flops 1000 | bytes 12058624 | tf_op jit(solution)/shard_map/load_high/pallas_call | solution.py:182
  15.3 2.6 %collective-permute-start.6 = (f32[128,128]{1,0:T(8,128)S(1)}, f32[128,128]{1,0:T(8,128)S(1)}, u32[]{:S(2)}, u32[]{:S(2)}) collective-permute-start(f32[128,128]{1,0:T(8,128)S(1)} %add_add_fusion.2.sent_ref), channel_id=1, source_target_pairs={{0,24},{1,25},{2,26},{3,27},{4,28},{5,29},{6,30},{7,31},{8,16},{9,... | collective-permute-start | bytes 196616 | tf_op jit(solution)/shard_map/ppermute | solution.py:389
  17.9 0.5 collective-permute-start.5
  18.4 0.3 collective-permute-start.4
  18.7 3.6 %grams_high.1 = (f32[128,128]{1,0:T(8,128)S(1)}, f32[64,256]{1,0:T(8,128)S(1)}, bf16[256,256]{1,0:T(8,128)(2,1)S(1)}, bf16[256,256]{1,0:T(8,128)(2,1)S(1)}, f32[...) custom-call(f32[64,4096]{1,0:T(8,128)S(1)} %copy-done, ...), custom_call_target="tpu_custom_call" | custom-call | flops 3200000000 | bytes 11534336 | tf_op jit(solution)/shard_map/grams_high/pallas_call | solution.py:227
  22.5 3.0 %collective-permute-start.7 = (f32[4,128,128]{2,1,0:T(8,128)S(1)}, f32[4,128,128]{2,1,0:T(8,128)S(1)}, u32[]{:S(2)}, u32[]{:S(2)}) collective-permute-start(f32[4,128,128]{2,1,0:T(8,128)S(1)} %pad_maximum_fusion.mine_ref), channel_id=1, source_target_pairs={{0,1},{1,0},{2,3},{3,2},{4,5},{5,4},{6,7},{7,6},{8,9},{9,8},{10,11... | collective-permute-start | bytes 786440 | tf_op jit(solution)/shard_map/ppermute | solution.py:389
  25.6 1.2 %collective-permute-done.7.other_ref = f32[4,128,128]{2,1,0:T(8,128)S(1)} collective-permute-done((f32[4,128,128]{2,1,0:T(8,128)S(1)}, f32[4,128,128]{2,1,0:T(8,128)S(1)}, u32[]{:S(2)}, u32[]{:S(2)}) %collective-permute-start.7) | collective-permute-done | bytes 262176 | tf_op jit(solution)/shard_map/ppermute | solution.py:389
  26.7 0.7 %coefficients_low.1 = (f32[64,256]{1,0:T(8,128)S(1)}, f32[128,128]{1,0:T(8,128)S(1)}, f32[128,128]{1,0:T(8,128)S(1)}) custom-call(f32[4,128,128]{2,1,0:T(8,128)S(1)} %pad_maximum_fusion.mine_ref, f32[4,128,128]{2,1,0:T(8,128)S(1)} %collective-permute-done.7.other_ref, bf16[3,256,256]{2,1,0:T(8,128)(2,1)S(1)} %get-tuple-element.41.ch_ref, ...), custom_call_target="tpu_custom_call" | custom-call | flops 120000000 | bytes 1500000 | tf_op jit(solution)/shard_map/coefficients_low/pallas_call | solution.py:283
  27.5 0.5 collective-permute-start.8
  27.9 0.9 %collective-permute-done.8 = f32[128,128]{1,0:T(8,128)S(1)} collective-permute-done((f32[128,128]{1,0:T(8,128)S(1)}, f32[128,128]{1,0:T(8,128)S(1)}, u32[]{:S(2)}, u32[]{:S(2)}) %collective-permute-start.8) | collective-permute-done | bytes 65568 | tf_op jit(solution)/shard_map/ppermute | solution.py:389
  28.8 2.3 %collective-permute-start.11 = (f32[128,128]{1,0:T(8,128)S(1)}, f32[128,128]{1,0:T(8,128)S(1)}, u32[]{:S(2)}, u32[]{:S(2)}) collective-permute-start(f32[128,128]{1,0:T(8,128)S(1)} %add.37.sent_ref), channel_id=1, source_target_pairs={{0,24},{1,7},{2,4},{3,27},{4,2},{5,29},{6,30},{7,1},{8,14},{9,17},... | collective-permute-start | bytes 196616 | tf_op jit(solution)/shard_map/ppermute | solution.py:401
  31.4 1.0 %collective-permute-start.9 = (f32[128,128]{1,0:T(8,128)S(1)}, f32[128,128]{1,0:T(8,128)S(1)}, u32[]{:S(2)}, u32[]{:S(2)}) collective-permute-start(f32[128,128]{1,0:T(8,128)S(1)} %add.37.sent_ref), channel_id=1, source_target_pairs={{0,9},{1,2},{2,1},{3,10},{4,7},{5,12},{6,15},{7,4},{8,11},{9,0},{1... | collective-permute-start | bytes 196616 | tf_op jit(solution)/shard_map/ppermute | solution.py:401
  32.4 0.9 %update_low.1 = (f32[64,4096]{1,0:T(8,128)S(1)}, f32[128,128]{1,0:T(8,128)S(1)}) custom-call(f32[64,256]{1,0:T(8,128)S(1)} %get-tuple-element.47.t_ref, f32[64,4096]{1,0:T(8,128)S(1)} %copy-done, f32[128,4096]{1,0:T(8,128)S(1)} %get-tuple-element.38.u3_ref, f32[128,4096]{1,0:T(8,128)S(1)} %get-tuple-element.39.u2_ref, f32[128,128]{1,0:T(8,128)S(1)} %add.37.sent_ref), custom_call_target="tpu_custom_call" | custom-call | flops 402653184 | bytes 6291456 | tf_op jit(solution)/shard_map/update_low/pallas_call | solution.py:306
  33.4 3.0 %collective-permute-done.10 = f32[128,128]{1,0:T(8,128)S(1)} collective-permute-done((f32[128,128]{1,0:T(8,128)S(1)}, f32[128,128]{1,0:T(8,128)S(1)}, u32[]{:S(2)}, u32[]{:S(2)}) %collective-permute-start.10) | collective-permute-done | bytes 65568 | tf_op jit(solution)/shard_map/ppermute | solution.py:401
  36.4 1.7 %collective-permute-start.14 = (f32[128,128]{1,0:T(8,128)S(1)}, f32[128,128]{1,0:T(8,128)S(1)}, u32[]{:S(2)}, u32[]{:S(2)}) collective-permute-start(f32[128,128]{1,0:T(8,128)S(1)} %add_add_fusion.1.sent_ref), channel_id=1, source_target_pairs={{0,6},{1,25},{2,26},{3,5},{4,28},{5,3},{6,0},{7,31},{8,16},{9,15},... | collective-permute-start | bytes 196616 | tf_op jit(solution)/shard_map/ppermute | solution.py:401
  38.1 1.3 %collective-permute-start.13 = (f32[128,128]{1,0:T(8,128)S(1)}, f32[128,128]{1,0:T(8,128)S(1)}, u32[]{:S(2)}, u32[]{:S(2)}) collective-permute-start(f32[128,128]{1,0:T(8,128)S(1)} %add_add_fusion.1.sent_ref), channel_id=1, source_target_pairs={{0,5},{1,16},{2,19},{3,6},{4,21},{5,0},{6,3},{7,22},{8,25},{9,12},... | collective-permute-start | bytes 196616 | tf_op jit(solution)/shard_map/ppermute | solution.py:401
  39.4 0.6 collective-permute-start.12
  40.0 1.9 %pairs_high.1 = (f32[128,128]{1,0:T(8,128)S(1)}, bf16[256,4096]{1,0:T(8,128)(2,1)S(1)}, bf16[256,4096]{1,0:T(8,128)(2,1)S(1)}, bf16[3,256,256]{2,1,0:T(8,128)(2,1)S(1)}, bf16[3,256,256]{2,1,0:T(8,128)(2,1)S(1)}) custom-call(f32[128,4096]{1,0:T(8,128)S(1)} %get-tuple-element.33.u1_ref, f32[4,128,4096]{2,1,0:T(8,128)} %gen_ref.5, ...), custom_call_target="tpu_custom_call" | custom-call | flops 100000000 | bytes 8388608 | tf_op jit(solution)/shard_map/pairs_high/pallas_call | solution.py:330
  41.9 1.7 %collective-permute-done.13 = f32[128,128]{1,0:T(8,128)S(1)} collective-permute-done((f32[128,128]{1,0:T(8,128)S(1)}, f32[128,128]{1,0:T(8,128)S(1)}, u32[]{:S(2)}, u32[]{:S(2)}) %collective-permute-start.13) | collective-permute-done | bytes 65568 | tf_op jit(solution)/shard_map/ppermute | solution.py:401
  43.6 2.8 %collective-permute-start.17 = (f32[128,128]{1,0:T(8,128)S(1)}, f32[128,128]{1,0:T(8,128)S(1)}, u32[]{:S(2)}, u32[]{:S(2)}) collective-permute-start(f32[128,128]{1,0:T(8,128)S(1)} %add_add_fusion), channel_id=1, source_target_pairs={{0,96},{1,97},{2,98},{3,99},{4,100},{5,101},{6,102},{7,103},{8,104... | collective-permute-start | bytes 196616 | tf_op jit(solution)/shard_map/ppermute | solution.py:389
  46.4 0.3 collective-permute-start.16
  46.8 0.3 collective-permute-start.15
  47.1 1.3 %collective-permute-done.17 = f32[128,128]{1,0:T(8,128)S(1)} collective-permute-done((f32[128,128]{1,0:T(8,128)S(1)}, f32[128,128]{1,0:T(8,128)S(1)}, u32[]{:S(2)}, u32[]{:S(2)}) %collective-permute-start.17) | collective-permute-done | bytes 65568 | tf_op jit(solution)/shard_map/ppermute | solution.py:389
  48.4 2.6 %collective-permute-done.16 = f32[128,128]{1,0:T(8,128)S(1)} collective-permute-done((f32[128,128]{1,0:T(8,128)S(1)}, f32[128,128]{1,0:T(8,128)S(1)}, u32[]{:S(2)}, u32[]{:S(2)}) %collective-permute-start.16) | collective-permute-done | bytes 65568 | tf_op jit(solution)/shard_map/ppermute | solution.py:389
  51.1 2.2 %collective-permute-start.18 = (f32[4,128,128]{2,1,0:T(8,128)S(1)}, f32[4,128,128]{2,1,0:T(8,128)S(1)}, u32[]{:S(2)}, u32[]{:S(2)}) collective-permute-start(f32[4,128,128]{2,1,0:T(8,128)S(1)} %pad_maximum_fusion.1.mine_ref), channel_id=1, source_target_pairs={{0,1},{1,0},{2,3},{3,2},{4,5},{5,4},{6,7},{7,6},{8,9},{9,8},{10,11... | collective-permute-start | bytes 786440 | tf_op jit(solution)/shard_map/ppermute | solution.py:389
  53.3 1.2 %collective-permute-done.18.other_ref = f32[4,128,128]{2,1,0:T(8,128)S(1)} collective-permute-done((f32[4,128,128]{2,1,0:T(8,128)S(1)}, f32[4,128,128]{2,1,0:T(8,128)S(1)}, u32[]{:S(2)}, u32[]{:S(2)}) %collective-permute-start.18) | collective-permute-done | bytes 262176 | tf_op jit(solution)/shard_map/ppermute | solution.py:389
  54.4 2.1 %update_high.1 = f32[64,4096]{1,0:T(8,128)} custom-call(f32[4,128,128]{2,1,0:T(8,128)S(1)} %pad_maximum_fusion.1.mine_ref, f32[4,128,128]{2,1,0:T(8,128)S(1)} %collective-permute-done.18.other_ref, bf16[3,256,256]{2,1,0:T(8,128)(2,1)S(1)} %get-tuple-element.52.ch_ref, bf16[3,256,256]{2,1,0:T(8,128)(2,1)S(1)} %get-tuple-element.53.cl_ref, ...), custom_call_target="tpu_custom_call" | custom-call | flops 500000000 | bytes 7000000 | tf_op jit(solution)/shard_map/update_high/pallas_call | solution.py:376
  (22 shorter events, 0.6 us)
Async XLA Ops:
  3.8 2.4 %collective-permute-start = (f32[128,128]{1,0:T(8,128)S(1)}, f32[128,128]{1,0:T(8,128)S(1)}, u32[]{:S(2)}, u32[]{:S(2)}) collective-permute-start(f32[128,128]{1,0:T(8,128)S(1)} %get-tuple-element.32), channel_id=1, source_target_pairs={{0,1},{1,0},{2,3},{3,2},{4,5},{5,4},{6,7},{7,6},{8,9},{9,8},{10,11... | collective-permute-start | bytes 196616 | tf_op jit(solution)/shard_map/ppermute | solution.py:389
  6.2 12.5 %copy-start = (f32[64,4096]{1,0:T(8,128)S(1)}, f32[64,4096]{1,0:T(8,128)}, u32[]{:S(2)}) copy-start(f32[64,4096]{1,0:T(8,128)} %rhs_ref.5) | copy-start | bytes 3145732
  6.2 9.1 %collective-permute-start.3 = (f32[128,128]{1,0:T(8,128)S(1)}, f32[128,128]{1,0:T(8,128)S(1)}, u32[]{:S(2)}, u32[]{:S(2)}) collective-permute-start(f32[128,128]{1,0:T(8,128)S(1)} %add.33.sent_ref), channel_id=1, source_target_pairs={{0,6},{1,7},{2,4},{3,5},{4,2},{5,3},{6,0},{7,1},{8,14},{9,15},{10,... | collective-permute-start | bytes 196616 | tf_op jit(solution)/shard_map/ppermute | solution.py:389
  10.1 5.2 %collective-permute-start.2 = (f32[128,128]{1,0:T(8,128)S(1)}, f32[128,128]{1,0:T(8,128)S(1)}, u32[]{:S(2)}, u32[]{:S(2)}) collective-permute-start(f32[128,128]{1,0:T(8,128)S(1)} %add.33.sent_ref), channel_id=1, source_target_pairs={{0,4},{1,5},{2,6},{3,7},{4,0},{5,1},{6,2},{7,3},{8,12},{9,13},{10,... | collective-permute-start | bytes 196616 | tf_op jit(solution)/shard_map/ppermute | solution.py:389
  10.1 5.2 %collective-permute-start.1 = (f32[128,128]{1,0:T(8,128)S(1)}, f32[128,128]{1,0:T(8,128)S(1)}, u32[]{:S(2)}, u32[]{:S(2)}) collective-permute-start(f32[128,128]{1,0:T(8,128)S(1)} %add.33.sent_ref), channel_id=1, source_target_pairs={{0,2},{1,3},{2,0},{3,1},{4,6},{5,7},{6,4},{7,5},{8,10},{9,11},{10,... | collective-permute-start | bytes 196616 | tf_op jit(solution)/shard_map/ppermute | solution.py:389
  15.3 6.9 %collective-permute-start.6 = (f32[128,128]{1,0:T(8,128)S(1)}, f32[128,128]{1,0:T(8,128)S(1)}, u32[]{:S(2)}, u32[]{:S(2)}) collective-permute-start(f32[128,128]{1,0:T(8,128)S(1)} %add_add_fusion.2.sent_ref), channel_id=1, source_target_pairs={{0,24},{1,25},{2,26},{3,27},{4,28},{5,29},{6,30},{7,31},{8,16},{9,... | collective-permute-start | bytes 196616 | tf_op jit(solution)/shard_map/ppermute | solution.py:389
  17.9 4.6 %collective-permute-start.5 = (f32[128,128]{1,0:T(8,128)S(1)}, f32[128,128]{1,0:T(8,128)S(1)}, u32[]{:S(2)}, u32[]{:S(2)}) collective-permute-start(f32[128,128]{1,0:T(8,128)S(1)} %add_add_fusion.2.sent_ref), channel_id=1, source_target_pairs={{0,16},{1,17},{2,18},{3,19},{4,20},{5,21},{6,22},{7,23},{8,24},{9,... | collective-permute-start | bytes 196616 | tf_op jit(solution)/shard_map/ppermute | solution.py:389
  18.4 4.1 %collective-permute-start.4 = (f32[128,128]{1,0:T(8,128)S(1)}, f32[128,128]{1,0:T(8,128)S(1)}, u32[]{:S(2)}, u32[]{:S(2)}) collective-permute-start(f32[128,128]{1,0:T(8,128)S(1)} %add_add_fusion.2.sent_ref), channel_id=1, source_target_pairs={{0,8},{1,9},{2,10},{3,11},{4,12},{5,13},{6,14},{7,15},{8,0},{9,1},... | collective-permute-start | bytes 196616 | tf_op jit(solution)/shard_map/ppermute | solution.py:389
  22.5 4.2 %collective-permute-start.7 = (f32[4,128,128]{2,1,0:T(8,128)S(1)}, f32[4,128,128]{2,1,0:T(8,128)S(1)}, u32[]{:S(2)}, u32[]{:S(2)}) collective-permute-start(f32[4,128,128]{2,1,0:T(8,128)S(1)} %pad_maximum_fusion.mine_ref), channel_id=1, source_target_pairs={{0,1},{1,0},{2,3},{3,2},{4,5},{5,4},{6,7},{7,6},{8,9},{9,8},{10,11... | collective-permute-start | bytes 786440 | tf_op jit(solution)/shard_map/ppermute | solution.py:389
  27.5 1.4 %collective-permute-start.8 = (f32[128,128]{1,0:T(8,128)S(1)}, f32[128,128]{1,0:T(8,128)S(1)}, u32[]{:S(2)}, u32[]{:S(2)}) collective-permute-start(f32[128,128]{1,0:T(8,128)S(1)} %get-tuple-element.49), channel_id=1, source_target_pairs={{0,1},{1,0},{2,3},{3,2},{4,5},{5,4},{6,7},{7,6},{8,9},{9,8},{10,11... | collective-permute-start | bytes 196616 | tf_op jit(solution)/shard_map/ppermute | solution.py:389
  28.8 4.6 %collective-permute-start.11 = (f32[128,128]{1,0:T(8,128)S(1)}, f32[128,128]{1,0:T(8,128)S(1)}, u32[]{:S(2)}, u32[]{:S(2)}) collective-permute-start(f32[128,128]{1,0:T(8,128)S(1)} %add.37.sent_ref), channel_id=1, source_target_pairs={{0,24},{1,7},{2,4},{3,27},{4,2},{5,29},{6,30},{7,1},{8,14},{9,17},... | collective-permute-start | bytes 196616 | tf_op jit(solution)/shard_map/ppermute | solution.py:401
  31.2 5.2 %collective-permute-start.10 = (f32[128,128]{1,0:T(8,128)S(1)}, f32[128,128]{1,0:T(8,128)S(1)}, u32[]{:S(2)}, u32[]{:S(2)}) collective-permute-start(f32[128,128]{1,0:T(8,128)S(1)} %add.37.sent_ref), channel_id=1, source_target_pairs={{0,17},{1,4},{2,7},{3,18},{4,1},{5,20},{6,23},{7,2},{8,13},{9,24},... | collective-permute-start | bytes 196616 | tf_op jit(solution)/shard_map/ppermute | solution.py:401
  31.4 5.0 %collective-permute-start.9 = (f32[128,128]{1,0:T(8,128)S(1)}, f32[128,128]{1,0:T(8,128)S(1)}, u32[]{:S(2)}, u32[]{:S(2)}) collective-permute-start(f32[128,128]{1,0:T(8,128)S(1)} %add.37.sent_ref), channel_id=1, source_target_pairs={{0,9},{1,2},{2,1},{3,10},{4,7},{5,12},{6,15},{7,4},{8,11},{9,0},{1... | collective-permute-start | bytes 196616 | tf_op jit(solution)/shard_map/ppermute | solution.py:401
  36.4 5.5 %collective-permute-start.14 = (f32[128,128]{1,0:T(8,128)S(1)}, f32[128,128]{1,0:T(8,128)S(1)}, u32[]{:S(2)}, u32[]{:S(2)}) collective-permute-start(f32[128,128]{1,0:T(8,128)S(1)} %add_add_fusion.1.sent_ref), channel_id=1, source_target_pairs={{0,6},{1,25},{2,26},{3,5},{4,28},{5,3},{6,0},{7,31},{8,16},{9,15},... | collective-permute-start | bytes 196616 | tf_op jit(solution)/shard_map/ppermute | solution.py:401
  38.1 5.5 %collective-permute-start.13 = (f32[128,128]{1,0:T(8,128)S(1)}, f32[128,128]{1,0:T(8,128)S(1)}, u32[]{:S(2)}, u32[]{:S(2)}) collective-permute-start(f32[128,128]{1,0:T(8,128)S(1)} %add_add_fusion.1.sent_ref), channel_id=1, source_target_pairs={{0,5},{1,16},{2,19},{3,6},{4,21},{5,0},{6,3},{7,22},{8,25},{9,12},... | collective-permute-start | bytes 196616 | tf_op jit(solution)/shard_map/ppermute | solution.py:401
  39.4 4.2 %collective-permute-start.12 = (f32[128,128]{1,0:T(8,128)S(1)}, f32[128,128]{1,0:T(8,128)S(1)}, u32[]{:S(2)}, u32[]{:S(2)}) collective-permute-start(f32[128,128]{1,0:T(8,128)S(1)} %add_add_fusion.1.sent_ref), channel_id=1, source_target_pairs={{0,3},{1,8},{2,11},{3,0},{4,13},{5,6},{6,5},{7,14},{8,1},{9,10},{1... | collective-permute-start | bytes 196616 | tf_op jit(solution)/shard_map/ppermute | solution.py:401
  43.6 4.8 %collective-permute-start.17 = (f32[128,128]{1,0:T(8,128)S(1)}, f32[128,128]{1,0:T(8,128)S(1)}, u32[]{:S(2)}, u32[]{:S(2)}) collective-permute-start(f32[128,128]{1,0:T(8,128)S(1)} %add_add_fusion), channel_id=1, source_target_pairs={{0,96},{1,97},{2,98},{3,99},{4,100},{5,101},{6,102},{7,103},{8,104... | collective-permute-start | bytes 196616 | tf_op jit(solution)/shard_map/ppermute | solution.py:389
  46.4 4.6 %collective-permute-start.16 = (f32[128,128]{1,0:T(8,128)S(1)}, f32[128,128]{1,0:T(8,128)S(1)}, u32[]{:S(2)}, u32[]{:S(2)}) collective-permute-start(f32[128,128]{1,0:T(8,128)S(1)} %add_add_fusion), channel_id=1, source_target_pairs={{0,64},{1,65},{2,66},{3,67},{4,68},{5,69},{6,70},{7,71},{8,72},{9,... | collective-permute-start | bytes 196616 | tf_op jit(solution)/shard_map/ppermute | solution.py:389
  46.8 4.3 %collective-permute-start.15 = (f32[128,128]{1,0:T(8,128)S(1)}, f32[128,128]{1,0:T(8,128)S(1)}, u32[]{:S(2)}, u32[]{:S(2)}) collective-permute-start(f32[128,128]{1,0:T(8,128)S(1)} %add_add_fusion), channel_id=1, source_target_pairs={{0,32},{1,33},{2,34},{3,35},{4,36},{5,37},{6,38},{7,39},{8,40},{9,... | collective-permute-start | bytes 196616 | tf_op jit(solution)/shard_map/ppermute | solution.py:389
  51.1 3.3 %collective-permute-start.18 = (f32[4,128,128]{2,1,0:T(8,128)S(1)}, f32[4,128,128]{2,1,0:T(8,128)S(1)}, u32[]{:S(2)}, u32[]{:S(2)}) collective-permute-start(f32[4,128,128]{2,1,0:T(8,128)S(1)} %pad_maximum_fusion.1.mine_ref), channel_id=1, source_target_pairs={{0,1},{1,0},{2,3},{3,2},{4,5},{5,4},{6,7},{7,6},{8,9},{9,8},{10,11... | collective-permute-start | bytes 786440 | tf_op jit(solution)/shard_map/ppermute | solution.py:389

commit v9 on v8

--- a/solution.py
+++ b/solution.py
@@ -12,7 +12,7 @@
 RANK = 128
 RHS = 64
 DEVICES = 128
-LIMITS = (53, 39, 38, 38, 40, 40, 44)
+LIMITS = (53, 40, 38, 38, 40, 40, 44, 51)
 HBM = pl.BlockSpec(memory_space=pltpu.HBM)
 VMEM = pl.BlockSpec(memory_space=pltpu.VMEM)
 
@@ -21,7 +21,7 @@
 X_MASKS = (24, 16, 8)
 Y_MASKS = (96, 64, 32)
 X_PLACES = (3, 0, 1, 2)
-Y_PLACES = (3, 0, 1, 2)
+Y_PLACES = (3, 0, 2, 1)
 
 
 def position():
@@ -30,7 +30,7 @@
 
 
 def half_of(bit):
-    return bit[0] ^ bit[1] ^ bit[2] ^ bit[3] ^ bit[4]
+    return bit[0] ^ bit[1] ^ bit[2] ^ bit[3] ^ bit[4] ^ bit[5] ^ bit[6]
 
 
 def split(value):
@@ -116,7 +116,7 @@
     p3 = fold(acc3[...], RHS)
     p2 = fold(acc2[: 2 * RHS], RHS)
     g32 = fold(acc2[2 * RHS :], RANK)
-    first = position()[1][0] == 0
+    first = half_of(position()[1]) == 0
 
     @pl.when(first)
     def _():
@@ -159,16 +159,36 @@
     )(rhs, basis, gen)
 
 
-def load_kernel(basis_ref, gen_ref, cap_ref, sent_ref, sent_out,
-                v1_ref, v0_ref, u3_ref, u2_ref, u1_ref, caps_ref, sems):
+def nodes_kernel(cap_ref, sent_ref, sent_out, caps_ref, sems):
+    device, _ = position()
+    n3, n2, n1 = device >> 4, device >> 5, device >> 6
+    nodes = (7 + n3, 7 + (n3 ^ 1), 3 + n2, 1 + n1, 1 + (n1 ^ 1), 0)
+    copies = [pltpu.make_async_copy(cap_ref.at[n], caps_ref.at[i], sems.at[i]) for i, n in enumerate(nodes)]
+    for copy in copies:
+        copy.start()
+    sent_out[...] = sent_ref[...]
+    for copy in copies:
+        copy.wait()
+
+
+def nodes_step(cap, sent):
+    return pl.pallas_call(
+        nodes_kernel,
+        out_shape=(array(*sent.shape), array(6, 2 * RANK, 2 * RANK)),
+        in_specs=[HBM, VMEM],
+        out_specs=(VMEM, VMEM),
+        scratch_shapes=[pltpu.SemaphoreType.DMA((6,))],
+        compiler_params=params(LIMITS[7]),
+        cost_estimate=pl.CostEstimate(flops=1_000, bytes_accessed=1_572_864, transcendentals=0),
+        name="nodes",
+    )(cap, sent)
+
+
+def load_kernel(basis_ref, gen_ref, sent_ref, sent_out, v1_ref, v0_ref, u3_ref, u2_ref, u1_ref, sems):
     sources = [
         (basis_ref, 1, v1_ref), (basis_ref, 0, v0_ref),
         (gen_ref, 3, u3_ref), (gen_ref, 2, u2_ref), (gen_ref, 1, u1_ref),
     ]
-    device, _ = position()
-    n3, n2, n1 = device >> 4, device >> 5, device >> 6
-    nodes = (7 + n3, 7 + (n3 ^ 1), 3 + n2, 1 + n1, 1 + (n1 ^ 1), 0)
-    sources += [(cap_ref, node, caps_ref.at[i]) for i, node in enumerate(nodes)]
     copies = [pltpu.make_async_copy(ref.at[k], out, sems.at[i]) for i, (ref, k, out) in enumerate(sources)]
     for copy in copies:
         copy.start()
@@ -177,18 +197,23 @@
         copy.wait()
 
 
-def load_step(basis, gen, cap, sent):
+def load_step(basis, gen, sent):
     wide = array(*basis.shape[1:])
     return pl.pallas_call(
         load_kernel,
-        out_shape=(array(*sent.shape), wide, wide, wide, wide, wide, array(6, 2 * RANK, 2 * RANK)),
-        in_specs=[HBM, HBM, HBM, VMEM],
-        out_specs=(VMEM,) * 7,
-        scratch_shapes=[pltpu.SemaphoreType.DMA((11,))],
+        out_shape=(array(*sent.shape), wide, wide, wide, wide, wide),
+        in_specs=[HBM, HBM, VMEM],
+        out_specs=(VMEM,) * 6,
+        scratch_shapes=[pltpu.SemaphoreType.DMA((5,))],
         compiler_params=params(LIMITS[1]),
-        cost_estimate=pl.CostEstimate(flops=1_000, bytes_accessed=12_058_624, transcendentals=0),
+        cost_estimate=pl.CostEstimate(flops=1_000, bytes_accessed=10_485_760, transcendentals=0),
         name="load_high",
-    )(basis, gen, cap, sent)
+    )(basis, gen, sent)
+
+
+G_AT = RHS // 2
+G10_AT = G_AT + 2 * RANK
+SUM_ROWS = G10_AT + RANK // 4
 
 
 def ordered(caps_ref, base, s_high, s_low, high_ref, low_ref):
@@ -207,9 +232,10 @@
 
 
 def grams_kernel(rhs_ref, v1_ref, v0_ref, u3_ref, u2_ref, u1_ref, caps_ref, sent_ref, sent_out,
-                 p_ref, gh_ref, gl_ref, g10_ref, ch_ref, cl_ref):
+                 keep_ref, send_ref, ch_ref, cl_ref):
     sent_out[...] = sent_ref[...]
     _, bit = position()
+    low_half = half_of(bit) == 0
     ordered(caps_ref, 0, bit[3], bit[4], ch_ref, cl_ref)
     left = stacked([rhs_ref[...], u3_ref[...]])
     u2 = stacked([u2_ref[...]])
@@ -217,31 +243,38 @@
         right = stacked([ref[...]])
         cols = slice(k * RANK, (k + 1) * RANK)
         both = fold(contract(left, right), RHS + RANK)
-        p_ref[:, cols] = both[:RHS]
-        gh_ref[:RANK, cols], gl_ref[:RANK, cols] = split(both[RHS:])
-        gh_ref[RANK:, cols], gl_ref[RANK:, cols] = split(fold(contract(u2, right), RANK))
-    g10_ref[...] = fold(contract(stacked([u1_ref[...]]), right), RANK)
+        g2 = fold(contract(u2, right), RANK)
+        one, two = both[: RHS // 2], both[RHS // 2 : RHS]
+        keep_ref[: RHS // 2, cols] = jnp.where(low_half, one, two)
+        send_ref[: RHS // 2, cols] = jnp.where(low_half, two, one)
+        for ref in (keep_ref, send_ref):
+            ref[G_AT : G_AT + RANK, cols] = both[RHS:]
+            ref[G_AT + RANK : G10_AT, cols] = g2
+    g10 = fold(contract(stacked([u1_ref[...]]), right), RANK)
+    quarter = RANK // 4
+    parts = [jnp.concatenate([g10[i * quarter : (i + 1) * quarter] for i in pair], axis=1) for pair in ((0, 1), (2, 3))]
+    keep_ref[G10_AT:] = jnp.where(low_half, parts[0], parts[1])
+    send_ref[G10_AT:] = jnp.where(low_half, parts[1], parts[0])
 
 
 def grams_step(rhs, v1, v0, u3, u2, u1, caps, sent):
     return pl.pallas_call(
         grams_kernel,
         out_shape=(
-            array(*sent.shape), array(RHS, 2 * RANK), half_array(2 * RANK, 2 * RANK), half_array(2 * RANK, 2 * RANK),
-            array(RANK, RANK), half_array(3, 2 * RANK, 2 * RANK), half_array(3, 2 * RANK, 2 * RANK),
+            array(*sent.shape), array(SUM_ROWS, 2 * RANK), array(SUM_ROWS, 2 * RANK),
+            half_array(3, 2 * RANK, 2 * RANK), half_array(3, 2 * RANK, 2 * RANK),
         ),
         in_specs=[VMEM] * 8,
-        out_specs=(VMEM,) * 7,
+        out_specs=(VMEM,) * 5,
         compiler_params=params(LIMITS[2]),
         cost_estimate=pl.CostEstimate(flops=3_200_000_000, bytes_accessed=11_534_336, transcendentals=0),
         name="grams_high",
     )(rhs, v1, v0, u3, u2, u1, caps, sent)
 
 
-def middle_kernel(mine_ref, other_ref, ch_ref, cl_ref, p_ref, gh_ref, gl_ref, g10_ref,
-                  t_ref, keep_ref, send_ref):
+def middle_kernel(mine_ref, other_ref, ch_ref, cl_ref, keep_ref, come_ref, t_ref, part_ref):
     _, bit = position()
-    first = bit[0] == 0
+    first = half_of(bit) == 0
     p, g = [], []
     for m in range(4):
         mine, other = mine_ref[X_PLACES[m]], other_ref[X_PLACES[m]]
@@ -256,39 +289,27 @@
     joined = jnp.concatenate([q2[0] + q2[1], q2[2] + q2[3]], axis=1)
     coeff = jnp.concatenate([t[0], product_of(joined, ch_ref[2, :, :RANK], cl_ref[2, :, :RANK])], axis=1)
     t_ref[...] = coeff
-    q = p_ref[...] - product_of(coeff, gh_ref[...], gl_ref[...])
+    sums = keep_ref[...] + come_ref[...]
     half = RHS // 2
-
-    def put(ref, c):
-        rows = slice(c * half, (c + 1) * half)
-        ref[:half] = q[rows, :RANK]
-        ref[half : 2 * half] = q[rows, RANK:]
-        ref[2 * half :] = g10_ref[c * RHS : (c + 1) * RHS]
-
-    low_half = half_of(bit) == 0
-
-    @pl.when(low_half)
-    def _():
-        put(keep_ref, 0)
-        put(send_ref, 1)
-
-    @pl.when(jnp.logical_not(low_half))
-    def _():
-        put(keep_ref, 1)
-        put(send_ref, 0)
-
-
-def middle_step(mine, other, ch, cl, p, gh, gl, g10):
-    half = jax.ShapeDtypeStruct((RANK, RANK), F32)
+    rows = jnp.where(half_of(bit) == 0, coeff[:half], coeff[half:])
+    q = sums[:half] - product(rows, sums[G_AT:G10_AT])
+    part_ref[:half] = q[:, :RANK]
+    part_ref[half : 2 * half] = q[:, RANK:]
+    quarter = RANK // 4
+    part_ref[2 * half : 2 * half + quarter] = sums[G10_AT:, :RANK]
+    part_ref[2 * half + quarter :] = sums[G10_AT:, RANK:]
+
+
+def middle_step(mine, other, ch, cl, keep, come):
     return pl.pallas_call(
         middle_kernel,
-        out_shape=(jax.ShapeDtypeStruct((RHS, 2 * RANK), F32), half, half),
-        in_specs=[VMEM] * 8,
-        out_specs=(VMEM,) * 3,
+        out_shape=(array(RHS, 2 * RANK), array(RANK, RANK)),
+        in_specs=[VMEM] * 6,
+        out_specs=(VMEM,) * 2,
         compiler_params=params(LIMITS[3]),
         cost_estimate=pl.CostEstimate(flops=120_000_000, bytes_accessed=1_500_000, transcendentals=0),
         name="coefficients_low",
-    )(mine, other, ch, cl, p, gh, gl, g10)
+    )(mine, other, ch, cl, keep, come)
 
 
 def low_update_kernel(t_ref, rhs_ref, u3_ref, u2_ref, sent_ref, cur_ref, sent_out):
@@ -395,7 +416,7 @@
 
 def crossed(value, even, odd):
     def partner(i):
-        mask = odd if parity(i & 31) else even
+        mask = odd if parity(i) else even
         return i ^ mask ^ parity(mask)
 
     return lax.ppermute(value, "leaf", [(i, partner(i)) for i in range(DEVICES)])
@@ -413,24 +434,26 @@
 
 def body(rhs, basis, gen, cap):
     keep, send = first_step(rhs, basis, gen)
-    chip = keep + swap(send, CORE)
-    b, c, d = neighbours(chip, Z_MASKS)
-    chip, v1, v0, u3, u2, u1, caps = load_step(basis, gen, cap, chip)
+    other = swap(send, CORE)
+    keep, caps = nodes_step(cap, keep)
+    chip = keep + other
+    b, c, d = crossed_neighbours(chip, Z_MASKS, Z_MASKS)
+    chip, v1, v0, u3, u2, u1 = load_step(basis, gen, chip)
     line = chip + b + c + d
-    b, c, d = neighbours(line, X_MASKS)
-    line, p, gh, gl, g10, ch, cl = grams_step(rhs, v1, v0, u3, u2, u1, caps, line)
+    b, c, d = crossed_neighbours(line, X_MASKS, X_MASKS)
+    line, keep, send, ch, cl = grams_step(rhs, v1, v0, u3, u2, u1, caps, line)
+    come = swap(send, CORE)
     lines = jnp.stack([b, c, d, line])
     other = swap(lines, CORE)
-    t, keep, send = middle_step(lines, other, ch, cl, p, gh, gl, g10)
-    chip = keep + swap(send, CORE)
+    t, chip = middle_step(lines, other, ch, cl, keep, come)
     b, c, d = crossed_neighbours(chip, X_MASKS, Z_MASKS)
     current, chip = low_update(t, rhs, u3, u2, chip)
     part = chip + b + c + d
     b, c, d = crossed_neighbours(part, Z_MASKS, X_MASKS)
     part, high, low, ch, cl = pairs_step(u1, gen, caps, part)
     plane = part + b + c + d
-    b, c, d = neighbours(plane, Y_MASKS)
-    planes = jnp.stack([b, c, d, plane])
+    b, c, d = crossed_neighbours(plane, Y_MASKS, Y_MASKS)
+    planes = jnp.stack([b, d, c, plane])
     other = swap(planes, CORE)
     return last_step(planes, other, ch, cl, current, high, low)
 

time: 56.6 us -> 54.6 us (0.965)
  starting transfers between devices: 25.8 us -> 22.7 us
  Pallas kernels: 17.4 us -> 18.4 us
    ppermute x13 -> x4, starting transfers between devices: 18.6 us -> 2.77 us  [swap(): return lax.ppermute(value, 'leaf', [(i, i ^ mask) for i in range(DEVICES)])]
    ppermute x6 -> x15, starting transfers between devices: 7.23 us -> 20 us  [crossed(): lax.ppermute(value, 'leaf', [(i, partner(i)) for i in range(DEVICES)])]
    ppermute x6 -> x15, waiting for transfers between devices: 4.67 us -> 10.4 us  [crossed(): lax.ppermute(value, 'leaf', [(i, partner(i)) for i in range(DEVICES)])]
    ppermute x13 -> x4, waiting for transfers between devices: 8.35 us -> 2.68 us  [swap(): return lax.ppermute(value, 'leaf', [(i, i ^ mask) for i in range(DEVICES)])]
    pallas_call x2 -> x3, Pallas kernels: 4.28 us -> 5.64 us  [the longest x1 3.56 us: grams_step(): pl.pallas_call(grams_kernel, out_shape=(array(*sent.shape), array(SUM_ROW...]
  transfers between devices with their start and end apart: 19 -> 19, of which waited for: 9 -> 9; matrix products, arithmetic and copies ran while one was open for 0% -> 0% of each run, Pallas kernels for 19% -> 22%
where the time goes in v9:
time: 54.6 us; the launch traced here: 54.4 us
  starting transfers between devices  22.7 us (42%)
  Pallas kernels  18.4 us (34%)
  waiting for transfers between devices  13 us (24%)
    ppermute x15, starting transfers between devices, crossed(): lax.ppermute(value, 'leaf', [(i, partner(i)) for i in range(DEVICES)])  20 us
    ppermute x15, waiting for transfers between devices, crossed(): lax.ppermute(value, 'leaf', [(i, partner(i)) for i in range(DEVICES)])  10.4 us
    pallas_call x1, Pallas kernels, load_step(): pl.pallas_call(load_kernel, out_shape=(array(*sent.shape), wide, wide, wi...  4.11 us
    pallas_call x1, Pallas kernels, first_step(): pl.pallas_call(functools.partial(first_kernel, points), out_shape=(array(...  3.78 us
    pallas_call x1, Pallas kernels, grams_step(): pl.pallas_call(grams_kernel, out_shape=(array(*sent.shape), array(SUM_ROW...  3.56 us
    ppermute x4, starting transfers between devices, swap(): return lax.ppermute(value, 'leaf', [(i, i ^ mask) for i in range(DEVICES)])  2.77 us
    ppermute x4, waiting for transfers between devices, swap(): return lax.ppermute(value, 'leaf', [(i, i ^ mask) for i in range(DEVICES)])  2.68 us
    pallas_call x1, Pallas kernels, last_step(): pl.pallas_call(last_kernel, out_shape=array(*cur.shape), in_specs=[VMEM]...  2.08 us
  transfers between devices with their start and end apart: 19, of which 9 were waited for; matrix products, arithmetic and copies ran while one was open for 0% of the time, Pallas kernels for 22%

profile of v9, /device:TPU:1, one launch (start us, length us, event | category | flops | bytes accessed | tf_op | source)
XLA Modules:
  0.0 54.4 jit_solution(373884897325020925)
XLA Ops:
  0.0 3.8 %project_low.1 = (f32[128,128]{1,0:T(8,128)S(1)}, f32[128,128]{1,0:T(8,128)S(1)}) custom-call(f32[64,4096]{1,0:T(8,128)} %rhs_ref.5, f32[4,128,4096]{2,1,0:T(8,128)} %basis_ref.3, f32[4,128,4096]{2,1,0:T(8,128)} %gen_ref.5), custom_call_target="tpu_custom_call" | custom-call | flops 800000000 | bytes 7340032 | tf_op jit(solution)/shard_map/project_low/pallas_call | solution.py:145
  3.8 1.5 %collective-permute-start = (f32[128,128]{1,0:T(8,128)S(1)}, f32[128,128]{1,0:T(8,128)S(1)}, u32[]{:S(2)}, u32[]{:S(2)}) collective-permute-start(f32[128,128]{1,0:T(8,128)S(1)} %get-tuple-element.31), channel_id=1, source_target_pairs={{0,1},{1,0},{2,3},{3,2},{4,5},{5,4},{6,7},{7,6},{8,9},{9,8},{10,11... | collective-permute-start | bytes 196616 | tf_op jit(solution)/shard_map/ppermute | solution.py:410
  5.3 1.4 %nodes.1 = (f32[128,128]{1,0:T(8,128)S(1)}, f32[6,256,256]{2,1,0:T(8,128)S(1)}) custom-call(f32[15,256,256]{2,1,0:T(8,128)} %cap_ref.1, f32[128,128]{1,0:T(8,128)S(1)} %get-tuple-element.29.sent_ref), custom_call_target="tpu_custom_call" | custom-call | flops 1000 | bytes 1572864 | tf_op jit(solution)/shard_map/nodes/pallas_call | solution.py:175
  6.7 3.9 %collective-permute-start.3 = (f32[128,128]{1,0:T(8,128)S(1)}, f32[128,128]{1,0:T(8,128)S(1)}, u32[]{:S(2)}, u32[]{:S(2)}) collective-permute-start(f32[128,128]{1,0:T(8,128)S(1)} %add.30.sent_ref), channel_id=1, source_target_pairs={{0,6},{1,7},{2,4},{3,5},{4,2},{5,3},{6,0},{7,1},{8,14},{9,15},{10,... | collective-permute-start | bytes 196616 | tf_op jit(solution)/shard_map/ppermute | solution.py:422
  10.7 0.9 %collective-permute-start.1 = (f32[128,128]{1,0:T(8,128)S(1)}, f32[128,128]{1,0:T(8,128)S(1)}, u32[]{:S(2)}, u32[]{:S(2)}) collective-permute-start(f32[128,128]{1,0:T(8,128)S(1)} %add.30.sent_ref), channel_id=1, source_target_pairs={{0,3},{1,2},{2,1},{3,0},{4,7},{5,6},{6,5},{7,4},{8,11},{9,10},{10,... | collective-permute-start | bytes 196616 | tf_op jit(solution)/shard_map/ppermute | solution.py:422
  11.6 4.1 %load_high.1 = (f32[128,128]{1,0:T(8,128)S(1)}, f32[128,4096]{1,0:T(8,128)S(1)}, f32[128,4096]{1,0:T(8,128)S(1)}, f32[128,4096]{1,0:T(8,128)S(1)}, f32[128,4096]{1,0:T(8,128)S(1)}, /*index=5*/f32[128,4096]{1,0:T(8,128)S(1)}) custom-call(f32[4,128,4096]{2,1,0:T(8,128)} %basis_ref.3, f32[4,128,4096]{2,1,0:T(8,128)} %gen_ref.5, f32[128,128]{1,0:T(8,128)S(1)} %add.30.sent_ref), custom_call_target="tpu_custom_call" | custom-call | flops 1000 | bytes 10485760 | tf_op jit(solution)/shard_map/load_high/pallas_call | solution.py:202
  15.7 0.7 %collective-permute-done.2 = f32[128,128]{1,0:T(8,128)S(1)} collective-permute-done((f32[128,128]{1,0:T(8,128)S(1)}, f32[128,128]{1,0:T(8,128)S(1)}, u32[]{:S(2)}, u32[]{:S(2)}) %collective-permute-start.2) | collective-permute-done | bytes 65568 | tf_op jit(solution)/shard_map/ppermute | solution.py:422
  16.5 2.6 %collective-permute-start.6 = (f32[128,128]{1,0:T(8,128)S(1)}, f32[128,128]{1,0:T(8,128)S(1)}, u32[]{:S(2)}, u32[]{:S(2)}) collective-permute-start(f32[128,128]{1,0:T(8,128)S(1)} %add_add_fusion.2.sent_ref), channel_id=1, source_target_pairs={{0,24},{1,25},{2,26},{3,27},{4,28},{5,29},{6,30},{7,31},{8,16},{9,... | collective-permute-start | bytes 196616 | tf_op jit(solution)/shard_map/ppermute | solution.py:422
  19.0 0.8 %collective-permute-start.5 = (f32[128,128]{1,0:T(8,128)S(1)}, f32[128,128]{1,0:T(8,128)S(1)}, u32[]{:S(2)}, u32[]{:S(2)}) collective-permute-start(f32[128,128]{1,0:T(8,128)S(1)} %add_add_fusion.2.sent_ref), channel_id=1, source_target_pairs={{0,17},{1,16},{2,19},{3,18},{4,21},{5,20},{6,23},{7,22},{8,25},{9,... | collective-permute-start | bytes 196616 | tf_op jit(solution)/shard_map/ppermute | solution.py:422
  19.8 0.3 collective-permute-start.4
  20.1 3.6 %grams_high.1 = (f32[128,128]{1,0:T(8,128)S(1)}, f32[320,256]{1,0:T(8,128)S(1)}, f32[320,256]{1,0:T(8,128)S(1)}, bf16[3,256,256]{2,1,0:T(8,128)(2,1)S(1)}, bf16[3,256,256]{2,1,0:T(8,128)(2,1)S(1)}) custom-call(f32[64,4096]{1,0:T(8,128)S(1)} %copy-done, f32[128,4096]{1,0:T(8,128)S(1)} %get-tuple-element.35.v1_ref, f32[128,4096]{1,0:T(8,128)S(1)} %get-tuple-element.36.v0_ref, ...), custom_call_target="tpu_custom_call" | custom-call | flops 3200000000 | bytes 11534336 | tf_op jit(solution)/shard_map/grams_high/pallas_call | solution.py:261
  23.7 0.4 collective-permute-start.8
  24.1 0.8 %collective-permute-done.5 = f32[128,128]{1,0:T(8,128)S(1)} collective-permute-done((f32[128,128]{1,0:T(8,128)S(1)}, f32[128,128]{1,0:T(8,128)S(1)}, u32[]{:S(2)}, u32[]{:S(2)}) %collective-permute-start.5) | collective-permute-done | bytes 65568 | tf_op jit(solution)/shard_map/ppermute | solution.py:422
  25.1 1.5 %collective-permute-done.7.other_ref = f32[4,128,128]{2,1,0:T(8,128)S(1)} collective-permute-done((f32[4,128,128]{2,1,0:T(8,128)S(1)}, f32[4,128,128]{2,1,0:T(8,128)S(1)}, u32[]{:S(2)}, u32[]{:S(2)}) %collective-permute-start.7) | collective-permute-done | bytes 262176 | tf_op jit(solution)/shard_map/ppermute | solution.py:410
  26.6 0.7 %coefficients_low.1 = (f32[64,256]{1,0:T(8,128)S(1)}, f32[128,128]{1,0:T(8,128)S(1)}) custom-call(f32[4,128,128]{2,1,0:T(8,128)S(1)} %pad_maximum_fusion.mine_ref, f32[4,128,128]{2,1,0:T(8,128)S(1)} %collective-permute-done.7.other_ref, bf16[3,256,256]{2,1,0:T(8,128)(2,1)S(1)} %get-tuple-element.40.ch_ref, ...), custom_call_target="tpu_custom_call" | custom-call | flops 120000000 | bytes 1500000 | tf_op jit(solution)/shard_map/coefficients_low/pallas_call | solution.py:304
  27.3 2.0 %collective-permute-start.11 = (f32[128,128]{1,0:T(8,128)S(1)}, f32[128,128]{1,0:T(8,128)S(1)}, u32[]{:S(2)}, u32[]{:S(2)}) collective-permute-start(f32[128,128]{1,0:T(8,128)S(1)} %get-tuple-element.45.sent_ref), channel_id=1, source_target_pairs={{0,24},{1,7},{2,4},{3,27},{4,2},{5,29},{6,30},{7,1},{8,14},{9,17},... | collective-permute-start | bytes 196616 | tf_op jit(solution)/shard_map/ppermute | solution.py:422
  29.3 0.2 collective-permute-start.10
  29.5 1.3 %collective-permute-start.9 = (f32[128,128]{1,0:T(8,128)S(1)}, f32[128,128]{1,0:T(8,128)S(1)}, u32[]{:S(2)}, u32[]{:S(2)}) collective-permute-start(f32[128,128]{1,0:T(8,128)S(1)} %get-tuple-element.45.sent_ref), channel_id=1, source_target_pairs={{0,9},{1,2},{2,1},{3,10},{4,7},{5,12},{6,15},{7,4},{8,11},{9,0},{1... | collective-permute-start | bytes 196616 | tf_op jit(solution)/shard_map/ppermute | solution.py:422
  30.8 0.9 %update_low.1 = (f32[64,4096]{1,0:T(8,128)S(1)}, f32[128,128]{1,0:T(8,128)S(1)}) custom-call(f32[64,256]{1,0:T(8,128)S(1)} %get-tuple-element.44.t_ref, f32[64,4096]{1,0:T(8,128)S(1)} %copy-done, f32[128,4096]{1,0:T(8,128)S(1)} %get-tuple-element.37.u3_ref, f32[128,4096]{1,0:T(8,128)S(1)} %get-tuple-element.38.u2_ref, f32[128,128]{1,0:T(8,128)S(1)} %get-tuple-element.45.sent_ref), custom_call_target="tpu_custom_call" | custom-call | flops 402653184 | bytes 6291456 | tf_op jit(solution)/shard_map/update_low/pallas_call | solution.py:327
  31.9 2.5 %collective-permute-done.10 = f32[128,128]{1,0:T(8,128)S(1)} collective-permute-done((f32[128,128]{1,0:T(8,128)S(1)}, f32[128,128]{1,0:T(8,128)S(1)}, u32[]{:S(2)}, u32[]{:S(2)}) %collective-permute-start.10) | collective-permute-done | bytes 65568 | tf_op jit(solution)/shard_map/ppermute | solution.py:422
  34.5 1.9 %collective-permute-start.14 = (f32[128,128]{1,0:T(8,128)S(1)}, f32[128,128]{1,0:T(8,128)S(1)}, u32[]{:S(2)}, u32[]{:S(2)}) collective-permute-start(f32[128,128]{1,0:T(8,128)S(1)} %add_add_fusion.1.sent_ref), channel_id=1, source_target_pairs={{0,6},{1,25},{2,26},{3,5},{4,28},{5,3},{6,0},{7,31},{8,16},{9,15},... | collective-permute-start | bytes 196616 | tf_op jit(solution)/shard_map/ppermute | solution.py:422
  36.3 1.3 %collective-permute-start.13 = (f32[128,128]{1,0:T(8,128)S(1)}, f32[128,128]{1,0:T(8,128)S(1)}, u32[]{:S(2)}, u32[]{:S(2)}) collective-permute-start(f32[128,128]{1,0:T(8,128)S(1)} %add_add_fusion.1.sent_ref), channel_id=1, source_target_pairs={{0,5},{1,16},{2,19},{3,6},{4,21},{5,0},{6,3},{7,22},{8,25},{9,12},... | collective-permute-start | bytes 196616 | tf_op jit(solution)/shard_map/ppermute | solution.py:422
  37.7 0.4 collective-permute-start.12
  38.1 1.9 %pairs_high.1 = (f32[128,128]{1,0:T(8,128)S(1)}, bf16[256,4096]{1,0:T(8,128)(2,1)S(1)}, bf16[256,4096]{1,0:T(8,128)(2,1)S(1)}, bf16[3,256,256]{2,1,0:T(8,128)(2,1)S(1)}, bf16[3,256,256]{2,1,0:T(8,128)(2,1)S(1)}) custom-call(f32[128,4096]{1,0:T(8,128)S(1)} %get-tuple-element.32.u1_ref, f32[4,128,4096]{2,1,0:T(8,128)} %gen_ref.5, ...), custom_call_target="tpu_custom_call" | custom-call | flops 100000000 | bytes 8388608 | tf_op jit(solution)/shard_map/pairs_high/pallas_call | solution.py:351
  40.0 1.8 %collective-permute-done.13 = f32[128,128]{1,0:T(8,128)S(1)} collective-permute-done((f32[128,128]{1,0:T(8,128)S(1)}, f32[128,128]{1,0:T(8,128)S(1)}, u32[]{:S(2)}, u32[]{:S(2)}) %collective-permute-start.13) | collective-permute-done | bytes 65568 | tf_op jit(solution)/shard_map/ppermute | solution.py:422
  41.9 3.5 %collective-permute-start.17 = (f32[128,128]{1,0:T(8,128)S(1)}, f32[128,128]{1,0:T(8,128)S(1)}, u32[]{:S(2)}, u32[]{:S(2)}) collective-permute-start(f32[128,128]{1,0:T(8,128)S(1)} %add_add_fusion), channel_id=1, source_target_pairs={{0,65},{1,64},{2,67},{3,66},{4,69},{5,68},{6,71},{7,70},{8,73},{9,... | collective-permute-start | bytes 196616 | tf_op jit(solution)/shard_map/ppermute | solution.py:422
  45.4 0.8 %collective-permute-start.16 = (f32[128,128]{1,0:T(8,128)S(1)}, f32[128,128]{1,0:T(8,128)S(1)}, u32[]{:S(2)}, u32[]{:S(2)}) collective-permute-start(f32[128,128]{1,0:T(8,128)S(1)} %add_add_fusion), channel_id=1, source_target_pairs={{0,96},{1,97},{2,98},{3,99},{4,100},{5,101},{6,102},{7,103},{8,104... | collective-permute-start | bytes 196616 | tf_op jit(solution)/shard_map/ppermute | solution.py:422
  46.1 1.7 %collective-permute-done.17 = f32[128,128]{1,0:T(8,128)S(1)} collective-permute-done((f32[128,128]{1,0:T(8,128)S(1)}, f32[128,128]{1,0:T(8,128)S(1)}, u32[]{:S(2)}, u32[]{:S(2)}) %collective-permute-start.17) | collective-permute-done | bytes 65568 | tf_op jit(solution)/shard_map/ppermute | solution.py:422
  47.8 2.6 %collective-permute-done.16 = f32[128,128]{1,0:T(8,128)S(1)} collective-permute-done((f32[128,128]{1,0:T(8,128)S(1)}, f32[128,128]{1,0:T(8,128)S(1)}, u32[]{:S(2)}, u32[]{:S(2)}) %collective-permute-start.16) | collective-permute-done | bytes 65568 | tf_op jit(solution)/shard_map/ppermute | solution.py:422
  50.4 0.7 %collective-permute-start.18 = (f32[4,128,128]{2,1,0:T(8,128)S(1)}, f32[4,128,128]{2,1,0:T(8,128)S(1)}, u32[]{:S(2)}, u32[]{:S(2)}) collective-permute-start(f32[4,128,128]{2,1,0:T(8,128)S(1)} %pad_maximum_fusion.1.mine_ref), channel_id=1, source_target_pairs={{0,1},{1,0},{2,3},{3,2},{4,5},{5,4},{6,7},{7,6},{8,9},{9,8},{10,11... | collective-permute-start | bytes 786440 | tf_op jit(solution)/shard_map/ppermute | solution.py:410
  51.2 1.2 %collective-permute-done.18.other_ref = f32[4,128,128]{2,1,0:T(8,128)S(1)} collective-permute-done((f32[4,128,128]{2,1,0:T(8,128)S(1)}, f32[4,128,128]{2,1,0:T(8,128)S(1)}, u32[]{:S(2)}, u32[]{:S(2)}) %collective-permute-start.18) | collective-permute-done | bytes 262176 | tf_op jit(solution)/shard_map/ppermute | solution.py:410
  52.3 2.1 %update_high.1 = f32[64,4096]{1,0:T(8,128)} custom-call(f32[4,128,128]{2,1,0:T(8,128)S(1)} %pad_maximum_fusion.1.mine_ref, f32[4,128,128]{2,1,0:T(8,128)S(1)} %collective-permute-done.18.other_ref, bf16[3,256,256]{2,1,0:T(8,128)(2,1)S(1)} %get-tuple-element.48.ch_ref, bf16[3,256,256]{2,1,0:T(8,128)(2,1)S(1)} %get-tuple-element.49.cl_ref, ...), custom_call_target="tpu_custom_call" | custom-call | flops 500000000 | bytes 7000000 | tf_op jit(solution)/shard_map/update_high/pallas_call | solution.py:397
  (22 shorter events, 0.4 us)
Async XLA Ops:
  3.8 2.9 %collective-permute-start = (f32[128,128]{1,0:T(8,128)S(1)}, f32[128,128]{1,0:T(8,128)S(1)}, u32[]{:S(2)}, u32[]{:S(2)}) collective-permute-start(f32[128,128]{1,0:T(8,128)S(1)} %get-tuple-element.31), channel_id=1, source_target_pairs={{0,1},{1,0},{2,3},{3,2},{4,5},{5,4},{6,7},{7,6},{8,9},{9,8},{10,11... | collective-permute-start | bytes 196616 | tf_op jit(solution)/shard_map/ppermute | solution.py:410
  6.7 13.4 %copy-start = (f32[64,4096]{1,0:T(8,128)S(1)}, f32[64,4096]{1,0:T(8,128)}, u32[]{:S(2)}) copy-start(f32[64,4096]{1,0:T(8,128)} %rhs_ref.5) | copy-start | bytes 3145732
  6.7 9.0 %collective-permute-start.3 = (f32[128,128]{1,0:T(8,128)S(1)}, f32[128,128]{1,0:T(8,128)S(1)}, u32[]{:S(2)}, u32[]{:S(2)}) collective-permute-start(f32[128,128]{1,0:T(8,128)S(1)} %add.30.sent_ref), channel_id=1, source_target_pairs={{0,6},{1,7},{2,4},{3,5},{4,2},{5,3},{6,0},{7,1},{8,14},{9,15},{10,... | collective-permute-start | bytes 196616 | tf_op jit(solution)/shard_map/ppermute | solution.py:422
  10.6 5.8 %collective-permute-start.2 = (f32[128,128]{1,0:T(8,128)S(1)}, f32[128,128]{1,0:T(8,128)S(1)}, u32[]{:S(2)}, u32[]{:S(2)}) collective-permute-start(f32[128,128]{1,0:T(8,128)S(1)} %add.30.sent_ref), channel_id=1, source_target_pairs={{0,5},{1,4},{2,7},{3,6},{4,1},{5,0},{6,3},{7,2},{8,13},{9,12},{10,... | collective-permute-start | bytes 196616 | tf_op jit(solution)/shard_map/ppermute | solution.py:422
  10.7 5.8 %collective-permute-start.1 = (f32[128,128]{1,0:T(8,128)S(1)}, f32[128,128]{1,0:T(8,128)S(1)}, u32[]{:S(2)}, u32[]{:S(2)}) collective-permute-start(f32[128,128]{1,0:T(8,128)S(1)} %add.30.sent_ref), channel_id=1, source_target_pairs={{0,3},{1,2},{2,1},{3,0},{4,7},{5,6},{6,5},{7,4},{8,11},{9,10},{10,... | collective-permute-start | bytes 196616 | tf_op jit(solution)/shard_map/ppermute | solution.py:422
  16.5 7.6 %collective-permute-start.6 = (f32[128,128]{1,0:T(8,128)S(1)}, f32[128,128]{1,0:T(8,128)S(1)}, u32[]{:S(2)}, u32[]{:S(2)}) collective-permute-start(f32[128,128]{1,0:T(8,128)S(1)} %add_add_fusion.2.sent_ref), channel_id=1, source_target_pairs={{0,24},{1,25},{2,26},{3,27},{4,28},{5,29},{6,30},{7,31},{8,16},{9,... | collective-permute-start | bytes 196616 | tf_op jit(solution)/shard_map/ppermute | solution.py:422
  19.0 5.9 %collective-permute-start.5 = (f32[128,128]{1,0:T(8,128)S(1)}, f32[128,128]{1,0:T(8,128)S(1)}, u32[]{:S(2)}, u32[]{:S(2)}) collective-permute-start(f32[128,128]{1,0:T(8,128)S(1)} %add_add_fusion.2.sent_ref), channel_id=1, source_target_pairs={{0,17},{1,16},{2,19},{3,18},{4,21},{5,20},{6,23},{7,22},{8,25},{9,... | collective-permute-start | bytes 196616 | tf_op jit(solution)/shard_map/ppermute | solution.py:422
  19.8 5.1 %collective-permute-start.4 = (f32[128,128]{1,0:T(8,128)S(1)}, f32[128,128]{1,0:T(8,128)S(1)}, u32[]{:S(2)}, u32[]{:S(2)}) collective-permute-start(f32[128,128]{1,0:T(8,128)S(1)} %add_add_fusion.2.sent_ref), channel_id=1, source_target_pairs={{0,9},{1,8},{2,11},{3,10},{4,13},{5,12},{6,15},{7,14},{8,1},{9,0},... | collective-permute-start | bytes 196616 | tf_op jit(solution)/shard_map/ppermute | solution.py:422
  23.7 2.9 %collective-permute-start.8 = (f32[320,256]{1,0:T(8,128)S(1)}, f32[320,256]{1,0:T(8,128)S(1)}, u32[]{:S(2)}, u32[]{:S(2)}) collective-permute-start(f32[320,256]{1,0:T(8,128)S(1)} %get-tuple-element.43), channel_id=1, source_target_pairs={{0,1},{1,0},{2,3},{3,2},{4,5},{5,4},{6,7},{7,6},{8,9},{9,8},{10,11... | collective-permute-start | bytes 983048 | tf_op jit(solution)/shard_map/ppermute | solution.py:410
  25.0 1.6 %collective-permute-start.7 = (f32[4,128,128]{2,1,0:T(8,128)S(1)}, f32[4,128,128]{2,1,0:T(8,128)S(1)}, u32[]{:S(2)}, u32[]{:S(2)}) collective-permute-start(f32[4,128,128]{2,1,0:T(8,128)S(1)} %pad_maximum_fusion.mine_ref), channel_id=1, source_target_pairs={{0,1},{1,0},{2,3},{3,2},{4,5},{5,4},{6,7},{7,6},{8,9},{9,8},{10,11... | collective-permute-start | bytes 786440 | tf_op jit(solution)/shard_map/ppermute | solution.py:410
  27.3 4.6 %collective-permute-start.11 = (f32[128,128]{1,0:T(8,128)S(1)}, f32[128,128]{1,0:T(8,128)S(1)}, u32[]{:S(2)}, u32[]{:S(2)}) collective-permute-start(f32[128,128]{1,0:T(8,128)S(1)} %get-tuple-element.45.sent_ref), channel_id=1, source_target_pairs={{0,24},{1,7},{2,4},{3,27},{4,2},{5,29},{6,30},{7,1},{8,14},{9,17},... | collective-permute-start | bytes 196616 | tf_op jit(solution)/shard_map/ppermute | solution.py:422
  29.3 5.2 %collective-permute-start.10 = (f32[128,128]{1,0:T(8,128)S(1)}, f32[128,128]{1,0:T(8,128)S(1)}, u32[]{:S(2)}, u32[]{:S(2)}) collective-permute-start(f32[128,128]{1,0:T(8,128)S(1)} %get-tuple-element.45.sent_ref), channel_id=1, source_target_pairs={{0,17},{1,4},{2,7},{3,18},{4,1},{5,20},{6,23},{7,2},{8,13},{9,24},... | collective-permute-start | bytes 196616 | tf_op jit(solution)/shard_map/ppermute | solution.py:422
  29.5 5.0 %collective-permute-start.9 = (f32[128,128]{1,0:T(8,128)S(1)}, f32[128,128]{1,0:T(8,128)S(1)}, u32[]{:S(2)}, u32[]{:S(2)}) collective-permute-start(f32[128,128]{1,0:T(8,128)S(1)} %get-tuple-element.45.sent_ref), channel_id=1, source_target_pairs={{0,9},{1,2},{2,1},{3,10},{4,7},{5,12},{6,15},{7,4},{8,11},{9,0},{1... | collective-permute-start | bytes 196616 | tf_op jit(solution)/shard_map/ppermute | solution.py:422
  34.5 5.5 %collective-permute-start.14 = (f32[128,128]{1,0:T(8,128)S(1)}, f32[128,128]{1,0:T(8,128)S(1)}, u32[]{:S(2)}, u32[]{:S(2)}) collective-permute-start(f32[128,128]{1,0:T(8,128)S(1)} %add_add_fusion.1.sent_ref), channel_id=1, source_target_pairs={{0,6},{1,25},{2,26},{3,5},{4,28},{5,3},{6,0},{7,31},{8,16},{9,15},... | collective-permute-start | bytes 196616 | tf_op jit(solution)/shard_map/ppermute | solution.py:422
  36.3 5.5 %collective-permute-start.13 = (f32[128,128]{1,0:T(8,128)S(1)}, f32[128,128]{1,0:T(8,128)S(1)}, u32[]{:S(2)}, u32[]{:S(2)}) collective-permute-start(f32[128,128]{1,0:T(8,128)S(1)} %add_add_fusion.1.sent_ref), channel_id=1, source_target_pairs={{0,5},{1,16},{2,19},{3,6},{4,21},{5,0},{6,3},{7,22},{8,25},{9,12},... | collective-permute-start | bytes 196616 | tf_op jit(solution)/shard_map/ppermute | solution.py:422
  37.7 4.2 %collective-permute-start.12 = (f32[128,128]{1,0:T(8,128)S(1)}, f32[128,128]{1,0:T(8,128)S(1)}, u32[]{:S(2)}, u32[]{:S(2)}) collective-permute-start(f32[128,128]{1,0:T(8,128)S(1)} %add_add_fusion.1.sent_ref), channel_id=1, source_target_pairs={{0,3},{1,8},{2,11},{3,0},{4,13},{5,6},{6,5},{7,14},{8,1},{9,10},{1... | collective-permute-start | bytes 196616 | tf_op jit(solution)/shard_map/ppermute | solution.py:422
  41.9 5.9 %collective-permute-start.17 = (f32[128,128]{1,0:T(8,128)S(1)}, f32[128,128]{1,0:T(8,128)S(1)}, u32[]{:S(2)}, u32[]{:S(2)}) collective-permute-start(f32[128,128]{1,0:T(8,128)S(1)} %add_add_fusion), channel_id=1, source_target_pairs={{0,65},{1,64},{2,67},{3,66},{4,69},{5,68},{6,71},{7,70},{8,73},{9,... | collective-permute-start | bytes 196616 | tf_op jit(solution)/shard_map/ppermute | solution.py:422
  45.4 5.1 %collective-permute-start.16 = (f32[128,128]{1,0:T(8,128)S(1)}, f32[128,128]{1,0:T(8,128)S(1)}, u32[]{:S(2)}, u32[]{:S(2)}) collective-permute-start(f32[128,128]{1,0:T(8,128)S(1)} %add_add_fusion), channel_id=1, source_target_pairs={{0,96},{1,97},{2,98},{3,99},{4,100},{5,101},{6,102},{7,103},{8,104... | collective-permute-start | bytes 196616 | tf_op jit(solution)/shard_map/ppermute | solution.py:422
  46.1 4.3 %collective-permute-start.15 = (f32[128,128]{1,0:T(8,128)S(1)}, f32[128,128]{1,0:T(8,128)S(1)}, u32[]{:S(2)}, u32[]{:S(2)}) collective-permute-start(f32[128,128]{1,0:T(8,128)S(1)} %add_add_fusion), channel_id=1, source_target_pairs={{0,33},{1,32},{2,35},{3,34},{4,37},{5,36},{6,39},{7,38},{8,41},{9,... | collective-permute-start | bytes 196616 | tf_op jit(solution)/shard_map/ppermute | solution.py:422
  50.4 1.9 %collective-permute-start.18 = (f32[4,128,128]{2,1,0:T(8,128)S(1)}, f32[4,128,128]{2,1,0:T(8,128)S(1)}, u32[]{:S(2)}, u32[]{:S(2)}) collective-permute-start(f32[4,128,128]{2,1,0:T(8,128)S(1)} %pad_maximum_fusion.1.mine_ref), channel_id=1, source_target_pairs={{0,1},{1,0},{2,3},{3,2},{4,5},{5,4},{6,7},{7,6},{8,9},{9,8},{10,11... | collective-permute-start | bytes 786440 | tf_op jit(solution)/shard_map/ppermute | solution.py:410

commit v10 on v9

--- a/solution.py
+++ b/solution.py
@@ -12,7 +12,7 @@
 RANK = 128
 RHS = 64
 DEVICES = 128
-LIMITS = (53, 40, 38, 38, 40, 40, 44, 51)
+LIMITS = (53, 40, 38, 38, 40, 47, 44, 51, 47)
 HBM = pl.BlockSpec(memory_space=pltpu.HBM)
 VMEM = pl.BlockSpec(memory_space=pltpu.VMEM)
 
@@ -159,35 +159,30 @@
     )(rhs, basis, gen)
 
 
-def nodes_kernel(cap_ref, sent_ref, sent_out, caps_ref, sems):
-    device, _ = position()
-    n3, n2, n1 = device >> 4, device >> 5, device >> 6
-    nodes = (7 + n3, 7 + (n3 ^ 1), 3 + n2, 1 + n1, 1 + (n1 ^ 1), 0)
-    copies = [pltpu.make_async_copy(cap_ref.at[n], caps_ref.at[i], sems.at[i]) for i, n in enumerate(nodes)]
-    for copy in copies:
-        copy.start()
+def early_kernel(gen_ref, sent_ref, sent_out, u1_ref, sem):
+    copy = pltpu.make_async_copy(gen_ref.at[1], u1_ref, sem)
+    copy.start()
     sent_out[...] = sent_ref[...]
-    for copy in copies:
-        copy.wait()
-
-
-def nodes_step(cap, sent):
-    return pl.pallas_call(
-        nodes_kernel,
-        out_shape=(array(*sent.shape), array(6, 2 * RANK, 2 * RANK)),
+    copy.wait()
+
+
+def early_step(gen, sent):
+    return pl.pallas_call(
+        early_kernel,
+        out_shape=(array(*sent.shape), array(*gen.shape[1:])),
         in_specs=[HBM, VMEM],
         out_specs=(VMEM, VMEM),
-        scratch_shapes=[pltpu.SemaphoreType.DMA((6,))],
+        scratch_shapes=[pltpu.SemaphoreType.DMA(())],
         compiler_params=params(LIMITS[7]),
-        cost_estimate=pl.CostEstimate(flops=1_000, bytes_accessed=1_572_864, transcendentals=0),
-        name="nodes",
-    )(cap, sent)
-
-
-def load_kernel(basis_ref, gen_ref, sent_ref, sent_out, v1_ref, v0_ref, u3_ref, u2_ref, u1_ref, sems):
+        cost_estimate=pl.CostEstimate(flops=1_000, bytes_accessed=2_097_152, transcendentals=0),
+        name="load_early",
+    )(gen, sent)
+
+
+def load_kernel(basis_ref, gen_ref, sent_ref, sent_out, v1_ref, v0_ref, u3_ref, u2_ref, sems):
     sources = [
         (basis_ref, 1, v1_ref), (basis_ref, 0, v0_ref),
-        (gen_ref, 3, u3_ref), (gen_ref, 2, u2_ref), (gen_ref, 1, u1_ref),
+        (gen_ref, 3, u3_ref), (gen_ref, 2, u2_ref),
     ]
     copies = [pltpu.make_async_copy(ref.at[k], out, sems.at[i]) for i, (ref, k, out) in enumerate(sources)]
     for copy in copies:
@@ -201,12 +196,12 @@
     wide = array(*basis.shape[1:])
     return pl.pallas_call(
         load_kernel,
-        out_shape=(array(*sent.shape), wide, wide, wide, wide, wide),
+        out_shape=(array(*sent.shape), wide, wide, wide, wide),
         in_specs=[HBM, HBM, VMEM],
-        out_specs=(VMEM,) * 6,
-        scratch_shapes=[pltpu.SemaphoreType.DMA((5,))],
+        out_specs=(VMEM,) * 5,
+        scratch_shapes=[pltpu.SemaphoreType.DMA((4,))],
         compiler_params=params(LIMITS[1]),
-        cost_estimate=pl.CostEstimate(flops=1_000, bytes_accessed=10_485_760, transcendentals=0),
+        cost_estimate=pl.CostEstimate(flops=1_000, bytes_accessed=8_388_608, transcendentals=0),
         name="load_high",
     )(basis, gen, sent)
 
@@ -216,13 +211,13 @@
 SUM_ROWS = G10_AT + RANK // 4
 
 
-def ordered(caps_ref, base, s_high, s_low, high_ref, low_ref):
+def ordered(caps_ref, s_high, s_low, high_ref, low_ref):
     for i, (s, columns) in enumerate(((s_high, 2), (s_high, 2), (s_low, 1))):
         for r, row in enumerate((1 - s, s)):
             for c, col in enumerate((s, 1 - s)[:columns]):
                 high, low = split(
                     caps_ref[
-                        base + i,
+                        i,
                         pl.ds(pl.multiple_of(row * RANK, RANK), RANK),
                         pl.ds(pl.multiple_of(col * RANK, RANK), RANK),
                     ]
@@ -231,12 +226,11 @@
                 low_ref[i, r * RANK : (r + 1) * RANK, c * RANK : (c + 1) * RANK] = low
 
 
-def grams_kernel(rhs_ref, v1_ref, v0_ref, u3_ref, u2_ref, u1_ref, caps_ref, sent_ref, sent_out,
-                 keep_ref, send_ref, ch_ref, cl_ref):
+def grams_kernel(rhs_ref, v1_ref, v0_ref, u3_ref, u2_ref, u1_ref, sent_ref, sent_out,
+                 keep_ref, send_ref):
     sent_out[...] = sent_ref[...]
     _, bit = position()
     low_half = half_of(bit) == 0
-    ordered(caps_ref, 0, bit[3], bit[4], ch_ref, cl_ref)
     left = stacked([rhs_ref[...], u3_ref[...]])
     u2 = stacked([u2_ref[...]])
     for k, ref in enumerate((v1_ref, v0_ref)):
@@ -257,19 +251,56 @@
     send_ref[G10_AT:] = jnp.where(low_half, parts[1], parts[0])
 
 
-def grams_step(rhs, v1, v0, u3, u2, u1, caps, sent):
+def grams_step(rhs, v1, v0, u3, u2, u1, sent):
     return pl.pallas_call(
         grams_kernel,
         out_shape=(
             array(*sent.shape), array(SUM_ROWS, 2 * RANK), array(SUM_ROWS, 2 * RANK),
-            half_array(3, 2 * RANK, 2 * RANK), half_array(3, 2 * RANK, 2 * RANK),
         ),
-        in_specs=[VMEM] * 8,
-        out_specs=(VMEM,) * 5,
+        in_specs=[VMEM] * 7,
+        out_specs=(VMEM,) * 3,
         compiler_params=params(LIMITS[2]),
         cost_estimate=pl.CostEstimate(flops=3_200_000_000, bytes_accessed=11_534_336, transcendentals=0),
         name="grams_high",
-    )(rhs, v1, v0, u3, u2, u1, caps, sent)
+    )(rhs, v1, v0, u3, u2, u1, sent)
+
+
+def fetch_nodes(cap_ref, nodes, caps_ref, sems):
+    copies = [pltpu.make_async_copy(cap_ref.at[n], caps_ref.at[i], sems.at[i]) for i, n in enumerate(nodes)]
+    for copy in copies:
+        copy.start()
+    return copies
+
+
+def nodes_kernel(cap_ref, sent_ref, sent_out, ch_ref, cl_ref, caps_ref, sems):
+    device, bit = position()
+    n3, n2 = device >> 4, device >> 5
+    copies = fetch_nodes(cap_ref, (7 + n3, 7 + (n3 ^ 1), 3 + n2), caps_ref, sems)
+    sent_out[...] = sent_ref[...]
+    for copy in copies:
+        copy.wait()
+    ordered(caps_ref, bit[3], bit[4], ch_ref, cl_ref)
+
+
+def nodes_step(cap, sent):
+    nodes = half_array(3, 2 * RANK, 2 * RANK)
+    return pl.pallas_call(
+        nodes_kernel,
+        out_shape=(array(*sent.shape), nodes, nodes),
+        in_specs=[HBM, VMEM],
+        out_specs=(VMEM,) * 3,
+        scratch_shapes=[pltpu.VMEM((3, 2 * RANK, 2 * RANK), F32), pltpu.SemaphoreType.DMA((3,))],
+        compiler_params=params(LIMITS[8]),
+        cost_estimate=pl.CostEstimate(flops=1_000, bytes_accessed=786_432, transcendentals=0),
+        name="nodes_low",
+    )(cap, sent)
+
+
+def upper(t, g, q, high, low):
+    sides = (slice(0, RANK), slice(0, RANK), slice(RANK, 2 * RANK), slice(RANK, 2 * RANK))
+    moved = jnp.concatenate([product_of(g[m], high[side], low[side]) for m, side in enumerate(sides)], axis=0)
+    joined = jnp.concatenate([q[0] + q[1], q[2] + q[3]], axis=1)
+    return product_of(joined, high, low) - product(jnp.concatenate(t, axis=1), moved)
 
 
 def middle_kernel(mine_ref, other_ref, ch_ref, cl_ref, keep_ref, come_ref, t_ref, part_ref):
@@ -285,14 +316,15 @@
         joined = jnp.concatenate([p[pair][:RHS], p[pair + 1][:RHS]], axis=1)
         both = product_of(joined, ch_ref[pair // 2], cl_ref[pair // 2])
         t += [both[:, :RANK], both[:, RANK:]]
-    q2 = [p[m][RHS:] - product(t[m], g[m]) for m in range(4)]
-    joined = jnp.concatenate([q2[0] + q2[1], q2[2] + q2[3]], axis=1)
-    coeff = jnp.concatenate([t[0], product_of(joined, ch_ref[2, :, :RANK], cl_ref[2, :, :RANK])], axis=1)
-    t_ref[...] = coeff
+    above = upper(t, g, [p[m][RHS:] for m in range(4)], ch_ref[2, :, :RANK], cl_ref[2, :, :RANK])
+    t_ref[:, :RANK] = t[0]
+    t_ref[:, RANK:] = above
     sums = keep_ref[...] + come_ref[...]
     half = RHS // 2
-    rows = jnp.where(half_of(bit) == 0, coeff[:half], coeff[half:])
-    q = sums[:half] - product(rows, sums[G_AT:G10_AT])
+    low_half = half_of(bit) == 0
+    grams = sums[G_AT:G10_AT]
+    q = sums[:half] - product(jnp.where(low_half, t[0][:half], t[0][half:]), grams[:RANK])
+    q = q - product(jnp.where(low_half, above[:half], above[half:]), grams[RANK:])
     part_ref[:half] = q[:, :RANK]
     part_ref[half : 2 * half] = q[:, RANK:]
     quarter = RANK // 4
@@ -335,29 +367,37 @@
     )(t, rhs, u3, u2, sent)
 
 
-def pairs_kernel(u1_ref, gen_ref, caps_ref, sent_ref, sent_out, high_ref, low_ref, ch_ref, cl_ref, u0_ref, sem):
+def pairs_kernel(u1_ref, gen_ref, cap_ref, sent_ref, sent_out, high_ref, low_ref, ch_ref, cl_ref,
+                 u0_ref, caps_ref, sem, sems):
     copy = pltpu.make_async_copy(gen_ref.at[0], u0_ref, sem)
     copy.start()
     sent_out[...] = sent_ref[...]
-    _, bit = position()
-    ordered(caps_ref, 3, bit[5], bit[6], ch_ref, cl_ref)
+    device, bit = position()
+    n1 = device >> 6
+    copies = fetch_nodes(cap_ref, (1 + n1, 1 + (n1 ^ 1), 0), caps_ref, sems)
     high_ref[:RANK], low_ref[:RANK] = split(u1_ref[...])
+    for node in copies:
+        node.wait()
+    ordered(caps_ref, bit[5], bit[6], ch_ref, cl_ref)
     copy.wait()
     high_ref[RANK:], low_ref[RANK:] = split(u0_ref[...])
 
 
-def pairs_step(u1, gen, caps, sent):
+def pairs_step(u1, gen, cap, sent):
     pair, nodes = half_array(2 * RANK, u1.shape[1]), half_array(3, 2 * RANK, 2 * RANK)
     return pl.pallas_call(
         pairs_kernel,
         out_shape=(array(*sent.shape), pair, pair, nodes, nodes),
-        in_specs=[VMEM, HBM, VMEM, VMEM],
+        in_specs=[VMEM, HBM, HBM, VMEM],
         out_specs=(VMEM,) * 5,
-        scratch_shapes=[pltpu.VMEM(u1.shape, F32), pltpu.SemaphoreType.DMA(())],
+        scratch_shapes=[
+            pltpu.VMEM(u1.shape, F32), pltpu.VMEM((3, 2 * RANK, 2 * RANK), F32),
+            pltpu.SemaphoreType.DMA(()), pltpu.SemaphoreType.DMA((3,)),
+        ],
         compiler_params=params(LIMITS[5]),
         cost_estimate=pl.CostEstimate(flops=100_000_000, bytes_accessed=8_388_608, transcendentals=0),
         name="pairs_high",
-    )(u1, gen, caps, sent)
+    )(u1, gen, cap, sent)
 
 
 def last_kernel(mine_ref, other_ref, ch_ref, cl_ref, cur_ref, high_ref, low_ref, out_ref,
@@ -377,9 +417,8 @@
         joined = jnp.concatenate([q1[pair], q1[pair + 1]], axis=1)
         both = product_of(joined, ch_ref[pair // 2], cl_ref[pair // 2])
         t += [both[:, :RANK], both[:, RANK:]]
-    r = [q0[m] - product(t[m], g[m]) for m in range(4)]
-    joined = jnp.concatenate([r[0] + r[1], r[2] + r[3]], axis=1)
-    th, tl = split(jnp.concatenate([t[0], product_of(joined, ch_ref[2, :, :RANK], cl_ref[2, :, :RANK])], axis=1))
+    above = upper(t, g, q0, ch_ref[2, :, :RANK], cl_ref[2, :, :RANK])
+    th, tl = split(jnp.concatenate([t[0], above], axis=1))
     left = jnp.concatenate([th, tl], axis=0)
     copies = []
     for i, cols in enumerate(spans((2,) * 4, cur_ref.shape[1])):
@@ -435,22 +474,23 @@
 def body(rhs, basis, gen, cap):
     keep, send = first_step(rhs, basis, gen)
     other = swap(send, CORE)
-    keep, caps = nodes_step(cap, keep)
+    keep, u1 = early_step(gen, keep)
     chip = keep + other
     b, c, d = crossed_neighbours(chip, Z_MASKS, Z_MASKS)
-    chip, v1, v0, u3, u2, u1 = load_step(basis, gen, chip)
+    chip, v1, v0, u3, u2 = load_step(basis, gen, chip)
     line = chip + b + c + d
     b, c, d = crossed_neighbours(line, X_MASKS, X_MASKS)
-    line, keep, send, ch, cl = grams_step(rhs, v1, v0, u3, u2, u1, caps, line)
+    line, keep, send = grams_step(rhs, v1, v0, u3, u2, u1, line)
     come = swap(send, CORE)
     lines = jnp.stack([b, c, d, line])
     other = swap(lines, CORE)
+    lines, ch, cl = nodes_step(cap, lines)
     t, chip = middle_step(lines, other, ch, cl, keep, come)
     b, c, d = crossed_neighbours(chip, X_MASKS, Z_MASKS)
     current, chip = low_update(t, rhs, u3, u2, chip)
     part = chip + b + c + d
     b, c, d = crossed_neighbours(part, Z_MASKS, X_MASKS)
-    part, high, low, ch, cl = pairs_step(u1, gen, caps, part)
+    part, high, low, ch, cl = pairs_step(u1, gen, cap, part)
     plane = part + b + c + d
     b, c, d = crossed_neighbours(plane, Y_MASKS, Y_MASKS)
     planes = jnp.stack([b, d, c, plane])

time: 54.6 us -> 54.3 us (level)
    pallas_call x1, Pallas kernels: 4.11 us -> 3.5 us  [load_step(): pl.pallas_call(load_kernel, out_shape=(array(*sent.shape), wide, wide, wi...]
    pallas_call x1 -> x2, Pallas kernels: 1.4 us -> 1.83 us  [the longest x1 1.6 us: early_step(): pl.pallas_call(early_kernel, out_shape=(array(*sent.shape), array(*gen.sh...]
where the time goes in v10:
time: 54.3 us; the launch traced here: 54.2 us
  starting transfers between devices  22.8 us (42%)
  Pallas kernels  18.3 us (34%)
  waiting for transfers between devices  12.7 us (23%)
    ppermute x15, starting transfers between devices, crossed(): lax.ppermute(value, 'leaf', [(i, partner(i)) for i in range(DEVICES)])  20 us
    ppermute x15, waiting for transfers between devices, crossed(): lax.ppermute(value, 'leaf', [(i, partner(i)) for i in range(DEVICES)])  10.3 us
    pallas_call x1, Pallas kernels, first_step(): pl.pallas_call(functools.partial(first_kernel, points), out_shape=(array(...  3.78 us
    pallas_call x1, Pallas kernels, load_step(): pl.pallas_call(load_kernel, out_shape=(array(*sent.shape), wide, wide, wi...  3.5 us
    pallas_call x1, Pallas kernels, grams_step(): pl.pallas_call(grams_kernel, out_shape=(array(*sent.shape), array(SUM_ROW...  3.47 us
    ppermute x4, starting transfers between devices, swap(): return lax.ppermute(value, 'leaf', [(i, i ^ mask) for i in range(DEVICES)])  2.82 us
    ppermute x4, waiting for transfers between devices, swap(): return lax.ppermute(value, 'leaf', [(i, i ^ mask) for i in range(DEVICES)])  2.45 us
    pallas_call x1, Pallas kernels, pairs_step(): pl.pallas_call(pairs_kernel, out_shape=(array(*sent.shape), pair, pair, n...  2.19 us
  transfers between devices with their start and end apart: 19, of which 9 were waited for; matrix products, arithmetic and copies ran while one was open for 0% of the time, Pallas kernels for 22%

profile of v10, /device:TPU:1, one launch (start us, length us, event | category | flops | bytes accessed | tf_op | source)
XLA Modules:
  0.0 54.2 jit_solution(9561059586180731906)
XLA Ops:
  0.0 3.8 %project_low.1 = (f32[128,128]{1,0:T(8,128)S(1)}, f32[128,128]{1,0:T(8,128)S(1)}) custom-call(f32[64,4096]{1,0:T(8,128)} %rhs_ref.5, f32[4,128,4096]{2,1,0:T(8,128)} %basis_ref.3, f32[4,128,4096]{2,1,0:T(8,128)} %gen_ref.7), custom_call_target="tpu_custom_call" | custom-call | flops 800000000 | bytes 7340032 | tf_op jit(solution)/shard_map/project_low/pallas_call | solution.py:145
  3.8 1.5 %collective-permute-start = (f32[128,128]{1,0:T(8,128)S(1)}, f32[128,128]{1,0:T(8,128)S(1)}, u32[]{:S(2)}, u32[]{:S(2)}) collective-permute-start(f32[128,128]{1,0:T(8,128)S(1)} %get-tuple-element.32), channel_id=1, source_target_pairs={{0,1},{1,0},{2,3},{3,2},{4,5},{5,4},{6,7},{7,6},{8,9},{9,8},{10,11... | collective-permute-start | bytes 196616 | tf_op jit(solution)/shard_map/ppermute | solution.py:449
  5.3 1.6 %load_early.1 = (f32[128,128]{1,0:T(8,128)S(1)}, f32[128,4096]{1,0:T(8,128)S(1)}) custom-call(f32[4,128,4096]{2,1,0:T(8,128)} %gen_ref.7, f32[128,128]{1,0:T(8,128)S(1)} %get-tuple-element.29.sent_ref), custom_call_target="tpu_custom_call" | custom-call | flops 1000 | bytes 2097152 | tf_op jit(solution)/shard_map/load_early/pallas_call | solution.py:170
  6.9 3.9 %collective-permute-start.3 = (f32[128,128]{1,0:T(8,128)S(1)}, f32[128,128]{1,0:T(8,128)S(1)}, u32[]{:S(2)}, u32[]{:S(2)}) collective-permute-start(f32[128,128]{1,0:T(8,128)S(1)} %add.30.sent_ref), channel_id=1, source_target_pairs={{0,6},{1,7},{2,4},{3,5},{4,2},{5,3},{6,0},{7,1},{8,14},{9,15},{10,... | collective-permute-start | bytes 196616 | tf_op jit(solution)/shard_map/ppermute | solution.py:461
  10.9 0.9 %collective-permute-start.1 = (f32[128,128]{1,0:T(8,128)S(1)}, f32[128,128]{1,0:T(8,128)S(1)}, u32[]{:S(2)}, u32[]{:S(2)}) collective-permute-start(f32[128,128]{1,0:T(8,128)S(1)} %add.30.sent_ref), channel_id=1, source_target_pairs={{0,3},{1,2},{2,1},{3,0},{4,7},{5,6},{6,5},{7,4},{8,11},{9,10},{10,... | collective-permute-start | bytes 196616 | tf_op jit(solution)/shard_map/ppermute | solution.py:461
  11.8 3.5 %load_high.1 = (f32[128,128]{1,0:T(8,128)S(1)}, f32[128,4096]{1,0:T(8,128)S(1)}, f32[128,4096]{1,0:T(8,128)S(1)}, f32[128,4096]{1,0:T(8,128)S(1)}, f32[128,4096]{1,0:T(8,128)S(1)}) custom-call(f32[4,128,4096]{2,1,0:T(8,128)} %basis_ref.3, f32[4,128,4096]{2,1,0:T(8,128)} %gen_ref.7, f32[128,128]{1,0:T(8,128)S(1)} %add.30.sent_ref), custom_call_target="tpu_custom_call" | custom-call | flops 1000 | bytes 8388608 | tf_op jit(solution)/shard_map/load_high/pallas_call | solution.py:197
  15.3 1.3 %collective-permute-done.2 = f32[128,128]{1,0:T(8,128)S(1)} collective-permute-done((f32[128,128]{1,0:T(8,128)S(1)}, f32[128,128]{1,0:T(8,128)S(1)}, u32[]{:S(2)}, u32[]{:S(2)}) %collective-permute-start.2) | collective-permute-done | bytes 65568 | tf_op jit(solution)/shard_map/ppermute | solution.py:461
  16.7 2.6 %collective-permute-start.6 = (f32[128,128]{1,0:T(8,128)S(1)}, f32[128,128]{1,0:T(8,128)S(1)}, u32[]{:S(2)}, u32[]{:S(2)}) collective-permute-start(f32[128,128]{1,0:T(8,128)S(1)} %add_add_fusion.2.sent_ref), channel_id=1, source_target_pairs={{0,24},{1,25},{2,26},{3,27},{4,28},{5,29},{6,30},{7,31},{8,16},{9,... | collective-permute-start | bytes 196616 | tf_op jit(solution)/shard_map/ppermute | solution.py:461
  19.3 0.8 %collective-permute-start.5 = (f32[128,128]{1,0:T(8,128)S(1)}, f32[128,128]{1,0:T(8,128)S(1)}, u32[]{:S(2)}, u32[]{:S(2)}) collective-permute-start(f32[128,128]{1,0:T(8,128)S(1)} %add_add_fusion.2.sent_ref), channel_id=1, source_target_pairs={{0,17},{1,16},{2,19},{3,18},{4,21},{5,20},{6,23},{7,22},{8,25},{9,... | collective-permute-start | bytes 196616 | tf_op jit(solution)/shard_map/ppermute | solution.py:461
  20.0 0.3 collective-permute-start.4
  20.3 3.5 %grams_high.1 = (f32[128,128]{1,0:T(8,128)S(1)}, f32[320,256]{1,0:T(8,128)S(1)}, f32[320,256]{1,0:T(8,128)S(1)}) custom-call(f32[64,4096]{1,0:T(8,128)S(1)} %copy-done.1, f32[128,4096]{1,0:T(8,128)S(1)} %get-tuple-element.34.v1_ref, f32[128,4096]{1,0:T(8,128)S(1)} %get-tuple-element.35.v0_ref, f32[128,4096]{1,0:T(8,128)S(1)} %get-tuple-element.36.u3_ref, ...), custom_call_target="tpu_custom_call" | custom-call | flops 3200000000 | bytes 11534336 | tf_op jit(solution)/shard_map/grams_high/pallas_call | solution.py:255
  23.8 0.4 collective-permute-start.8
  24.2 0.9 %collective-permute-done.5 = f32[128,128]{1,0:T(8,128)S(1)} collective-permute-done((f32[128,128]{1,0:T(8,128)S(1)}, f32[128,128]{1,0:T(8,128)S(1)}, u32[]{:S(2)}, u32[]{:S(2)}) %collective-permute-start.5) | collective-permute-done | bytes 65568 | tf_op jit(solution)/shard_map/ppermute | solution.py:461
  25.3 0.2 nodes_low.1
  25.5 1.3 %collective-permute-done.7.other_ref = f32[4,128,128]{2,1,0:T(8,128)S(1)} collective-permute-done((f32[4,128,128]{2,1,0:T(8,128)S(1)}, f32[4,128,128]{2,1,0:T(8,128)S(1)}, u32[]{:S(2)}, u32[]{:S(2)}) %collective-permute-start.7) | collective-permute-done | bytes 262176 | tf_op jit(solution)/shard_map/ppermute | solution.py:449
  26.8 0.6 %coefficients_low.1 = (f32[64,256]{1,0:T(8,128)S(1)}, f32[128,128]{1,0:T(8,128)S(1)}) custom-call(f32[4,128,128]{2,1,0:T(8,128)S(1)} %get-tuple-element.39.mine_ref, f32[4,128,128]{2,1,0:T(8,128)S(1)} %collective-permute-done.7.other_ref, bf16[3,256,256]{2,1,0:T(8,128)(2,1)S(1)} %get-tuple-element.40.ch_ref, ...), custom_call_target="tpu_custom_call" | custom-call | flops 120000000 | bytes 1500000 | tf_op jit(solution)/shard_map/coefficients_low/pallas_call | solution.py:336
  27.4 1.7 %collective-permute-start.11 = (f32[128,128]{1,0:T(8,128)S(1)}, f32[128,128]{1,0:T(8,128)S(1)}, u32[]{:S(2)}, u32[]{:S(2)}) collective-permute-start(f32[128,128]{1,0:T(8,128)S(1)} %get-tuple-element.45.sent_ref), channel_id=1, source_target_pairs={{0,24},{1,7},{2,4},{3,27},{4,2},{5,29},{6,30},{7,1},{8,14},{9,17},... | collective-permute-start | bytes 196616 | tf_op jit(solution)/shard_map/ppermute | solution.py:461
  29.2 1.8 %collective-permute-start.9 = (f32[128,128]{1,0:T(8,128)S(1)}, f32[128,128]{1,0:T(8,128)S(1)}, u32[]{:S(2)}, u32[]{:S(2)}) collective-permute-start(f32[128,128]{1,0:T(8,128)S(1)} %get-tuple-element.45.sent_ref), channel_id=1, source_target_pairs={{0,9},{1,2},{2,1},{3,10},{4,7},{5,12},{6,15},{7,4},{8,11},{9,0},{1... | collective-permute-start | bytes 196616 | tf_op jit(solution)/shard_map/ppermute | solution.py:461
  31.0 0.9 %update_low.1 = (f32[64,4096]{1,0:T(8,128)S(1)}, f32[128,128]{1,0:T(8,128)S(1)}) custom-call(f32[64,256]{1,0:T(8,128)S(1)} %get-tuple-element.44.t_ref, f32[64,4096]{1,0:T(8,128)S(1)} %copy-done.1, f32[128,4096]{1,0:T(8,128)S(1)} %get-tuple-element.36.u3_ref, f32[128,4096]{1,0:T(8,128)S(1)} %get-tuple-element.37.u2_ref, ...), custom_call_target="tpu_custom_call" | custom-call | flops 402653184 | bytes 6291456 | tf_op jit(solution)/shard_map/update_low/pallas_call | solution.py:359
  32.1 2.4 %collective-permute-done.10 = f32[128,128]{1,0:T(8,128)S(1)} collective-permute-done((f32[128,128]{1,0:T(8,128)S(1)}, f32[128,128]{1,0:T(8,128)S(1)}, u32[]{:S(2)}, u32[]{:S(2)}) %collective-permute-start.10) | collective-permute-done | bytes 65568 | tf_op jit(solution)/shard_map/ppermute | solution.py:461
  34.5 1.6 %collective-permute-start.14 = (f32[128,128]{1,0:T(8,128)S(1)}, f32[128,128]{1,0:T(8,128)S(1)}, u32[]{:S(2)}, u32[]{:S(2)}) collective-permute-start(f32[128,128]{1,0:T(8,128)S(1)} %add_add_fusion.1.sent_ref), channel_id=1, source_target_pairs={{0,6},{1,25},{2,26},{3,5},{4,28},{5,3},{6,0},{7,31},{8,16},{9,15},... | collective-permute-start | bytes 196616 | tf_op jit(solution)/shard_map/ppermute | solution.py:461
  36.1 1.3 %collective-permute-start.13 = (f32[128,128]{1,0:T(8,128)S(1)}, f32[128,128]{1,0:T(8,128)S(1)}, u32[]{:S(2)}, u32[]{:S(2)}) collective-permute-start(f32[128,128]{1,0:T(8,128)S(1)} %add_add_fusion.1.sent_ref), channel_id=1, source_target_pairs={{0,5},{1,16},{2,19},{3,6},{4,21},{5,0},{6,3},{7,22},{8,25},{9,12},... | collective-permute-start | bytes 196616 | tf_op jit(solution)/shard_map/ppermute | solution.py:461
  37.5 0.7 %collective-permute-start.12 = (f32[128,128]{1,0:T(8,128)S(1)}, f32[128,128]{1,0:T(8,128)S(1)}, u32[]{:S(2)}, u32[]{:S(2)}) collective-permute-start(f32[128,128]{1,0:T(8,128)S(1)} %add_add_fusion.1.sent_ref), channel_id=1, source_target_pairs={{0,3},{1,8},{2,11},{3,0},{4,13},{5,6},{6,5},{7,14},{8,1},{9,10},{1... | collective-permute-start | bytes 196616 | tf_op jit(solution)/shard_map/ppermute | solution.py:461
  38.1 2.2 %pairs_high.1 = (f32[128,128]{1,0:T(8,128)S(1)}, bf16[256,4096]{1,0:T(8,128)(2,1)S(1)}, bf16[256,4096]{1,0:T(8,128)(2,1)S(1)}, bf16[3,256,256]{2,1,0:T(8,128)(2,1)S(1)}, bf16[3,256,256]{2,1,0:T(8,128)(2,1)S(1)}) custom-call(f32[128,4096]{1,0:T(8,128)S(1)} %get-tuple-element.30.u1_ref, f32[4,128,4096]{2,1,0:T(8,128)} %gen_ref.7, f32[15,256,256]{2,1,0:T(8,128)} %cap_ref.3, ...), custom_call_target="tpu_custom_call" | custom-call | flops 100000000 | bytes 8388608 | tf_op jit(solution)/shard_map/pairs_high/pallas_call | solution.py:388
  40.3 1.3 %collective-permute-done.13 = f32[128,128]{1,0:T(8,128)S(1)} collective-permute-done((f32[128,128]{1,0:T(8,128)S(1)}, f32[128,128]{1,0:T(8,128)S(1)}, u32[]{:S(2)}, u32[]{:S(2)}) %collective-permute-start.13) | collective-permute-done | bytes 65568 | tf_op jit(solution)/shard_map/ppermute | solution.py:461
  41.6 3.5 %collective-permute-start.17 = (f32[128,128]{1,0:T(8,128)S(1)}, f32[128,128]{1,0:T(8,128)S(1)}, u32[]{:S(2)}, u32[]{:S(2)}) collective-permute-start(f32[128,128]{1,0:T(8,128)S(1)} %add_add_fusion), channel_id=1, source_target_pairs={{0,65},{1,64},{2,67},{3,66},{4,69},{5,68},{6,71},{7,70},{8,73},{9,... | collective-permute-start | bytes 196616 | tf_op jit(solution)/shard_map/ppermute | solution.py:461
  45.1 0.8 %collective-permute-start.16 = (f32[128,128]{1,0:T(8,128)S(1)}, f32[128,128]{1,0:T(8,128)S(1)}, u32[]{:S(2)}, u32[]{:S(2)}) collective-permute-start(f32[128,128]{1,0:T(8,128)S(1)} %add_add_fusion), channel_id=1, source_target_pairs={{0,96},{1,97},{2,98},{3,99},{4,100},{5,101},{6,102},{7,103},{8,104... | collective-permute-start | bytes 196616 | tf_op jit(solution)/shard_map/ppermute | solution.py:461
  45.9 1.7 %collective-permute-done.17 = f32[128,128]{1,0:T(8,128)S(1)} collective-permute-done((f32[128,128]{1,0:T(8,128)S(1)}, f32[128,128]{1,0:T(8,128)S(1)}, u32[]{:S(2)}, u32[]{:S(2)}) %collective-permute-start.17) | collective-permute-done | bytes 65568 | tf_op jit(solution)/shard_map/ppermute | solution.py:461
  47.6 2.5 %collective-permute-done.16 = f32[128,128]{1,0:T(8,128)S(1)} collective-permute-done((f32[128,128]{1,0:T(8,128)S(1)}, f32[128,128]{1,0:T(8,128)S(1)}, u32[]{:S(2)}, u32[]{:S(2)}) %collective-permute-start.16) | collective-permute-done | bytes 65568 | tf_op jit(solution)/shard_map/ppermute | solution.py:461
  50.2 0.8 %collective-permute-start.18 = (f32[4,128,128]{2,1,0:T(8,128)S(1)}, f32[4,128,128]{2,1,0:T(8,128)S(1)}, u32[]{:S(2)}, u32[]{:S(2)}) collective-permute-start(f32[4,128,128]{2,1,0:T(8,128)S(1)} %pad_maximum_fusion.1.mine_ref), channel_id=1, source_target_pairs={{0,1},{1,0},{2,3},{3,2},{4,5},{5,4},{6,7},{7,6},{8,9},{9,8},{10,11... | collective-permute-start | bytes 786440 | tf_op jit(solution)/shard_map/ppermute | solution.py:449
  51.0 1.2 %collective-permute-done.18.other_ref = f32[4,128,128]{2,1,0:T(8,128)S(1)} collective-permute-done((f32[4,128,128]{2,1,0:T(8,128)S(1)}, f32[4,128,128]{2,1,0:T(8,128)S(1)}, u32[]{:S(2)}, u32[]{:S(2)}) %collective-permute-start.18) | collective-permute-done | bytes 262176 | tf_op jit(solution)/shard_map/ppermute | solution.py:449
  52.1 2.0 %update_high.1 = f32[64,4096]{1,0:T(8,128)} custom-call(f32[4,128,128]{2,1,0:T(8,128)S(1)} %pad_maximum_fusion.1.mine_ref, f32[4,128,128]{2,1,0:T(8,128)S(1)} %collective-permute-done.18.other_ref, bf16[3,256,256]{2,1,0:T(8,128)(2,1)S(1)} %get-tuple-element.48.ch_ref, bf16[3,256,256]{2,1,0:T(8,128)(2,1)S(1)} %get-tuple-element.49.cl_ref, ...), custom_call_target="tpu_custom_call" | custom-call | flops 500000000 | bytes 7000000 | tf_op jit(solution)/shard_map/update_high/pallas_call | solution.py:436
  (25 shorter events, 0.5 us)
Async XLA Ops:
  3.8 3.1 %collective-permute-start = (f32[128,128]{1,0:T(8,128)S(1)}, f32[128,128]{1,0:T(8,128)S(1)}, u32[]{:S(2)}, u32[]{:S(2)}) collective-permute-start(f32[128,128]{1,0:T(8,128)S(1)} %get-tuple-element.32), channel_id=1, source_target_pairs={{0,1},{1,0},{2,3},{3,2},{4,5},{5,4},{6,7},{7,6},{8,9},{9,8},{10,11... | collective-permute-start | bytes 196616 | tf_op jit(solution)/shard_map/ppermute | solution.py:449
  6.9 13.4 %copy-start.1 = (f32[64,4096]{1,0:T(8,128)S(1)}, f32[64,4096]{1,0:T(8,128)}, u32[]{:S(2)}) copy-start(f32[64,4096]{1,0:T(8,128)} %rhs_ref.5) | copy-start | bytes 3145732
  6.9 8.4 %collective-permute-start.3 = (f32[128,128]{1,0:T(8,128)S(1)}, f32[128,128]{1,0:T(8,128)S(1)}, u32[]{:S(2)}, u32[]{:S(2)}) collective-permute-start(f32[128,128]{1,0:T(8,128)S(1)} %add.30.sent_ref), channel_id=1, source_target_pairs={{0,6},{1,7},{2,4},{3,5},{4,2},{5,3},{6,0},{7,1},{8,14},{9,15},{10,... | collective-permute-start | bytes 196616 | tf_op jit(solution)/shard_map/ppermute | solution.py:461
  10.8 5.8 %collective-permute-start.2 = (f32[128,128]{1,0:T(8,128)S(1)}, f32[128,128]{1,0:T(8,128)S(1)}, u32[]{:S(2)}, u32[]{:S(2)}) collective-permute-start(f32[128,128]{1,0:T(8,128)S(1)} %add.30.sent_ref), channel_id=1, source_target_pairs={{0,5},{1,4},{2,7},{3,6},{4,1},{5,0},{6,3},{7,2},{8,13},{9,12},{10,... | collective-permute-start | bytes 196616 | tf_op jit(solution)/shard_map/ppermute | solution.py:461
  10.9 5.8 %collective-permute-start.1 = (f32[128,128]{1,0:T(8,128)S(1)}, f32[128,128]{1,0:T(8,128)S(1)}, u32[]{:S(2)}, u32[]{:S(2)}) collective-permute-start(f32[128,128]{1,0:T(8,128)S(1)} %add.30.sent_ref), channel_id=1, source_target_pairs={{0,3},{1,2},{2,1},{3,0},{4,7},{5,6},{6,5},{7,4},{8,11},{9,10},{10,... | collective-permute-start | bytes 196616 | tf_op jit(solution)/shard_map/ppermute | solution.py:461
  16.7 7.5 %collective-permute-start.6 = (f32[128,128]{1,0:T(8,128)S(1)}, f32[128,128]{1,0:T(8,128)S(1)}, u32[]{:S(2)}, u32[]{:S(2)}) collective-permute-start(f32[128,128]{1,0:T(8,128)S(1)} %add_add_fusion.2.sent_ref), channel_id=1, source_target_pairs={{0,24},{1,25},{2,26},{3,27},{4,28},{5,29},{6,30},{7,31},{8,16},{9,... | collective-permute-start | bytes 196616 | tf_op jit(solution)/shard_map/ppermute | solution.py:461
  19.3 5.9 %collective-permute-start.5 = (f32[128,128]{1,0:T(8,128)S(1)}, f32[128,128]{1,0:T(8,128)S(1)}, u32[]{:S(2)}, u32[]{:S(2)}) collective-permute-start(f32[128,128]{1,0:T(8,128)S(1)} %add_add_fusion.2.sent_ref), channel_id=1, source_target_pairs={{0,17},{1,16},{2,19},{3,18},{4,21},{5,20},{6,23},{7,22},{8,25},{9,... | collective-permute-start | bytes 196616 | tf_op jit(solution)/shard_map/ppermute | solution.py:461
  20.0 5.1 %collective-permute-start.4 = (f32[128,128]{1,0:T(8,128)S(1)}, f32[128,128]{1,0:T(8,128)S(1)}, u32[]{:S(2)}, u32[]{:S(2)}) collective-permute-start(f32[128,128]{1,0:T(8,128)S(1)} %add_add_fusion.2.sent_ref), channel_id=1, source_target_pairs={{0,9},{1,8},{2,11},{3,10},{4,13},{5,12},{6,15},{7,14},{8,1},{9,0},... | collective-permute-start | bytes 196616 | tf_op jit(solution)/shard_map/ppermute | solution.py:461
  20.3 5.0 %copy-start = (f32[15,256,256]{2,1,0:T(8,128)S(1)}, f32[15,256,256]{2,1,0:T(8,128)}, u32[]{:S(2)}) copy-start(f32[15,256,256]{2,1,0:T(8,128)} %cap_ref.3) | copy-start | bytes 11796484
  23.8 3.0 %collective-permute-start.8 = (f32[320,256]{1,0:T(8,128)S(1)}, f32[320,256]{1,0:T(8,128)S(1)}, u32[]{:S(2)}, u32[]{:S(2)}) collective-permute-start(f32[320,256]{1,0:T(8,128)S(1)} %get-tuple-element.43), channel_id=1, source_target_pairs={{0,1},{1,0},{2,3},{3,2},{4,5},{5,4},{6,7},{7,6},{8,9},{9,8},{10,11... | collective-permute-start | bytes 983048 | tf_op jit(solution)/shard_map/ppermute | solution.py:449
  25.2 1.6 %collective-permute-start.7 = (f32[4,128,128]{2,1,0:T(8,128)S(1)}, f32[4,128,128]{2,1,0:T(8,128)S(1)}, u32[]{:S(2)}, u32[]{:S(2)}) collective-permute-start(f32[4,128,128]{2,1,0:T(8,128)S(1)} %pad_maximum_fusion.sent_ref), channel_id=1, source_target_pairs={{0,1},{1,0},{2,3},{3,2},{4,5},{5,4},{6,7},{7,6},{8,9},{9,8},{10,11... | collective-permute-start | bytes 786440 | tf_op jit(solution)/shard_map/ppermute | solution.py:449
  27.4 4.7 %collective-permute-start.11 = (f32[128,128]{1,0:T(8,128)S(1)}, f32[128,128]{1,0:T(8,128)S(1)}, u32[]{:S(2)}, u32[]{:S(2)}) collective-permute-start(f32[128,128]{1,0:T(8,128)S(1)} %get-tuple-element.45.sent_ref), channel_id=1, source_target_pairs={{0,24},{1,7},{2,4},{3,27},{4,2},{5,29},{6,30},{7,1},{8,14},{9,17},... | collective-permute-start | bytes 196616 | tf_op jit(solution)/shard_map/ppermute | solution.py:461
  29.1 5.4 %collective-permute-start.10 = (f32[128,128]{1,0:T(8,128)S(1)}, f32[128,128]{1,0:T(8,128)S(1)}, u32[]{:S(2)}, u32[]{:S(2)}) collective-permute-start(f32[128,128]{1,0:T(8,128)S(1)} %get-tuple-element.45.sent_ref), channel_id=1, source_target_pairs={{0,17},{1,4},{2,7},{3,18},{4,1},{5,20},{6,23},{7,2},{8,13},{9,24},... | collective-permute-start | bytes 196616 | tf_op jit(solution)/shard_map/ppermute | solution.py:461
  29.2 5.3 %collective-permute-start.9 = (f32[128,128]{1,0:T(8,128)S(1)}, f32[128,128]{1,0:T(8,128)S(1)}, u32[]{:S(2)}, u32[]{:S(2)}) collective-permute-start(f32[128,128]{1,0:T(8,128)S(1)} %get-tuple-element.45.sent_ref), channel_id=1, source_target_pairs={{0,9},{1,2},{2,1},{3,10},{4,7},{5,12},{6,15},{7,4},{8,11},{9,0},{1... | collective-permute-start | bytes 196616 | tf_op jit(solution)/shard_map/ppermute | solution.py:461
  34.5 5.8 %collective-permute-start.14 = (f32[128,128]{1,0:T(8,128)S(1)}, f32[128,128]{1,0:T(8,128)S(1)}, u32[]{:S(2)}, u32[]{:S(2)}) collective-permute-start(f32[128,128]{1,0:T(8,128)S(1)} %add_add_fusion.1.sent_ref), channel_id=1, source_target_pairs={{0,6},{1,25},{2,26},{3,5},{4,28},{5,3},{6,0},{7,31},{8,16},{9,15},... | collective-permute-start | bytes 196616 | tf_op jit(solution)/shard_map/ppermute | solution.py:461
  36.1 5.5 %collective-permute-start.13 = (f32[128,128]{1,0:T(8,128)S(1)}, f32[128,128]{1,0:T(8,128)S(1)}, u32[]{:S(2)}, u32[]{:S(2)}) collective-permute-start(f32[128,128]{1,0:T(8,128)S(1)} %add_add_fusion.1.sent_ref), channel_id=1, source_target_pairs={{0,5},{1,16},{2,19},{3,6},{4,21},{5,0},{6,3},{7,22},{8,25},{9,12},... | collective-permute-start | bytes 196616 | tf_op jit(solution)/shard_map/ppermute | solution.py:461
  37.5 4.1 %collective-permute-start.12 = (f32[128,128]{1,0:T(8,128)S(1)}, f32[128,128]{1,0:T(8,128)S(1)}, u32[]{:S(2)}, u32[]{:S(2)}) collective-permute-start(f32[128,128]{1,0:T(8,128)S(1)} %add_add_fusion.1.sent_ref), channel_id=1, source_target_pairs={{0,3},{1,8},{2,11},{3,0},{4,13},{5,6},{6,5},{7,14},{8,1},{9,10},{1... | collective-permute-start | bytes 196616 | tf_op jit(solution)/shard_map/ppermute | solution.py:461
  41.6 6.0 %collective-permute-start.17 = (f32[128,128]{1,0:T(8,128)S(1)}, f32[128,128]{1,0:T(8,128)S(1)}, u32[]{:S(2)}, u32[]{:S(2)}) collective-permute-start(f32[128,128]{1,0:T(8,128)S(1)} %add_add_fusion), channel_id=1, source_target_pairs={{0,65},{1,64},{2,67},{3,66},{4,69},{5,68},{6,71},{7,70},{8,73},{9,... | collective-permute-start | bytes 196616 | tf_op jit(solution)/shard_map/ppermute | solution.py:461
  45.1 5.0 %collective-permute-start.16 = (f32[128,128]{1,0:T(8,128)S(1)}, f32[128,128]{1,0:T(8,128)S(1)}, u32[]{:S(2)}, u32[]{:S(2)}) collective-permute-start(f32[128,128]{1,0:T(8,128)S(1)} %add_add_fusion), channel_id=1, source_target_pairs={{0,96},{1,97},{2,98},{3,99},{4,100},{5,101},{6,102},{7,103},{8,104... | collective-permute-start | bytes 196616 | tf_op jit(solution)/shard_map/ppermute | solution.py:461
  45.9 4.2 %collective-permute-start.15 = (f32[128,128]{1,0:T(8,128)S(1)}, f32[128,128]{1,0:T(8,128)S(1)}, u32[]{:S(2)}, u32[]{:S(2)}) collective-permute-start(f32[128,128]{1,0:T(8,128)S(1)} %add_add_fusion), channel_id=1, source_target_pairs={{0,33},{1,32},{2,35},{3,34},{4,37},{5,36},{6,39},{7,38},{8,41},{9,... | collective-permute-start | bytes 196616 | tf_op jit(solution)/shard_map/ppermute | solution.py:461
  50.2 2.0 %collective-permute-start.18 = (f32[4,128,128]{2,1,0:T(8,128)S(1)}, f32[4,128,128]{2,1,0:T(8,128)S(1)}, u32[]{:S(2)}, u32[]{:S(2)}) collective-permute-start(f32[4,128,128]{2,1,0:T(8,128)S(1)} %pad_maximum_fusion.1.mine_ref), channel_id=1, source_target_pairs={{0,1},{1,0},{2,3},{3,2},{4,5},{5,4},{6,7},{7,6},{8,9},{9,8},{10,11... | collective-permute-start | bytes 786440 | tf_op jit(solution)/shard_map/ppermute | solution.py:449

commit v11 on v10

--- a/solution.py
+++ b/solution.py
@@ -478,7 +478,7 @@
     chip = keep + other
     b, c, d = crossed_neighbours(chip, Z_MASKS, Z_MASKS)
     chip, v1, v0, u3, u2 = load_step(basis, gen, chip)
-    line = chip + b + c + d
+    line = chip + b + d + c
     b, c, d = crossed_neighbours(line, X_MASKS, X_MASKS)
     line, keep, send = grams_step(rhs, v1, v0, u3, u2, u1, line)
     come = swap(send, CORE)

time: 54.3 us -> 54.2 us (level)
  waiting for transfers between devices: 12.7 us -> 11.1 us
  starting transfers between devices: 22.8 us -> 24.3 us
    ppermute x15, waiting for transfers between devices: 10.3 us -> 9.01 us  [crossed(): lax.ppermute(value, 'leaf', [(i, partner(i)) for i in range(DEVICES)])]
    ppermute x4, starting transfers between devices: 2.82 us -> 3.85 us  [swap(): return lax.ppermute(value, 'leaf', [(i, i ^ mask) for i in range(DEVICES)])]
  transfers between devices with their start and end apart: 19 -> 19, of which waited for: 9 -> 7; matrix products, arithmetic and copies ran while one was open for 0% -> 0% of each run, Pallas kernels for 22% -> 22%
where the time goes in v11:
time: 54.2 us; the launch traced here: 54 us
  starting transfers between devices  24.3 us (45%)
  Pallas kernels  18.3 us (34%)
  waiting for transfers between devices  11.1 us (20%)
    ppermute x15, starting transfers between devices, crossed(): lax.ppermute(value, 'leaf', [(i, partner(i)) for i in range(DEVICES)])  20.5 us
    ppermute x15, waiting for transfers between devices, crossed(): lax.ppermute(value, 'leaf', [(i, partner(i)) for i in range(DEVICES)])  9.01 us
    ppermute x4, starting transfers between devices, swap(): return lax.ppermute(value, 'leaf', [(i, i ^ mask) for i in range(DEVICES)])  3.85 us
    pallas_call x1, Pallas kernels, first_step(): pl.pallas_call(functools.partial(first_kernel, points), out_shape=(array(...  3.78 us
    pallas_call x1, Pallas kernels, load_step(): pl.pallas_call(load_kernel, out_shape=(array(*sent.shape), wide, wide, wi...  3.5 us
    pallas_call x1, Pallas kernels, grams_step(): pl.pallas_call(grams_kernel, out_shape=(array(*sent.shape), array(SUM_ROW...  3.47 us
    pallas_call x1, Pallas kernels, pairs_step(): pl.pallas_call(pairs_kernel, out_shape=(array(*sent.shape), pair, pair, n...  2.19 us
    ppermute x4, waiting for transfers between devices, swap(): return lax.ppermute(value, 'leaf', [(i, i ^ mask) for i in range(DEVICES)])  2.11 us
  transfers between devices with their start and end apart: 19, of which 7 were waited for; matrix products, arithmetic and copies ran while one was open for 0% of the time, Pallas kernels for 22%

profile of v11, /device:TPU:1, one launch (start us, length us, event | category | flops | bytes accessed | tf_op | source)
XLA Modules:
  0.0 54.0 jit_solution(11713163392180691576)
XLA Ops:
  0.0 3.8 %project_low.1 = (f32[128,128]{1,0:T(8,128)S(1)}, f32[128,128]{1,0:T(8,128)S(1)}) custom-call(f32[64,4096]{1,0:T(8,128)} %rhs_ref.5, f32[4,128,4096]{2,1,0:T(8,128)} %basis_ref.3, f32[4,128,4096]{2,1,0:T(8,128)} %gen_ref.7), custom_call_target="tpu_custom_call" | custom-call | flops 800000000 | bytes 7340032 | tf_op jit(solution)/shard_map/project_low/pallas_call | solution.py:145
  3.8 1.5 %collective-permute-start = (f32[128,128]{1,0:T(8,128)S(1)}, f32[128,128]{1,0:T(8,128)S(1)}, u32[]{:S(2)}, u32[]{:S(2)}) collective-permute-start(f32[128,128]{1,0:T(8,128)S(1)} %get-tuple-element.32), channel_id=1, source_target_pairs={{0,1},{1,0},{2,3},{3,2},{4,5},{5,4},{6,7},{7,6},{8,9},{9,8},{10,11... | collective-permute-start | bytes 196616 | tf_op jit(solution)/shard_map/ppermute | solution.py:449
  5.3 1.6 %load_early.1 = (f32[128,128]{1,0:T(8,128)S(1)}, f32[128,4096]{1,0:T(8,128)S(1)}) custom-call(f32[4,128,4096]{2,1,0:T(8,128)} %gen_ref.7, f32[128,128]{1,0:T(8,128)S(1)} %get-tuple-element.29.sent_ref), custom_call_target="tpu_custom_call" | custom-call | flops 1000 | bytes 2097152 | tf_op jit(solution)/shard_map/load_early/pallas_call | solution.py:170
  6.9 3.7 %collective-permute-start.3 = (f32[128,128]{1,0:T(8,128)S(1)}, f32[128,128]{1,0:T(8,128)S(1)}, u32[]{:S(2)}, u32[]{:S(2)}) collective-permute-start(f32[128,128]{1,0:T(8,128)S(1)} %add.30.sent_ref), channel_id=1, source_target_pairs={{0,5},{1,4},{2,7},{3,6},{4,1},{5,0},{6,3},{7,2},{8,13},{9,12},{10,... | collective-permute-start | bytes 196616 | tf_op jit(solution)/shard_map/ppermute | solution.py:461
  10.6 0.4 collective-permute-start.2
  11.0 0.7 %collective-permute-start.1 = (f32[128,128]{1,0:T(8,128)S(1)}, f32[128,128]{1,0:T(8,128)S(1)}, u32[]{:S(2)}, u32[]{:S(2)}) collective-permute-start(f32[128,128]{1,0:T(8,128)S(1)} %add.30.sent_ref), channel_id=1, source_target_pairs={{0,3},{1,2},{2,1},{3,0},{4,7},{5,6},{6,5},{7,4},{8,11},{9,10},{10,... | collective-permute-start | bytes 196616 | tf_op jit(solution)/shard_map/ppermute | solution.py:461
  11.7 3.5 %load_high.1 = (f32[128,128]{1,0:T(8,128)S(1)}, f32[128,4096]{1,0:T(8,128)S(1)}, f32[128,4096]{1,0:T(8,128)S(1)}, f32[128,4096]{1,0:T(8,128)S(1)}, f32[128,4096]{1,0:T(8,128)S(1)}) custom-call(f32[4,128,4096]{2,1,0:T(8,128)} %basis_ref.3, f32[4,128,4096]{2,1,0:T(8,128)} %gen_ref.7, f32[128,128]{1,0:T(8,128)S(1)} %add.30.sent_ref), custom_call_target="tpu_custom_call" | custom-call | flops 1000 | bytes 8388608 | tf_op jit(solution)/shard_map/load_high/pallas_call | solution.py:197
  15.2 0.4 collective-permute-done.1
  15.7 2.6 %collective-permute-start.6 = (f32[128,128]{1,0:T(8,128)S(1)}, f32[128,128]{1,0:T(8,128)S(1)}, u32[]{:S(2)}, u32[]{:S(2)}) collective-permute-start(f32[128,128]{1,0:T(8,128)S(1)} %add_add_fusion.2.sent_ref), channel_id=1, source_target_pairs={{0,24},{1,25},{2,26},{3,27},{4,28},{5,29},{6,30},{7,31},{8,16},{9,... | collective-permute-start | bytes 196616 | tf_op jit(solution)/shard_map/ppermute | solution.py:461
  18.2 1.6 %collective-permute-start.5 = (f32[128,128]{1,0:T(8,128)S(1)}, f32[128,128]{1,0:T(8,128)S(1)}, u32[]{:S(2)}, u32[]{:S(2)}) collective-permute-start(f32[128,128]{1,0:T(8,128)S(1)} %add_add_fusion.2.sent_ref), channel_id=1, source_target_pairs={{0,17},{1,16},{2,19},{3,18},{4,21},{5,20},{6,23},{7,22},{8,25},{9,... | collective-permute-start | bytes 196616 | tf_op jit(solution)/shard_map/ppermute | solution.py:461
  19.8 3.5 %grams_high.1 = (f32[128,128]{1,0:T(8,128)S(1)}, f32[320,256]{1,0:T(8,128)S(1)}, f32[320,256]{1,0:T(8,128)S(1)}) custom-call(f32[64,4096]{1,0:T(8,128)S(1)} %copy-done.1, f32[128,4096]{1,0:T(8,128)S(1)} %get-tuple-element.34.v1_ref, f32[128,4096]{1,0:T(8,128)S(1)} %get-tuple-element.35.v0_ref, f32[128,4096]{1,0:T(8,128)S(1)} %get-tuple-element.36.u3_ref, ...), custom_call_target="tpu_custom_call" | custom-call | flops 3200000000 | bytes 11534336 | tf_op jit(solution)/shard_map/grams_high/pallas_call | solution.py:255
  23.3 0.7 %collective-permute-start.8 = (f32[320,256]{1,0:T(8,128)S(1)}, f32[320,256]{1,0:T(8,128)S(1)}, u32[]{:S(2)}, u32[]{:S(2)}) collective-permute-start(f32[320,256]{1,0:T(8,128)S(1)} %get-tuple-element.43), channel_id=1, source_target_pairs={{0,1},{1,0},{2,3},{3,2},{4,5},{5,4},{6,7},{7,6},{8,9},{9,8},{10,11... | collective-permute-start | bytes 983048 | tf_op jit(solution)/shard_map/ppermute | solution.py:449
  24.1 0.8 %collective-permute-start.7 = (f32[4,128,128]{2,1,0:T(8,128)S(1)}, f32[4,128,128]{2,1,0:T(8,128)S(1)}, u32[]{:S(2)}, u32[]{:S(2)}) collective-permute-start(f32[4,128,128]{2,1,0:T(8,128)S(1)} %pad_maximum_fusion.sent_ref), channel_id=1, source_target_pairs={{0,1},{1,0},{2,3},{3,2},{4,5},{5,4},{6,7},{7,6},{8,9},{9,8},{10,11... | collective-permute-start | bytes 786440 | tf_op jit(solution)/shard_map/ppermute | solution.py:449
  25.1 0.9 %collective-permute-done.7.other_ref = f32[4,128,128]{2,1,0:T(8,128)S(1)} collective-permute-done((f32[4,128,128]{2,1,0:T(8,128)S(1)}, f32[4,128,128]{2,1,0:T(8,128)S(1)}, u32[]{:S(2)}, u32[]{:S(2)}) %collective-permute-start.7) | collective-permute-done | bytes 262176 | tf_op jit(solution)/shard_map/ppermute | solution.py:449
  26.1 0.6 %coefficients_low.1 = (f32[64,256]{1,0:T(8,128)S(1)}, f32[128,128]{1,0:T(8,128)S(1)}) custom-call(f32[4,128,128]{2,1,0:T(8,128)S(1)} %get-tuple-element.39.mine_ref, f32[4,128,128]{2,1,0:T(8,128)S(1)} %collective-permute-done.7.other_ref, bf16[3,256,256]{2,1,0:T(8,128)(2,1)S(1)} %get-tuple-element.40.ch_ref, ...), custom_call_target="tpu_custom_call" | custom-call | flops 120000000 | bytes 1500000 | tf_op jit(solution)/shard_map/coefficients_low/pallas_call | solution.py:336
  26.7 2.4 %collective-permute-start.11 = (f32[128,128]{1,0:T(8,128)S(1)}, f32[128,128]{1,0:T(8,128)S(1)}, u32[]{:S(2)}, u32[]{:S(2)}) collective-permute-start(f32[128,128]{1,0:T(8,128)S(1)} %get-tuple-element.45.sent_ref), channel_id=1, source_target_pairs={{0,24},{1,7},{2,4},{3,27},{4,2},{5,29},{6,30},{7,1},{8,14},{9,17},... | collective-permute-start | bytes 196616 | tf_op jit(solution)/shard_map/ppermute | solution.py:461
  29.1 0.3 collective-permute-start.10
  29.4 0.9 %collective-permute-start.9 = (f32[128,128]{1,0:T(8,128)S(1)}, f32[128,128]{1,0:T(8,128)S(1)}, u32[]{:S(2)}, u32[]{:S(2)}) collective-permute-start(f32[128,128]{1,0:T(8,128)S(1)} %get-tuple-element.45.sent_ref), channel_id=1, source_target_pairs={{0,9},{1,2},{2,1},{3,10},{4,7},{5,12},{6,15},{7,4},{8,11},{9,0},{1... | collective-permute-start | bytes 196616 | tf_op jit(solution)/shard_map/ppermute | solution.py:461
  30.3 0.9 %update_low.1 = (f32[64,4096]{1,0:T(8,128)S(1)}, f32[128,128]{1,0:T(8,128)S(1)}) custom-call(f32[64,256]{1,0:T(8,128)S(1)} %get-tuple-element.44.t_ref, f32[64,4096]{1,0:T(8,128)S(1)} %copy-done.1, f32[128,4096]{1,0:T(8,128)S(1)} %get-tuple-element.36.u3_ref, f32[128,4096]{1,0:T(8,128)S(1)} %get-tuple-element.37.u2_ref, ...), custom_call_target="tpu_custom_call" | custom-call | flops 402653184 | bytes 6291456 | tf_op jit(solution)/shard_map/update_low/pallas_call | solution.py:359
  31.3 3.1 %collective-permute-done.10 = f32[128,128]{1,0:T(8,128)S(1)} collective-permute-done((f32[128,128]{1,0:T(8,128)S(1)}, f32[128,128]{1,0:T(8,128)S(1)}, u32[]{:S(2)}, u32[]{:S(2)}) %collective-permute-start.10) | collective-permute-done | bytes 65568 | tf_op jit(solution)/shard_map/ppermute | solution.py:461
  34.3 1.7 %collective-permute-start.14 = (f32[128,128]{1,0:T(8,128)S(1)}, f32[128,128]{1,0:T(8,128)S(1)}, u32[]{:S(2)}, u32[]{:S(2)}) collective-permute-start(f32[128,128]{1,0:T(8,128)S(1)} %add_add_fusion.1.sent_ref), channel_id=1, source_target_pairs={{0,6},{1,25},{2,26},{3,5},{4,28},{5,3},{6,0},{7,31},{8,16},{9,15},... | collective-permute-start | bytes 196616 | tf_op jit(solution)/shard_map/ppermute | solution.py:461
  36.0 1.3 %collective-permute-start.13 = (f32[128,128]{1,0:T(8,128)S(1)}, f32[128,128]{1,0:T(8,128)S(1)}, u32[]{:S(2)}, u32[]{:S(2)}) collective-permute-start(f32[128,128]{1,0:T(8,128)S(1)} %add_add_fusion.1.sent_ref), channel_id=1, source_target_pairs={{0,5},{1,16},{2,19},{3,6},{4,21},{5,0},{6,3},{7,22},{8,25},{9,12},... | collective-permute-start | bytes 196616 | tf_op jit(solution)/shard_map/ppermute | solution.py:461
  37.3 0.6 %collective-permute-start.12 = (f32[128,128]{1,0:T(8,128)S(1)}, f32[128,128]{1,0:T(8,128)S(1)}, u32[]{:S(2)}, u32[]{:S(2)}) collective-permute-start(f32[128,128]{1,0:T(8,128)S(1)} %add_add_fusion.1.sent_ref), channel_id=1, source_target_pairs={{0,3},{1,8},{2,11},{3,0},{4,13},{5,6},{6,5},{7,14},{8,1},{9,10},{1... | collective-permute-start | bytes 196616 | tf_op jit(solution)/shard_map/ppermute | solution.py:461
  38.0 2.2 %pairs_high.1 = (f32[128,128]{1,0:T(8,128)S(1)}, bf16[256,4096]{1,0:T(8,128)(2,1)S(1)}, bf16[256,4096]{1,0:T(8,128)(2,1)S(1)}, bf16[3,256,256]{2,1,0:T(8,128)(2,1)S(1)}, bf16[3,256,256]{2,1,0:T(8,128)(2,1)S(1)}) custom-call(f32[128,4096]{1,0:T(8,128)S(1)} %get-tuple-element.30.u1_ref, f32[4,128,4096]{2,1,0:T(8,128)} %gen_ref.7, f32[15,256,256]{2,1,0:T(8,128)} %cap_ref.3, ...), custom_call_target="tpu_custom_call" | custom-call | flops 100000000 | bytes 8388608 | tf_op jit(solution)/shard_map/pairs_high/pallas_call | solution.py:388
  40.2 1.3 %collective-permute-done.13 = f32[128,128]{1,0:T(8,128)S(1)} collective-permute-done((f32[128,128]{1,0:T(8,128)S(1)}, f32[128,128]{1,0:T(8,128)S(1)}, u32[]{:S(2)}, u32[]{:S(2)}) %collective-permute-start.13) | collective-permute-done | bytes 65568 | tf_op jit(solution)/shard_map/ppermute | solution.py:461
  41.5 3.5 %collective-permute-start.17 = (f32[128,128]{1,0:T(8,128)S(1)}, f32[128,128]{1,0:T(8,128)S(1)}, u32[]{:S(2)}, u32[]{:S(2)}) collective-permute-start(f32[128,128]{1,0:T(8,128)S(1)} %add_add_fusion), channel_id=1, source_target_pairs={{0,65},{1,64},{2,67},{3,66},{4,69},{5,68},{6,71},{7,70},{8,73},{9,... | collective-permute-start | bytes 196616 | tf_op jit(solution)/shard_map/ppermute | solution.py:461
  45.0 0.8 %collective-permute-start.16 = (f32[128,128]{1,0:T(8,128)S(1)}, f32[128,128]{1,0:T(8,128)S(1)}, u32[]{:S(2)}, u32[]{:S(2)}) collective-permute-start(f32[128,128]{1,0:T(8,128)S(1)} %add_add_fusion), channel_id=1, source_target_pairs={{0,96},{1,97},{2,98},{3,99},{4,100},{5,101},{6,102},{7,103},{8,104... | collective-permute-start | bytes 196616 | tf_op jit(solution)/shard_map/ppermute | solution.py:461
  45.8 1.7 %collective-permute-done.17 = f32[128,128]{1,0:T(8,128)S(1)} collective-permute-done((f32[128,128]{1,0:T(8,128)S(1)}, f32[128,128]{1,0:T(8,128)S(1)}, u32[]{:S(2)}, u32[]{:S(2)}) %collective-permute-start.17) | collective-permute-done | bytes 65568 | tf_op jit(solution)/shard_map/ppermute | solution.py:461
  47.5 2.5 %collective-permute-done.16 = f32[128,128]{1,0:T(8,128)S(1)} collective-permute-done((f32[128,128]{1,0:T(8,128)S(1)}, f32[128,128]{1,0:T(8,128)S(1)}, u32[]{:S(2)}, u32[]{:S(2)}) %collective-permute-start.16) | collective-permute-done | bytes 65568 | tf_op jit(solution)/shard_map/ppermute | solution.py:461
  50.0 0.8 %collective-permute-start.18 = (f32[4,128,128]{2,1,0:T(8,128)S(1)}, f32[4,128,128]{2,1,0:T(8,128)S(1)}, u32[]{:S(2)}, u32[]{:S(2)}) collective-permute-start(f32[4,128,128]{2,1,0:T(8,128)S(1)} %pad_maximum_fusion.1.mine_ref), channel_id=1, source_target_pairs={{0,1},{1,0},{2,3},{3,2},{4,5},{5,4},{6,7},{7,6},{8,9},{9,8},{10,11... | collective-permute-start | bytes 786440 | tf_op jit(solution)/shard_map/ppermute | solution.py:449
  50.8 1.2 %collective-permute-done.18.other_ref = f32[4,128,128]{2,1,0:T(8,128)S(1)} collective-permute-done((f32[4,128,128]{2,1,0:T(8,128)S(1)}, f32[4,128,128]{2,1,0:T(8,128)S(1)}, u32[]{:S(2)}, u32[]{:S(2)}) %collective-permute-start.18) | collective-permute-done | bytes 262176 | tf_op jit(solution)/shard_map/ppermute | solution.py:449
  52.0 2.0 %update_high.1 = f32[64,4096]{1,0:T(8,128)} custom-call(f32[4,128,128]{2,1,0:T(8,128)S(1)} %pad_maximum_fusion.1.mine_ref, f32[4,128,128]{2,1,0:T(8,128)S(1)} %collective-permute-done.18.other_ref, bf16[3,256,256]{2,1,0:T(8,128)(2,1)S(1)} %get-tuple-element.48.ch_ref, bf16[3,256,256]{2,1,0:T(8,128)(2,1)S(1)} %get-tuple-element.49.cl_ref, ...), custom_call_target="tpu_custom_call" | custom-call | flops 500000000 | bytes 7000000 | tf_op jit(solution)/shard_map/update_high/pallas_call | solution.py:436
  (25 shorter events, 0.4 us)
Async XLA Ops:
  3.8 3.1 %collective-permute-start = (f32[128,128]{1,0:T(8,128)S(1)}, f32[128,128]{1,0:T(8,128)S(1)}, u32[]{:S(2)}, u32[]{:S(2)}) collective-permute-start(f32[128,128]{1,0:T(8,128)S(1)} %get-tuple-element.32), channel_id=1, source_target_pairs={{0,1},{1,0},{2,3},{3,2},{4,5},{5,4},{6,7},{7,6},{8,9},{9,8},{10,11... | collective-permute-start | bytes 196616 | tf_op jit(solution)/shard_map/ppermute | solution.py:449
  6.9 12.9 %copy-start.1 = (f32[64,4096]{1,0:T(8,128)S(1)}, f32[64,4096]{1,0:T(8,128)}, u32[]{:S(2)}) copy-start(f32[64,4096]{1,0:T(8,128)} %rhs_ref.5) | copy-start | bytes 3145732
  6.9 8.3 %collective-permute-start.3 = (f32[128,128]{1,0:T(8,128)S(1)}, f32[128,128]{1,0:T(8,128)S(1)}, u32[]{:S(2)}, u32[]{:S(2)}) collective-permute-start(f32[128,128]{1,0:T(8,128)S(1)} %add.30.sent_ref), channel_id=1, source_target_pairs={{0,5},{1,4},{2,7},{3,6},{4,1},{5,0},{6,3},{7,2},{8,13},{9,12},{10,... | collective-permute-start | bytes 196616 | tf_op jit(solution)/shard_map/ppermute | solution.py:461
  10.6 4.6 %collective-permute-start.2 = (f32[128,128]{1,0:T(8,128)S(1)}, f32[128,128]{1,0:T(8,128)S(1)}, u32[]{:S(2)}, u32[]{:S(2)}) collective-permute-start(f32[128,128]{1,0:T(8,128)S(1)} %add.30.sent_ref), channel_id=1, source_target_pairs={{0,6},{1,7},{2,4},{3,5},{4,2},{5,3},{6,0},{7,1},{8,14},{9,15},{10,... | collective-permute-start | bytes 196616 | tf_op jit(solution)/shard_map/ppermute | solution.py:461
  11.0 4.6 %collective-permute-start.1 = (f32[128,128]{1,0:T(8,128)S(1)}, f32[128,128]{1,0:T(8,128)S(1)}, u32[]{:S(2)}, u32[]{:S(2)}) collective-permute-start(f32[128,128]{1,0:T(8,128)S(1)} %add.30.sent_ref), channel_id=1, source_target_pairs={{0,3},{1,2},{2,1},{3,0},{4,7},{5,6},{6,5},{7,4},{8,11},{9,10},{10,... | collective-permute-start | bytes 196616 | tf_op jit(solution)/shard_map/ppermute | solution.py:461
  15.7 8.4 %collective-permute-start.6 = (f32[128,128]{1,0:T(8,128)S(1)}, f32[128,128]{1,0:T(8,128)S(1)}, u32[]{:S(2)}, u32[]{:S(2)}) collective-permute-start(f32[128,128]{1,0:T(8,128)S(1)} %add_add_fusion.2.sent_ref), channel_id=1, source_target_pairs={{0,24},{1,25},{2,26},{3,27},{4,28},{5,29},{6,30},{7,31},{8,16},{9,... | collective-permute-start | bytes 196616 | tf_op jit(solution)/shard_map/ppermute | solution.py:461
  18.2 5.8 %collective-permute-start.5 = (f32[128,128]{1,0:T(8,128)S(1)}, f32[128,128]{1,0:T(8,128)S(1)}, u32[]{:S(2)}, u32[]{:S(2)}) collective-permute-start(f32[128,128]{1,0:T(8,128)S(1)} %add_add_fusion.2.sent_ref), channel_id=1, source_target_pairs={{0,17},{1,16},{2,19},{3,18},{4,21},{5,20},{6,23},{7,22},{8,25},{9,... | collective-permute-start | bytes 196616 | tf_op jit(solution)/shard_map/ppermute | solution.py:461
  19.8 4.2 %collective-permute-start.4 = (f32[128,128]{1,0:T(8,128)S(1)}, f32[128,128]{1,0:T(8,128)S(1)}, u32[]{:S(2)}, u32[]{:S(2)}) collective-permute-start(f32[128,128]{1,0:T(8,128)S(1)} %add_add_fusion.2.sent_ref), channel_id=1, source_target_pairs={{0,9},{1,8},{2,11},{3,10},{4,13},{5,12},{6,15},{7,14},{8,1},{9,0},... | collective-permute-start | bytes 196616 | tf_op jit(solution)/shard_map/ppermute | solution.py:461
  19.8 5.1 %copy-start = (f32[15,256,256]{2,1,0:T(8,128)S(1)}, f32[15,256,256]{2,1,0:T(8,128)}, u32[]{:S(2)}) copy-start(f32[15,256,256]{2,1,0:T(8,128)} %cap_ref.3) | copy-start | bytes 11796484
  23.3 2.8 %collective-permute-start.8 = (f32[320,256]{1,0:T(8,128)S(1)}, f32[320,256]{1,0:T(8,128)S(1)}, u32[]{:S(2)}, u32[]{:S(2)}) collective-permute-start(f32[320,256]{1,0:T(8,128)S(1)} %get-tuple-element.43), channel_id=1, source_target_pairs={{0,1},{1,0},{2,3},{3,2},{4,5},{5,4},{6,7},{7,6},{8,9},{9,8},{10,11... | collective-permute-start | bytes 983048 | tf_op jit(solution)/shard_map/ppermute | solution.py:449
  24.1 2.0 %collective-permute-start.7 = (f32[4,128,128]{2,1,0:T(8,128)S(1)}, f32[4,128,128]{2,1,0:T(8,128)S(1)}, u32[]{:S(2)}, u32[]{:S(2)}) collective-permute-start(f32[4,128,128]{2,1,0:T(8,128)S(1)} %pad_maximum_fusion.sent_ref), channel_id=1, source_target_pairs={{0,1},{1,0},{2,3},{3,2},{4,5},{5,4},{6,7},{7,6},{8,9},{9,8},{10,11... | collective-permute-start | bytes 786440 | tf_op jit(solution)/shard_map/ppermute | solution.py:449
  26.7 4.6 %collective-permute-start.11 = (f32[128,128]{1,0:T(8,128)S(1)}, f32[128,128]{1,0:T(8,128)S(1)}, u32[]{:S(2)}, u32[]{:S(2)}) collective-permute-start(f32[128,128]{1,0:T(8,128)S(1)} %get-tuple-element.45.sent_ref), channel_id=1, source_target_pairs={{0,24},{1,7},{2,4},{3,27},{4,2},{5,29},{6,30},{7,1},{8,14},{9,17},... | collective-permute-start | bytes 196616 | tf_op jit(solution)/shard_map/ppermute | solution.py:461
  29.1 5.2 %collective-permute-start.10 = (f32[128,128]{1,0:T(8,128)S(1)}, f32[128,128]{1,0:T(8,128)S(1)}, u32[]{:S(2)}, u32[]{:S(2)}) collective-permute-start(f32[128,128]{1,0:T(8,128)S(1)} %get-tuple-element.45.sent_ref), channel_id=1, source_target_pairs={{0,17},{1,4},{2,7},{3,18},{4,1},{5,20},{6,23},{7,2},{8,13},{9,24},... | collective-permute-start | bytes 196616 | tf_op jit(solution)/shard_map/ppermute | solution.py:461
  29.4 4.9 %collective-permute-start.9 = (f32[128,128]{1,0:T(8,128)S(1)}, f32[128,128]{1,0:T(8,128)S(1)}, u32[]{:S(2)}, u32[]{:S(2)}) collective-permute-start(f32[128,128]{1,0:T(8,128)S(1)} %get-tuple-element.45.sent_ref), channel_id=1, source_target_pairs={{0,9},{1,2},{2,1},{3,10},{4,7},{5,12},{6,15},{7,4},{8,11},{9,0},{1... | collective-permute-start | bytes 196616 | tf_op jit(solution)/shard_map/ppermute | solution.py:461
  34.3 5.8 %collective-permute-start.14 = (f32[128,128]{1,0:T(8,128)S(1)}, f32[128,128]{1,0:T(8,128)S(1)}, u32[]{:S(2)}, u32[]{:S(2)}) collective-permute-start(f32[128,128]{1,0:T(8,128)S(1)} %add_add_fusion.1.sent_ref), channel_id=1, source_target_pairs={{0,6},{1,25},{2,26},{3,5},{4,28},{5,3},{6,0},{7,31},{8,16},{9,15},... | collective-permute-start | bytes 196616 | tf_op jit(solution)/shard_map/ppermute | solution.py:461
  36.0 5.5 %collective-permute-start.13 = (f32[128,128]{1,0:T(8,128)S(1)}, f32[128,128]{1,0:T(8,128)S(1)}, u32[]{:S(2)}, u32[]{:S(2)}) collective-permute-start(f32[128,128]{1,0:T(8,128)S(1)} %add_add_fusion.1.sent_ref), channel_id=1, source_target_pairs={{0,5},{1,16},{2,19},{3,6},{4,21},{5,0},{6,3},{7,22},{8,25},{9,12},... | collective-permute-start | bytes 196616 | tf_op jit(solution)/shard_map/ppermute | solution.py:461
  37.3 4.2 %collective-permute-start.12 = (f32[128,128]{1,0:T(8,128)S(1)}, f32[128,128]{1,0:T(8,128)S(1)}, u32[]{:S(2)}, u32[]{:S(2)}) collective-permute-start(f32[128,128]{1,0:T(8,128)S(1)} %add_add_fusion.1.sent_ref), channel_id=1, source_target_pairs={{0,3},{1,8},{2,11},{3,0},{4,13},{5,6},{6,5},{7,14},{8,1},{9,10},{1... | collective-permute-start | bytes 196616 | tf_op jit(solution)/shard_map/ppermute | solution.py:461
  41.5 6.0 %collective-permute-start.17 = (f32[128,128]{1,0:T(8,128)S(1)}, f32[128,128]{1,0:T(8,128)S(1)}, u32[]{:S(2)}, u32[]{:S(2)}) collective-permute-start(f32[128,128]{1,0:T(8,128)S(1)} %add_add_fusion), channel_id=1, source_target_pairs={{0,65},{1,64},{2,67},{3,66},{4,69},{5,68},{6,71},{7,70},{8,73},{9,... | collective-permute-start | bytes 196616 | tf_op jit(solution)/shard_map/ppermute | solution.py:461
  45.0 5.0 %collective-permute-start.16 = (f32[128,128]{1,0:T(8,128)S(1)}, f32[128,128]{1,0:T(8,128)S(1)}, u32[]{:S(2)}, u32[]{:S(2)}) collective-permute-start(f32[128,128]{1,0:T(8,128)S(1)} %add_add_fusion), channel_id=1, source_target_pairs={{0,96},{1,97},{2,98},{3,99},{4,100},{5,101},{6,102},{7,103},{8,104... | collective-permute-start | bytes 196616 | tf_op jit(solution)/shard_map/ppermute | solution.py:461
  45.8 4.2 %collective-permute-start.15 = (f32[128,128]{1,0:T(8,128)S(1)}, f32[128,128]{1,0:T(8,128)S(1)}, u32[]{:S(2)}, u32[]{:S(2)}) collective-permute-start(f32[128,128]{1,0:T(8,128)S(1)} %add_add_fusion), channel_id=1, source_target_pairs={{0,33},{1,32},{2,35},{3,34},{4,37},{5,36},{6,39},{7,38},{8,41},{9,... | collective-permute-start | bytes 196616 | tf_op jit(solution)/shard_map/ppermute | solution.py:461
  50.0 2.0 %collective-permute-start.18 = (f32[4,128,128]{2,1,0:T(8,128)S(1)}, f32[4,128,128]{2,1,0:T(8,128)S(1)}, u32[]{:S(2)}, u32[]{:S(2)}) collective-permute-start(f32[4,128,128]{2,1,0:T(8,128)S(1)} %pad_maximum_fusion.1.mine_ref), channel_id=1, source_target_pairs={{0,1},{1,0},{2,3},{3,2},{4,5},{5,4},{6,7},{7,6},{8,9},{9,8},{10,11... | collective-permute-start | bytes 786440 | tf_op jit(solution)/shard_map/ppermute | solution.py:449

commit v12 on v11

--- a/solution.py
+++ b/solution.py
@@ -160,7 +160,7 @@
 
 
 def early_kernel(gen_ref, sent_ref, sent_out, u1_ref, sem):
-    copy = pltpu.make_async_copy(gen_ref.at[1], u1_ref, sem)
+    copy = pltpu.make_async_copy(gen_ref.at[1, :RHS], u1_ref, sem)
     copy.start()
     sent_out[...] = sent_ref[...]
     copy.wait()
@@ -169,22 +169,23 @@
 def early_step(gen, sent):
     return pl.pallas_call(
         early_kernel,
-        out_shape=(array(*sent.shape), array(*gen.shape[1:])),
+        out_shape=(array(*sent.shape), array(RHS, gen.shape[2])),
         in_specs=[HBM, VMEM],
         out_specs=(VMEM, VMEM),
         scratch_shapes=[pltpu.SemaphoreType.DMA(())],
         compiler_params=params(LIMITS[7]),
-        cost_estimate=pl.CostEstimate(flops=1_000, bytes_accessed=2_097_152, transcendentals=0),
+        cost_estimate=pl.CostEstimate(flops=1_000, bytes_accessed=1_048_576, transcendentals=0),
         name="load_early",
     )(gen, sent)
 
 
-def load_kernel(basis_ref, gen_ref, sent_ref, sent_out, v1_ref, v0_ref, u3_ref, u2_ref, sems):
+def load_kernel(basis_ref, gen_ref, sent_ref, sent_out, v1_ref, v0_ref, u3_ref, u2_ref, rest_ref, sems):
     sources = [
         (basis_ref, 1, v1_ref), (basis_ref, 0, v0_ref),
         (gen_ref, 3, u3_ref), (gen_ref, 2, u2_ref),
     ]
     copies = [pltpu.make_async_copy(ref.at[k], out, sems.at[i]) for i, (ref, k, out) in enumerate(sources)]
+    copies.append(pltpu.make_async_copy(gen_ref.at[1, RHS:], rest_ref, sems.at[4]))
     for copy in copies:
         copy.start()
     sent_out[...] = sent_ref[...]
@@ -196,10 +197,10 @@
     wide = array(*basis.shape[1:])
     return pl.pallas_call(
         load_kernel,
-        out_shape=(array(*sent.shape), wide, wide, wide, wide),
+        out_shape=(array(*sent.shape), wide, wide, wide, wide, array(RHS, basis.shape[2])),
         in_specs=[HBM, HBM, VMEM],
-        out_specs=(VMEM,) * 5,
-        scratch_shapes=[pltpu.SemaphoreType.DMA((4,))],
+        out_specs=(VMEM,) * 6,
+        scratch_shapes=[pltpu.SemaphoreType.DMA((5,))],
         compiler_params=params(LIMITS[1]),
         cost_estimate=pl.CostEstimate(flops=1_000, bytes_accessed=8_388_608, transcendentals=0),
         name="load_high",
@@ -226,7 +227,7 @@
                 low_ref[i, r * RANK : (r + 1) * RANK, c * RANK : (c + 1) * RANK] = low
 
 
-def grams_kernel(rhs_ref, v1_ref, v0_ref, u3_ref, u2_ref, u1_ref, sent_ref, sent_out,
+def grams_kernel(rhs_ref, v1_ref, v0_ref, u3_ref, u2_ref, u1_ref, rest_ref, sent_ref, sent_out,
                  keep_ref, send_ref):
     sent_out[...] = sent_ref[...]
     _, bit = position()
@@ -244,25 +245,25 @@
         for ref in (keep_ref, send_ref):
             ref[G_AT : G_AT + RANK, cols] = both[RHS:]
             ref[G_AT + RANK : G10_AT, cols] = g2
-    g10 = fold(contract(stacked([u1_ref[...]]), right), RANK)
+    g10 = fold(contract(stacked([u1_ref[...], rest_ref[...]]), right), RANK)
     quarter = RANK // 4
     parts = [jnp.concatenate([g10[i * quarter : (i + 1) * quarter] for i in pair], axis=1) for pair in ((0, 1), (2, 3))]
     keep_ref[G10_AT:] = jnp.where(low_half, parts[0], parts[1])
     send_ref[G10_AT:] = jnp.where(low_half, parts[1], parts[0])
 
 
-def grams_step(rhs, v1, v0, u3, u2, u1, sent):
+def grams_step(rhs, v1, v0, u3, u2, u1, rest, sent):
     return pl.pallas_call(
         grams_kernel,
         out_shape=(
             array(*sent.shape), array(SUM_ROWS, 2 * RANK), array(SUM_ROWS, 2 * RANK),
         ),
-        in_specs=[VMEM] * 7,
+        in_specs=[VMEM] * 8,
         out_specs=(VMEM,) * 3,
         compiler_params=params(LIMITS[2]),
         cost_estimate=pl.CostEstimate(flops=3_200_000_000, bytes_accessed=11_534_336, transcendentals=0),
         name="grams_high",
-    )(rhs, v1, v0, u3, u2, u1, sent)
+    )(rhs, v1, v0, u3, u2, u1, rest, sent)
 
 
 def fetch_nodes(cap_ref, nodes, caps_ref, sems):
@@ -367,7 +368,7 @@
     )(t, rhs, u3, u2, sent)
 
 
-def pairs_kernel(u1_ref, gen_ref, cap_ref, sent_ref, sent_out, high_ref, low_ref, ch_ref, cl_ref,
+def pairs_kernel(u1_ref, rest_ref, gen_ref, cap_ref, sent_ref, sent_out, high_ref, low_ref, ch_ref, cl_ref,
                  u0_ref, caps_ref, sem, sems):
     copy = pltpu.make_async_copy(gen_ref.at[0], u0_ref, sem)
     copy.start()
@@ -375,7 +376,8 @@
     device, bit = position()
     n1 = device >> 6
     copies = fetch_nodes(cap_ref, (1 + n1, 1 + (n1 ^ 1), 0), caps_ref, sems)
-    high_ref[:RANK], low_ref[:RANK] = split(u1_ref[...])
+    high_ref[:RHS], low_ref[:RHS] = split(u1_ref[...])
+    high_ref[RHS:RANK], low_ref[RHS:RANK] = split(rest_ref[...])
     for node in copies:
         node.wait()
     ordered(caps_ref, bit[5], bit[6], ch_ref, cl_ref)
@@ -383,21 +385,21 @@
     high_ref[RANK:], low_ref[RANK:] = split(u0_ref[...])
 
 
-def pairs_step(u1, gen, cap, sent):
+def pairs_step(u1, rest, gen, cap, sent):
     pair, nodes = half_array(2 * RANK, u1.shape[1]), half_array(3, 2 * RANK, 2 * RANK)
     return pl.pallas_call(
         pairs_kernel,
         out_shape=(array(*sent.shape), pair, pair, nodes, nodes),
-        in_specs=[VMEM, HBM, HBM, VMEM],
+        in_specs=[VMEM, VMEM, HBM, HBM, VMEM],
         out_specs=(VMEM,) * 5,
         scratch_shapes=[
-            pltpu.VMEM(u1.shape, F32), pltpu.VMEM((3, 2 * RANK, 2 * RANK), F32),
+            pltpu.VMEM((RANK, u1.shape[1]), F32), pltpu.VMEM((3, 2 * RANK, 2 * RANK), F32),
             pltpu.SemaphoreType.DMA(()), pltpu.SemaphoreType.DMA((3,)),
         ],
         compiler_params=params(LIMITS[5]),
         cost_estimate=pl.CostEstimate(flops=100_000_000, bytes_accessed=8_388_608, transcendentals=0),
         name="pairs_high",
-    )(u1, gen, cap, sent)
+    )(u1, rest, gen, cap, sent)
 
 
 def last_kernel(mine_ref, other_ref, ch_ref, cl_ref, cur_ref, high_ref, low_ref, out_ref,
@@ -477,10 +479,10 @@
     keep, u1 = early_step(gen, keep)
     chip = keep + other
     b, c, d = crossed_neighbours(chip, Z_MASKS, Z_MASKS)
-    chip, v1, v0, u3, u2 = load_step(basis, gen, chip)
+    chip, v1, v0, u3, u2, rest = load_step(basis, gen, chip)
     line = chip + b + d + c
     b, c, d = crossed_neighbours(line, X_MASKS, X_MASKS)
-    line, keep, send = grams_step(rhs, v1, v0, u3, u2, u1, line)
+    line, keep, send = grams_step(rhs, v1, v0, u3, u2, u1, rest, line)
     come = swap(send, CORE)
     lines = jnp.stack([b, c, d, line])
     other = swap(lines, CORE)
@@ -490,7 +492,7 @@
     current, chip = low_update(t, rhs, u3, u2, chip)
     part = chip + b + c + d
     b, c, d = crossed_neighbours(part, Z_MASKS, X_MASKS)
-    part, high, low, ch, cl = pairs_step(u1, gen, cap, part)
+    part, high, low, ch, cl = pairs_step(u1, rest, gen, cap, part)
     plane = part + b + c + d
     b, c, d = crossed_neighbours(plane, Y_MASKS, Y_MASKS)
     planes = jnp.stack([b, d, c, plane])

time: 54.2 us -> 53.8 us (level)
  no operation moved by 1% of the time
where the time goes in v12:
time: 53.8 us; the launch traced here: 53.7 us
  starting transfers between devices  24.3 us (45%)
  Pallas kernels  18.2 us (34%)
  waiting for transfers between devices  10.9 us (20%)
    ppermute x15, starting transfers between devices, crossed(): lax.ppermute(value, 'leaf', [(i, partner(i)) for i in range(DEVICES)])  20.5 us
    ppermute x15, waiting for transfers between devices, crossed(): lax.ppermute(value, 'leaf', [(i, partner(i)) for i in range(DEVICES)])  8.77 us
    ppermute x4, starting transfers between devices, swap(): return lax.ppermute(value, 'leaf', [(i, i ^ mask) for i in range(DEVICES)])  3.85 us
    pallas_call x1, Pallas kernels, first_step(): pl.pallas_call(functools.partial(first_kernel, points), out_shape=(array(...  3.78 us
    pallas_call x1, Pallas kernels, load_step(): pl.pallas_call(load_kernel, out_shape=(array(*sent.shape), wide, wide, wi...  3.73 us
    pallas_call x1, Pallas kernels, grams_step(): pl.pallas_call(grams_kernel, out_shape=(array(*sent.shape), array(SUM_ROW...  3.47 us
    pallas_call x1, Pallas kernels, pairs_step(): pl.pallas_call(pairs_kernel, out_shape=(array(*sent.shape), pair, pair, n...  2.19 us
    ppermute x4, waiting for transfers between devices, swap(): return lax.ppermute(value, 'leaf', [(i, i ^ mask) for i in range(DEVICES)])  2.11 us
  transfers between devices with their start and end apart: 19, of which 7 were waited for; matrix products, arithmetic and copies ran while one was open for 0% of the time, Pallas kernels for 22%

profile of v12, /device:TPU:1, one launch (start us, length us, event | category | flops | bytes accessed | tf_op | source)
XLA Modules:
  0.0 53.7 jit_solution(12011290295336121561)
XLA Ops:
  0.0 3.8 %project_low.1 = (f32[128,128]{1,0:T(8,128)S(1)}, f32[128,128]{1,0:T(8,128)S(1)}) custom-call(f32[64,4096]{1,0:T(8,128)} %rhs_ref.5, f32[4,128,4096]{2,1,0:T(8,128)} %basis_ref.3, f32[4,128,4096]{2,1,0:T(8,128)} %gen_ref.7), custom_call_target="tpu_custom_call" | custom-call | flops 800000000 | bytes 7340032 | tf_op jit(solution)/shard_map/project_low/pallas_call | solution.py:145
  3.8 1.5 %collective-permute-start = (f32[128,128]{1,0:T(8,128)S(1)}, f32[128,128]{1,0:T(8,128)S(1)}, u32[]{:S(2)}, u32[]{:S(2)}) collective-permute-start(f32[128,128]{1,0:T(8,128)S(1)} %get-tuple-element.33), channel_id=1, source_target_pairs={{0,1},{1,0},{2,3},{3,2},{4,5},{5,4},{6,7},{7,6},{8,9},{9,8},{10,11... | collective-permute-start | bytes 196616 | tf_op jit(solution)/shard_map/ppermute | solution.py:451
  5.3 1.2 %load_early.1 = (f32[128,128]{1,0:T(8,128)S(1)}, f32[64,4096]{1,0:T(8,128)S(1)}) custom-call(f32[4,128,4096]{2,1,0:T(8,128)} %gen_ref.7, f32[128,128]{1,0:T(8,128)S(1)} %get-tuple-element.30.sent_ref), custom_call_target="tpu_custom_call" | custom-call | flops 1000 | bytes 1048576 | tf_op jit(solution)/shard_map/load_early/pallas_call | solution.py:170
  6.6 3.7 %collective-permute-start.3 = (f32[128,128]{1,0:T(8,128)S(1)}, f32[128,128]{1,0:T(8,128)S(1)}, u32[]{:S(2)}, u32[]{:S(2)}) collective-permute-start(f32[128,128]{1,0:T(8,128)S(1)} %add.30.sent_ref), channel_id=1, source_target_pairs={{0,5},{1,4},{2,7},{3,6},{4,1},{5,0},{6,3},{7,2},{8,13},{9,12},{10,... | collective-permute-start | bytes 196616 | tf_op jit(solution)/shard_map/ppermute | solution.py:463
  10.2 0.4 collective-permute-start.2
  10.7 0.7 %collective-permute-start.1 = (f32[128,128]{1,0:T(8,128)S(1)}, f32[128,128]{1,0:T(8,128)S(1)}, u32[]{:S(2)}, u32[]{:S(2)}) collective-permute-start(f32[128,128]{1,0:T(8,128)S(1)} %add.30.sent_ref), channel_id=1, source_target_pairs={{0,3},{1,2},{2,1},{3,0},{4,7},{5,6},{6,5},{7,4},{8,11},{9,10},{10,... | collective-permute-start | bytes 196616 | tf_op jit(solution)/shard_map/ppermute | solution.py:463
  11.3 3.7 %load_high.1 = (f32[128,128]{1,0:T(8,128)S(1)}, f32[128,4096]{1,0:T(8,128)S(1)}, f32[128,4096]{1,0:T(8,128)S(1)}, f32[128,4096]{1,0:T(8,128)S(1)}, f32[128,4096]{1,0:T(8,128)S(1)}, /*index=5*/f32[64,4096]{1,0:T(8,128)S(1)}) custom-call(f32[4,128,4096]{2,1,0:T(8,128)} %basis_ref.3, f32[4,128,4096]{2,1,0:T(8,128)} %gen_ref.7, f32[128,128]{1,0:T(8,128)S(1)} %add.30.sent_ref), custom_call_target="tpu_custom_call" | custom-call | flops 1000 | bytes 8388608 | tf_op jit(solution)/shard_map/load_high/pallas_call | solution.py:198
  15.3 2.6 %collective-permute-start.6 = (f32[128,128]{1,0:T(8,128)S(1)}, f32[128,128]{1,0:T(8,128)S(1)}, u32[]{:S(2)}, u32[]{:S(2)}) collective-permute-start(f32[128,128]{1,0:T(8,128)S(1)} %add_add_fusion.2.sent_ref), channel_id=1, source_target_pairs={{0,24},{1,25},{2,26},{3,27},{4,28},{5,29},{6,30},{7,31},{8,16},{9,... | collective-permute-start | bytes 196616 | tf_op jit(solution)/shard_map/ppermute | solution.py:463
  17.8 1.6 %collective-permute-start.5 = (f32[128,128]{1,0:T(8,128)S(1)}, f32[128,128]{1,0:T(8,128)S(1)}, u32[]{:S(2)}, u32[]{:S(2)}) collective-permute-start(f32[128,128]{1,0:T(8,128)S(1)} %add_add_fusion.2.sent_ref), channel_id=1, source_target_pairs={{0,17},{1,16},{2,19},{3,18},{4,21},{5,20},{6,23},{7,22},{8,25},{9,... | collective-permute-start | bytes 196616 | tf_op jit(solution)/shard_map/ppermute | solution.py:463
  19.5 3.5 %grams_high.1 = (f32[128,128]{1,0:T(8,128)S(1)}, f32[320,256]{1,0:T(8,128)S(1)}, f32[320,256]{1,0:T(8,128)S(1)}) custom-call(f32[64,4096]{1,0:T(8,128)S(1)} %copy-done.1, f32[128,4096]{1,0:T(8,128)S(1)} %get-tuple-element.36.v1_ref, f32[128,4096]{1,0:T(8,128)S(1)} %get-tuple-element.37.v0_ref, f32[128,4096]{1,0:T(8,128)S(1)} %get-tuple-element.38.u3_ref, ...), custom_call_target="tpu_custom_call" | custom-call | flops 3200000000 | bytes 11534336 | tf_op jit(solution)/shard_map/grams_high/pallas_call | solution.py:256
  22.9 0.7 %collective-permute-start.8 = (f32[320,256]{1,0:T(8,128)S(1)}, f32[320,256]{1,0:T(8,128)S(1)}, u32[]{:S(2)}, u32[]{:S(2)}) collective-permute-start(f32[320,256]{1,0:T(8,128)S(1)} %get-tuple-element.45), channel_id=1, source_target_pairs={{0,1},{1,0},{2,3},{3,2},{4,5},{5,4},{6,7},{7,6},{8,9},{9,8},{10,11... | collective-permute-start | bytes 983048 | tf_op jit(solution)/shard_map/ppermute | solution.py:451
  23.7 0.8 %collective-permute-start.7 = (f32[4,128,128]{2,1,0:T(8,128)S(1)}, f32[4,128,128]{2,1,0:T(8,128)S(1)}, u32[]{:S(2)}, u32[]{:S(2)}) collective-permute-start(f32[4,128,128]{2,1,0:T(8,128)S(1)} %pad_maximum_fusion.sent_ref), channel_id=1, source_target_pairs={{0,1},{1,0},{2,3},{3,2},{4,5},{5,4},{6,7},{7,6},{8,9},{9,8},{10,11... | collective-permute-start | bytes 786440 | tf_op jit(solution)/shard_map/ppermute | solution.py:451
  24.5 0.2 nodes_low.1
  24.8 0.9 %collective-permute-done.7.other_ref = f32[4,128,128]{2,1,0:T(8,128)S(1)} collective-permute-done((f32[4,128,128]{2,1,0:T(8,128)S(1)}, f32[4,128,128]{2,1,0:T(8,128)S(1)}, u32[]{:S(2)}, u32[]{:S(2)}) %collective-permute-start.7) | collective-permute-done | bytes 262176 | tf_op jit(solution)/shard_map/ppermute | solution.py:451
  25.7 0.6 %coefficients_low.1 = (f32[64,256]{1,0:T(8,128)S(1)}, f32[128,128]{1,0:T(8,128)S(1)}) custom-call(f32[4,128,128]{2,1,0:T(8,128)S(1)} %get-tuple-element.41.mine_ref, f32[4,128,128]{2,1,0:T(8,128)S(1)} %collective-permute-done.7.other_ref, bf16[3,256,256]{2,1,0:T(8,128)(2,1)S(1)} %get-tuple-element.42.ch_ref, ...), custom_call_target="tpu_custom_call" | custom-call | flops 120000000 | bytes 1500000 | tf_op jit(solution)/shard_map/coefficients_low/pallas_call | solution.py:337
  26.3 2.4 %collective-permute-start.11 = (f32[128,128]{1,0:T(8,128)S(1)}, f32[128,128]{1,0:T(8,128)S(1)}, u32[]{:S(2)}, u32[]{:S(2)}) collective-permute-start(f32[128,128]{1,0:T(8,128)S(1)} %get-tuple-element.47.sent_ref), channel_id=1, source_target_pairs={{0,24},{1,7},{2,4},{3,27},{4,2},{5,29},{6,30},{7,1},{8,14},{9,17},... | collective-permute-start | bytes 196616 | tf_op jit(solution)/shard_map/ppermute | solution.py:463
  28.7 0.6 %collective-permute-start.10 = (f32[128,128]{1,0:T(8,128)S(1)}, f32[128,128]{1,0:T(8,128)S(1)}, u32[]{:S(2)}, u32[]{:S(2)}) collective-permute-start(f32[128,128]{1,0:T(8,128)S(1)} %get-tuple-element.47.sent_ref), channel_id=1, source_target_pairs={{0,17},{1,4},{2,7},{3,18},{4,1},{5,20},{6,23},{7,2},{8,13},{9,24},... | collective-permute-start | bytes 196616 | tf_op jit(solution)/shard_map/ppermute | solution.py:463
  29.3 0.7 %collective-permute-start.9 = (f32[128,128]{1,0:T(8,128)S(1)}, f32[128,128]{1,0:T(8,128)S(1)}, u32[]{:S(2)}, u32[]{:S(2)}) collective-permute-start(f32[128,128]{1,0:T(8,128)S(1)} %get-tuple-element.47.sent_ref), channel_id=1, source_target_pairs={{0,9},{1,2},{2,1},{3,10},{4,7},{5,12},{6,15},{7,4},{8,11},{9,0},{1... | collective-permute-start | bytes 196616 | tf_op jit(solution)/shard_map/ppermute | solution.py:463
  29.9 0.9 %update_low.1 = (f32[64,4096]{1,0:T(8,128)S(1)}, f32[128,128]{1,0:T(8,128)S(1)}) custom-call(f32[64,256]{1,0:T(8,128)S(1)} %get-tuple-element.46.t_ref, f32[64,4096]{1,0:T(8,128)S(1)} %copy-done.1, f32[128,4096]{1,0:T(8,128)S(1)} %get-tuple-element.38.u3_ref, f32[128,4096]{1,0:T(8,128)S(1)} %get-tuple-element.39.u2_ref, ...), custom_call_target="tpu_custom_call" | custom-call | flops 402653184 | bytes 6291456 | tf_op jit(solution)/shard_map/update_low/pallas_call | solution.py:360
  30.9 3.1 %collective-permute-done.10 = f32[128,128]{1,0:T(8,128)S(1)} collective-permute-done((f32[128,128]{1,0:T(8,128)S(1)}, f32[128,128]{1,0:T(8,128)S(1)}, u32[]{:S(2)}, u32[]{:S(2)}) %collective-permute-start.10) | collective-permute-done | bytes 65568 | tf_op jit(solution)/shard_map/ppermute | solution.py:463
  34.0 1.7 %collective-permute-start.14 = (f32[128,128]{1,0:T(8,128)S(1)}, f32[128,128]{1,0:T(8,128)S(1)}, u32[]{:S(2)}, u32[]{:S(2)}) collective-permute-start(f32[128,128]{1,0:T(8,128)S(1)} %add_add_fusion.1.sent_ref), channel_id=1, source_target_pairs={{0,6},{1,25},{2,26},{3,5},{4,28},{5,3},{6,0},{7,31},{8,16},{9,15},... | collective-permute-start | bytes 196616 | tf_op jit(solution)/shard_map/ppermute | solution.py:463
  35.6 1.3 %collective-permute-start.13 = (f32[128,128]{1,0:T(8,128)S(1)}, f32[128,128]{1,0:T(8,128)S(1)}, u32[]{:S(2)}, u32[]{:S(2)}) collective-permute-start(f32[128,128]{1,0:T(8,128)S(1)} %add_add_fusion.1.sent_ref), channel_id=1, source_target_pairs={{0,5},{1,16},{2,19},{3,6},{4,21},{5,0},{6,3},{7,22},{8,25},{9,12},... | collective-permute-start | bytes 196616 | tf_op jit(solution)/shard_map/ppermute | solution.py:463
  37.0 0.6 %collective-permute-start.12 = (f32[128,128]{1,0:T(8,128)S(1)}, f32[128,128]{1,0:T(8,128)S(1)}, u32[]{:S(2)}, u32[]{:S(2)}) collective-permute-start(f32[128,128]{1,0:T(8,128)S(1)} %add_add_fusion.1.sent_ref), channel_id=1, source_target_pairs={{0,3},{1,8},{2,11},{3,0},{4,13},{5,6},{6,5},{7,14},{8,1},{9,10},{1... | collective-permute-start | bytes 196616 | tf_op jit(solution)/shard_map/ppermute | solution.py:463
  37.6 2.2 %pairs_high.1 = (f32[128,128]{1,0:T(8,128)S(1)}, bf16[256,4096]{1,0:T(8,128)(2,1)S(1)}, bf16[256,4096]{1,0:T(8,128)(2,1)S(1)}, bf16[3,256,256]{2,1,0:T(8,128)(2,1)S(1)}, bf16[3,256,256]{2,1,0:T(8,128)(2,1)S(1)}) custom-call(f32[64,4096]{1,0:T(8,128)S(1)} %get-tuple-element.31.u1_ref, f32[64,4096]{1,0:T(8,128)S(1)} %get-tuple-element.34.rest_ref, ...), custom_call_target="tpu_custom_call" | custom-call | flops 100000000 | bytes 8388608 | tf_op jit(solution)/shard_map/pairs_high/pallas_call | solution.py:390
  39.8 1.3 %collective-permute-done.13 = f32[128,128]{1,0:T(8,128)S(1)} collective-permute-done((f32[128,128]{1,0:T(8,128)S(1)}, f32[128,128]{1,0:T(8,128)S(1)}, u32[]{:S(2)}, u32[]{:S(2)}) %collective-permute-start.13) | collective-permute-done | bytes 65568 | tf_op jit(solution)/shard_map/ppermute | solution.py:463
  41.1 3.5 %collective-permute-start.17 = (f32[128,128]{1,0:T(8,128)S(1)}, f32[128,128]{1,0:T(8,128)S(1)}, u32[]{:S(2)}, u32[]{:S(2)}) collective-permute-start(f32[128,128]{1,0:T(8,128)S(1)} %add_add_fusion), channel_id=1, source_target_pairs={{0,65},{1,64},{2,67},{3,66},{4,69},{5,68},{6,71},{7,70},{8,73},{9,... | collective-permute-start | bytes 196616 | tf_op jit(solution)/shard_map/ppermute | solution.py:463
  44.7 0.8 %collective-permute-start.16 = (f32[128,128]{1,0:T(8,128)S(1)}, f32[128,128]{1,0:T(8,128)S(1)}, u32[]{:S(2)}, u32[]{:S(2)}) collective-permute-start(f32[128,128]{1,0:T(8,128)S(1)} %add_add_fusion), channel_id=1, source_target_pairs={{0,96},{1,97},{2,98},{3,99},{4,100},{5,101},{6,102},{7,103},{8,104... | collective-permute-start | bytes 196616 | tf_op jit(solution)/shard_map/ppermute | solution.py:463
  45.4 1.7 %collective-permute-done.17 = f32[128,128]{1,0:T(8,128)S(1)} collective-permute-done((f32[128,128]{1,0:T(8,128)S(1)}, f32[128,128]{1,0:T(8,128)S(1)}, u32[]{:S(2)}, u32[]{:S(2)}) %collective-permute-start.17) | collective-permute-done | bytes 65568 | tf_op jit(solution)/shard_map/ppermute | solution.py:463
  47.1 2.5 %collective-permute-done.16 = f32[128,128]{1,0:T(8,128)S(1)} collective-permute-done((f32[128,128]{1,0:T(8,128)S(1)}, f32[128,128]{1,0:T(8,128)S(1)}, u32[]{:S(2)}, u32[]{:S(2)}) %collective-permute-start.16) | collective-permute-done | bytes 65568 | tf_op jit(solution)/shard_map/ppermute | solution.py:463
  49.7 0.8 %collective-permute-start.18 = (f32[4,128,128]{2,1,0:T(8,128)S(1)}, f32[4,128,128]{2,1,0:T(8,128)S(1)}, u32[]{:S(2)}, u32[]{:S(2)}) collective-permute-start(f32[4,128,128]{2,1,0:T(8,128)S(1)} %pad_maximum_fusion.1.mine_ref), channel_id=1, source_target_pairs={{0,1},{1,0},{2,3},{3,2},{4,5},{5,4},{6,7},{7,6},{8,9},{9,8},{10,11... | collective-permute-start | bytes 786440 | tf_op jit(solution)/shard_map/ppermute | solution.py:451
  50.5 1.2 %collective-permute-done.18.other_ref = f32[4,128,128]{2,1,0:T(8,128)S(1)} collective-permute-done((f32[4,128,128]{2,1,0:T(8,128)S(1)}, f32[4,128,128]{2,1,0:T(8,128)S(1)}, u32[]{:S(2)}, u32[]{:S(2)}) %collective-permute-start.18) | collective-permute-done | bytes 262176 | tf_op jit(solution)/shard_map/ppermute | solution.py:451
  51.6 2.0 %update_high.1 = f32[64,4096]{1,0:T(8,128)} custom-call(f32[4,128,128]{2,1,0:T(8,128)S(1)} %pad_maximum_fusion.1.mine_ref, f32[4,128,128]{2,1,0:T(8,128)S(1)} %collective-permute-done.18.other_ref, bf16[3,256,256]{2,1,0:T(8,128)(2,1)S(1)} %get-tuple-element.50.ch_ref, bf16[3,256,256]{2,1,0:T(8,128)(2,1)S(1)} %get-tuple-element.51.cl_ref, ...), custom_call_target="tpu_custom_call" | custom-call | flops 500000000 | bytes 7000000 | tf_op jit(solution)/shard_map/update_high/pallas_call | solution.py:438
  (25 shorter events, 0.3 us)
Async XLA Ops:
  3.8 2.7 %collective-permute-start = (f32[128,128]{1,0:T(8,128)S(1)}, f32[128,128]{1,0:T(8,128)S(1)}, u32[]{:S(2)}, u32[]{:S(2)}) collective-permute-start(f32[128,128]{1,0:T(8,128)S(1)} %get-tuple-element.33), channel_id=1, source_target_pairs={{0,1},{1,0},{2,3},{3,2},{4,5},{5,4},{6,7},{7,6},{8,9},{9,8},{10,11... | collective-permute-start | bytes 196616 | tf_op jit(solution)/shard_map/ppermute | solution.py:451
  6.5 12.9 %copy-start.1 = (f32[64,4096]{1,0:T(8,128)S(1)}, f32[64,4096]{1,0:T(8,128)}, u32[]{:S(2)}) copy-start(f32[64,4096]{1,0:T(8,128)} %rhs_ref.5) | copy-start | bytes 3145732
  6.6 8.5 %collective-permute-start.3 = (f32[128,128]{1,0:T(8,128)S(1)}, f32[128,128]{1,0:T(8,128)S(1)}, u32[]{:S(2)}, u32[]{:S(2)}) collective-permute-start(f32[128,128]{1,0:T(8,128)S(1)} %add.30.sent_ref), channel_id=1, source_target_pairs={{0,5},{1,4},{2,7},{3,6},{4,1},{5,0},{6,3},{7,2},{8,13},{9,12},{10,... | collective-permute-start | bytes 196616 | tf_op jit(solution)/shard_map/ppermute | solution.py:463
  10.2 4.9 %collective-permute-start.2 = (f32[128,128]{1,0:T(8,128)S(1)}, f32[128,128]{1,0:T(8,128)S(1)}, u32[]{:S(2)}, u32[]{:S(2)}) collective-permute-start(f32[128,128]{1,0:T(8,128)S(1)} %add.30.sent_ref), channel_id=1, source_target_pairs={{0,6},{1,7},{2,4},{3,5},{4,2},{5,3},{6,0},{7,1},{8,14},{9,15},{10,... | collective-permute-start | bytes 196616 | tf_op jit(solution)/shard_map/ppermute | solution.py:463
  10.7 4.6 %collective-permute-start.1 = (f32[128,128]{1,0:T(8,128)S(1)}, f32[128,128]{1,0:T(8,128)S(1)}, u32[]{:S(2)}, u32[]{:S(2)}) collective-permute-start(f32[128,128]{1,0:T(8,128)S(1)} %add.30.sent_ref), channel_id=1, source_target_pairs={{0,3},{1,2},{2,1},{3,0},{4,7},{5,6},{6,5},{7,4},{8,11},{9,10},{10,... | collective-permute-start | bytes 196616 | tf_op jit(solution)/shard_map/ppermute | solution.py:463
  15.3 8.4 %collective-permute-start.6 = (f32[128,128]{1,0:T(8,128)S(1)}, f32[128,128]{1,0:T(8,128)S(1)}, u32[]{:S(2)}, u32[]{:S(2)}) collective-permute-start(f32[128,128]{1,0:T(8,128)S(1)} %add_add_fusion.2.sent_ref), channel_id=1, source_target_pairs={{0,24},{1,25},{2,26},{3,27},{4,28},{5,29},{6,30},{7,31},{8,16},{9,... | collective-permute-start | bytes 196616 | tf_op jit(solution)/shard_map/ppermute | solution.py:463
  17.8 5.8 %collective-permute-start.5 = (f32[128,128]{1,0:T(8,128)S(1)}, f32[128,128]{1,0:T(8,128)S(1)}, u32[]{:S(2)}, u32[]{:S(2)}) collective-permute-start(f32[128,128]{1,0:T(8,128)S(1)} %add_add_fusion.2.sent_ref), channel_id=1, source_target_pairs={{0,17},{1,16},{2,19},{3,18},{4,21},{5,20},{6,23},{7,22},{8,25},{9,... | collective-permute-start | bytes 196616 | tf_op jit(solution)/shard_map/ppermute | solution.py:463
  19.5 4.2 %collective-permute-start.4 = (f32[128,128]{1,0:T(8,128)S(1)}, f32[128,128]{1,0:T(8,128)S(1)}, u32[]{:S(2)}, u32[]{:S(2)}) collective-permute-start(f32[128,128]{1,0:T(8,128)S(1)} %add_add_fusion.2.sent_ref), channel_id=1, source_target_pairs={{0,9},{1,8},{2,11},{3,10},{4,13},{5,12},{6,15},{7,14},{8,1},{9,0},... | collective-permute-start | bytes 196616 | tf_op jit(solution)/shard_map/ppermute | solution.py:463
  19.5 5.1 %copy-start = (f32[15,256,256]{2,1,0:T(8,128)S(1)}, f32[15,256,256]{2,1,0:T(8,128)}, u32[]{:S(2)}) copy-start(f32[15,256,256]{2,1,0:T(8,128)} %cap_ref.3) | copy-start | bytes 11796484
  22.9 2.8 %collective-permute-start.8 = (f32[320,256]{1,0:T(8,128)S(1)}, f32[320,256]{1,0:T(8,128)S(1)}, u32[]{:S(2)}, u32[]{:S(2)}) collective-permute-start(f32[320,256]{1,0:T(8,128)S(1)} %get-tuple-element.45), channel_id=1, source_target_pairs={{0,1},{1,0},{2,3},{3,2},{4,5},{5,4},{6,7},{7,6},{8,9},{9,8},{10,11... | collective-permute-start | bytes 983048 | tf_op jit(solution)/shard_map/ppermute | solution.py:451
  23.7 2.0 %collective-permute-start.7 = (f32[4,128,128]{2,1,0:T(8,128)S(1)}, f32[4,128,128]{2,1,0:T(8,128)S(1)}, u32[]{:S(2)}, u32[]{:S(2)}) collective-permute-start(f32[4,128,128]{2,1,0:T(8,128)S(1)} %pad_maximum_fusion.sent_ref), channel_id=1, source_target_pairs={{0,1},{1,0},{2,3},{3,2},{4,5},{5,4},{6,7},{7,6},{8,9},{9,8},{10,11... | collective-permute-start | bytes 786440 | tf_op jit(solution)/shard_map/ppermute | solution.py:451
  26.3 4.6 %collective-permute-start.11 = (f32[128,128]{1,0:T(8,128)S(1)}, f32[128,128]{1,0:T(8,128)S(1)}, u32[]{:S(2)}, u32[]{:S(2)}) collective-permute-start(f32[128,128]{1,0:T(8,128)S(1)} %get-tuple-element.47.sent_ref), channel_id=1, source_target_pairs={{0,24},{1,7},{2,4},{3,27},{4,2},{5,29},{6,30},{7,1},{8,14},{9,17},... | collective-permute-start | bytes 196616 | tf_op jit(solution)/shard_map/ppermute | solution.py:463
  28.7 5.2 %collective-permute-start.10 = (f32[128,128]{1,0:T(8,128)S(1)}, f32[128,128]{1,0:T(8,128)S(1)}, u32[]{:S(2)}, u32[]{:S(2)}) collective-permute-start(f32[128,128]{1,0:T(8,128)S(1)} %get-tuple-element.47.sent_ref), channel_id=1, source_target_pairs={{0,17},{1,4},{2,7},{3,18},{4,1},{5,20},{6,23},{7,2},{8,13},{9,24},... | collective-permute-start | bytes 196616 | tf_op jit(solution)/shard_map/ppermute | solution.py:463
  29.3 4.7 %collective-permute-start.9 = (f32[128,128]{1,0:T(8,128)S(1)}, f32[128,128]{1,0:T(8,128)S(1)}, u32[]{:S(2)}, u32[]{:S(2)}) collective-permute-start(f32[128,128]{1,0:T(8,128)S(1)} %get-tuple-element.47.sent_ref), channel_id=1, source_target_pairs={{0,9},{1,2},{2,1},{3,10},{4,7},{5,12},{6,15},{7,4},{8,11},{9,0},{1... | collective-permute-start | bytes 196616 | tf_op jit(solution)/shard_map/ppermute | solution.py:463
  34.0 5.8 %collective-permute-start.14 = (f32[128,128]{1,0:T(8,128)S(1)}, f32[128,128]{1,0:T(8,128)S(1)}, u32[]{:S(2)}, u32[]{:S(2)}) collective-permute-start(f32[128,128]{1,0:T(8,128)S(1)} %add_add_fusion.1.sent_ref), channel_id=1, source_target_pairs={{0,6},{1,25},{2,26},{3,5},{4,28},{5,3},{6,0},{7,31},{8,16},{9,15},... | collective-permute-start | bytes 196616 | tf_op jit(solution)/shard_map/ppermute | solution.py:463
  35.6 5.5 %collective-permute-start.13 = (f32[128,128]{1,0:T(8,128)S(1)}, f32[128,128]{1,0:T(8,128)S(1)}, u32[]{:S(2)}, u32[]{:S(2)}) collective-permute-start(f32[128,128]{1,0:T(8,128)S(1)} %add_add_fusion.1.sent_ref), channel_id=1, source_target_pairs={{0,5},{1,16},{2,19},{3,6},{4,21},{5,0},{6,3},{7,22},{8,25},{9,12},... | collective-permute-start | bytes 196616 | tf_op jit(solution)/shard_map/ppermute | solution.py:463
  37.0 4.2 %collective-permute-start.12 = (f32[128,128]{1,0:T(8,128)S(1)}, f32[128,128]{1,0:T(8,128)S(1)}, u32[]{:S(2)}, u32[]{:S(2)}) collective-permute-start(f32[128,128]{1,0:T(8,128)S(1)} %add_add_fusion.1.sent_ref), channel_id=1, source_target_pairs={{0,3},{1,8},{2,11},{3,0},{4,13},{5,6},{6,5},{7,14},{8,1},{9,10},{1... | collective-permute-start | bytes 196616 | tf_op jit(solution)/shard_map/ppermute | solution.py:463
  41.1 6.0 %collective-permute-start.17 = (f32[128,128]{1,0:T(8,128)S(1)}, f32[128,128]{1,0:T(8,128)S(1)}, u32[]{:S(2)}, u32[]{:S(2)}) collective-permute-start(f32[128,128]{1,0:T(8,128)S(1)} %add_add_fusion), channel_id=1, source_target_pairs={{0,65},{1,64},{2,67},{3,66},{4,69},{5,68},{6,71},{7,70},{8,73},{9,... | collective-permute-start | bytes 196616 | tf_op jit(solution)/shard_map/ppermute | solution.py:463
  44.7 5.0 %collective-permute-start.16 = (f32[128,128]{1,0:T(8,128)S(1)}, f32[128,128]{1,0:T(8,128)S(1)}, u32[]{:S(2)}, u32[]{:S(2)}) collective-permute-start(f32[128,128]{1,0:T(8,128)S(1)} %add_add_fusion), channel_id=1, source_target_pairs={{0,96},{1,97},{2,98},{3,99},{4,100},{5,101},{6,102},{7,103},{8,104... | collective-permute-start | bytes 196616 | tf_op jit(solution)/shard_map/ppermute | solution.py:463
  45.4 4.2 %collective-permute-start.15 = (f32[128,128]{1,0:T(8,128)S(1)}, f32[128,128]{1,0:T(8,128)S(1)}, u32[]{:S(2)}, u32[]{:S(2)}) collective-permute-start(f32[128,128]{1,0:T(8,128)S(1)} %add_add_fusion), channel_id=1, source_target_pairs={{0,33},{1,32},{2,35},{3,34},{4,37},{5,36},{6,39},{7,38},{8,41},{9,... | collective-permute-start | bytes 196616 | tf_op jit(solution)/shard_map/ppermute | solution.py:463
  49.7 2.0 %collective-permute-start.18 = (f32[4,128,128]{2,1,0:T(8,128)S(1)}, f32[4,128,128]{2,1,0:T(8,128)S(1)}, u32[]{:S(2)}, u32[]{:S(2)}) collective-permute-start(f32[4,128,128]{2,1,0:T(8,128)S(1)} %pad_maximum_fusion.1.mine_ref), channel_id=1, source_target_pairs={{0,1},{1,0},{2,3},{3,2},{4,5},{5,4},{6,7},{7,6},{8,9},{9,8},{10,11... | collective-permute-start | bytes 786440 | tf_op jit(solution)/shard_map/ppermute | solution.py:451
